TPU v7x, 256 devices: a whole 4x4x8 slice. The times are simulated.
256 devices in a mesh: shard: 16 (over z_hi, y), example: 16 (over z_lo, x, core).
Axes of the slice: x: 4, y: 4, z: 8 (z_hi: 4, z_lo: 2; z = z_hi * 2 + z_lo), core: 2. Of those that a mesh axis runs over, the one named last changes fastest.
Arguments:
- train_in: bfloat16 [16, 512, 5120], P('example', 'shard'), may hold values from -6 to 6
- train_grad: bfloat16 [16, 512, 6912], P('example', 'shard'), may hold values from -6 to 6
- seq_lens: int32 [16], P('example'), may hold values from 128 to 512
- basis_in: bfloat16 [5120, 5120], P(None, 'shard'), may hold values from -0.078125 to 0.078125
- basis_out: bfloat16 [6912, 6912], P(None, 'example'), may hold values from -0.078125 to 0.078125
- eigvals: float32 [5120, 6912], P('shard', 'example'), may hold values from 0.01 to 90, as said below
- query_in: bfloat16 [32, 32, 5120], P('example'), may hold values from -6 to 6
- query_out: bfloat16 [32, 32, 6912], P('shard'), may hold values from -6 to 6
Outputs:
- scores: float32 [32, 16], P('shard', 'example')
Inputs may be any that keep to these rules, and one draw needn't show every extreme that they name: `eigvals`: positive.
All inputs are finite; a program needn't handle non-finite values.
Results may differ from a plain program's by a relative error of at most 0.0051.
Values may be sent and summed in bfloat16 or wider, within the bound.
No kernel may reach another device: no remote copies, remote signals or barrier semaphores. Data moves between devices by JAX's collectives and lax.ppermute only.
A program may use at most 128 MiB of HBM per device.

v0:
```python
import math

import jax
import jax.numpy as jnp
from jax import lax
from jax.experimental import pallas as pl
from jax.experimental.pallas import tpu as pltpu
from jax.sharding import PartitionSpec as P

D = 5120
H = 6912
SEQLEN = 512
RANK = 32
NSEQ = 16
QUERIES = 32
BF16 = jnp.bfloat16
F32 = jnp.float32

SHARD_Y = {d: [(i, i // 4 * 4 + (i + d) % 4) for i in range(16)] for d in (1, -1, 2)}
SHARD_Z = {d: [(i, (i + 4 * d) % 16) for i in range(16)] for d in (1, -1)}
EXAMPLE_X = {d: [(i, i // 8 * 8 + (i + 2 * d) % 8) for i in range(16)] for d in (1, -1)}
EXAMPLE_CORE = [(i, i ^ 1) for i in range(16)]
EXAMPLE_Z = [(i, i ^ 8) for i in range(16)]
AWAY = (0, -1, 1, 2)


def ring4(block, axis, steps):
    half = block.shape[0] // 2
    below = lax.ppermute(block, axis, steps[1])
    above = lax.ppermute(block, axis, steps[-1])
    far_top = lax.ppermute(below[:half], axis, steps[1])
    far_bottom = lax.ppermute(above[half:], axis, steps[-1])
    return [block, below, above, jnp.concatenate([far_top, far_bottom], 0)]


def exchange_y(blocks):
    sent = {d: lax.ppermute(blocks(d), "shard", SHARD_Y[d]) for d in (1, -1, 2)}
    return [blocks(0), sent[1], sent[-1], sent[2]]


def three_terms(value):
    first = lax.reduce_precision(value, 8, 7)
    rest = value - first
    second = lax.reduce_precision(rest, 8, 7)
    return first, second, rest - second


def corner(value, shape):
    row = lax.broadcasted_iota(jnp.int32, shape, 0)
    col = lax.broadcasted_iota(jnp.int32, shape, 1)
    out = jnp.zeros(shape, F32)
    for k, term in enumerate(three_terms(value)):
        out = jnp.where((row == k) & (col == 0), term, out)
    return out.astype(BF16)


def score_kernel(
    z_place, place, slot, ein, ql, eout, qr, eig, total_eig, out, inverse, right, grads, scaled
):
    n = pl.program_id(0)
    di = ein.shape[2]

    @pl.when(n == 0)
    def _():
        damping = (0.1 / (D * H)) * jnp.sum(total_eig[...].astype(F32))
        inverse[...] = 1.0 / (eig[...] + damping)
        for k in range(16):
            start = pl.multiple_of(place[k] * 64, 64)
            right[pl.ds(start, 64), :] = qr[64 * k : 64 * k + 64, :]
        out[...] = jnp.zeros_like(out)

    first = pl.multiple_of(slot[n] * 32, 32)
    for k in range(4):
        start = pl.multiple_of(z_place[k] * 32, 32)
        grads[pl.ds(start, 32), :] = eout[k, pl.ds(first, 32), :]
    for k in range(4):
        pair = jnp.dot(ein[0, k], grads[...], preferred_element_type=F32)
        scaled[di * k : di * k + di, :] = (pair * inverse[di * k : di * k + di, :]).astype(BF16)
    width = scaled.shape[1]
    sums = []
    for k in range(4):
        left = ql[4 * k : 4 * k + 4].reshape(256, ql.shape[-1])
        part = jnp.dot(left, scaled[...], preferred_element_type=F32)
        part = part * right[256 * k : 256 * k + 256, :].astype(F32)
        sums.append(jnp.sum(part.reshape(8, RANK, width), axis=1))
    total = jnp.sum(jnp.concatenate(sums, 0), axis=1, keepdims=True)
    lane = lax.broadcasted_iota(jnp.int32, out.shape, 1)
    out[...] = jnp.where(lane == n, total, out[...])


def score_call(z_place, place, slot, ein, ql, eout, qr, eig, total_eig):
    di, dj = ein.shape[2], eout.shape[2]

    def whole(x):
        return pl.BlockSpec(x.shape, lambda n, rank=x.ndim: (0,) * rank)

    return pl.pallas_call(
        score_kernel,
        grid=(NSEQ,),
        in_specs=[pl.BlockSpec(memory_space=pltpu.SMEM)] * 3
        + [pl.BlockSpec((1, 4, di, 128), lambda n: (n, 0, 0, 0))]
        + [whole(x) for x in (ql, eout, qr, eig, total_eig)],
        out_specs=pl.BlockSpec((QUERIES, 128), lambda n: (0, 0)),
        out_shape=jax.ShapeDtypeStruct((QUERIES, 128), F32),
        scratch_shapes=[
            pltpu.VMEM((4 * di, dj), F32),
            pltpu.VMEM((16 * 64, dj), BF16),
            pltpu.VMEM((128, dj), BF16),
            pltpu.VMEM((4 * di, dj), BF16),
        ],
        compiler_params=pltpu.CompilerParams(vmem_limit_bytes=48 * 1024 * 1024),
        cost_estimate=pl.CostEstimate(
            flops=20_000_000_000, bytes_accessed=16_000_000, transcendentals=0
        ),
    )(z_place, place, slot, ein, ql, eout, qr, eig, total_eig)


def shards(train_in, train_grad, seq_lens, basis_in, basis_out, eigvals, query_in, query_out):
    me = lax.axis_index("shard")
    example = lax.axis_index("example")
    my_z, my_y = me // 4, me % 4
    z_place = jnp.stack([(my_z + d) % 4 for d in AWAY]).astype(jnp.int32)
    place = jnp.stack(
        [(my_z + dz) % 4 * 4 + (my_y + dy) % 4 for dy in AWAY for dz in AWAY]
    ).astype(jnp.int32)
    seq = jnp.arange(NSEQ, dtype=jnp.int32)
    x_off = (seq // 2 - example // 2) % 4
    x_slot = jnp.where(x_off == 0, 0, jnp.where(x_off == 3, 1, jnp.where(x_off == 1, 2, 3)))
    slot = (
        ((seq % 2) != (example % 2)).astype(jnp.int32) * 8
        + x_slot * 2
        + ((seq // 8) != (example // 8)).astype(jnp.int32)
    ).astype(jnp.int32)

    rows_all = lax.all_gather(train_in[0], "shard", axis=0)

    block = jnp.concatenate([train_grad[0], corner(jnp.sum(eigvals), (32, 128))], 1)
    block = jnp.concatenate([block, lax.ppermute(block, "example", EXAMPLE_Z)], 0)
    block = jnp.concatenate(ring4(block, "example", EXAMPLE_X), 0)
    other = lax.ppermute(block, "example", EXAMPLE_CORE)
    eig_example = jnp.sum(block[:, H:].astype(F32)) + jnp.sum(other[:, H:].astype(F32))
    query_right = jnp.dot(
        query_out.reshape(64, H), basis_out, preferred_element_type=F32
    ).astype(BF16)
    part_out = [
        jnp.dot(b[:, :H], basis_out, preferred_element_type=F32).astype(BF16)
        for b in (block, other)
    ]
    dj = basis_out.shape[1]
    z_blocks = ring4(
        jnp.concatenate(part_out + [query_right, corner(eig_example, (32, dj))], 0),
        "shard",
        SHARD_Z,
    )
    eout = jnp.stack([b[: NSEQ * 32] for b in z_blocks])
    eig_z = sum(jnp.sum(b[NSEQ * 32 + 64 :].astype(F32)) for b in z_blocks)
    right_z = jnp.concatenate(
        [b[NSEQ * 32 : NSEQ * 32 + 64] for b in z_blocks] + [corner(eig_z, (16, dj))], 0
    )
    right_blocks = exchange_y(lambda d: right_z)
    qr = jnp.concatenate([b[:256] for b in right_blocks], 0)
    total_eig = jnp.concatenate([b[256:] for b in right_blocks], 0)

    eig = jnp.concatenate(ring4(eigvals, "shard", SHARD_Y), 0)
    query_left = jnp.dot(
        query_in.reshape(64, D), basis_in, preferred_element_type=F32
    ).astype(BF16)
    query_left = jnp.concatenate(exchange_y(lambda d: query_left), 1)
    query_left, rows_all = lax.optimization_barrier((query_left, rows_all))
    ql = lax.all_gather(query_left, "example", axis=0)

    own_in = jnp.dot(rows_all.reshape(SEQLEN, D), basis_in, preferred_element_type=F32)
    token = jnp.arange(SEQLEN, dtype=jnp.int32)[:, None]
    own_in = jnp.where(token < seq_lens[0], own_in, 0.0).astype(BF16)
    own_in = own_in.reshape(4, 4, 32, own_in.shape[1])

    def tokens_of(d):
        part = lax.dynamic_index_in_dim(own_in, (my_y + d) % 4, 1, keepdims=False)
        return part.reshape(128, own_in.shape[3])

    ein = jnp.stack([part.T for part in exchange_y(tokens_of)])
    ein, ql = lax.optimization_barrier((ein, ql))
    ein = lax.all_gather(ein, "example", axis=0)

    partial = score_call(z_place, place, slot, ein, ql, eout, qr, eig, total_eig)[:, :NSEQ]
    pieces = partial.reshape(16, 2, 16).transpose(0, 2, 1).reshape(256, 2)
    pieces = lax.all_to_all(pieces, ("shard", "example"), 0, 0, tiled=True)
    normalizer = 1.0 / math.sqrt(RANK * D * H * SEQLEN)
    return (jnp.sum(pieces, axis=0) * normalizer).reshape(2, 1)


def solution(mesh):
    placed = (
        P("example", "shard", None),
        P("example", "shard", None),
        P("example"),
        P(None, "shard"),
        P(None, "example"),
        P("shard", "example"),
        P("example", None, None),
        P("shard", None, None),
    )
    return jax.shard_map(
        shards, mesh=mesh, in_specs=placed, out_specs=P("shard", "example"), check_vma=False
    )
```

profile of v0, /device:TPU:1, one launch (start us, length us, event | category | flops | bytes accessed | tf_op | source)
XLA Modules:
  0.0 380.0 jit_solution(6323502741406466417)
XLA Ops:
  8.5 2.2 convolution_convert_fusion.1
  10.6 2.2 collective-permute-start
  12.9 1.5 collective-permute-start.1
  14.4 1.6 collective-permute-start.2
  15.9 2.6 constant_dynamic-update-slice_fusion.17
  19.7 81.9 %all-gather.6.cloned.1.call-done = bf16[16,32,5120]{2,1,0:T(8,128)(2,1)} async-done(((bf16[1,32,5120]{2,1,0:T(8,128)(2,1)}), bf16[16,32,5120]{2,1,0:T(8,128)(2,1)}) %all-gather.6.cloned.1.call-update) | async-done | bytes 5242896 | tf_op jit(solution)/shard_map/all_gather | solution.py:135
  105.3 1.4 select_convert_fusion.2
  106.7 2.0 pad_maximum_fusion.4
  110.1 14.4 %collective-permute-done.6 = bf16[32,7040]{1,0:T(8,128)(2,1)} collective-permute-done((bf16[32,7040]{1,0:T(8,128)(2,1)}, bf16[32,7040]{1,0:T(8,128)(2,1)}, u32[]{:S(2)}, u32[]{:S(2)}) %collective-permute-start.6) | collective-permute-done | bytes 450592 | tf_op jit(solution)/shard_map/ppermute | solution.py:138
  125.9 3.0 collective-permute-start.8
  128.8 1.8 constant_dynamic-update-slice_fusion.4
  130.7 19.7 %collective-permute-done.7 = bf16[64,7040]{1,0:T(8,128)(2,1)S(1)} collective-permute-done((bf16[64,7040]{1,0:T(8,128)(2,1)S(1)}, bf16[64,7040]{1,0:T(8,128)(2,1)S(1)}, u32[]{:S(2)}, u32[]{:S(2)}) %collective-permute-start.7) | collective-permute-done | bytes 901152 | tf_op jit(solution)/shard_map/ppermute | solution.py:29
  151.2 2.2 collective-permute-start.9
  155.2 1.7 collective-permute-start.10
  156.8 5.1 %fusion.4 = bf16[512,320]{0,1:T(8,128)(2,1)} fusion(bf16[512,5120]{1,0:T(8,128)(2,1)} %bitcast.86, bf16[5120,320]{0,1:T(8,128)(2,1)S(1)} %copy-done, pred[512]{0:T(512)(128)(4,1)S(1)} %iota_compare_fusion.1), kind=kOutput, calls=%fused_computation.6 | convolution fusion | flops 1678049280 | bytes 8847872 | tf_op jit(solution)/shard_map/dot_general | solution.py:172
  161.9 1.9 copy.16
  165.9 1.8 collective-permute-start.4
  169.0 2.2 constant_dynamic-update-slice_fusion.3
  171.2 2.1 collective-permute-done.5
  174.2 1.9 copy.17
  176.1 2.2 constant_dynamic-update-slice_fusion.2
  178.3 1.8 constant_dynamic-update-slice_fusion.1
  180.1 1.8 constant_dynamic-update-slice_fusion
  181.9 3.2 collective-permute-start.11
  185.1 2.7 collective-permute-start.20
  189.1 5.8 %constant_dynamic-update-slice_fusion.9 = (bf16[272,432]{1,0:T(8,128)(2,1)}, bf16[1024,432]{1,0:T(8,128)(2,1)}, bf16[64,432]{1,0:T(8,128)(2,1)}) fusion(bf16[64,6912]{1,0:T(8,128)(2,1)} %bitcast.75, bf16[6912,432]{0,1:T(8,128)(2,1)} %param.12), kind=kOutput, calls=%fused_computation.40 | convolution fusion | flops 382233600 | bytes 7053312 | tf_op jit(solution)/shard_map/dot_general | solution.py:142
  194.9 8.1 %collective-permute-done.19 = f32[320,432]{1,0:T(8,128)} collective-permute-done((f32[320,432]{1,0:T(8,128)}, f32[320,432]{1,0:T(8,128)}, u32[]{:S(2)}, u32[]{:S(2)}) %collective-permute-start.19) | collective-permute-done | bytes 552992 | tf_op jit(solution)/shard_map/ppermute | solution.py:29
  203.0 1.7 slice.127
  204.7 1.7 slice.128
  206.5 2.7 collective-permute-start.22
  209.1 2.0 constant_dynamic-update-slice_fusion.16
  211.8 4.8 %fusion.5 = bf16[256,432]{1,0:T(8,128)(2,1)S(1)} fusion(bf16[6912,432]{0,1:T(8,128)(2,1)} %param.12, bf16[256,7040]{1,0:T(8,128)(2,1)S(1)} %copy-done.11), kind=kOutput, calls=%fused_computation.7 | convolution fusion | flops 1528934400 | bytes 9732096 | tf_op jit(solution)/shard_map/dot_general | solution.py:146
  216.6 1.5 convert_reduce_fusion.2
  221.8 5.8 %fusion.8 = bf16[256,432]{1,0:T(8,128)(2,1)S(1)} fusion(bf16[6912,432]{0,1:T(8,128)(2,1)} %param.12, bf16[256,7040]{1,0:T(8,128)(2,1)} %collective-permute-done.11), kind=kOutput, calls=%fused_computation.8 | convolution fusion | flops 1528934400 | bytes 9732096 | tf_op jit(solution)/shard_map/dot_general | solution.py:146
  227.7 1.4 select_convert_fusion
  230.0 2.1 copy.20
  232.2 2.0 collective-permute-start.12
  234.1 1.6 collective-permute-start.13
  235.7 2.0 constant_dynamic-update-slice_fusion.15
  237.7 1.7 constant_dynamic-update-slice_fusion.14
  239.4 1.7 constant_dynamic-update-slice_fusion.13.eig
  241.2 2.8 convert_reduce_fusion.5
  244.0 1.8 maximum_bitcast_fusion
  245.8 14.9 %collective-permute-done.13 = bf16[608,432]{0,1:T(8,128)(2,1)S(1)} collective-permute-done((bf16[608,432]{0,1:T(8,128)(2,1)}, bf16[608,432]{0,1:T(8,128)(2,1)S(1)}, u32[]{:S(2)}, u32[]{:S(2)}) %collective-permute-start.13) | collective-permute-done | bytes 525344 | tf_op jit(solution)/shard_map/ppermute | solution.py:30
  262.4 1.8 copy.37
  264.3 2.4 collective-permute-start.15
  266.7 1.7 slice.116
  268.4 1.9 copy.36
  270.3 1.6 convert_reduce_fusion.1
  271.9 1.6 convert_reduce_fusion
  275.6 1.8 slice.114
  277.4 2.1 copy.34
  279.5 1.8 slice.115
  281.3 2.0 copy.35
  286.6 1.5 slice_dynamic-update-slice_fusion.4
  288.1 1.4 convert_reduce_fusion.4
  292.5 2.0 select_convert_fusion.1
  294.5 2.7 collective-permute-start.17
  298.3 3.0 pad_maximum_fusion.eout
  302.7 5.0 %collective-permute-done.18 = bf16[272,432]{1,0:T(8,128)(2,1)S(1)} collective-permute-done((bf16[272,432]{1,0:T(8,128)(2,1)}, bf16[272,432]{1,0:T(8,128)(2,1)S(1)}, u32[]{:S(2)}, u32[]{:S(2)}) %collective-permute-start.18) | collective-permute-done | bytes 235040 | tf_op jit(solution)/shard_map/ppermute | solution.py:37
  308.9 1.6 copy-done.1
  311.7 1.7 copy-done.5
  313.4 33.8 %shard_map.82 = f32[32,128]{1,0:T(8,128)S(1)} custom-call(s32[4]{0:T(128)S(1)} %pad_add_fusion.z_place, s32[16]{0:T(128)S(1)} %stack.117.place, s32[16]{0:T(128)S(1)} %fusion.12.slot, bf16[16,4,320,128]{3,2,1,0:T(8,128)(2,1)} %bitcast.85, bf16[16,64,1280]{2,1,0:T(8,128)(2,1)S(1)} %bitcast.69, bf16[4,512,432]{2,1,0:T(8,128)(2,1)S(1)} %copy-done.1, ...), custom_call_target="tpu_custom_call" | custom-call | flops 20000000000 | bytes 16000000 | tf_op jit(solution)/shard_map/pallas_call | solution.py:97
  347.4 25.3 %all_to_all.9 = f32[256,1,2]{2,1,0:T(1,128)S(1)} all-to-all(f32[256,1,2]{2,1,0:T(1,128)S(1)} %bitcast.77), channel_id=1, replica_groups=mesh['shard'=16,'example'=16] {'shard','example'}, dimensions={0} | all-to-all | bytes 4096 | tf_op jit(solution)/shard_map/all_to_all | solution.py:187
  (110 shorter events, 25.8 us)
Async XLA Ops:
  6.5 1.9 copy-start
  6.5 95.1 %all-gather.6.cloned.1.call-start = ((), (), s32[]{:S(2)}) async-start(), calls=%async_computation.1 | async-start | bytes 5570560 | tf_op jit(solution)/shard_map/all_gather | solution.py:135
  7.3 166.9 %all-gather.8.cloned.1.call-start = ((), (), s32[]{:S(2)}) async-start(), calls=%async_computation.2 | async-start | bytes 2785280 | tf_op jit(solution)/shard_map/all_gather | solution.py:170
  10.6 7.9 %collective-permute-start = (bf16[64,320]{1,0:T(8,128)(2,1)S(1)}, bf16[64,320]{1,0:T(8,128)(2,1)S(1)}, u32[]{:S(2)}, u32[]{:S(2)}) collective-permute-start(bf16[64,320]{1,0:T(8,128)(2,1)S(1)} %convolution_convert_fusion.1), channel_id=1, source_target_pairs={{0,16},{16,32},{32,48},{48,0},{64,80},{80,96},{96,112},{112,64},{1... | collective-permute-start | bytes 122888 | tf_op jit(solution)/shard_map/ppermute | solution.py:37
  12.9 5.7 %collective-permute-start.1 = (bf16[64,320]{1,0:T(8,128)(2,1)S(1)}, bf16[64,320]{1,0:T(8,128)(2,1)S(1)}, u32[]{:S(2)}, u32[]{:S(2)}) collective-permute-start(bf16[64,320]{1,0:T(8,128)(2,1)S(1)} %convolution_convert_fusion.1), channel_id=1, source_target_pairs={{0,48},{16,0},{32,16},{48,32},{64,112},{80,64},{96,80},{112,96},{1... | collective-permute-start | bytes 122888 | tf_op jit(solution)/shard_map/ppermute | solution.py:37
  14.4 4.6 %collective-permute-start.2 = (bf16[64,320]{1,0:T(8,128)(2,1)S(1)}, bf16[64,320]{1,0:T(8,128)(2,1)S(1)}, u32[]{:S(2)}, u32[]{:S(2)}) collective-permute-start(bf16[64,320]{1,0:T(8,128)(2,1)S(1)} %convolution_convert_fusion.1), channel_id=1, source_target_pairs={{0,32},{16,48},{32,0},{48,16},{64,96},{80,112},{96,64},{112,80},{1... | collective-permute-start | bytes 122888 | tf_op jit(solution)/shard_map/ppermute | solution.py:37
  15.9 139.2 %copy-start.12 = (pred[32]{0:T(512)(128)(4,1)}, pred[32]{0:T(512)(128)(4,1)S(1)}, u32[]{:S(2)}) copy-start(pred[32]{0:T(512)(128)(4,1)S(1)} %get-tuple-element.32) | copy-start | bytes 100
  15.9 139.2 %copy-start.14 = (pred[32]{0:T(512)(128)(4,1)}, pred[32]{0:T(512)(128)(4,1)S(1)}, u32[]{:S(2)}) copy-start(pred[32]{0:T(512)(128)(4,1)S(1)} %get-tuple-element.33) | copy-start | bytes 100
  18.6 143.4 %copy-start.16 = (pred[32]{0:T(512)(128)(4,1)}, pred[32]{0:T(512)(128)(4,1)S(1)}, u32[]{:S(2)}) copy-start(pred[32]{0:T(512)(128)(4,1)S(1)} %iota_compare_fusion.8) | copy-start | bytes 100
  101.6 207.3 %all-gather.10.cloned.1.call-start = ((), (), s32[]{:S(2)}) async-start(), calls=%async_computation.3 | async-start | bytes 5570560 | tf_op jit(solution)/shard_map/all_gather | solution.py:183
  108.7 15.8 %collective-permute-start.6 = (bf16[32,7040]{1,0:T(8,128)(2,1)}, bf16[32,7040]{1,0:T(8,128)(2,1)}, u32[]{:S(2)}, u32[]{:S(2)}) collective-permute-start(bf16[32,7040]{1,0:T(8,128)(2,1)} %get-tuple-element.15), channel_id=1, source_target_pairs={{0,8},{1,9},{2,10},{3,11},{4,12},{5,13},{6,14},{7,15},{8,0},{9,1},... | collective-permute-start | bytes 1351688 | tf_op jit(solution)/shard_map/ppermute | solution.py:138
  125.8 24.6 %collective-permute-start.7 = (bf16[64,7040]{1,0:T(8,128)(2,1)S(1)}, bf16[64,7040]{1,0:T(8,128)(2,1)S(1)}, u32[]{:S(2)}, u32[]{:S(2)}) collective-permute-start(bf16[64,7040]{1,0:T(8,128)(2,1)S(1)} %pad_maximum_fusion.1), channel_id=1, source_target_pairs={{0,2},{1,3},{2,4},{3,5},{4,6},{5,7},{6,0},{7,1},{8,10},{9,11},{10,... | collective-permute-start | bytes 2703368 | tf_op jit(solution)/shard_map/ppermute | solution.py:29
  125.9 27.6 %collective-permute-start.8 = (bf16[64,7040]{1,0:T(8,128)(2,1)S(1)}, bf16[64,7040]{1,0:T(8,128)(2,1)S(1)}, u32[]{:S(2)}, u32[]{:S(2)}) collective-permute-start(bf16[64,7040]{1,0:T(8,128)(2,1)S(1)} %pad_maximum_fusion.1), channel_id=1, source_target_pairs={{0,6},{1,7},{2,0},{3,1},{4,2},{5,3},{6,4},{7,5},{8,14},{9,15},{10,... | collective-permute-start | bytes 2703368 | tf_op jit(solution)/shard_map/ppermute | solution.py:30
  150.4 4.8 %copy-start.7 = (bf16[64,7040]{1,0:T(8,128)(2,1)}, bf16[64,7040]{1,0:T(8,128)(2,1)S(1)}, u32[]{:S(2)}) copy-start(bf16[64,7040]{1,0:T(8,128)(2,1)S(1)} %collective-permute-done.7) | copy-start | bytes 2703364
  151.2 27.0 %collective-permute-start.9 = (bf16[32,7040]{1,0:T(8,128)(2,1)}, bf16[32,7040]{1,0:T(8,128)(2,1)}, u32[]{:S(2)}, u32[]{:S(2)}) collective-permute-start(bf16[32,7040]{1,0:T(8,128)(2,1)} %slice.108), channel_id=1, source_target_pairs={{0,2},{1,3},{2,4},{3,5},{4,6},{5,7},{6,0},{7,1},{8,10},{9,11},{10,... | collective-permute-start | bytes 1351688 | tf_op jit(solution)/shard_map/ppermute | solution.py:31
  153.4 0.9 copy-start.6
  155.2 24.9 %collective-permute-start.10 = (bf16[32,7040]{1,0:T(8,128)(2,1)}, bf16[32,7040]{1,0:T(8,128)(2,1)}, u32[]{:S(2)}, u32[]{:S(2)}) collective-permute-start(bf16[32,7040]{1,0:T(8,128)(2,1)} %slice.109), channel_id=1, source_target_pairs={{0,6},{1,7},{2,0},{3,1},{4,2},{5,3},{6,4},{7,5},{8,14},{9,15},{10,... | collective-permute-start | bytes 1351688 | tf_op jit(solution)/shard_map/ppermute | solution.py:32
  165.0 6.3 %collective-permute-start.3 = (bf16[128,320]{1,0:T(8,128)(2,1)S(1)}, bf16[128,320]{1,0:T(8,128)(2,1)S(1)}, u32[]{:S(2)}, u32[]{:S(2)}) collective-permute-start(bf16[128,320]{1,0:T(8,128)(2,1)S(1)} %bitcast.82), channel_id=1, source_target_pairs={{0,16},{16,32},{32,48},{48,0},{64,80},{80,96},{96,112},{112,64},{1... | collective-permute-start | bytes 245768 | tf_op jit(solution)/shard_map/ppermute | solution.py:37
  165.9 5.3 %collective-permute-start.4 = (bf16[128,320]{1,0:T(8,128)(2,1)S(1)}, bf16[128,320]{1,0:T(8,128)(2,1)S(1)}, u32[]{:S(2)}, u32[]{:S(2)}) collective-permute-start(bf16[128,320]{1,0:T(8,128)(2,1)S(1)} %bitcast.80), channel_id=1, source_target_pairs={{0,48},{16,0},{32,16},{48,32},{64,112},{80,64},{96,80},{112,96},{1... | collective-permute-start | bytes 245768 | tf_op jit(solution)/shard_map/ppermute | solution.py:37
  167.7 5.6 %collective-permute-start.5 = (bf16[128,320]{1,0:T(8,128)(2,1)S(1)}, bf16[128,320]{1,0:T(8,128)(2,1)S(1)}, u32[]{:S(2)}, u32[]{:S(2)}) collective-permute-start(bf16[128,320]{1,0:T(8,128)(2,1)S(1)} %bitcast.79), channel_id=1, source_target_pairs={{0,32},{16,48},{32,0},{48,16},{64,96},{80,112},{96,64},{112,80},{1... | collective-permute-start | bytes 245768 | tf_op jit(solution)/shard_map/ppermute | solution.py:37
  181.9 34.7 %collective-permute-start.11 = (bf16[256,7040]{1,0:T(8,128)(2,1)}, bf16[256,7040]{1,0:T(8,128)(2,1)}, u32[]{:S(2)}, u32[]{:S(2)}) collective-permute-start(bf16[256,7040]{1,0:T(8,128)(2,1)} %constant_dynamic-update-slice_fusion), channel_id=1, source_target_pairs={{0,1},{1,0},{2,3},{3,2},{4,5},{5,4},{6,7},{7,6},{8,9},{9,8},{10,11... | collective-permute-start | bytes 10813448 | tf_op jit(solution)/shard_map/ppermute | solution.py:140
  185.1 17.9 %collective-permute-start.19 = (f32[320,432]{1,0:T(8,128)}, f32[320,432]{1,0:T(8,128)}, u32[]{:S(2)}, u32[]{:S(2)}) collective-permute-start(f32[320,432]{1,0:T(8,128)} %param.13), channel_id=1, source_target_pairs={{0,16},{16,32},{32,48},{48,0},{64,80},{80,96},{96,112},{112,64},{1... | collective-permute-start | bytes 1658888 | tf_op jit(solution)/shard_map/ppermute | solution.py:29
  185.1 19.6 %collective-permute-start.20 = (f32[320,432]{1,0:T(8,128)}, f32[320,432]{1,0:T(8,128)}, u32[]{:S(2)}, u32[]{:S(2)}) collective-permute-start(f32[320,432]{1,0:T(8,128)} %param.13), channel_id=1, source_target_pairs={{0,48},{16,0},{32,16},{48,32},{64,112},{80,64},{96,80},{112,96},{1... | collective-permute-start | bytes 1658888 | tf_op jit(solution)/shard_map/ppermute | solution.py:30
  189.1 22.0 %copy-start.11 = (bf16[256,7040]{1,0:T(8,128)(2,1)S(1)}, bf16[256,7040]{1,0:T(8,128)(2,1)}, u32[]{:S(2)}) copy-start(bf16[256,7040]{1,0:T(8,128)(2,1)} %constant_dynamic-update-slice_fusion) | copy-start | bytes 10813444
  204.7 33.0 %collective-permute-start.21 = (f32[160,432]{1,0:T(8,128)}, f32[160,432]{1,0:T(8,128)}, u32[]{:S(2)}, u32[]{:S(2)}) collective-permute-start(f32[160,432]{1,0:T(8,128)} %slice.127), channel_id=1, source_target_pairs={{0,16},{16,32},{32,48},{48,0},{64,80},{80,96},{96,112},{112,64},{1... | collective-permute-start | bytes 829448 | tf_op jit(solution)/shard_map/ppermute | solution.py:31
  206.5 33.0 %collective-permute-start.22 = (f32[160,432]{1,0:T(8,128)}, f32[160,432]{1,0:T(8,128)}, u32[]{:S(2)}, u32[]{:S(2)}) collective-permute-start(f32[160,432]{1,0:T(8,128)} %slice.128), channel_id=1, source_target_pairs={{0,48},{16,0},{32,16},{48,32},{64,112},{80,64},{96,80},{112,96},{1... | collective-permute-start | bytes 829448 | tf_op jit(solution)/shard_map/ppermute | solution.py:32
  221.8 5.8 %copy-start.13 = (pred[32]{0:T(512)(128)(4,1)S(1)}, pred[32]{0:T(512)(128)(4,1)}, u32[]{:S(2)}) copy-start(pred[32]{0:T(512)(128)(4,1)} %copy-done.12) | copy-start | bytes 100
  221.8 5.8 %copy-start.15 = (pred[32]{0:T(512)(128)(4,1)S(1)}, pred[32]{0:T(512)(128)(4,1)}, u32[]{:S(2)}) copy-start(pred[32]{0:T(512)(128)(4,1)} %copy-done.14) | copy-start | bytes 100
  221.8 5.8 %copy-start.17 = (pred[32]{0:T(512)(128)(4,1)S(1)}, pred[32]{0:T(512)(128)(4,1)}, u32[]{:S(2)}) copy-start(pred[32]{0:T(512)(128)(4,1)} %copy-done.16) | copy-start | bytes 100
  221.8 7.3 %copy-start.10 = (bf16[64,432]{1,0:T(8,128)(2,1)S(1)}, bf16[64,432]{1,0:T(8,128)(2,1)}, u32[]{:S(2)}) copy-start(bf16[64,432]{1,0:T(8,128)(2,1)} %get-tuple-element.31) | copy-start | bytes 165892
  227.7 1.5 copy-start.9
  232.2 34.5 %collective-permute-start.12 = (bf16[608,432]{0,1:T(8,128)(2,1)}, bf16[608,432]{0,1:T(8,128)(2,1)}, u32[]{:S(2)}, u32[]{:S(2)}) collective-permute-start(bf16[608,432]{0,1:T(8,128)(2,1)} %copy.20), channel_id=1, source_target_pairs={{0,64},{16,80},{32,96},{48,112},{64,128},{80,144},{96,160},{112,17... | collective-permute-start | bytes 1575944 | tf_op jit(solution)/shard_map/ppermute | solution.py:29
  234.1 26.6 %collective-permute-start.13 = (bf16[608,432]{0,1:T(8,128)(2,1)}, bf16[608,432]{0,1:T(8,128)(2,1)S(1)}, u32[]{:S(2)}, u32[]{:S(2)}) collective-permute-start(bf16[608,432]{0,1:T(8,128)(2,1)} %copy.20), channel_id=1, source_target_pairs={{0,192},{16,208},{32,224},{48,240},{64,0},{80,16},{96,32},{112,48}... | collective-permute-start | bytes 1575944 | tf_op jit(solution)/shard_map/ppermute | solution.py:30
  260.7 0.8 copy-start.8
  262.4 30.0 %copy-start.18 = (pred[16]{0:T(512)(128)(4,1)S(1)}, pred[16]{0:T(512)(128)(4,1)}, u32[]{:S(2)}) copy-start(pred[16]{0:T(512)(128)(4,1)} %iota_compare_fusion.4) | copy-start | bytes 52
  262.4 30.0 %copy-start.19 = (pred[16]{0:T(512)(128)(4,1)S(1)}, pred[16]{0:T(512)(128)(4,1)}, u32[]{:S(2)}) copy-start(pred[16]{0:T(512)(128)(4,1)} %get-tuple-element.34) | copy-start | bytes 52
  262.4 30.0 %copy-start.20 = (pred[16]{0:T(512)(128)(4,1)S(1)}, pred[16]{0:T(512)(128)(4,1)}, u32[]{:S(2)}) copy-start(pred[16]{0:T(512)(128)(4,1)} %get-tuple-element.35) | copy-start | bytes 52
  264.3 22.3 %collective-permute-start.15 = (bf16[304,432]{1,0:T(8,128)(2,1)}, bf16[304,432]{1,0:T(8,128)(2,1)}, u32[]{:S(2)}, u32[]{:S(2)}) collective-permute-start(bf16[304,432]{1,0:T(8,128)(2,1)} %copy.37), channel_id=1, source_target_pairs={{0,192},{16,208},{32,224},{48,240},{64,0},{80,16},{96,32},{112,48}... | collective-permute-start | bytes 787976 | tf_op jit(solution)/shard_map/ppermute | solution.py:32
  270.3 26.9 %collective-permute-start.14 = (bf16[304,432]{1,0:T(8,128)(2,1)}, bf16[304,432]{1,0:T(8,128)(2,1)}, u32[]{:S(2)}, u32[]{:S(2)}) collective-permute-start(bf16[304,432]{1,0:T(8,128)(2,1)} %copy.36), channel_id=1, source_target_pairs={{0,64},{16,80},{32,96},{48,112},{64,128},{80,144},{96,160},{112,17... | collective-permute-start | bytes 787976 | tf_op jit(solution)/shard_map/ppermute | solution.py:31
  292.4 15.3 %copy-start.2 = (bf16[1024,432]{1,0:T(8,128)(2,1)S(1)}, bf16[1024,432]{1,0:T(8,128)(2,1)}, u32[]{:S(2)}) copy-start(bf16[1024,432]{1,0:T(8,128)(2,1)} %get-tuple-element.22) | copy-start | bytes 2654212
  294.5 7.9 %collective-permute-start.16 = (bf16[272,432]{1,0:T(8,128)(2,1)}, bf16[272,432]{1,0:T(8,128)(2,1)S(1)}, u32[]{:S(2)}, u32[]{:S(2)}) collective-permute-start(bf16[272,432]{1,0:T(8,128)(2,1)} %get-tuple-element.30), channel_id=1, source_target_pairs={{0,16},{16,32},{32,48},{48,0},{64,80},{80,96},{96,112},{112,64},{1... | collective-permute-start | bytes 705032 | tf_op jit(solution)/shard_map/ppermute | solution.py:37
  294.5 8.2 %collective-permute-start.17 = (bf16[272,432]{1,0:T(8,128)(2,1)}, bf16[272,432]{1,0:T(8,128)(2,1)S(1)}, u32[]{:S(2)}, u32[]{:S(2)}) collective-permute-start(bf16[272,432]{1,0:T(8,128)(2,1)} %get-tuple-element.30), channel_id=1, source_target_pairs={{0,48},{16,0},{32,16},{48,32},{64,112},{80,64},{96,80},{112,96},{1... | collective-permute-start | bytes 705032 | tf_op jit(solution)/shard_map/ppermute | solution.py:37
  297.2 10.5 %collective-permute-start.18 = (bf16[272,432]{1,0:T(8,128)(2,1)}, bf16[272,432]{1,0:T(8,128)(2,1)S(1)}, u32[]{:S(2)}, u32[]{:S(2)}) collective-permute-start(bf16[272,432]{1,0:T(8,128)(2,1)} %get-tuple-element.30), channel_id=1, source_target_pairs={{0,32},{16,48},{32,0},{48,16},{64,96},{80,112},{96,64},{112,80},{1... | collective-permute-start | bytes 705032 | tf_op jit(solution)/shard_map/ppermute | solution.py:37
  307.8 1.1 copy-start.3
  308.9 1.6 copy-start.1
  310.5 1.2 copy-start.4
  311.7 1.7 copy-start.5
Sparse Core Ops, SparseCore 0:
  9.8 91.7 all-gather.5
  103.4 39.5 all-gather.7
  176.2 40.6 all-gather.9
where the time goes:
time: 382 us; the launch traced here: 380 us
  waiting for transfers between devices  149 us (39%)
  local copies, waits for them, and re-layouts  58 us (15%)
  starting transfers between devices  34.4 us (9%)
  Pallas kernels  33.8 us (9%)
  other arithmetic  30.1 us (8%)
  between operations  26.3 us (7%)
  blocking collectives  25.3 us (7%)
  matrix products  23.6 us (6%)
    all_gather x1, waiting for transfers between devices, shards(): rows_all = lax.all_gather(train_in[0], 'shard', axis=0)  81.9 us
    pallas_call x1, Pallas kernels, score_call(): pl.pallas_call(score_kernel, grid=(NSEQ,), in_specs=[pl.BlockSpec(memory_...  33.8 us
    unnamed x60, local copies, waits for them, and re-layouts  33.1 us
    ppermute x3, waiting for transfers between devices, ring4(): below = lax.ppermute(block, axis, steps[1])  27.8 us
    all_to_all x1, blocking collectives, shards(): pieces = lax.all_to_all(pieces, ('shard', 'example'), 0, 0, tiled=True)  25.3 us
    ppermute x3, waiting for transfers between devices, ring4(): above = lax.ppermute(block, axis, steps[-1])  15 us
    ppermute x1, waiting for transfers between devices, shards(): lax.ppermute(block, 'example', EXAMPLE_Z)  14.4 us
    ppermute x9, starting transfers between devices, exchange_y(): sent = {d: lax.ppermute(blocks(d), 'shard', SHARD_Y[d]) for d in (1, -1, 2)}  12.1 us
  transfers between devices with their start and end apart: 26, of which 10 were waited for; matrix products, arithmetic and copies ran while one was open for 27% of the time, Pallas kernels for 0%

commit v1 on v0

v1 whole, which is shorter than its diff:
```python
import math

import jax
import jax.numpy as jnp
from jax import lax
from jax.experimental import pallas as pl
from jax.experimental.layout import Layout, with_layout_constraint
from jax.experimental.pallas import tpu as pltpu
from jax.sharding import PartitionSpec as P

D = 5120
H = 6912
SEQLEN = 512
RANK = 32
NSEQ = 16
QUERIES = 32
BF16 = jnp.bfloat16
F32 = jnp.float32

SHARD_Y = {d: [(i, i // 4 * 4 + (i + d) % 4) for i in range(16)] for d in (1, -1, 2)}
SHARD_Z = {d: [(i, (i + 4 * d) % 16) for i in range(16)] for d in (1, -1, 2)}
EXAMPLE_X = {d: [(i, i // 8 * 8 + (i + 2 * d) % 8) for i in range(16)] for d in (1, -1)}
EXAMPLE_CORE = [(i, i ^ 1) for i in range(16)]
EXAMPLE_Z = [(i, i ^ 8) for i in range(16)]
AWAY = (0, -1, 1, 2)


def ring4(block, axis, steps, cut):
    below = lax.ppermute(block, axis, steps[1])
    above = lax.ppermute(block, axis, steps[-1])
    far_top = lax.ppermute(below[:cut], axis, steps[1])
    far_bottom = lax.ppermute(above[cut:], axis, steps[-1])
    return [block, below, above, far_top, far_bottom]


def exchange(blocks, steps):
    sent = {d: lax.ppermute(blocks(d), "shard", steps[d]) for d in (1, -1, 2)}
    return [blocks(0), sent[1], sent[-1], sent[2]]


def three_terms(value):
    first = lax.reduce_precision(value, 8, 7)
    rest = value - first
    second = lax.reduce_precision(rest, 8, 7)
    return first, second, rest - second


def corner(value, shape):
    row = lax.broadcasted_iota(jnp.int32, shape, 0)
    col = lax.broadcasted_iota(jnp.int32, shape, 1)
    out = jnp.zeros(shape, F32)
    for k, term in enumerate(three_terms(value)):
        out = jnp.where((row == k) & (col == 0), term, out)
    return out.astype(BF16)


def score_kernel(
    z_place, place, slot, ein, ql,
    out_0, out_1, out_2, out_top, out_bottom,
    qr_0, qr_1, qr_2, qr_3,
    eig_0, eig_1, eig_2, eig_top, eig_bottom,
    out, inverse, right, grads, scaled,
):
    n = pl.program_id(0)
    di = ein.shape[2]

    @pl.when(n == 0)
    def _():
        damping = (0.1 / (D * H)) * jnp.sum(ql[:, 64:, :].astype(F32))
        row = 0
        for eig in (eig_0, eig_1, eig_2, eig_top, eig_bottom):
            inverse[row : row + eig.shape[0], :] = 1.0 / (eig[...] + damping)
            row += eig.shape[0]
        for ky, qr in enumerate((qr_0, qr_1, qr_2, qr_3)):
            for kz in range(4):
                start = pl.multiple_of(place[4 * ky + kz] * 64, 64)
                right[pl.ds(start, 64), :] = qr[64 * kz : 64 * kz + 64, :]
        out[...] = jnp.zeros_like(out)

    first = pl.multiple_of(slot[n] * 32, 32)
    starts = [pl.multiple_of(z_place[k] * 32, 32) for k in range(4)]
    for k, rows in enumerate((out_0, out_1, out_2)):
        grads[pl.ds(starts[k], 32), :] = rows[pl.ds(first, 32), :]
    cut = out_top.shape[0]

    @pl.when(first < cut)
    def _():
        grads[pl.ds(starts[3], 32), :] = out_top[pl.ds(first, 32), :]

    @pl.when(first >= cut)
    def _():
        grads[pl.ds(starts[3], 32), :] = out_bottom[pl.ds(first - cut, 32), :]

    for k in range(4):
        pair = jnp.dot(ein[0, k], grads[...], preferred_element_type=F32)
        scaled[di * k : di * k + di, :] = (pair * inverse[di * k : di * k + di, :]).astype(BF16)
    width = scaled.shape[1]
    sums = []
    for k in range(4):
        left = ql[4 * k : 4 * k + 4, :64, :].reshape(256, ql.shape[-1])
        part = jnp.dot(left, scaled[...], preferred_element_type=F32)
        part = part * right[256 * k : 256 * k + 256, :].astype(F32)
        sums.append(jnp.sum(part.reshape(8, RANK, width), axis=1))
    total = jnp.sum(jnp.concatenate(sums, 0), axis=1, keepdims=True)
    lane = lax.broadcasted_iota(jnp.int32, out.shape, 1)
    out[...] = jnp.where(lane == n, total, out[...])


def score_call(places, ein, rest):
    di, dj = ein.shape[2], rest[1].shape[1]

    def whole(x):
        return pl.BlockSpec(x.shape, lambda n, rank=x.ndim: (0,) * rank)

    return pl.pallas_call(
        score_kernel,
        grid=(NSEQ,),
        in_specs=[pl.BlockSpec(memory_space=pltpu.SMEM)] * 3
        + [pl.BlockSpec((1, 4, di, 128), lambda n: (n, 0, 0, 0))]
        + [whole(x) for x in rest],
        out_specs=pl.BlockSpec((QUERIES, 128), lambda n: (0, 0)),
        out_shape=jax.ShapeDtypeStruct((QUERIES, 128), F32),
        scratch_shapes=[
            pltpu.VMEM((4 * di, dj), F32),
            pltpu.VMEM((16 * 64, dj), BF16),
            pltpu.VMEM((128, dj), BF16),
            pltpu.VMEM((4 * di, dj), BF16),
        ],
        compiler_params=pltpu.CompilerParams(vmem_limit_bytes=48 * 1024 * 1024),
        cost_estimate=pl.CostEstimate(
            flops=20_000_000_000, bytes_accessed=16_000_000, transcendentals=0
        ),
    )(*places, ein, *rest)


def shards(train_in, train_grad, seq_lens, basis_in, basis_out, eigvals, query_in, query_out):
    me = lax.axis_index("shard")
    example = lax.axis_index("example")
    my_z, my_y = me // 4, me % 4
    z_place = jnp.stack([(my_z + d) % 4 for d in AWAY]).astype(jnp.int32)
    place = jnp.stack(
        [(my_z + dz) % 4 * 4 + (my_y + dy) % 4 for dy in AWAY for dz in AWAY]
    ).astype(jnp.int32)
    seq = jnp.arange(NSEQ, dtype=jnp.int32)
    x_off = (seq // 2 - example // 2) % 4
    x_slot = jnp.where(x_off == 0, 0, jnp.where(x_off == 3, 1, jnp.where(x_off == 1, 2, 3)))
    slot = (
        ((seq % 2) != (example % 2)).astype(jnp.int32) * 8
        + x_slot * 2
        + ((seq // 8) != (example // 8)).astype(jnp.int32)
    ).astype(jnp.int32)
    di, dj = eigvals.shape

    rows_all = lax.all_gather(train_in[0], "shard", axis=0)

    block = jnp.concatenate([train_grad[0], lax.ppermute(train_grad[0], "example", EXAMPLE_Z)], 0)
    block = jnp.concatenate(ring4(block, "example", EXAMPLE_X, 32), 0)
    other = lax.ppermute(block, "example", EXAMPLE_CORE)
    part_out = jnp.concatenate(
        [
            jnp.dot(b, basis_out, preferred_element_type=F32).astype(BF16)
            for b in (block, other)
        ],
        0,
    )
    part_out = with_layout_constraint(part_out, Layout(major_to_minor=(0, 1)))
    eout = ring4(part_out, "shard", SHARD_Z, 256)

    query_left = jnp.dot(
        query_in.reshape(64, D), basis_in, preferred_element_type=F32
    ).astype(BF16)
    query_left = jnp.concatenate([query_left, corner(jnp.sum(eigvals), (16, di))], 0)
    left_blocks = exchange(lambda d: query_left, SHARD_Y)
    eig_y = sum(jnp.sum(b[64:].astype(F32)) for b in left_blocks)
    query_right = jnp.dot(
        query_out.reshape(64, H), basis_out, preferred_element_type=F32
    ).astype(BF16)
    query_right = jnp.concatenate([query_right, corner(eig_y, (16, dj))], 0)
    right_blocks = exchange(lambda d: query_right, SHARD_Z)
    eig_shard = sum(jnp.sum(b[64:].astype(F32)) for b in right_blocks)
    right_z = jnp.concatenate([b[:64] for b in right_blocks], 0)
    right = exchange(lambda d: right_z, SHARD_Y)
    eig = ring4(eigvals, "shard", SHARD_Y, di // 2)
    left = jnp.concatenate(
        [jnp.concatenate([b[:64] for b in left_blocks], 1), corner(eig_shard, (16, 4 * di))], 0
    )
    left, rows_all = lax.optimization_barrier((left, rows_all))
    flag = jnp.isnan(part_out[-1, 0])
    left = jnp.where(flag, jnp.zeros_like(left), left)
    ql = lax.all_gather(left, "example", axis=0)

    own_in = jnp.dot(rows_all.reshape(SEQLEN, D), basis_in, preferred_element_type=F32)
    token = jnp.arange(SEQLEN, dtype=jnp.int32)[:, None]
    live = jnp.where(flag, 0, seq_lens[0])
    own_in = jnp.where(token < live, own_in, 0.0).astype(BF16)
    own_in = own_in.reshape(4, 4, 32, di)

    def tokens_of(d):
        part = lax.dynamic_index_in_dim(own_in, (my_y + d) % 4, 1, keepdims=False)
        return part.reshape(128, di)

    ein = jnp.stack([part.T for part in exchange(tokens_of, SHARD_Y)])
    ein, ql = lax.optimization_barrier((ein, ql))
    ein = lax.all_gather(ein, "example", axis=0)

    partial = score_call((z_place, place, slot), ein, [ql, *eout, *right, *eig])[:, :NSEQ]
    pieces = partial.reshape(16, 2, 16).transpose(0, 2, 1).reshape(256, 2)
    pieces = lax.all_to_all(pieces, ("shard", "example"), 0, 0, tiled=True)
    normalizer = 1.0 / math.sqrt(RANK * D * H * SEQLEN)
    return (jnp.sum(pieces, axis=0) * normalizer).reshape(2, 1)


def solution(mesh):
    placed = (
        P("example", "shard", None),
        P("example", "shard", None),
        P("example"),
        P(None, "shard"),
        P(None, "example"),
        P("shard", "example"),
        P("example", None, None),
        P("shard", None, None),
    )
    return jax.shard_map(
        shards, mesh=mesh, in_specs=placed, out_specs=P("shard", "example"), check_vma=False
    )
```

time: 382 us -> 317 us (0.83)
  waiting for transfers between devices: 149 us -> 92.1 us
  local copies, waits for them, and re-layouts: 58 us -> 36.8 us
  starting transfers between devices: 34.4 us -> 47.8 us
    all_gather x1, waiting for transfers between devices: 81.9 us -> 0.02 us  [shards(): rows_all = lax.all_gather(train_in[0], 'shard', axis=0)]
    all_gather x1, waiting for transfers between devices: 0.01 us -> 20.8 us  [shards(): ql = lax.all_gather(left, 'example', axis=0)]
    unnamed x60 -> x41, local copies, waits for them, and re-layouts: 33.1 us -> 15.1 us
    ppermute x3, waiting for transfers between devices: 15 us -> 0.01 us  [ring4(): above = lax.ppermute(block, axis, steps[-1])]
    ppermute x16 -> x19, starting transfers between devices: 21.8 us -> 34.3 us  [the longest x12 23.7 us: exchange(): sent = {d: lax.ppermute(blocks(d), 'shard', steps[d]) for d in (1, -1, 2)}]
    ppermute x3, waiting for transfers between devices: 27.8 us -> 39.3 us  [ring4(): below = lax.ppermute(block, axis, steps[1])]
    ppermute x16 -> x19, waiting for transfers between devices: 23.2 us -> 31.9 us  [the longest x3 17.5 us: ring4(): far_top = lax.ppermute(below[:cut], axis, steps[1])]
    another operation x4 -> x1, other arithmetic: 6.88 us -> 0.83 us  [shards(): ein = jnp.stack([part.T for part in exchange(tokens_of, SHARD_Y)])]
  transfers between devices with their start and end apart: 26 -> 29, of which waited for: 10 -> 10; matrix products, arithmetic and copies ran while one was open for 27% -> 24% of each run, Pallas kernels for 0% -> 0%
where the time goes in v1:
time: 317 us; the launch traced here: 315 us
  waiting for transfers between devices  92.1 us (29%)
  starting transfers between devices  47.8 us (15%)
  local copies, waits for them, and re-layouts  36.8 us (12%)
  Pallas kernels  35.5 us (11%)
  between operations  28.7 us (9%)
  other arithmetic  27.9 us (9%)
  matrix products  24.4 us (8%)
  blocking collectives  21.6 us (7%)
    ppermute x3, waiting for transfers between devices, ring4(): below = lax.ppermute(block, axis, steps[1])  39.3 us
    pallas_call x1, Pallas kernels, score_call(): pl.pallas_call(score_kernel, grid=(NSEQ,), in_specs=[pl.BlockSpec(memory_...  35.5 us
    ppermute x12, starting transfers between devices, exchange(): sent = {d: lax.ppermute(blocks(d), 'shard', steps[d]) for d in (1, -1, 2)}  23.7 us
    all_to_all x1, blocking collectives, shards(): pieces = lax.all_to_all(pieces, ('shard', 'example'), 0, 0, tiled=True)  21.6 us
    all_gather x1, waiting for transfers between devices, shards(): ql = lax.all_gather(left, 'example', axis=0)  20.8 us
    ppermute x3, waiting for transfers between devices, ring4(): far_top = lax.ppermute(below[:cut], axis, steps[1])  17.5 us
    unnamed x41, local copies, waits for them, and re-layouts  15.1 us
    dot_general x2, matrix products, shards(): jnp.dot(b, basis_out, preferred_element_type=F32).astype(BF16)  12.4 us
  transfers between devices with their start and end apart: 29, of which 10 were waited for; matrix products, arithmetic and copies ran while one was open for 24% of the time, Pallas kernels for 0%

profile of v1, /device:TPU:1, one launch (start us, length us, event | category | flops | bytes accessed | tf_op | source)
XLA Modules:
  0.0 314.8 jit_solution(8847740006209617405)
XLA Ops:
  6.5 2.5 collective-permute-start
  9.1 9.1 %collective-permute-done = bf16[32,6912]{1,0:T(8,128)(2,1)} collective-permute-done((bf16[32,6912]{1,0:T(8,128)(2,1)}, bf16[32,6912]{1,0:T(8,128)(2,1)}, u32[]{:S(2)}, u32[]{:S(2)}) %collective-permute-start) | collective-permute-done | bytes 442400 | tf_op jit(solution)/shard_map/ppermute | solution.py:156
  18.2 1.2 pad_maximum_fusion
  19.4 2.2 collective-permute-start.1
  21.6 1.4 collective-permute-start.2
  22.9 1.8 constant_dynamic-update-slice_fusion.5
  24.8 1.8 constant_dynamic-update-slice_fusion.4
  26.6 14.4 %collective-permute-done.1 = bf16[64,6912]{1,0:T(8,128)(2,1)S(1)} collective-permute-done((bf16[64,6912]{1,0:T(8,128)(2,1)S(1)}, bf16[64,6912]{1,0:T(8,128)(2,1)S(1)}, u32[]{:S(2)}, u32[]{:S(2)}) %collective-permute-start.1) | collective-permute-done | bytes 884768 | tf_op jit(solution)/shard_map/ppermute | solution.py:29
  41.6 2.3 collective-permute-start.4
  43.9 1.0 constant_dynamic-update-slice_fusion.3
  44.9 1.0 constant_dynamic-update-slice_fusion.2
  45.9 5.7 %collective-permute-done.3 = bf16[32,6912]{1,0:T(8,128)(2,1)S(1)} collective-permute-done((bf16[32,6912]{1,0:T(8,128)(2,1)S(1)}, bf16[32,6912]{1,0:T(8,128)(2,1)S(1)}, u32[]{:S(2)}, u32[]{:S(2)}) %collective-permute-start.3) | collective-permute-done | bytes 442400 | tf_op jit(solution)/shard_map/ppermute | solution.py:31
  53.2 3.4 %collective-permute-start.5 = (bf16[256,6912]{1,0:T(8,128)(2,1)}, bf16[256,6912]{1,0:T(8,128)(2,1)}, u32[]{:S(2)}, u32[]{:S(2)}) collective-permute-start(bf16[256,6912]{1,0:T(8,128)(2,1)} %constant_dynamic-update-slice_fusion), channel_id=1, source_target_pairs={{0,1},{1,0},{2,3},{3,2},{4,5},{5,4},{6,7},{7,6},{8,9},{9,8},{10,11... | collective-permute-start | bytes 10616840 | tf_op jit(solution)/shard_map/ppermute | solution.py:158
  56.5 1.9 reduce_sum.90
  62.0 1.4 select_convert_fusion.2
  63.5 2.2 convolution_convert_fusion.3
  66.3 1.8 collective-permute-start.6
  68.1 1.4 collective-permute-start.7
  69.5 1.6 collective-permute-start.8
  71.7 2.0 convert_reduce_fusion.7
  73.7 4.7 %convolution_convert_fusion.2 = bf16[64,432]{1,0:T(8,128)(2,1)S(1)} fusion(bf16[64,6912]{1,0:T(8,128)(2,1)S(1)} %bitcast.70, bf16[6912,432]{0,1:T(8,128)(2,1)} %param.12), kind=kOutput, calls=%fused_computation.4 | convolution fusion | flops 382233600 | bytes 6912000 | tf_op jit(solution)/shard_map/dot_general | solution.py:175
  85.7 1.3 select_convert_fusion.1
  87.6 2.9 collective-permute-start.9
  90.5 2.5 collective-permute-start.10
  93.0 4.3 %collective-permute-start.11 = (bf16[80,432]{1,0:T(8,128)(2,1)}, bf16[80,432]{1,0:T(8,128)(2,1)}, u32[]{:S(2)}, u32[]{:S(2)}) collective-permute-start(bf16[80,432]{1,0:T(8,128)(2,1)} %pad_maximum_fusion.5), channel_id=1, source_target_pairs={{0,128},{16,144},{32,160},{48,176},{64,192},{80,208},{96,224},{112... | collective-permute-start | bytes 207368 | tf_op jit(solution)/shard_map/ppermute | solution.py:37
  97.3 1.4 slice.85
  98.8 1.4 slice.86
  101.1 2.6 convert_reduce_fusion.3
  103.8 1.3 convert_reduce_fusion.2
  106.4 1.3 convert_reduce_fusion.1
  108.3 1.3 convert_reduce_fusion
  112.7 2.0 select_convert_fusion
  115.4 6.2 %convolution_convert_fusion = bf16[256,432]{0,1:T(8,128)(2,1)} fusion(bf16[256,6912]{1,0:T(8,128)(2,1)} %collective-permute-done.5, bf16[6912,432]{0,1:T(8,128)(2,1)} %param.12), kind=kOutput, calls=%fused_computation.2 | convolution fusion | flops 1528934400 | bytes 9732096 | tf_op jit(solution)/shard_map/dot_general | solution.py:161
  121.6 1.1 copy.23
  124.5 1.6 broadcast_select_fusion
  127.0 5.1 %fusion = bf16[512,320]{0,1:T(8,128)(2,1)} fusion(bf16[512,5120]{1,0:T(8,128)(2,1)} %bitcast.80, bf16[5120,320]{0,1:T(8,128)(2,1)S(1)} %copy-done, pred[512]{0:T(512)(128)(4,1)S(1)} %iota_compare_fusion.3), kind=kOutput, calls=%fused_computation.1 | convolution fusion | flops 1678049280 | bytes 8847872 | tf_op jit(solution)/shard_map/dot_general | solution.py:192
  132.1 1.9 copy.24
  134.0 1.1 constant_dynamic-slice_fusion.3
  135.1 4.3 %collective-permute-start.14 = (bf16[128,320]{1,0:T(8,128)(2,1)S(1)}, bf16[128,320]{1,0:T(8,128)(2,1)S(1)}, u32[]{:S(2)}, u32[]{:S(2)}) collective-permute-start(bf16[128,320]{1,0:T(8,128)(2,1)S(1)} %bitcast.77), channel_id=1, source_target_pairs={{0,32},{16,48},{32,0},{48,16},{64,96},{80,112},{96,64},{112,80},{1... | collective-permute-start | bytes 245768 | tf_op jit(solution)/shard_map/ppermute | solution.py:37
  141.7 1.5 collective-permute-done.13
  143.2 1.4 collective-permute-done.12
  145.5 20.8 %all-gather.8.cloned.1.call-done = bf16[1280,1280]{1,0:T(8,128)(2,1)} async-done(((bf16[80,1280]{1,0:T(8,128)(2,1)}), bf16[1280,1280]{1,0:T(8,128)(2,1)}) %all-gather.8.cloned.1.call-update) | async-done | bytes 3276816 | tf_op jit(solution)/shard_map/all_gather | solution.py:190
  166.3 1.9 copy.25
  168.2 1.3 collective-permute-start.22
  169.5 1.5 collective-permute-start.23
  171.0 6.2 %convolution_convert_fusion.1 = bf16[256,432]{0,1:T(8,128)(2,1)} fusion(bf16[256,6912]{1,0:T(8,128)(2,1)} %constant_dynamic-update-slice_fusion, bf16[6912,432]{0,1:T(8,128)(2,1)} %param.12), kind=kOutput, calls=%fused_computation.3 | convolution fusion | flops 1528934400 | bytes 9732096 | tf_op jit(solution)/shard_map/dot_general | solution.py:161
  177.2 1.8 copy.22
  178.9 1.8 pad_maximum_fusion.1.out_0
  180.8 2.3 collective-permute-start.15
  183.1 1.5 collective-permute-start.16
  188.1 2.6 collective-permute-start.20
  190.7 1.7 slice.98
  192.5 1.7 slice.99
  194.2 24.9 %collective-permute-done.15.out_1 = bf16[512,432]{1,0:T(8,128)(2,1)} collective-permute-done((bf16[512,432]{1,0:T(8,128)(2,1)}, bf16[512,432]{1,0:T(8,128)(2,1)}, u32[]{:S(2)}, u32[]{:S(2)}) %collective-permute-start.15) | collective-permute-done | bytes 442400 | tf_op jit(solution)/shard_map/ppermute | solution.py:29
  219.1 1.6 collective-permute-start.25
  221.4 1.0 slice.93
  223.0 1.0 slice.94
  224.0 0.9 collective-permute-start.17
  225.0 2.7 collective-permute-start.18
  228.9 1.5 collective-permute-done.21.qr_3
  231.1 11.8 %collective-permute-done.17.out_top = bf16[256,432]{1,0:T(8,128)(2,1)S(1)} collective-permute-done((bf16[256,432]{1,0:T(8,128)(2,1)S(1)}, bf16[256,432]{1,0:T(8,128)(2,1)S(1)}, u32[]{:S(2)}, u32[]{:S(2)}) %collective-permute-start.17) | collective-permute-done | bytes 221216 | tf_op jit(solution)/shard_map/ppermute | solution.py:31
  244.3 1.1 copy-done.1
  250.2 35.5 %shard_map.82 = f32[32,128]{1,0:T(8,128)S(1)} custom-call(s32[4]{0:T(128)S(1)} %copy-done.3, s32[16]{0:T(128)S(1)} %copy-done.2, s32[16]{0:T(128)S(1)} %copy-done.4, bf16[16,4,320,128]{3,2,1,0:T(8,128)(2,1)} %bitcast.81, bf16[16,80,1280]{2,1,0:T(8,128)(2,1)} %bitcast.82, bf16[512,432]{1,0:T(8,128)(2,1)} %pad_maximum_fusion.1.out_0, ...), custom_call_target="tpu_custom_call" | custom-call | flops 20000000000 | bytes 16000000 | tf_op jit(solution)/shard_map/pallas_call | solution.py:115
  285.9 21.6 %all_to_all.9 = f32[256,1,2]{2,1,0:T(1,128)S(1)} all-to-all(f32[256,1,2]{2,1,0:T(1,128)S(1)} %bitcast.72), channel_id=1, replica_groups=mesh['shard'=16,'example'=16] {'shard','example'}, dimensions={0} | all-to-all | bytes 4096 | tf_op jit(solution)/shard_map/all_to_all | solution.py:208
  (97 shorter events, 26.0 us)
Async XLA Ops:
  6.5 56.9 %copy-start = (bf16[5120,320]{0,1:T(8,128)(2,1)S(1)}, bf16[5120,320]{0,1:T(8,128)(2,1)}, u32[]{:S(2)}) copy-start(bf16[5120,320]{0,1:T(8,128)(2,1)} %param.11) | copy-start | bytes 9830404
  6.5 118.0 %all-gather.6.cloned.1.call-start = ((), (), s32[]{:S(2)}) async-start(), calls=%async_computation.1 | async-start | bytes 5570560 | tf_op jit(solution)/shard_map/all_gather | solution.py:154
  6.5 11.6 %collective-permute-start = (bf16[32,6912]{1,0:T(8,128)(2,1)}, bf16[32,6912]{1,0:T(8,128)(2,1)}, u32[]{:S(2)}, u32[]{:S(2)}) collective-permute-start(bf16[32,6912]{1,0:T(8,128)(2,1)} %bitcast.67), channel_id=1, source_target_pairs={{0,8},{1,9},{2,10},{3,11},{4,12},{5,13},{6,14},{7,15},{8,0},{9,1},... | collective-permute-start | bytes 1327112 | tf_op jit(solution)/shard_map/ppermute | solution.py:156
  9.0 157.2 %all-gather.8.cloned.1.call-start = ((), (), s32[]{:S(2)}) async-start(), calls=%async_computation.2 | async-start | bytes 3481600 | tf_op jit(solution)/shard_map/all_gather | solution.py:190
  19.4 21.6 %collective-permute-start.1 = (bf16[64,6912]{1,0:T(8,128)(2,1)S(1)}, bf16[64,6912]{1,0:T(8,128)(2,1)S(1)}, u32[]{:S(2)}, u32[]{:S(2)}) collective-permute-start(bf16[64,6912]{1,0:T(8,128)(2,1)S(1)} %pad_maximum_fusion), channel_id=1, source_target_pairs={{0,2},{1,3},{2,4},{3,5},{4,6},{5,7},{6,0},{7,1},{8,10},{9,11},{10,... | collective-permute-start | bytes 2654216 | tf_op jit(solution)/shard_map/ppermute | solution.py:29
  21.6 20.0 %collective-permute-start.2 = (bf16[64,6912]{1,0:T(8,128)(2,1)S(1)}, bf16[64,6912]{1,0:T(8,128)(2,1)S(1)}, u32[]{:S(2)}, u32[]{:S(2)}) collective-permute-start(bf16[64,6912]{1,0:T(8,128)(2,1)S(1)} %pad_maximum_fusion), channel_id=1, source_target_pairs={{0,6},{1,7},{2,0},{3,1},{4,2},{5,3},{6,4},{7,5},{8,14},{9,15},{10,... | collective-permute-start | bytes 2654216 | tf_op jit(solution)/shard_map/ppermute | solution.py:30
  41.0 10.5 %collective-permute-start.3 = (bf16[32,6912]{1,0:T(8,128)(2,1)S(1)}, bf16[32,6912]{1,0:T(8,128)(2,1)S(1)}, u32[]{:S(2)}, u32[]{:S(2)}) collective-permute-start(bf16[32,6912]{1,0:T(8,128)(2,1)S(1)} %slice.81), channel_id=1, source_target_pairs={{0,2},{1,3},{2,4},{3,5},{4,6},{5,7},{6,0},{7,1},{8,10},{9,11},{10,... | collective-permute-start | bytes 1327112 | tf_op jit(solution)/shard_map/ppermute | solution.py:31
  41.6 10.7 %collective-permute-start.4 = (bf16[32,6912]{1,0:T(8,128)(2,1)S(1)}, bf16[32,6912]{1,0:T(8,128)(2,1)S(1)}, u32[]{:S(2)}, u32[]{:S(2)}) collective-permute-start(bf16[32,6912]{1,0:T(8,128)(2,1)S(1)} %slice.82), channel_id=1, source_target_pairs={{0,6},{1,7},{2,0},{3,1},{4,2},{5,3},{6,4},{7,5},{8,14},{9,15},{10,... | collective-permute-start | bytes 1327112 | tf_op jit(solution)/shard_map/ppermute | solution.py:32
  53.2 62.2 %collective-permute-start.5 = (bf16[256,6912]{1,0:T(8,128)(2,1)}, bf16[256,6912]{1,0:T(8,128)(2,1)}, u32[]{:S(2)}, u32[]{:S(2)}) collective-permute-start(bf16[256,6912]{1,0:T(8,128)(2,1)} %constant_dynamic-update-slice_fusion), channel_id=1, source_target_pairs={{0,1},{1,0},{2,3},{3,2},{4,5},{5,4},{6,7},{7,6},{8,9},{9,8},{10,11... | collective-permute-start | bytes 10616840 | tf_op jit(solution)/shard_map/ppermute | solution.py:158
  62.0 11.7 %copy-start.11 = (bf16[2,32,6912]{2,1,0:T(8,128)(2,1)S(1)}, bf16[2,32,6912]{2,1,0:T(8,128)(2,1)}, u32[]{:S(2)}) copy-start(bf16[2,32,6912]{2,1,0:T(8,128)(2,1)} %param.15) | copy-start | bytes 2654212
  62.0 23.6 %copy-start.15 = (pred[16]{0:T(512)(128)(4,1)}, pred[16]{0:T(512)(128)(4,1)S(1)}, u32[]{:S(2)}) copy-start(pred[16]{0:T(512)(128)(4,1)S(1)} %get-tuple-element.17) | copy-start | bytes 52
  62.0 23.6 %copy-start.16 = (pred[16]{0:T(512)(128)(4,1)}, pred[16]{0:T(512)(128)(4,1)S(1)}, u32[]{:S(2)}) copy-start(pred[16]{0:T(512)(128)(4,1)S(1)} %get-tuple-element.18) | copy-start | bytes 52
  66.3 12.1 %collective-permute-start.6 = (bf16[80,320]{1,0:T(8,128)(2,1)}, bf16[80,320]{1,0:T(8,128)(2,1)S(1)}, u32[]{:S(2)}, u32[]{:S(2)}) collective-permute-start(bf16[80,320]{1,0:T(8,128)(2,1)} %pad_maximum_fusion.6), channel_id=1, source_target_pairs={{0,16},{16,32},{32,48},{48,0},{64,80},{80,96},{96,112},{112,64},{1... | collective-permute-start | bytes 153608 | tf_op jit(solution)/shard_map/ppermute | solution.py:37
  68.1 10.9 %collective-permute-start.7 = (bf16[80,320]{1,0:T(8,128)(2,1)}, bf16[80,320]{1,0:T(8,128)(2,1)S(1)}, u32[]{:S(2)}, u32[]{:S(2)}) collective-permute-start(bf16[80,320]{1,0:T(8,128)(2,1)} %pad_maximum_fusion.6), channel_id=1, source_target_pairs={{0,48},{16,0},{32,16},{48,32},{64,112},{80,64},{96,80},{112,96},{1... | collective-permute-start | bytes 153608 | tf_op jit(solution)/shard_map/ppermute | solution.py:37
  69.5 12.6 %collective-permute-start.8 = (bf16[80,320]{1,0:T(8,128)(2,1)}, bf16[80,320]{1,0:T(8,128)(2,1)S(1)}, u32[]{:S(2)}, u32[]{:S(2)}) collective-permute-start(bf16[80,320]{1,0:T(8,128)(2,1)} %pad_maximum_fusion.6), channel_id=1, source_target_pairs={{0,32},{16,48},{32,0},{48,16},{64,96},{80,112},{96,64},{112,80},{1... | collective-permute-start | bytes 153608 | tf_op jit(solution)/shard_map/ppermute | solution.py:37
  78.3 20.4 %copy-start.12 = (bf16[64,432]{1,0:T(8,128)(2,1)}, bf16[64,432]{1,0:T(8,128)(2,1)S(1)}, u32[]{:S(2)}) copy-start(bf16[64,432]{1,0:T(8,128)(2,1)S(1)} %convolution_convert_fusion.2) | copy-start | bytes 165892
  78.4 20.4 %copy-start.17 = (pred[432]{0:T(512)(128)(4,1)}, pred[432]{0:T(512)(128)(4,1)S(1)}, u32[]{:S(2)}) copy-start(pred[432]{0:T(512)(128)(4,1)S(1)} %iota_compare_fusion.1) | copy-start | bytes 1300
  79.0 0.6 copy-start.13
  82.1 10.9 %copy-start.14 = (bf16[80,320]{1,0:T(8,128)(2,1)}, bf16[80,320]{1,0:T(8,128)(2,1)S(1)}, u32[]{:S(2)}) copy-start(bf16[80,320]{1,0:T(8,128)(2,1)S(1)} %collective-permute-done.8) | copy-start | bytes 153604
  87.6 16.2 %collective-permute-start.9 = (bf16[80,432]{1,0:T(8,128)(2,1)}, bf16[80,432]{1,0:T(8,128)(2,1)}, u32[]{:S(2)}, u32[]{:S(2)}) collective-permute-start(bf16[80,432]{1,0:T(8,128)(2,1)} %pad_maximum_fusion.5), channel_id=1, source_target_pairs={{0,64},{16,80},{32,96},{48,112},{64,128},{80,144},{96,160},{112,17... | collective-permute-start | bytes 207368 | tf_op jit(solution)/shard_map/ppermute | solution.py:37
  90.5 15.9 %collective-permute-start.10 = (bf16[80,432]{1,0:T(8,128)(2,1)}, bf16[80,432]{1,0:T(8,128)(2,1)}, u32[]{:S(2)}, u32[]{:S(2)}) collective-permute-start(bf16[80,432]{1,0:T(8,128)(2,1)} %pad_maximum_fusion.5), channel_id=1, source_target_pairs={{0,192},{16,208},{32,224},{48,240},{64,0},{80,16},{96,32},{112,48}... | collective-permute-start | bytes 207368 | tf_op jit(solution)/shard_map/ppermute | solution.py:37
  93.0 15.3 %collective-permute-start.11 = (bf16[80,432]{1,0:T(8,128)(2,1)}, bf16[80,432]{1,0:T(8,128)(2,1)}, u32[]{:S(2)}, u32[]{:S(2)}) collective-permute-start(bf16[80,432]{1,0:T(8,128)(2,1)} %pad_maximum_fusion.5), channel_id=1, source_target_pairs={{0,128},{16,144},{32,160},{48,176},{64,192},{80,208},{96,224},{112... | collective-permute-start | bytes 207368 | tf_op jit(solution)/shard_map/ppermute | solution.py:37
  126.2 118.1 %all-gather.10.cloned.1.call-start = ((), (), s32[]{:S(2)}) async-start(), calls=%async_computation.3 | async-start | bytes 5570560 | tf_op jit(solution)/shard_map/all_gather | solution.py:204
  135.1 6.7 %collective-permute-start.14 = (bf16[128,320]{1,0:T(8,128)(2,1)S(1)}, bf16[128,320]{1,0:T(8,128)(2,1)S(1)}, u32[]{:S(2)}, u32[]{:S(2)}) collective-permute-start(bf16[128,320]{1,0:T(8,128)(2,1)S(1)} %bitcast.77), channel_id=1, source_target_pairs={{0,32},{16,48},{32,0},{48,16},{64,96},{80,112},{96,64},{112,80},{1... | collective-permute-start | bytes 245768 | tf_op jit(solution)/shard_map/ppermute | solution.py:37
  139.4 3.9 %collective-permute-start.13 = (bf16[128,320]{1,0:T(8,128)(2,1)S(1)}, bf16[128,320]{1,0:T(8,128)(2,1)S(1)}, u32[]{:S(2)}, u32[]{:S(2)}) collective-permute-start(bf16[128,320]{1,0:T(8,128)(2,1)S(1)} %bitcast.75), channel_id=1, source_target_pairs={{0,48},{16,0},{32,16},{48,32},{64,112},{80,64},{96,80},{112,96},{1... | collective-permute-start | bytes 245768 | tf_op jit(solution)/shard_map/ppermute | solution.py:37
  140.0 4.7 %collective-permute-start.12 = (bf16[128,320]{1,0:T(8,128)(2,1)S(1)}, bf16[128,320]{1,0:T(8,128)(2,1)S(1)}, u32[]{:S(2)}, u32[]{:S(2)}) collective-permute-start(bf16[128,320]{1,0:T(8,128)(2,1)S(1)} %bitcast.74), channel_id=1, source_target_pairs={{0,16},{16,32},{32,48},{48,0},{64,80},{80,96},{96,112},{112,64},{1... | collective-permute-start | bytes 245768 | tf_op jit(solution)/shard_map/ppermute | solution.py:37
  168.2 19.9 %collective-permute-start.22 = (f32[320,432]{1,0:T(8,128)}, f32[320,432]{1,0:T(8,128)}, u32[]{:S(2)}, u32[]{:S(2)}) collective-permute-start(f32[320,432]{1,0:T(8,128)} %eig_0.1), channel_id=1, source_target_pairs={{0,16},{16,32},{32,48},{48,0},{64,80},{80,96},{96,112},{112,64},{1... | collective-permute-start | bytes 1658888 | tf_op jit(solution)/shard_map/ppermute | solution.py:29
  169.5 23.0 %collective-permute-start.23 = (f32[320,432]{1,0:T(8,128)}, f32[320,432]{1,0:T(8,128)}, u32[]{:S(2)}, u32[]{:S(2)}) collective-permute-start(f32[320,432]{1,0:T(8,128)} %eig_0.1), channel_id=1, source_target_pairs={{0,48},{16,0},{32,16},{48,32},{64,112},{80,64},{96,80},{112,96},{1... | collective-permute-start | bytes 1658888 | tf_op jit(solution)/shard_map/ppermute | solution.py:30
  180.8 38.3 %collective-permute-start.15 = (bf16[512,432]{1,0:T(8,128)(2,1)}, bf16[512,432]{1,0:T(8,128)(2,1)}, u32[]{:S(2)}, u32[]{:S(2)}) collective-permute-start(bf16[512,432]{1,0:T(8,128)(2,1)} %pad_maximum_fusion.1.out_0), channel_id=1, source_target_pairs={{0,64},{16,80},{32,96},{48,112},{64,128},{80,144},{96,160},{112,17... | collective-permute-start | bytes 1327112 | tf_op jit(solution)/shard_map/ppermute | solution.py:29
  183.1 39.3 %collective-permute-start.16 = (bf16[512,432]{1,0:T(8,128)(2,1)}, bf16[512,432]{1,0:T(8,128)(2,1)}, u32[]{:S(2)}, u32[]{:S(2)}) collective-permute-start(bf16[512,432]{1,0:T(8,128)(2,1)} %pad_maximum_fusion.1.out_0), channel_id=1, source_target_pairs={{0,192},{16,208},{32,224},{48,240},{64,0},{80,16},{96,32},{112,48}... | collective-permute-start | bytes 1327112 | tf_op jit(solution)/shard_map/ppermute | solution.py:30
  188.0 36.0 %collective-permute-start.19 = (bf16[256,432]{1,0:T(8,128)(2,1)S(1)}, bf16[256,432]{1,0:T(8,128)(2,1)}, u32[]{:S(2)}, u32[]{:S(2)}) collective-permute-start(bf16[256,432]{1,0:T(8,128)(2,1)S(1)} %pad_maximum_fusion.3.qr_0), channel_id=1, source_target_pairs={{0,16},{16,32},{32,48},{48,0},{64,80},{80,96},{96,112},{112,64},{1... | collective-permute-start | bytes 663560 | tf_op jit(solution)/shard_map/ppermute | solution.py:37
  188.1 36.9 %collective-permute-start.20 = (bf16[256,432]{1,0:T(8,128)(2,1)S(1)}, bf16[256,432]{1,0:T(8,128)(2,1)}, u32[]{:S(2)}, u32[]{:S(2)}) collective-permute-start(bf16[256,432]{1,0:T(8,128)(2,1)S(1)} %pad_maximum_fusion.3.qr_0), channel_id=1, source_target_pairs={{0,48},{16,0},{32,16},{48,32},{64,112},{80,64},{96,80},{112,96},{1... | collective-permute-start | bytes 663560 | tf_op jit(solution)/shard_map/ppermute | solution.py:37
  192.5 38.6 %collective-permute-start.24 = (f32[160,432]{1,0:T(8,128)}, f32[160,432]{1,0:T(8,128)}, u32[]{:S(2)}, u32[]{:S(2)}) collective-permute-start(f32[160,432]{1,0:T(8,128)} %slice.98), channel_id=1, source_target_pairs={{0,16},{16,32},{32,48},{48,0},{64,80},{80,96},{96,112},{112,64},{1... | collective-permute-start | bytes 829448 | tf_op jit(solution)/shard_map/ppermute | solution.py:31
  219.1 12.0 %collective-permute-start.25 = (f32[160,432]{1,0:T(8,128)}, f32[160,432]{1,0:T(8,128)}, u32[]{:S(2)}, u32[]{:S(2)}) collective-permute-start(f32[160,432]{1,0:T(8,128)} %slice.99), channel_id=1, source_target_pairs={{0,48},{16,0},{32,16},{48,32},{64,112},{80,64},{96,80},{112,96},{1... | collective-permute-start | bytes 829448 | tf_op jit(solution)/shard_map/ppermute | solution.py:32
  222.4 7.9 %collective-permute-start.21 = (bf16[256,432]{1,0:T(8,128)(2,1)S(1)}, bf16[256,432]{1,0:T(8,128)(2,1)S(1)}, u32[]{:S(2)}, u32[]{:S(2)}) collective-permute-start(bf16[256,432]{1,0:T(8,128)(2,1)S(1)} %pad_maximum_fusion.3.qr_0), channel_id=1, source_target_pairs={{0,32},{16,48},{32,0},{48,16},{64,96},{80,112},{96,64},{112,80},{1... | collective-permute-start | bytes 663560 | tf_op jit(solution)/shard_map/ppermute | solution.py:37
  224.0 18.9 %collective-permute-start.17 = (bf16[256,432]{1,0:T(8,128)(2,1)S(1)}, bf16[256,432]{1,0:T(8,128)(2,1)S(1)}, u32[]{:S(2)}, u32[]{:S(2)}) collective-permute-start(bf16[256,432]{1,0:T(8,128)(2,1)S(1)} %slice.93), channel_id=1, source_target_pairs={{0,64},{16,80},{32,96},{48,112},{64,128},{80,144},{96,160},{112,17... | collective-permute-start | bytes 663560 | tf_op jit(solution)/shard_map/ppermute | solution.py:31
  225.0 18.6 %collective-permute-start.18 = (bf16[256,432]{1,0:T(8,128)(2,1)S(1)}, bf16[256,432]{1,0:T(8,128)(2,1)S(1)}, u32[]{:S(2)}, u32[]{:S(2)}) collective-permute-start(bf16[256,432]{1,0:T(8,128)(2,1)S(1)} %slice.94), channel_id=1, source_target_pairs={{0,192},{16,208},{32,224},{48,240},{64,0},{80,16},{96,32},{112,48}... | collective-permute-start | bytes 663560 | tf_op jit(solution)/shard_map/ppermute | solution.py:32
  230.4 0.7 copy-start.5
  242.9 0.7 copy-start.7
  243.6 0.7 copy-start.9
  244.3 1.1 copy-start.1
  245.4 0.7 copy-start.2
  246.0 0.6 copy-start.3
  246.7 0.7 copy-start.4
  247.4 0.9 copy-start.6
  248.3 0.9 copy-start.8
  249.3 0.9 copy-start.10
Sparse Core Ops, SparseCore 0:
  9.8 95.3 all-gather.5
  126.3 39.9 all-gather.7
  168.3 65.7 all-gather.9

commit v2 on v1

--- a/solution.py
+++ b/solution.py
@@ -55,18 +55,21 @@
 
 
 def score_kernel(
-    z_place, place, slot, ein, ql,
+    z_place, place, slot, ein,
+    ql_0, ql_1, ql_2, ql_top, ql_bottom,
     out_0, out_1, out_2, out_top, out_bottom,
     qr_0, qr_1, qr_2, qr_3,
     eig_0, eig_1, eig_2, eig_top, eig_bottom,
-    out, inverse, right, grads, scaled,
+    out, inverse, left, ql_3, right, out_3, grads, scaled,
 ):
     n = pl.program_id(0)
     di = ein.shape[2]
 
     @pl.when(n == 0)
     def _():
-        damping = (0.1 / (D * H)) * jnp.sum(ql[:, 64:, :].astype(F32))
+        damping = (0.1 / (D * H)) * sum(
+            jnp.sum(qr[256:, :].astype(F32)) for qr in (qr_0, qr_1, qr_2, qr_3)
+        )
         row = 0
         for eig in (eig_0, eig_1, eig_2, eig_top, eig_bottom):
             inverse[row : row + eig.shape[0], :] = 1.0 / (eig[...] + damping)
@@ -75,30 +78,29 @@
             for kz in range(4):
                 start = pl.multiple_of(place[4 * ky + kz] * 64, 64)
                 right[pl.ds(start, 64), :] = qr[64 * kz : 64 * kz + 64, :]
+        for far, top, bottom in ((out_3, out_top, out_bottom), (ql_3, ql_top, ql_bottom)):
+            far[: top.shape[0], :] = top[...]
+            far[top.shape[0] :, :] = bottom[...]
+        for e in range(NSEQ):
+            first = pl.multiple_of(slot[e] * 32, 32)
+            parts = [ql[pl.ds(first, 32), :] for ql in (ql_0, ql_1, ql_2, ql_3)]
+            left[64 * e : 64 * e + 32, :] = jnp.concatenate([p[:, :di] for p in parts], 1)
+            left[64 * e + 32 : 64 * e + 64, :] = jnp.concatenate([p[:, di:] for p in parts], 1)
         out[...] = jnp.zeros_like(out)
 
     first = pl.multiple_of(slot[n] * 32, 32)
-    starts = [pl.multiple_of(z_place[k] * 32, 32) for k in range(4)]
-    for k, rows in enumerate((out_0, out_1, out_2)):
-        grads[pl.ds(starts[k], 32), :] = rows[pl.ds(first, 32), :]
-    cut = out_top.shape[0]
-
-    @pl.when(first < cut)
-    def _():
-        grads[pl.ds(starts[3], 32), :] = out_top[pl.ds(first, 32), :]
-
-    @pl.when(first >= cut)
-    def _():
-        grads[pl.ds(starts[3], 32), :] = out_bottom[pl.ds(first - cut, 32), :]
-
+    for k, rows in enumerate((out_0, out_1, out_2, out_3)):
+        start = pl.multiple_of(z_place[k] * 32, 32)
+        grads[pl.ds(start, 32), :] = rows[pl.ds(first, 32), :]
     for k in range(4):
         pair = jnp.dot(ein[0, k], grads[...], preferred_element_type=F32)
         scaled[di * k : di * k + di, :] = (pair * inverse[di * k : di * k + di, :]).astype(BF16)
     width = scaled.shape[1]
     sums = []
     for k in range(4):
-        left = ql[4 * k : 4 * k + 4, :64, :].reshape(256, ql.shape[-1])
-        part = jnp.dot(left, scaled[...], preferred_element_type=F32)
+        part = jnp.dot(
+            left[256 * k : 256 * k + 256, :], scaled[...], preferred_element_type=F32
+        )
         part = part * right[256 * k : 256 * k + 256, :].astype(F32)
         sums.append(jnp.sum(part.reshape(8, RANK, width), axis=1))
     total = jnp.sum(jnp.concatenate(sums, 0), axis=1, keepdims=True)
@@ -107,7 +109,7 @@
 
 
 def score_call(places, ein, rest):
-    di, dj = ein.shape[2], rest[1].shape[1]
+    di, dj = ein.shape[2], rest[5].shape[1]
 
     def whole(x):
         return pl.BlockSpec(x.shape, lambda n, rank=x.ndim: (0,) * rank)
@@ -122,7 +124,10 @@
         out_shape=jax.ShapeDtypeStruct((QUERIES, 128), F32),
         scratch_shapes=[
             pltpu.VMEM((4 * di, dj), F32),
+            pltpu.VMEM((16 * 64, 4 * di), BF16),
+            pltpu.VMEM((NSEQ * 32, 2 * di), BF16),
             pltpu.VMEM((16 * 64, dj), BF16),
+            pltpu.VMEM((NSEQ * 32, dj), BF16),
             pltpu.VMEM((128, dj), BF16),
             pltpu.VMEM((4 * di, dj), BF16),
         ],
@@ -153,41 +158,40 @@
 
     rows_all = lax.all_gather(train_in[0], "shard", axis=0)
 
-    block = jnp.concatenate([train_grad[0], lax.ppermute(train_grad[0], "example", EXAMPLE_Z)], 0)
+    query_left = jnp.dot(
+        query_in.reshape(64, D), basis_in, preferred_element_type=F32
+    ).astype(BF16)
+    block = jnp.concatenate(
+        [train_grad[0], query_left[:32], query_left[32:], corner(jnp.sum(eigvals), (32, 128))], 1
+    )
+    block = jnp.concatenate([block, lax.ppermute(block, "example", EXAMPLE_Z)], 0)
     block = jnp.concatenate(ring4(block, "example", EXAMPLE_X, 32), 0)
     other = lax.ppermute(block, "example", EXAMPLE_CORE)
     part_out = jnp.concatenate(
         [
-            jnp.dot(b, basis_out, preferred_element_type=F32).astype(BF16)
+            jnp.dot(b[:, :H], basis_out, preferred_element_type=F32).astype(BF16)
             for b in (block, other)
         ],
         0,
     )
     part_out = with_layout_constraint(part_out, Layout(major_to_minor=(0, 1)))
     eout = ring4(part_out, "shard", SHARD_Z, 256)
-
-    query_left = jnp.dot(
-        query_in.reshape(64, D), basis_in, preferred_element_type=F32
-    ).astype(BF16)
-    query_left = jnp.concatenate([query_left, corner(jnp.sum(eigvals), (16, di))], 0)
-    left_blocks = exchange(lambda d: query_left, SHARD_Y)
-    eig_y = sum(jnp.sum(b[64:].astype(F32)) for b in left_blocks)
+    left = jnp.concatenate([b[:, H : H + 2 * di] for b in (block, other)], 0)
+    left = ring4(left, "shard", SHARD_Y, 256)
+    eig_example = jnp.sum(
+        jnp.concatenate([b[:, H + 2 * di :] for b in (block, other)], 0).astype(F32)
+    )
+
     query_right = jnp.dot(
         query_out.reshape(64, H), basis_out, preferred_element_type=F32
     ).astype(BF16)
-    query_right = jnp.concatenate([query_right, corner(eig_y, (16, dj))], 0)
+    query_right = jnp.concatenate([query_right, corner(eig_example, (16, dj))], 0)
     right_blocks = exchange(lambda d: query_right, SHARD_Z)
-    eig_shard = sum(jnp.sum(b[64:].astype(F32)) for b in right_blocks)
-    right_z = jnp.concatenate([b[:64] for b in right_blocks], 0)
+    eig_z = jnp.sum(jnp.concatenate([b[64:] for b in right_blocks], 0).astype(F32))
+    right_z = jnp.concatenate([b[:64] for b in right_blocks] + [corner(eig_z, (16, dj))], 0)
     right = exchange(lambda d: right_z, SHARD_Y)
     eig = ring4(eigvals, "shard", SHARD_Y, di // 2)
-    left = jnp.concatenate(
-        [jnp.concatenate([b[:64] for b in left_blocks], 1), corner(eig_shard, (16, 4 * di))], 0
-    )
-    left, rows_all = lax.optimization_barrier((left, rows_all))
     flag = jnp.isnan(part_out[-1, 0])
-    left = jnp.where(flag, jnp.zeros_like(left), left)
-    ql = lax.all_gather(left, "example", axis=0)
 
     own_in = jnp.dot(rows_all.reshape(SEQLEN, D), basis_in, preferred_element_type=F32)
     token = jnp.arange(SEQLEN, dtype=jnp.int32)[:, None]
@@ -200,10 +204,10 @@
         return part.reshape(128, di)
 
     ein = jnp.stack([part.T for part in exchange(tokens_of, SHARD_Y)])
-    ein, ql = lax.optimization_barrier((ein, ql))
+    ein = jnp.where(jnp.isnan(eout[1][0, 0] + eout[2][0, 0]), jnp.zeros_like(ein), ein)
     ein = lax.all_gather(ein, "example", axis=0)
 
-    partial = score_call((z_place, place, slot), ein, [ql, *eout, *right, *eig])[:, :NSEQ]
+    partial = score_call((z_place, place, slot), ein, [*left, *eout, *right, *eig])[:, :NSEQ]
     pieces = partial.reshape(16, 2, 16).transpose(0, 2, 1).reshape(256, 2)
     pieces = lax.all_to_all(pieces, ("shard", "example"), 0, 0, tiled=True)
     normalizer = 1.0 / math.sqrt(RANK * D * H * SEQLEN)

time: 317 us -> 305 us (0.962)
  waiting for transfers between devices: 92.1 us -> 66.9 us
  blocking collectives: 21.6 us -> 43 us
  other arithmetic: 27.9 us -> 18.9 us
    all_gather x1, waiting for transfers between devices: 0.02 us -> 24.8 us  [shards(): rows_all = lax.all_gather(train_in[0], 'shard', axis=0)]
    all_to_all x1, blocking collectives: 21.6 us -> 43 us  [shards(): pieces = lax.all_to_all(pieces, ('shard', 'example'), 0, 0, tiled=True)]
    all_gather x1 -> x0, waiting for transfers between devices: 20.8 us -> none  [shards(): ql = lax.all_gather(left, 'example', axis=0)]
    ppermute x3 -> x4, waiting for transfers between devices: 39.3 us -> 20.1 us  [ring4(): below = lax.ppermute(block, axis, steps[1])]
    ppermute x3 -> x4, waiting for transfers between devices: 17.5 us -> 6.61 us  [ring4(): far_top = lax.ppermute(below[:cut], axis, steps[1])]
    reduce_sum x8 -> x2, other arithmetic: 10.4 us -> 1.3 us  [the longest x1 0.66 us: shards(): jnp.sum(jnp.concatenate([b[:, H + 2 * di:] for b in (block, other)], 0).a...]
    ppermute x12 -> x9, starting transfers between devices: 23.7 us -> 15.8 us  [exchange(): sent = {d: lax.ppermute(blocks(d), 'shard', steps[d]) for d in (1, -1, 2)}]
    ppermute x3 -> x4, starting transfers between devices: 4.31 us -> 8.41 us  [ring4(): above = lax.ppermute(block, axis, steps[-1])]
  transfers between devices with their start and end apart: 29 -> 29, of which waited for: 10 -> 9; matrix products, arithmetic and copies ran while one was open for 24% -> 21% of each run, Pallas kernels for 0% -> 0%
where the time goes in v2:
time: 305 us; the launch traced here: 304 us
  waiting for transfers between devices  66.9 us (22%)
  starting transfers between devices  48.5 us (16%)
  blocking collectives  43 us (14%)
  local copies, waits for them, and re-layouts  38.9 us (13%)
  Pallas kernels  35.5 us (12%)
  between operations  27.7 us (9%)
  matrix products  24.6 us (8%)
  other arithmetic  18.9 us (6%)
    all_to_all x1, blocking collectives, shards(): pieces = lax.all_to_all(pieces, ('shard', 'example'), 0, 0, tiled=True)  43 us
    pallas_call x1, Pallas kernels, score_call(): pl.pallas_call(score_kernel, grid=(NSEQ,), in_specs=[pl.BlockSpec(memory_...  35.5 us
    all_gather x1, waiting for transfers between devices, shards(): rows_all = lax.all_gather(train_in[0], 'shard', axis=0)  24.8 us
    ppermute x4, waiting for transfers between devices, ring4(): below = lax.ppermute(block, axis, steps[1])  20.1 us
    ppermute x9, starting transfers between devices, exchange(): sent = {d: lax.ppermute(blocks(d), 'shard', steps[d]) for d in (1, -1, 2)}  15.8 us
    unnamed x34, local copies, waits for them, and re-layouts  14.3 us
    dot_general x2, matrix products, shards(): jnp.dot(b[:, :H], basis_out, preferred_element_type=F32).astype(BF16)  11.8 us
    ppermute x4, starting transfers between devices, ring4(): far_bottom = lax.ppermute(above[cut:], axis, steps[-1])  10.2 us
  transfers between devices with their start and end apart: 29, of which 9 were waited for; matrix products, arithmetic and copies ran while one was open for 21% of the time, Pallas kernels for 0%

profile of v2, /device:TPU:1, one launch (start us, length us, event | category | flops | bytes accessed | tf_op | source)
XLA Modules:
  0.0 304.0 jit_solution(4551922958351509682)
XLA Ops:
  6.6 2.0 reduce_sum.36
  12.2 2.2 convolution_convert_fusion.1
  14.4 1.3 select_convert_fusion
  15.8 1.9 concatenate.35
  17.6 2.5 collective-permute-start
  20.2 10.1 %collective-permute-done = bf16[32,7680]{1,0:T(8,128)(2,1)} collective-permute-done((bf16[32,7680]{1,0:T(8,128)(2,1)}, bf16[32,7680]{1,0:T(8,128)(2,1)}, u32[]{:S(2)}, u32[]{:S(2)}) %collective-permute-start) | collective-permute-done | bytes 491552 | tf_op jit(solution)/shard_map/ppermute | solution.py:167
  30.3 1.2 pad_maximum_fusion
  31.6 2.2 collective-permute-start.1
  33.8 1.4 collective-permute-start.2
  35.1 1.9 constant_dynamic-update-slice_fusion.5
  37.0 1.9 constant_dynamic-update-slice_fusion.4
  38.9 16.4 %collective-permute-done.1 = bf16[64,7680]{1,0:T(8,128)(2,1)S(1)} collective-permute-done((bf16[64,7680]{1,0:T(8,128)(2,1)S(1)}, bf16[64,7680]{1,0:T(8,128)(2,1)S(1)}, u32[]{:S(2)}, u32[]{:S(2)}) %collective-permute-start.1) | collective-permute-done | bytes 983072 | tf_op jit(solution)/shard_map/ppermute | solution.py:29
  55.9 2.3 collective-permute-start.4
  58.2 1.0 constant_dynamic-update-slice_fusion.3
  59.2 1.0 constant_dynamic-update-slice_fusion.2
  60.3 6.6 %collective-permute-done.3 = bf16[32,7680]{1,0:T(8,128)(2,1)S(1)} collective-permute-done((bf16[32,7680]{1,0:T(8,128)(2,1)S(1)}, bf16[32,7680]{1,0:T(8,128)(2,1)S(1)}, u32[]{:S(2)}, u32[]{:S(2)}) %collective-permute-start.3) | collective-permute-done | bytes 491552 | tf_op jit(solution)/shard_map/ppermute | solution.py:31
  68.6 3.4 %collective-permute-start.5 = (bf16[256,7680]{1,0:T(8,128)(2,1)}, bf16[256,7680]{1,0:T(8,128)(2,1)}, u32[]{:S(2)}, u32[]{:S(2)}) collective-permute-start(bf16[256,7680]{1,0:T(8,128)(2,1)} %constant_dynamic-update-slice_fusion), channel_id=1, source_target_pairs={{0,1},{1,0},{2,3},{3,2},{4,5},{5,4},{6,7},{7,6},{8,9},{9,8},{10,11... | collective-permute-start | bytes 11796488 | tf_op jit(solution)/shard_map/ppermute | solution.py:169
  72.6 5.5 %fusion.5 = bf16[256,432]{0,1:T(8,128)(2,1)S(1)} fusion(bf16[6912,432]{0,1:T(8,128)(2,1)} %param.12, bf16[256,7680]{1,0:T(8,128)(2,1)} %constant_dynamic-update-slice_fusion), kind=kOutput, calls=%fused_computation.6 | convolution fusion | flops 1528934400 | bytes 9732096 | tf_op jit(solution)/shard_map/dot_general | solution.py:172
  79.0 6.3 %fusion.8 = bf16[256,432]{0,1:T(8,128)(2,1)} fusion(bf16[6912,432]{0,1:T(8,128)(2,1)} %param.12, bf16[256,7680]{1,0:T(8,128)(2,1)} %collective-permute-done.5), kind=kOutput, calls=%fused_computation.7 | convolution fusion | flops 1528934400 | bytes 9732096 | tf_op jit(solution)/shard_map/dot_general | solution.py:172
  85.3 1.1 copy.30
  86.4 1.8 pad_maximum_fusion.2.out_0
  88.2 3.4 %collective-permute-start.6 = (bf16[512,432]{1,0:T(8,128)(2,1)}, bf16[512,432]{1,0:T(8,128)(2,1)}, u32[]{:S(2)}, u32[]{:S(2)}) collective-permute-start(bf16[512,432]{1,0:T(8,128)(2,1)} %pad_maximum_fusion.2.out_0), channel_id=1, source_target_pairs={{0,64},{16,80},{32,96},{48,112},{64,128},{80,144},{96,160},{112,17... | collective-permute-start | bytes 1327112 | tf_op jit(solution)/shard_map/ppermute | solution.py:29
  91.6 2.5 collective-permute-start.7
  95.9 24.8 %all-gather.3.cloned.1.call-done = bf16[16,32,5120]{2,1,0:T(8,128)(2,1)} async-done(((bf16[1,32,5120]{2,1,0:T(8,128)(2,1)}), bf16[16,32,5120]{2,1,0:T(8,128)(2,1)}) %all-gather.3.cloned.1.call-update) | async-done | bytes 5242896 | tf_op jit(solution)/shard_map/all_gather | solution.py:159
  120.7 5.1 %fusion.4 = bf16[512,320]{0,1:T(8,128)(2,1)} fusion(bf16[512,5120]{1,0:T(8,128)(2,1)} %bitcast.75, bf16[5120,320]{0,1:T(8,128)(2,1)S(1)} %copy-done, pred[512]{0:T(512)(128)(4,1)S(1)} %iota_compare_fusion.1), kind=kOutput, calls=%fused_computation.5 | convolution fusion | flops 1678049280 | bytes 8847872 | tf_op jit(solution)/shard_map/dot_general | solution.py:196
  125.8 1.9 copy.31
  127.7 1.1 constant_dynamic-slice_fusion.3
  129.1 2.8 collective-permute-start.9
  131.9 1.1 collective-permute-start.10
  133.0 1.1 slice.111
  134.2 1.2 slice.112
  136.9 0.8 maximum_select_fusion
  137.8 1.9 copy.32
  139.7 0.9 collective-permute-start.23
  140.7 1.8 collective-permute-start.24
  144.1 5.5 %constant_dynamic-update-slice_fusion.7 = (bf16[272,432]{1,0:T(8,128)(2,1)S(1)}, bf16[64,432]{1,0:T(8,128)(2,1)}) fusion(bf16[64,6912]{1,0:T(8,128)(2,1)} %bitcast.64, bf16[6912,432]{0,1:T(8,128)(2,1)} %param.12), kind=kOutput, calls=%fused_computation.35 | convolution fusion | flops 382233600 | bytes 6977536 | tf_op jit(solution)/shard_map/dot_general | solution.py:185
  149.5 3.1 %collective-permute-done.23.eig_1 = f32[320,432]{1,0:T(8,128)S(1)} collective-permute-done((f32[320,432]{1,0:T(8,128)}, f32[320,432]{1,0:T(8,128)S(1)}, u32[]{:S(2)}, u32[]{:S(2)}) %collective-permute-start.23) | collective-permute-done | bytes 552992 | tf_op jit(solution)/shard_map/ppermute | solution.py:29
  154.7 2.2 collective-permute-start.26
  157.7 1.7 slice.114
  159.5 0.8 slice.121
  164.5 2.0 fusion.11
  166.5 0.9 pad_maximum_fusion.3
  167.4 4.5 %collective-permute-start.17 = (bf16[80,432]{1,0:T(8,128)(2,1)S(1)}, bf16[80,432]{1,0:T(8,128)(2,1)S(1)}, u32[]{:S(2)}, u32[]{:S(2)}) collective-permute-start(bf16[80,432]{1,0:T(8,128)(2,1)S(1)} %pad_maximum_fusion.3), channel_id=1, source_target_pairs={{0,64},{16,80},{32,96},{48,112},{64,128},{80,144},{96,160},{112,17... | collective-permute-start | bytes 207368 | tf_op jit(solution)/shard_map/ppermute | solution.py:37
  171.9 2.9 collective-permute-start.18
  174.8 2.0 collective-permute-start.19
  176.8 1.0 slice.115
  177.8 1.9 pad_maximum_fusion.1.ql_0
  179.7 2.7 collective-permute-start.12
  182.4 2.2 collective-permute-done.19
  189.5 0.8 slice_dynamic-update-slice_fusion
  190.4 2.0 constant_dynamic-update-slice_fusion.6.qr_0
  193.1 2.1 collective-permute-start.21
  195.2 1.8 slice.116
  197.0 1.8 slice.117
  198.7 2.7 collective-permute-start.14
  202.0 1.0 slice.118
  203.0 1.0 slice.119
  204.6 3.0 collective-permute-start.16
  208.8 2.6 collective-permute-done.22.qr_3
  212.9 0.9 copy-done.2
  215.8 0.9 copy-done.7
  216.7 0.9 copy-done.9
  217.7 35.5 %shard_map.82 = f32[32,128]{1,0:T(8,128)S(1)} custom-call(s32[4]{0:T(128)S(1)} %copy-done.4, s32[16]{0:T(128)S(1)} %copy-done.3, s32[16]{0:T(128)S(1)} %copy-done.5, bf16[16,4,320,128]{3,2,1,0:T(8,128)(2,1)} %all-gather.5.cloned.1.call-done.ein, bf16[512,640]{1,0:T(8,128)(2,1)} %pad_maximum_fusion.1.ql_0, bf16[512,640]{1,0:T(8,128)(2,1)} %collective-permute-done.11.ql_1, ...), custom_call_target="tpu_custom_call" | custom-call | flops 20000000000 | bytes 16000000 | tf_op jit(solution)/shard_map/pallas_call | solution.py:117
  253.3 43.0 %all_to_all.9 = f32[256,1,2]{2,1,0:T(1,128)S(1)} all-to-all(f32[256,1,2]{2,1,0:T(1,128)S(1)} %bitcast.66), channel_id=1, replica_groups=mesh['shard'=16,'example'=16] {'shard','example'}, dimensions={0} | all-to-all | bytes 4096 | tf_op jit(solution)/shard_map/all_to_all | solution.py:212
  (87 shorter events, 18.2 us)
Async XLA Ops:
  6.5 5.7 %copy-start = (bf16[5120,320]{0,1:T(8,128)(2,1)S(1)}, bf16[5120,320]{0,1:T(8,128)(2,1)}, u32[]{:S(2)}) copy-start(bf16[5120,320]{0,1:T(8,128)(2,1)} %param.11) | copy-start | bytes 9830404
  6.5 114.2 %all-gather.3.cloned.1.call-start = ((), (), s32[]{:S(2)}) async-start(), calls=%async_computation.1 | async-start | bytes 5570560 | tf_op jit(solution)/shard_map/all_gather | solution.py:159
  17.6 12.7 %collective-permute-start = (bf16[32,7680]{1,0:T(8,128)(2,1)}, bf16[32,7680]{1,0:T(8,128)(2,1)}, u32[]{:S(2)}, u32[]{:S(2)}) collective-permute-start(bf16[32,7680]{1,0:T(8,128)(2,1)} %concatenate.35), channel_id=1, source_target_pairs={{0,8},{1,9},{2,10},{3,11},{4,12},{5,13},{6,14},{7,15},{8,0},{9,1},... | collective-permute-start | bytes 1474568 | tf_op jit(solution)/shard_map/ppermute | solution.py:167
  20.1 192.8 %all-gather.5.cloned.1.call-start = ((), (), s32[]{:S(2)}) async-start(), calls=%async_computation.2 | async-start | bytes 5570560 | tf_op jit(solution)/shard_map/all_gather | solution.py:208
  31.6 23.7 %collective-permute-start.1 = (bf16[64,7680]{1,0:T(8,128)(2,1)S(1)}, bf16[64,7680]{1,0:T(8,128)(2,1)S(1)}, u32[]{:S(2)}, u32[]{:S(2)}) collective-permute-start(bf16[64,7680]{1,0:T(8,128)(2,1)S(1)} %pad_maximum_fusion), channel_id=1, source_target_pairs={{0,2},{1,3},{2,4},{3,5},{4,6},{5,7},{6,0},{7,1},{8,10},{9,11},{10,... | collective-permute-start | bytes 2949128 | tf_op jit(solution)/shard_map/ppermute | solution.py:29
  33.8 22.0 %collective-permute-start.2 = (bf16[64,7680]{1,0:T(8,128)(2,1)S(1)}, bf16[64,7680]{1,0:T(8,128)(2,1)S(1)}, u32[]{:S(2)}, u32[]{:S(2)}) collective-permute-start(bf16[64,7680]{1,0:T(8,128)(2,1)S(1)} %pad_maximum_fusion), channel_id=1, source_target_pairs={{0,6},{1,7},{2,0},{3,1},{4,2},{5,3},{6,4},{7,5},{8,14},{9,15},{10,... | collective-permute-start | bytes 2949128 | tf_op jit(solution)/shard_map/ppermute | solution.py:30
  55.3 11.5 %collective-permute-start.3 = (bf16[32,7680]{1,0:T(8,128)(2,1)S(1)}, bf16[32,7680]{1,0:T(8,128)(2,1)S(1)}, u32[]{:S(2)}, u32[]{:S(2)}) collective-permute-start(bf16[32,7680]{1,0:T(8,128)(2,1)S(1)} %slice.107), channel_id=1, source_target_pairs={{0,2},{1,3},{2,4},{3,5},{4,6},{5,7},{6,0},{7,1},{8,10},{9,11},{10,... | collective-permute-start | bytes 1474568 | tf_op jit(solution)/shard_map/ppermute | solution.py:31
  55.9 11.9 %collective-permute-start.4 = (bf16[32,7680]{1,0:T(8,128)(2,1)S(1)}, bf16[32,7680]{1,0:T(8,128)(2,1)S(1)}, u32[]{:S(2)}, u32[]{:S(2)}) collective-permute-start(bf16[32,7680]{1,0:T(8,128)(2,1)S(1)} %slice.108), channel_id=1, source_target_pairs={{0,6},{1,7},{2,0},{3,1},{4,2},{5,3},{6,4},{7,5},{8,14},{9,15},{10,... | collective-permute-start | bytes 1474568 | tf_op jit(solution)/shard_map/ppermute | solution.py:32
  68.6 10.4 %collective-permute-start.5 = (bf16[256,7680]{1,0:T(8,128)(2,1)}, bf16[256,7680]{1,0:T(8,128)(2,1)}, u32[]{:S(2)}, u32[]{:S(2)}) collective-permute-start(bf16[256,7680]{1,0:T(8,128)(2,1)} %constant_dynamic-update-slice_fusion), channel_id=1, source_target_pairs={{0,1},{1,0},{2,3},{3,2},{4,5},{5,4},{6,7},{7,6},{8,9},{9,8},{10,11... | collective-permute-start | bytes 11796488 | tf_op jit(solution)/shard_map/ppermute | solution.py:169
  88.2 44.9 %collective-permute-start.6 = (bf16[512,432]{1,0:T(8,128)(2,1)}, bf16[512,432]{1,0:T(8,128)(2,1)}, u32[]{:S(2)}, u32[]{:S(2)}) collective-permute-start(bf16[512,432]{1,0:T(8,128)(2,1)} %pad_maximum_fusion.2.out_0), channel_id=1, source_target_pairs={{0,64},{16,80},{32,96},{48,112},{64,128},{80,144},{96,160},{112,17... | collective-permute-start | bytes 1327112 | tf_op jit(solution)/shard_map/ppermute | solution.py:29
  91.6 42.6 %collective-permute-start.7 = (bf16[512,432]{1,0:T(8,128)(2,1)}, bf16[512,432]{1,0:T(8,128)(2,1)}, u32[]{:S(2)}, u32[]{:S(2)}) collective-permute-start(bf16[512,432]{1,0:T(8,128)(2,1)} %pad_maximum_fusion.2.out_0), channel_id=1, source_target_pairs={{0,192},{16,208},{32,224},{48,240},{64,0},{80,16},{96,32},{112,48}... | collective-permute-start | bytes 1327112 | tf_op jit(solution)/shard_map/ppermute | solution.py:30
  128.8 7.8 %collective-permute-start.8 = (bf16[128,320]{1,0:T(8,128)(2,1)S(1)}, bf16[128,320]{1,0:T(8,128)(2,1)S(1)}, u32[]{:S(2)}, u32[]{:S(2)}) collective-permute-start(bf16[128,320]{1,0:T(8,128)(2,1)S(1)} %bitcast.71), channel_id=1, source_target_pairs={{0,16},{16,32},{32,48},{48,0},{64,80},{80,96},{96,112},{112,64},{1... | collective-permute-start | bytes 245768 | tf_op jit(solution)/shard_map/ppermute | solution.py:37
  129.1 7.6 %collective-permute-start.9 = (bf16[128,320]{1,0:T(8,128)(2,1)S(1)}, bf16[128,320]{1,0:T(8,128)(2,1)S(1)}, u32[]{:S(2)}, u32[]{:S(2)}) collective-permute-start(bf16[128,320]{1,0:T(8,128)(2,1)S(1)} %bitcast.70), channel_id=1, source_target_pairs={{0,48},{16,0},{32,16},{48,32},{64,112},{80,64},{96,80},{112,96},{1... | collective-permute-start | bytes 245768 | tf_op jit(solution)/shard_map/ppermute | solution.py:37
  131.9 5.0 %collective-permute-start.10 = (bf16[128,320]{1,0:T(8,128)(2,1)S(1)}, bf16[128,320]{1,0:T(8,128)(2,1)S(1)}, u32[]{:S(2)}, u32[]{:S(2)}) collective-permute-start(bf16[128,320]{1,0:T(8,128)(2,1)S(1)} %bitcast.69), channel_id=1, source_target_pairs={{0,32},{16,48},{32,0},{48,16},{64,96},{80,112},{96,64},{112,80},{1... | collective-permute-start | bytes 245768 | tf_op jit(solution)/shard_map/ppermute | solution.py:37
  139.7 12.9 %collective-permute-start.23 = (f32[320,432]{1,0:T(8,128)}, f32[320,432]{1,0:T(8,128)S(1)}, u32[]{:S(2)}, u32[]{:S(2)}) collective-permute-start(f32[320,432]{1,0:T(8,128)} %eig_0.1), channel_id=1, source_target_pairs={{0,16},{16,32},{32,48},{48,0},{64,80},{80,96},{96,112},{112,64},{1... | collective-permute-start | bytes 1658888 | tf_op jit(solution)/shard_map/ppermute | solution.py:29
  140.7 13.2 %collective-permute-start.24 = (f32[320,432]{1,0:T(8,128)}, f32[320,432]{1,0:T(8,128)S(1)}, u32[]{:S(2)}, u32[]{:S(2)}) collective-permute-start(f32[320,432]{1,0:T(8,128)} %eig_0.1), channel_id=1, source_target_pairs={{0,48},{16,0},{32,16},{48,32},{64,112},{80,64},{96,80},{112,96},{1... | collective-permute-start | bytes 1658888 | tf_op jit(solution)/shard_map/ppermute | solution.py:30
  152.6 5.1 %copy-start.10 = (f32[320,432]{1,0:T(8,128)}, f32[320,432]{1,0:T(8,128)S(1)}, u32[]{:S(2)}) copy-start(f32[320,432]{1,0:T(8,128)S(1)} %collective-permute-done.23.eig_1) | copy-start | bytes 1658884
  153.4 45.3 %collective-permute-start.25 = (f32[160,432]{1,0:T(8,128)}, f32[160,432]{1,0:T(8,128)}, u32[]{:S(2)}, u32[]{:S(2)}) collective-permute-start(f32[160,432]{1,0:T(8,128)} %slice.128), channel_id=1, source_target_pairs={{0,16},{16,32},{32,48},{48,0},{64,80},{80,96},{96,112},{112,64},{1... | collective-permute-start | bytes 829448 | tf_op jit(solution)/shard_map/ppermute | solution.py:31
  153.9 5.6 %copy-start.11 = (f32[320,432]{1,0:T(8,128)}, f32[320,432]{1,0:T(8,128)S(1)}, u32[]{:S(2)}) copy-start(f32[320,432]{1,0:T(8,128)S(1)} %collective-permute-done.24.eig_2) | copy-start | bytes 1658884
  154.7 46.7 %collective-permute-start.26 = (f32[160,432]{1,0:T(8,128)}, f32[160,432]{1,0:T(8,128)}, u32[]{:S(2)}, u32[]{:S(2)}) collective-permute-start(f32[160,432]{1,0:T(8,128)} %slice.129), channel_id=1, source_target_pairs={{0,48},{16,0},{32,16},{48,32},{64,112},{80,64},{96,80},{112,96},{1... | collective-permute-start | bytes 829448 | tf_op jit(solution)/shard_map/ppermute | solution.py:32
  167.4 12.2 %collective-permute-start.17 = (bf16[80,432]{1,0:T(8,128)(2,1)S(1)}, bf16[80,432]{1,0:T(8,128)(2,1)S(1)}, u32[]{:S(2)}, u32[]{:S(2)}) collective-permute-start(bf16[80,432]{1,0:T(8,128)(2,1)S(1)} %pad_maximum_fusion.3), channel_id=1, source_target_pairs={{0,64},{16,80},{32,96},{48,112},{64,128},{80,144},{96,160},{112,17... | collective-permute-start | bytes 207368 | tf_op jit(solution)/shard_map/ppermute | solution.py:37
  171.9 7.8 %collective-permute-start.18 = (bf16[80,432]{1,0:T(8,128)(2,1)S(1)}, bf16[80,432]{1,0:T(8,128)(2,1)S(1)}, u32[]{:S(2)}, u32[]{:S(2)}) collective-permute-start(bf16[80,432]{1,0:T(8,128)(2,1)S(1)} %pad_maximum_fusion.3), channel_id=1, source_target_pairs={{0,192},{16,208},{32,224},{48,240},{64,0},{80,16},{96,32},{112,48}... | collective-permute-start | bytes 207368 | tf_op jit(solution)/shard_map/ppermute | solution.py:37
  174.8 9.9 %collective-permute-start.19 = (bf16[80,432]{1,0:T(8,128)(2,1)S(1)}, bf16[80,432]{1,0:T(8,128)(2,1)S(1)}, u32[]{:S(2)}, u32[]{:S(2)}) collective-permute-start(bf16[80,432]{1,0:T(8,128)(2,1)S(1)} %pad_maximum_fusion.3), channel_id=1, source_target_pairs={{0,128},{16,144},{32,160},{48,176},{64,192},{80,208},{96,224},{112... | collective-permute-start | bytes 207368 | tf_op jit(solution)/shard_map/ppermute | solution.py:37
  179.6 13.4 %collective-permute-start.11 = (bf16[512,640]{1,0:T(8,128)(2,1)}, bf16[512,640]{1,0:T(8,128)(2,1)}, u32[]{:S(2)}, u32[]{:S(2)}) collective-permute-start(bf16[512,640]{1,0:T(8,128)(2,1)} %pad_maximum_fusion.1.ql_0), channel_id=1, source_target_pairs={{0,16},{16,32},{32,48},{48,0},{64,80},{80,96},{96,112},{112,64},{1... | collective-permute-start | bytes 1966088 | tf_op jit(solution)/shard_map/ppermute | solution.py:29
  179.7 17.3 %collective-permute-start.12 = (bf16[512,640]{1,0:T(8,128)(2,1)}, bf16[512,640]{1,0:T(8,128)(2,1)}, u32[]{:S(2)}, u32[]{:S(2)}) collective-permute-start(bf16[512,640]{1,0:T(8,128)(2,1)} %pad_maximum_fusion.1.ql_0), channel_id=1, source_target_pairs={{0,48},{16,0},{32,16},{48,32},{64,112},{80,64},{96,80},{112,96},{1... | collective-permute-start | bytes 1966088 | tf_op jit(solution)/shard_map/ppermute | solution.py:30
  184.6 0.6 copy-start.12
  192.4 20.5 %copy-start.1 = (bf16[272,432]{1,0:T(8,128)(2,1)}, bf16[272,432]{1,0:T(8,128)(2,1)S(1)}, u32[]{:S(2)}) copy-start(bf16[272,432]{1,0:T(8,128)(2,1)S(1)} %constant_dynamic-update-slice_fusion.6.qr_0) | copy-start | bytes 705028
  192.4 11.5 %collective-permute-start.20 = (bf16[272,432]{1,0:T(8,128)(2,1)S(1)}, bf16[272,432]{1,0:T(8,128)(2,1)}, u32[]{:S(2)}, u32[]{:S(2)}) collective-permute-start(bf16[272,432]{1,0:T(8,128)(2,1)S(1)} %constant_dynamic-update-slice_fusion.6.qr_0), channel_id=1, source_target_pairs={{0,16},{16,32},{32,48},{48,0},{64,80},{80,96},{96,112},{112,64},{1... | collective-permute-start | bytes 705032 | tf_op jit(solution)/shard_map/ppermute | solution.py:37
  193.1 11.5 %collective-permute-start.21 = (bf16[272,432]{1,0:T(8,128)(2,1)S(1)}, bf16[272,432]{1,0:T(8,128)(2,1)}, u32[]{:S(2)}, u32[]{:S(2)}) collective-permute-start(bf16[272,432]{1,0:T(8,128)(2,1)S(1)} %constant_dynamic-update-slice_fusion.6.qr_0), channel_id=1, source_target_pairs={{0,48},{16,0},{32,16},{48,32},{64,112},{80,64},{96,80},{112,96},{1... | collective-permute-start | bytes 705032 | tf_op jit(solution)/shard_map/ppermute | solution.py:37
  197.0 15.9 %collective-permute-start.13 = (bf16[256,640]{1,0:T(8,128)(2,1)}, bf16[256,640]{1,0:T(8,128)(2,1)}, u32[]{:S(2)}, u32[]{:S(2)}) collective-permute-start(bf16[256,640]{1,0:T(8,128)(2,1)} %slice.116), channel_id=1, source_target_pairs={{0,16},{16,32},{32,48},{48,0},{64,80},{80,96},{96,112},{112,64},{1... | collective-permute-start | bytes 983048 | tf_op jit(solution)/shard_map/ppermute | solution.py:31
  198.7 14.2 %collective-permute-start.14 = (bf16[256,640]{1,0:T(8,128)(2,1)}, bf16[256,640]{1,0:T(8,128)(2,1)}, u32[]{:S(2)}, u32[]{:S(2)}) collective-permute-start(bf16[256,640]{1,0:T(8,128)(2,1)} %slice.117), channel_id=1, source_target_pairs={{0,48},{16,0},{32,16},{48,32},{64,112},{80,64},{96,80},{112,96},{1... | collective-permute-start | bytes 983048 | tf_op jit(solution)/shard_map/ppermute | solution.py:32
  201.4 10.1 %collective-permute-start.22 = (bf16[272,432]{1,0:T(8,128)(2,1)S(1)}, bf16[272,432]{1,0:T(8,128)(2,1)}, u32[]{:S(2)}, u32[]{:S(2)}) collective-permute-start(bf16[272,432]{1,0:T(8,128)(2,1)S(1)} %constant_dynamic-update-slice_fusion.6.qr_0), channel_id=1, source_target_pairs={{0,32},{16,48},{32,0},{48,16},{64,96},{80,112},{96,64},{112,80},{1... | collective-permute-start | bytes 705032 | tf_op jit(solution)/shard_map/ppermute | solution.py:37
  204.0 7.5 %collective-permute-start.15 = (bf16[256,432]{1,0:T(8,128)(2,1)S(1)}, bf16[256,432]{1,0:T(8,128)(2,1)S(1)}, u32[]{:S(2)}, u32[]{:S(2)}) collective-permute-start(bf16[256,432]{1,0:T(8,128)(2,1)S(1)} %slice.118), channel_id=1, source_target_pairs={{0,64},{16,80},{32,96},{48,112},{64,128},{80,144},{96,160},{112,17... | collective-permute-start | bytes 663560 | tf_op jit(solution)/shard_map/ppermute | solution.py:31
  204.6 7.6 %collective-permute-start.16 = (bf16[256,432]{1,0:T(8,128)(2,1)S(1)}, bf16[256,432]{1,0:T(8,128)(2,1)S(1)}, u32[]{:S(2)}, u32[]{:S(2)}) collective-permute-start(bf16[256,432]{1,0:T(8,128)(2,1)S(1)} %slice.119), channel_id=1, source_target_pairs={{0,192},{16,208},{32,224},{48,240},{64,0},{80,16},{96,32},{112,48}... | collective-permute-start | bytes 663560 | tf_op jit(solution)/shard_map/ppermute | solution.py:32
  211.5 0.7 copy-start.6
  212.2 0.7 copy-start.8
  212.9 1.0 copy-start.2
  213.9 0.6 copy-start.3
  214.5 0.7 copy-start.4
  215.2 0.6 copy-start.5
  215.8 0.9 copy-start.7
  216.7 0.9 copy-start.9
Sparse Core Ops, SparseCore 0:
  20.3 100.4 all-gather.2
  139.8 57.5 all-gather.4

commit v3 on v0

v3 whole, which is shorter than its diff:
```python
import math

import jax
import jax.numpy as jnp
from jax import lax
from jax.experimental import pallas as pl
from jax.experimental.layout import Layout, with_layout_constraint
from jax.experimental.pallas import tpu as pltpu
from jax.sharding import PartitionSpec as P

D = 5120
H = 6912
SEQLEN = 512
RANK = 32
NSEQ = 16
QUERIES = 32
BF16 = jnp.bfloat16
F32 = jnp.float32

SHARD_Y = {d: [(i, i // 4 * 4 + (i + d) % 4) for i in range(16)] for d in (1, -1)}
SHARD_Z = {d: [(i, (i + 4 * d) % 16) for i in range(16)] for d in (1, -1)}
EXAMPLE_X = {d: [(i, i // 8 * 8 + (i + 2 * d) % 8) for i in range(16)] for d in (1, -1)}
EXAMPLE_CORE = [(i, i ^ 1) for i in range(16)]
EXAMPLE_Z = [(i, i ^ 8) for i in range(16)]
AWAY = (0, -1, 1, 2)


def ring4(block, axis, steps, cut):
    below = lax.ppermute(block, axis, steps[1])
    above = lax.ppermute(block, axis, steps[-1])
    far_top = lax.ppermute(below[:cut], axis, steps[1])
    far_bottom = lax.ppermute(above[cut:], axis, steps[-1])
    return [block, below, above, far_top, far_bottom]


def three_terms(value):
    first = lax.reduce_precision(value, 8, 7)
    rest = value - first
    second = lax.reduce_precision(rest, 8, 7)
    return first, second, rest - second


def corner(value, shape):
    row = lax.broadcasted_iota(jnp.int32, shape, 0)
    col = lax.broadcasted_iota(jnp.int32, shape, 1)
    out = jnp.zeros(shape, F32)
    for k, term in enumerate(three_terms(value)):
        out = jnp.where((row == k) & (col == 0), term, out)
    return out.astype(BF16)


def score_kernel(
    place, slot, ein, ql,
    own_0, own_1, own_2, own_top, own_bottom,
    z_0, z_1, z_2, z_top, z_bottom,
    eig, out, inverse, left, right, own_3, z_3, grads,
):
    n = pl.program_id(0)
    dj = eig.shape[1]
    owns = (own_0, own_1, own_2, own_3)
    others = (z_0, z_1, z_2, z_3)
    size = own_0.shape[0]
    blocks = [(owns[y], 0) if z == 0 else (others[y], size * (z - 1)) for y in range(4) for z in range(4)]
    after = NSEQ * 32

    @pl.when(n == 0)
    def _():
        for far, top, bottom in ((own_3, own_top, own_bottom), (z_3, z_top, z_bottom)):
            far[: top.shape[0], :] = top[...]
            far[top.shape[0] :, :] = bottom[...]
        total = 0.0
        for k, (ref, row) in enumerate(blocks):
            start = pl.multiple_of(place[k] * 64, 64)
            right[pl.ds(start, 64), :] = ref[row + after : row + after + 64, :dj]
            total += jnp.sum(ref[row : row + 16, dj:].astype(F32))
        inverse[...] = 1.0 / (eig[...] + (0.1 / (D * H)) * total)
        for e in range(NSEQ):
            left[64 * e : 64 * e + 64, :] = ql[e].T[:64, :]
        out[...] = jnp.zeros_like(out)

    first = pl.multiple_of(slot[n] * 32, 32)
    for k, (ref, row) in enumerate(blocks):
        start = pl.multiple_of(place[k] * 32, 32)
        grads[pl.ds(start, 32), :] = ref[pl.ds(row + first, 32), :]
    pair = jnp.dot(ein[0], grads[...], preferred_element_type=F32)[:, :dj]
    scaled = (pair * inverse[...]).astype(BF16)
    width = scaled.shape[1]
    sums = []
    for k in range(4):
        part = jnp.dot(left[256 * k : 256 * k + 256, :], scaled, preferred_element_type=F32)
        part = part * right[256 * k : 256 * k + 256, :].astype(F32)
        sums.append(jnp.sum(part.reshape(8, RANK, width), axis=1))
    total = jnp.sum(jnp.concatenate(sums, 0), axis=1, keepdims=True)
    lane = lax.broadcasted_iota(jnp.int32, out.shape, 1)
    out[...] = jnp.where(lane == n, total, out[...])


def score_call(place, slot, ein, blocks, eigvals):
    di, dj = eigvals.shape

    def whole(x):
        return pl.BlockSpec(x.shape, lambda n, rank=x.ndim: (0,) * rank)

    return pl.pallas_call(
        score_kernel,
        grid=(NSEQ,),
        in_specs=[pl.BlockSpec(memory_space=pltpu.SMEM)] * 2
        + [
            pl.BlockSpec((1, di, SEQLEN), lambda n: (n, 0, 0)),
            pl.BlockSpec((16, di, 128), lambda n: (0, 0, 4)),
        ]
        + [whole(x) for x in (*blocks, eigvals)],
        out_specs=pl.BlockSpec((QUERIES, 128), lambda n: (0, 0)),
        out_shape=jax.ShapeDtypeStruct((QUERIES, 128), F32),
        scratch_shapes=[
            pltpu.VMEM((di, dj), F32),
            pltpu.VMEM((16 * 64, di), BF16),
            pltpu.VMEM((16 * 64, dj), BF16),
            pltpu.VMEM(blocks[0].shape, BF16),
            pltpu.VMEM(blocks[5].shape, BF16),
            pltpu.VMEM((SEQLEN, blocks[0].shape[1]), BF16),
        ],
        compiler_params=pltpu.CompilerParams(vmem_limit_bytes=48 * 1024 * 1024),
        cost_estimate=pl.CostEstimate(
            flops=10_000_000_000, bytes_accessed=16_000_000, transcendentals=0
        ),
    )(place, slot, ein, ein, *blocks, eigvals)


def shards(train_in, train_grad, seq_lens, basis_in, basis_out, eigvals, query_in, query_out):
    me = lax.axis_index("shard")
    example = lax.axis_index("example")
    place = jnp.stack(
        [(me // 4 + dz) % 4 * 4 + (me % 4 + dy) % 4 for dy in AWAY for dz in AWAY]
    ).astype(jnp.int32)
    seq = jnp.arange(NSEQ, dtype=jnp.int32)
    x_off = (seq // 2 - example // 2) % 4
    x_slot = jnp.where(x_off == 0, 0, jnp.where(x_off == 3, 1, jnp.where(x_off == 1, 2, 3)))
    slot = (
        ((seq % 2) != (example % 2)).astype(jnp.int32) * 8
        + x_slot * 2
        + ((seq // 8) != (example // 8)).astype(jnp.int32)
    ).astype(jnp.int32)
    di, dj = eigvals.shape
    row_major = Layout(major_to_minor=(0, 1))

    rows_all = lax.all_gather(train_in[0], "shard", axis=0)

    block = jnp.concatenate([train_grad[0], corner(jnp.sum(eigvals), (32, 128))], 1)
    block = jnp.concatenate([block, lax.ppermute(block, "example", EXAMPLE_Z)], 0)
    block = jnp.concatenate(ring4(block, "example", EXAMPLE_X, 32), 0)
    other = lax.ppermute(block, "example", EXAMPLE_CORE)
    eig_example = jnp.sum(
        jnp.concatenate([block[:, H:], other[:, H:]], 0).astype(F32)
    )
    query_right = jnp.dot(
        query_out.reshape(64, H), basis_out, preferred_element_type=F32
    ).astype(BF16)
    part_out = [
        jnp.dot(b[:, :H], basis_out, preferred_element_type=F32).astype(BF16)
        for b in (block, other)
    ]
    part_out = jnp.concatenate(part_out + [query_right], 0)
    sums = corner(eig_example, (part_out.shape[0], 512 - dj))
    part_out = with_layout_constraint(jnp.concatenate([part_out, sums], 1), row_major)
    z_blocks = ring4(part_out, "shard", SHARD_Z, 288)
    z_others = jnp.concatenate(z_blocks[1:], 0)
    blocks = ring4(part_out, "shard", SHARD_Y, 288) + ring4(z_others, "shard", SHARD_Y, 864)

    flag = jnp.isnan(part_out[256, 0])
    own_in = jnp.dot(rows_all.reshape(SEQLEN, D), basis_in, preferred_element_type=F32)
    token = jnp.arange(SEQLEN, dtype=jnp.int32)[:, None]
    live = jnp.where(flag, 0, seq_lens[0])
    own_in = jnp.where(token < live, own_in, 0.0).astype(BF16)
    query_left = jnp.dot(
        query_in.reshape(64, D), basis_in, preferred_element_type=F32
    ).astype(BF16)
    spare = jnp.zeros((di, 64), BF16)
    ein = jnp.concatenate([own_in.T, query_left.T, spare], 1)
    late = jnp.isnan(sum(b[0, 0] for b in z_blocks[1:] + blocks[1:3]))
    ein = jnp.where(late, jnp.zeros_like(ein), ein)
    ein = lax.all_gather(ein, "example", axis=0)

    partial = score_call(place, slot, ein, blocks, eigvals)[:, :NSEQ]
    pieces = partial.reshape(16, 2, 16).transpose(0, 2, 1).reshape(256, 2)
    pieces = lax.all_to_all(pieces, ("shard", "example"), 0, 0, tiled=True)
    normalizer = 1.0 / math.sqrt(RANK * D * H * SEQLEN)
    return (jnp.sum(pieces, axis=0) * normalizer).reshape(2, 1)


def solution(mesh):
    placed = (
        P("example", "shard", None),
        P("example", "shard", None),
        P("example"),
        P(None, "shard"),
        P(None, "example"),
        P("shard", "example"),
        P("example", None, None),
        P("shard", None, None),
    )
    return jax.shard_map(
        shards, mesh=mesh, in_specs=placed, out_specs=P("shard", "example"), check_vma=False
    )
```

time: 382 us -> 297 us (0.78)
  waiting for transfers between devices: 149 us -> 123 us
  local copies, waits for them, and re-layouts: 58 us -> 33.4 us
  other arithmetic: 30.1 us -> 12.5 us
  Pallas kernels: 33.8 us -> 23.1 us
  matrix products: 23.6 us -> 18.4 us
    all_gather x1, waiting for transfers between devices: 81.9 us -> 0.02 us  [shards(): rows_all = lax.all_gather(train_in[0], 'shard', axis=0)]
    ppermute x3 -> x4, waiting for transfers between devices: 27.8 us -> 89.4 us  [ring4(): below = lax.ppermute(block, axis, steps[1])]
    unnamed x60 -> x29, local copies, waits for them, and re-layouts: 33.1 us -> 13 us
    ppermute x15 -> x8, waiting for transfers between devices: 8.78 us -> 24.2 us  [the longest x4 21.9 us: ring4(): far_top = lax.ppermute(below[:cut], axis, steps[1])]
    ppermute x3 -> x4, waiting for transfers between devices: 15 us -> 0.01 us  [ring4(): above = lax.ppermute(block, axis, steps[-1])]
    pallas_call x1, Pallas kernels: 33.8 us -> 23.1 us  [score_call(): pl.pallas_call(score_kernel, grid=(NSEQ,), in_specs=[pl.BlockSpec(memory_...]
    ppermute x15 -> x8, starting transfers between devices: 21 us -> 11.8 us  [the longest x4 10.3 us: ring4(): far_bottom = lax.ppermute(above[cut:], axis, steps[-1])]
    another operation x5 -> x0, other arithmetic: 6.95 us -> none  [the longest x3 6.01 us: shards(): eout = jnp.stack([b[:NSEQ * 32] for b in z_blocks])]
  transfers between devices with their start and end apart: 26 -> 20, of which waited for: 10 -> 7; matrix products, arithmetic and copies ran while one was open for 27% -> 16% of each run, Pallas kernels for 0% -> 0%
where the time goes in v3:
time: 297 us; the launch traced here: 296 us
  waiting for transfers between devices  123 us (41%)
  local copies, waits for them, and re-layouts  33.4 us (11%)
  starting transfers between devices  32.5 us (11%)
  blocking collectives  26.7 us (9%)
  between operations  26.7 us (9%)
  Pallas kernels  23.1 us (8%)
  matrix products  18.4 us (6%)
  other arithmetic  12.5 us (4%)
    ppermute x4, waiting for transfers between devices, ring4(): below = lax.ppermute(block, axis, steps[1])  89.4 us
    all_to_all x1, blocking collectives, shards(): pieces = lax.all_to_all(pieces, ('shard', 'example'), 0, 0, tiled=True)  26.7 us
    pallas_call x1, Pallas kernels, score_call(): pl.pallas_call(score_kernel, grid=(NSEQ,), in_specs=[pl.BlockSpec(memory_...  23.1 us
    ppermute x4, waiting for transfers between devices, ring4(): far_top = lax.ppermute(below[:cut], axis, steps[1])  21.9 us
    unnamed x29, local copies, waits for them, and re-layouts  13 us
    ppermute x4, starting transfers between devices, ring4(): far_bottom = lax.ppermute(above[cut:], axis, steps[-1])  10.3 us
    ppermute x1, waiting for transfers between devices, shards(): lax.ppermute(block, 'example', EXAMPLE_Z)  9.25 us
    dot_general x2, matrix products, shards(): jnp.dot(b[:, :H], basis_out, preferred_element_type=F32).astype(BF16)  8.78 us
  transfers between devices with their start and end apart: 20, of which 7 were waited for; matrix products, arithmetic and copies ran while one was open for 16% of the time, Pallas kernels for 0%

profile of v3, /device:TPU:1, one launch (start us, length us, event | category | flops | bytes accessed | tf_op | source)
XLA Modules:
  0.0 296.1 jit_solution(4317801541989999319)
XLA Ops:
  6.6 2.0 reduce_sum.27
  12.2 1.4 select_convert_fusion.1
  13.6 2.0 pad_maximum_fusion.2
  15.6 2.5 collective-permute-start
  18.1 9.3 %collective-permute-done = bf16[32,7040]{1,0:T(8,128)(2,1)} collective-permute-done((bf16[32,7040]{1,0:T(8,128)(2,1)}, bf16[32,7040]{1,0:T(8,128)(2,1)}, u32[]{:S(2)}, u32[]{:S(2)}) %collective-permute-start) | collective-permute-done | bytes 450592 | tf_op jit(solution)/shard_map/ppermute | solution.py:150
  27.4 1.2 pad_maximum_fusion
  28.6 2.2 collective-permute-start.1
  30.8 1.4 collective-permute-start.2
  32.1 1.9 constant_dynamic-update-slice_fusion.4
  34.0 16.6 %collective-permute-done.1 = bf16[64,7040]{1,0:T(8,128)(2,1)S(1)} collective-permute-done((bf16[64,7040]{1,0:T(8,128)(2,1)S(1)}, bf16[64,7040]{1,0:T(8,128)(2,1)S(1)}, u32[]{:S(2)}, u32[]{:S(2)}) %collective-permute-start.1) | collective-permute-done | bytes 901152 | tf_op jit(solution)/shard_map/ppermute | solution.py:29
  51.2 2.3 collective-permute-start.4
  53.5 1.0 constant_dynamic-update-slice_fusion.3
  54.5 1.0 constant_dynamic-update-slice_fusion.2
  55.5 5.8 %collective-permute-done.3 = bf16[32,7040]{1,0:T(8,128)(2,1)S(1)} collective-permute-done((bf16[32,7040]{1,0:T(8,128)(2,1)S(1)}, bf16[32,7040]{1,0:T(8,128)(2,1)S(1)}, u32[]{:S(2)}, u32[]{:S(2)}) %collective-permute-start.3) | collective-permute-done | bytes 450592 | tf_op jit(solution)/shard_map/ppermute | solution.py:31
  61.3 0.8 constant_dynamic-update-slice_fusion.1
  62.1 0.8 constant_dynamic-update-slice_fusion
  62.9 3.3 %collective-permute-start.5 = (bf16[256,7040]{1,0:T(8,128)(2,1)}, bf16[256,7040]{1,0:T(8,128)(2,1)}, u32[]{:S(2)}, u32[]{:S(2)}) collective-permute-start(bf16[256,7040]{1,0:T(8,128)(2,1)} %constant_dynamic-update-slice_fusion), channel_id=1, source_target_pairs={{0,1},{1,0},{2,3},{3,2},{4,5},{5,4},{6,7},{7,6},{8,9},{9,8},{10,11... | collective-permute-start | bytes 10813448 | tf_op jit(solution)/shard_map/ppermute | solution.py:152
  66.3 2.5 convolution_convert_fusion.1
  68.8 2.5 fusion.5
  71.3 1.8 copy.21
  73.1 0.8 slice.87
  78.3 6.3 %fusion.8 = bf16[256,432]{0,1:T(8,128)(2,1)} fusion(bf16[6912,432]{0,1:T(8,128)(2,1)} %param.12, bf16[256,7040]{1,0:T(8,128)(2,1)} %collective-permute-done.5), kind=kOutput, calls=%fused_computation.7 | convolution fusion | flops 1528934400 | bytes 9732096 | tf_op jit(solution)/shard_map/dot_general | solution.py:160
  84.6 1.1 copy.22
  85.7 1.6 select_convert_fusion
  87.2 2.0 pad_maximum_fusion.1.own_0
  89.2 3.3 %collective-permute-start.6 = (bf16[576,512]{1,0:T(8,128)(2,1)}, bf16[576,512]{1,0:T(8,128)(2,1)S(1)}, u32[]{:S(2)}, u32[]{:S(2)}) collective-permute-start(bf16[576,512]{1,0:T(8,128)(2,1)} %pad_maximum_fusion.1.own_0), channel_id=1, source_target_pairs={{0,64},{16,80},{32,96},{48,112},{64,128},{80,144},{96,160},{112,17... | collective-permute-start | bytes 1769480 | tf_op jit(solution)/shard_map/ppermute | solution.py:29
  92.5 2.5 collective-permute-start.7
  95.0 1.3 collective-permute-start.10
  96.3 1.4 collective-permute-start.11
  98.5 35.1 %collective-permute-done.6 = bf16[576,512]{1,0:T(8,128)(2,1)S(1)} collective-permute-done((bf16[576,512]{1,0:T(8,128)(2,1)}, bf16[576,512]{1,0:T(8,128)(2,1)S(1)}, u32[]{:S(2)}, u32[]{:S(2)}) %collective-permute-start.6) | collective-permute-done | bytes 589856 | tf_op jit(solution)/shard_map/ppermute | solution.py:29
  133.6 0.8 copy-done.3
  135.1 0.8 copy-done.4
  135.9 0.7 slice.92
  136.7 3.6 %collective-permute-start.9 = (bf16[288,512]{1,0:T(8,128)(2,1)}, bf16[288,512]{1,0:T(8,128)(2,1)}, u32[]{:S(2)}, u32[]{:S(2)}) collective-permute-start(bf16[288,512]{1,0:T(8,128)(2,1)} %slice.92), channel_id=1, source_target_pairs={{0,192},{16,208},{32,224},{48,240},{64,0},{80,16},{96,32},{112,48}... | collective-permute-start | bytes 884744 | tf_op jit(solution)/shard_map/ppermute | solution.py:32
  140.3 2.7 fusion.12
  144.8 1.2 slice.88
  146.0 1.2 slice.89
  148.5 1.2 slice.94
  149.7 1.2 slice.95
  150.9 1.2 slice.91
  152.7 1.2 slice.93
  155.8 4.4 %fusion.11 = bf16[1,320,512]{2,1,0:T(8,128)(2,1)S(1)} fusion(bf16[5120,320]{0,1:T(8,128)(2,1)S(1)} %copy-done, bf16[512,5120]{1,0:T(8,128)(2,1)} %bitcast.49, pred[512]{0:T(512)(128)(4,1)S(1)} %iota_compare_fusion.3), kind=kOutput, calls=%fused_computation.8 | convolution fusion | flops 1678049280 | bytes 8847872 | tf_op jit(solution)/shard_map/dot_general | solution.py:171
  160.2 0.9 maximum_select_fusion
  161.1 1.1 constant_dynamic-update-slice_fusion.9
  162.2 1.1 constant_dynamic-update-slice_fusion.8
  163.3 1.0 constant_dynamic-update-slice_fusion.7
  164.3 1.0 constant_dynamic-update-slice_fusion.6.z_0
  165.3 1.7 collective-permute-start.14
  167.0 1.0 collective-permute-start.15
  168.1 37.7 %collective-permute-done.14.z_1 = bf16[1728,512]{1,0:T(8,128)(2,1)S(1)} collective-permute-done((bf16[1728,512]{1,0:T(8,128)(2,1)S(1)}, bf16[1728,512]{1,0:T(8,128)(2,1)S(1)}, u32[]{:S(2)}, u32[]{:S(2)}) %collective-permute-start.14) | collective-permute-done | bytes 1769504 | tf_op jit(solution)/shard_map/ppermute | solution.py:29
  205.8 1.3 copy-done.6
  207.0 1.0 slice.99
  208.0 1.0 collective-permute-start.16
  209.0 1.2 copy-done.7
  210.2 1.0 slice.100
  211.2 1.7 collective-permute-start.17
  212.9 1.7 slice.97
  214.6 1.7 slice.98
  216.3 2.7 collective-permute-start.13
  219.0 16.1 %collective-permute-done.12.own_top = bf16[288,512]{1,0:T(8,128)(2,1)} collective-permute-done((bf16[288,512]{1,0:T(8,128)(2,1)}, bf16[288,512]{1,0:T(8,128)(2,1)}, u32[]{:S(2)}, u32[]{:S(2)}) %collective-permute-start.12) | collective-permute-done | bytes 294944 | tf_op jit(solution)/shard_map/ppermute | solution.py:31
  235.1 2.3 collective-permute-done.13.own_bottom
  237.4 1.1 copy-done.1
  238.5 23.1 %shard_map.82 = f32[32,128]{1,0:T(8,128)S(1)} custom-call(s32[16]{0:T(128)S(1)} %stack.67.place, s32[16]{0:T(128)S(1)} %fusion.13.slot, bf16[16,320,640]{2,1,0:T(8,128)(2,1)} %all-gather.5.cloned.1.call-done.ein.ql, bf16[16,320,640]{2,1,0:T(8,128)(2,1)} %all-gather.5.cloned.1.call-done.ein.ql, bf16[576,512]{1,0:T(8,128)(2,1)} %pad_maximum_fusion.1.own_0, ...), custom_call_target="tpu_custom_call" | custom-call | flops 10000000000 | bytes 16000000 | tf_op jit(solution)/shard_map/pallas_call | solution.py:104
  261.7 26.7 %all_to_all.9 = f32[256,1,2]{2,1,0:T(1,128)S(1)} all-to-all(f32[256,1,2]{2,1,0:T(1,128)S(1)} %bitcast.48), channel_id=1, replica_groups=mesh['shard'=16,'example'=16] {'shard','example'}, dimensions={0} | all-to-all | bytes 4096 | tf_op jit(solution)/shard_map/all_to_all | solution.py:186
  (57 shorter events, 3.9 us)
Async XLA Ops:
  6.5 133.7 %copy-start = (bf16[5120,320]{0,1:T(8,128)(2,1)S(1)}, bf16[5120,320]{0,1:T(8,128)(2,1)}, u32[]{:S(2)}) copy-start(bf16[5120,320]{0,1:T(8,128)(2,1)} %param.11) | copy-start | bytes 9830404
  6.5 149.2 %all-gather.3.cloned.1.call-start = ((), (), s32[]{:S(2)}) async-start(), calls=%async_computation.1 | async-start | bytes 5570560 | tf_op jit(solution)/shard_map/all_gather | solution.py:147
  15.6 11.8 %collective-permute-start = (bf16[32,7040]{1,0:T(8,128)(2,1)}, bf16[32,7040]{1,0:T(8,128)(2,1)}, u32[]{:S(2)}, u32[]{:S(2)}) collective-permute-start(bf16[32,7040]{1,0:T(8,128)(2,1)} %get-tuple-element.5), channel_id=1, source_target_pairs={{0,8},{1,9},{2,10},{3,11},{4,12},{5,13},{6,14},{7,15},{8,0},{9,1},... | collective-permute-start | bytes 1351688 | tf_op jit(solution)/shard_map/ppermute | solution.py:150
  18.1 219.3 %all-gather.5.cloned.1.call-start = ((), (), s32[]{:S(2)}) async-start(), calls=%async_computation.2 | async-start | bytes 6963200 | tf_op jit(solution)/shard_map/all_gather | solution.py:182
  28.6 22.0 %collective-permute-start.1 = (bf16[64,7040]{1,0:T(8,128)(2,1)S(1)}, bf16[64,7040]{1,0:T(8,128)(2,1)S(1)}, u32[]{:S(2)}, u32[]{:S(2)}) collective-permute-start(bf16[64,7040]{1,0:T(8,128)(2,1)S(1)} %pad_maximum_fusion), channel_id=1, source_target_pairs={{0,2},{1,3},{2,4},{3,5},{4,6},{5,7},{6,0},{7,1},{8,10},{9,11},{10,... | collective-permute-start | bytes 2703368 | tf_op jit(solution)/shard_map/ppermute | solution.py:29
  30.8 20.4 %collective-permute-start.2 = (bf16[64,7040]{1,0:T(8,128)(2,1)S(1)}, bf16[64,7040]{1,0:T(8,128)(2,1)S(1)}, u32[]{:S(2)}, u32[]{:S(2)}) collective-permute-start(bf16[64,7040]{1,0:T(8,128)(2,1)S(1)} %pad_maximum_fusion), channel_id=1, source_target_pairs={{0,6},{1,7},{2,0},{3,1},{4,2},{5,3},{6,4},{7,5},{8,14},{9,15},{10,... | collective-permute-start | bytes 2703368 | tf_op jit(solution)/shard_map/ppermute | solution.py:30
  34.0 32.3 %copy-start.2 = (bf16[6912,432]{0,1:T(8,128)(2,1)S(1)}, bf16[6912,432]{0,1:T(8,128)(2,1)}, u32[]{:S(2)}) copy-start(bf16[6912,432]{0,1:T(8,128)(2,1)} %param.12) | copy-start | bytes 17915908
  34.0 32.3 %copy-start.5 = (bf16[2,32,6912]{2,1,0:T(8,128)(2,1)S(1)}, bf16[2,32,6912]{2,1,0:T(8,128)(2,1)}, u32[]{:S(2)}) copy-start(bf16[2,32,6912]{2,1,0:T(8,128)(2,1)} %param.15) | copy-start | bytes 2654212
  50.6 10.7 %collective-permute-start.3 = (bf16[32,7040]{1,0:T(8,128)(2,1)S(1)}, bf16[32,7040]{1,0:T(8,128)(2,1)S(1)}, u32[]{:S(2)}, u32[]{:S(2)}) collective-permute-start(bf16[32,7040]{1,0:T(8,128)(2,1)S(1)} %slice.82), channel_id=1, source_target_pairs={{0,2},{1,3},{2,4},{3,5},{4,6},{5,7},{6,0},{7,1},{8,10},{9,11},{10,... | collective-permute-start | bytes 1351688 | tf_op jit(solution)/shard_map/ppermute | solution.py:31
  51.2 10.9 %collective-permute-start.4 = (bf16[32,7040]{1,0:T(8,128)(2,1)S(1)}, bf16[32,7040]{1,0:T(8,128)(2,1)S(1)}, u32[]{:S(2)}, u32[]{:S(2)}) collective-permute-start(bf16[32,7040]{1,0:T(8,128)(2,1)S(1)} %slice.83), channel_id=1, source_target_pairs={{0,6},{1,7},{2,0},{3,1},{4,2},{5,3},{6,4},{7,5},{8,14},{9,15},{10,... | collective-permute-start | bytes 1351688 | tf_op jit(solution)/shard_map/ppermute | solution.py:32
  62.9 5.9 %copy-start.10 = (bf16[256,7040]{1,0:T(8,128)(2,1)S(1)}, bf16[256,7040]{1,0:T(8,128)(2,1)}, u32[]{:S(2)}) copy-start(bf16[256,7040]{1,0:T(8,128)(2,1)} %constant_dynamic-update-slice_fusion) | copy-start | bytes 10813444
  62.9 10.2 %collective-permute-start.5 = (bf16[256,7040]{1,0:T(8,128)(2,1)}, bf16[256,7040]{1,0:T(8,128)(2,1)}, u32[]{:S(2)}, u32[]{:S(2)}) collective-permute-start(bf16[256,7040]{1,0:T(8,128)(2,1)} %constant_dynamic-update-slice_fusion), channel_id=1, source_target_pairs={{0,1},{1,0},{2,3},{3,2},{4,5},{5,4},{6,7},{7,6},{8,9},{9,8},{10,11... | collective-permute-start | bytes 10813448 | tf_op jit(solution)/shard_map/ppermute | solution.py:152
  89.2 44.4 %collective-permute-start.6 = (bf16[576,512]{1,0:T(8,128)(2,1)}, bf16[576,512]{1,0:T(8,128)(2,1)S(1)}, u32[]{:S(2)}, u32[]{:S(2)}) collective-permute-start(bf16[576,512]{1,0:T(8,128)(2,1)} %pad_maximum_fusion.1.own_0), channel_id=1, source_target_pairs={{0,64},{16,80},{32,96},{48,112},{64,128},{80,144},{96,160},{112,17... | collective-permute-start | bytes 1769480 | tf_op jit(solution)/shard_map/ppermute | solution.py:29
  92.5 42.6 %collective-permute-start.7 = (bf16[576,512]{1,0:T(8,128)(2,1)}, bf16[576,512]{1,0:T(8,128)(2,1)S(1)}, u32[]{:S(2)}, u32[]{:S(2)}) collective-permute-start(bf16[576,512]{1,0:T(8,128)(2,1)} %pad_maximum_fusion.1.own_0), channel_id=1, source_target_pairs={{0,192},{16,208},{32,224},{48,240},{64,0},{80,16},{96,32},{112,48}... | collective-permute-start | bytes 1769480 | tf_op jit(solution)/shard_map/ppermute | solution.py:30
  95.0 53.5 %collective-permute-start.10 = (bf16[576,512]{1,0:T(8,128)(2,1)}, bf16[576,512]{1,0:T(8,128)(2,1)}, u32[]{:S(2)}, u32[]{:S(2)}) collective-permute-start(bf16[576,512]{1,0:T(8,128)(2,1)} %pad_maximum_fusion.1.own_0), channel_id=1, source_target_pairs={{0,16},{16,32},{32,48},{48,0},{64,80},{80,96},{96,112},{112,64},{1... | collective-permute-start | bytes 1769480 | tf_op jit(solution)/shard_map/ppermute | solution.py:29
  96.3 53.4 %collective-permute-start.11 = (bf16[576,512]{1,0:T(8,128)(2,1)}, bf16[576,512]{1,0:T(8,128)(2,1)}, u32[]{:S(2)}, u32[]{:S(2)}) collective-permute-start(bf16[576,512]{1,0:T(8,128)(2,1)} %pad_maximum_fusion.1.own_0), channel_id=1, source_target_pairs={{0,48},{16,0},{32,16},{48,32},{64,112},{80,64},{96,80},{112,96},{1... | collective-permute-start | bytes 1769480 | tf_op jit(solution)/shard_map/ppermute | solution.py:30
  133.6 0.8 copy-start.3
  135.1 15.7 %collective-permute-start.8 = (bf16[288,512]{1,0:T(8,128)(2,1)}, bf16[288,512]{1,0:T(8,128)(2,1)}, u32[]{:S(2)}, u32[]{:S(2)}) collective-permute-start(bf16[288,512]{1,0:T(8,128)(2,1)} %slice.90), channel_id=1, source_target_pairs={{0,64},{16,80},{32,96},{48,112},{64,128},{80,144},{96,160},{112,17... | collective-permute-start | bytes 884744 | tf_op jit(solution)/shard_map/ppermute | solution.py:31
  135.1 0.8 copy-start.4
  136.7 16.0 %collective-permute-start.9 = (bf16[288,512]{1,0:T(8,128)(2,1)}, bf16[288,512]{1,0:T(8,128)(2,1)}, u32[]{:S(2)}, u32[]{:S(2)}) collective-permute-start(bf16[288,512]{1,0:T(8,128)(2,1)} %slice.92), channel_id=1, source_target_pairs={{0,192},{16,208},{32,224},{48,240},{64,0},{80,16},{96,32},{112,48}... | collective-permute-start | bytes 884744 | tf_op jit(solution)/shard_map/ppermute | solution.py:32
  155.8 4.4 %copy-start.9 = (bf16[1,320,64]{2,1,0:T(8,128)(2,1)S(1)}, bf16[1,320,64]{2,1,0:T(8,128)(2,1)}, u32[]{:S(2)}) copy-start(bf16[1,320,64]{2,1,0:T(8,128)(2,1)} %fusion.12) | copy-start | bytes 122884
  165.3 45.9 %copy-start.8 = (bf16[1728,512]{1,0:T(8,128)(2,1)}, bf16[1728,512]{1,0:T(8,128)(2,1)S(1)}, u32[]{:S(2)}) copy-start(bf16[1728,512]{1,0:T(8,128)(2,1)S(1)} %constant_dynamic-update-slice_fusion.6.z_0) | copy-start | bytes 5308420
  165.3 40.4 %collective-permute-start.14 = (bf16[1728,512]{1,0:T(8,128)(2,1)S(1)}, bf16[1728,512]{1,0:T(8,128)(2,1)S(1)}, u32[]{:S(2)}, u32[]{:S(2)}) collective-permute-start(bf16[1728,512]{1,0:T(8,128)(2,1)S(1)} %constant_dynamic-update-slice_fusion.6.z_0), channel_id=1, source_target_pairs={{0,16},{16,32},{32,48},{48,0},{64,80},{80,96},{96,112},{112,64},{1... | collective-permute-start | bytes 5308424 | tf_op jit(solution)/shard_map/ppermute | solution.py:29
  167.0 41.9 %collective-permute-start.15 = (bf16[1728,512]{1,0:T(8,128)(2,1)S(1)}, bf16[1728,512]{1,0:T(8,128)(2,1)S(1)}, u32[]{:S(2)}, u32[]{:S(2)}) collective-permute-start(bf16[1728,512]{1,0:T(8,128)(2,1)S(1)} %constant_dynamic-update-slice_fusion.6.z_0), channel_id=1, source_target_pairs={{0,48},{16,0},{32,16},{48,32},{64,112},{80,64},{96,80},{112,96},{1... | collective-permute-start | bytes 5308424 | tf_op jit(solution)/shard_map/ppermute | solution.py:30
  205.8 1.3 copy-start.6
  208.0 29.4 %collective-permute-start.16 = (bf16[864,512]{1,0:T(8,128)(2,1)}, bf16[864,512]{1,0:T(8,128)(2,1)}, u32[]{:S(2)}, u32[]{:S(2)}) collective-permute-start(bf16[864,512]{1,0:T(8,128)(2,1)} %slice.99), channel_id=1, source_target_pairs={{0,16},{16,32},{32,48},{48,0},{64,80},{80,96},{96,112},{112,64},{1... | collective-permute-start | bytes 2654216 | tf_op jit(solution)/shard_map/ppermute | solution.py:31
  209.0 1.2 copy-start.7
  211.2 26.2 %collective-permute-start.17 = (bf16[864,512]{1,0:T(8,128)(2,1)}, bf16[864,512]{1,0:T(8,128)(2,1)}, u32[]{:S(2)}, u32[]{:S(2)}) collective-permute-start(bf16[864,512]{1,0:T(8,128)(2,1)} %slice.100), channel_id=1, source_target_pairs={{0,48},{16,0},{32,16},{48,32},{64,112},{80,64},{96,80},{112,96},{1... | collective-permute-start | bytes 2654216 | tf_op jit(solution)/shard_map/ppermute | solution.py:32
  214.6 20.5 %collective-permute-start.12 = (bf16[288,512]{1,0:T(8,128)(2,1)}, bf16[288,512]{1,0:T(8,128)(2,1)}, u32[]{:S(2)}, u32[]{:S(2)}) collective-permute-start(bf16[288,512]{1,0:T(8,128)(2,1)} %slice.97), channel_id=1, source_target_pairs={{0,16},{16,32},{32,48},{48,0},{64,80},{80,96},{96,112},{112,64},{1... | collective-permute-start | bytes 884744 | tf_op jit(solution)/shard_map/ppermute | solution.py:31
  216.3 21.1 %collective-permute-start.13 = (bf16[288,512]{1,0:T(8,128)(2,1)}, bf16[288,512]{1,0:T(8,128)(2,1)}, u32[]{:S(2)}, u32[]{:S(2)}) collective-permute-start(bf16[288,512]{1,0:T(8,128)(2,1)} %slice.98), channel_id=1, source_target_pairs={{0,48},{16,0},{32,16},{48,32},{64,112},{80,64},{96,80},{112,96},{1... | collective-permute-start | bytes 884744 | tf_op jit(solution)/shard_map/ppermute | solution.py:32
  237.4 1.1 copy-start.1
Sparse Core Ops, SparseCore 0:
  18.2 98.8 all-gather.2
  161.2 46.4 all-gather.4

commit v4 on v3

--- a/solution.py
+++ b/solution.py
@@ -52,27 +52,36 @@
 def score_kernel(
     place, slot, ein, ql,
     own_0, own_1, own_2, own_top, own_bottom,
-    z_0, z_1, z_2, z_top, z_bottom,
-    eig, out, inverse, left, right, own_3, z_3, grads,
+    near_0, near_1, near_2, near_top, near_bottom,
+    last_0, last_1, last_2, last_top, last_bottom,
+    eig, out, inverse, left, right, own_3, near_3, last_3, grads,
 ):
     n = pl.program_id(0)
     dj = eig.shape[1]
-    owns = (own_0, own_1, own_2, own_3)
-    others = (z_0, z_1, z_2, z_3)
     size = own_0.shape[0]
-    blocks = [(owns[y], 0) if z == 0 else (others[y], size * (z - 1)) for y in range(4) for z in range(4)]
+    blocks = []
+    for own, near, last in (
+        (own_0, near_0, last_0),
+        (own_1, near_1, last_1),
+        (own_2, near_2, last_2),
+        (own_3, near_3, last_3),
+    ):
+        blocks += [(own, 0), (near, 0), (near, size), (last, 0)]
     after = NSEQ * 32
 
     @pl.when(n == 0)
     def _():
-        for far, top, bottom in ((own_3, own_top, own_bottom), (z_3, z_top, z_bottom)):
+        for far, top, bottom in (
+            (own_3, own_top, own_bottom),
+            (near_3, near_top, near_bottom),
+            (last_3, last_top, last_bottom),
+        ):
             far[: top.shape[0], :] = top[...]
             far[top.shape[0] :, :] = bottom[...]
-        total = 0.0
         for k, (ref, row) in enumerate(blocks):
             start = pl.multiple_of(place[k] * 64, 64)
             right[pl.ds(start, 64), :] = ref[row + after : row + after + 64, :dj]
-            total += jnp.sum(ref[row : row + 16, dj:].astype(F32))
+        total = jnp.sum(ql[:, :, 64:].astype(F32))
         inverse[...] = 1.0 / (eig[...] + (0.1 / (D * H)) * total)
         for e in range(NSEQ):
             left[64 * e : 64 * e + 64, :] = ql[e].T[:64, :]
@@ -118,6 +127,7 @@
             pltpu.VMEM((16 * 64, dj), BF16),
             pltpu.VMEM(blocks[0].shape, BF16),
             pltpu.VMEM(blocks[5].shape, BF16),
+            pltpu.VMEM(blocks[10].shape, BF16),
             pltpu.VMEM((SEQLEN, blocks[0].shape[1]), BF16),
         ],
         compiler_params=pltpu.CompilerParams(vmem_limit_bytes=48 * 1024 * 1024),
@@ -144,41 +154,41 @@
     di, dj = eigvals.shape
     row_major = Layout(major_to_minor=(0, 1))
 
-    rows_all = lax.all_gather(train_in[0], "shard", axis=0)
-
-    block = jnp.concatenate([train_grad[0], corner(jnp.sum(eigvals), (32, 128))], 1)
-    block = jnp.concatenate([block, lax.ppermute(block, "example", EXAMPLE_Z)], 0)
+    rows_all = lax.all_gather(
+        jnp.concatenate([train_in[0], corner(jnp.sum(eigvals), (32, 128))], 1), "shard", axis=0
+    )
+
+    block = jnp.concatenate([train_grad[0], lax.ppermute(train_grad[0], "example", EXAMPLE_Z)], 0)
     block = jnp.concatenate(ring4(block, "example", EXAMPLE_X, 32), 0)
     other = lax.ppermute(block, "example", EXAMPLE_CORE)
-    eig_example = jnp.sum(
-        jnp.concatenate([block[:, H:], other[:, H:]], 0).astype(F32)
-    )
     query_right = jnp.dot(
         query_out.reshape(64, H), basis_out, preferred_element_type=F32
     ).astype(BF16)
     part_out = [
-        jnp.dot(b[:, :H], basis_out, preferred_element_type=F32).astype(BF16)
+        jnp.dot(b, basis_out, preferred_element_type=F32).astype(BF16)
         for b in (block, other)
     ]
     part_out = jnp.concatenate(part_out + [query_right], 0)
-    sums = corner(eig_example, (part_out.shape[0], 512 - dj))
-    part_out = with_layout_constraint(jnp.concatenate([part_out, sums], 1), row_major)
+    part_out = with_layout_constraint(jnp.pad(part_out, ((0, 0), (0, 512 - dj))), row_major)
     z_blocks = ring4(part_out, "shard", SHARD_Z, 288)
-    z_others = jnp.concatenate(z_blocks[1:], 0)
-    blocks = ring4(part_out, "shard", SHARD_Y, 288) + ring4(z_others, "shard", SHARD_Y, 864)
-
-    flag = jnp.isnan(part_out[256, 0])
-    own_in = jnp.dot(rows_all.reshape(SEQLEN, D), basis_in, preferred_element_type=F32)
+    near = jnp.concatenate(z_blocks[1:3], 0)
+    last = jnp.concatenate(z_blocks[3:], 0)
+    blocks = (
+        ring4(part_out, "shard", SHARD_Y, 288)
+        + ring4(near, "shard", SHARD_Y, 576)
+        + ring4(last, "shard", SHARD_Y, 288)
+    )
+
+    flag = jnp.isnan(sum(b[0, 0] for b in z_blocks[1:3] + blocks[1:3]))
+    own_in = jnp.dot(rows_all[:, :, :D].reshape(SEQLEN, D), basis_in, preferred_element_type=F32)
     token = jnp.arange(SEQLEN, dtype=jnp.int32)[:, None]
     live = jnp.where(flag, 0, seq_lens[0])
     own_in = jnp.where(token < live, own_in, 0.0).astype(BF16)
     query_left = jnp.dot(
         query_in.reshape(64, D), basis_in, preferred_element_type=F32
     ).astype(BF16)
-    spare = jnp.zeros((di, 64), BF16)
-    ein = jnp.concatenate([own_in.T, query_left.T, spare], 1)
-    late = jnp.isnan(sum(b[0, 0] for b in z_blocks[1:] + blocks[1:3]))
-    ein = jnp.where(late, jnp.zeros_like(ein), ein)
+    eig_shard = corner(jnp.sum(rows_all[:, :, D:].astype(F32)), (di, 64))
+    ein = jnp.concatenate([own_in.T, query_left.T, eig_shard], 1)
     ein = lax.all_gather(ein, "example", axis=0)
 
     partial = score_call(place, slot, ein, blocks, eigvals)[:, :NSEQ]

time: 297 us -> 288 us (0.970)
  waiting for transfers between devices: 123 us -> 104 us
  starting transfers between devices: 32.5 us -> 40.9 us
  local copies, waits for them, and re-layouts: 33.4 us -> 37.4 us
    ppermute x4 -> x5, waiting for transfers between devices: 89.4 us -> 54.2 us  [ring4(): below = lax.ppermute(block, axis, steps[1])]
    ppermute x4 -> x5, waiting for transfers between devices: 21.9 us -> 33.1 us  [ring4(): far_top = lax.ppermute(below[:cut], axis, steps[1])]
    ppermute x1, waiting for transfers between devices: 9.25 us -> 0.66 us  [shards(): lax.ppermute(train_grad[0], 'example', EXAMPLE_Z)]
    ppermute x4 -> x5, waiting for transfers between devices: 2.26 us -> 10.7 us  [ring4(): far_bottom = lax.ppermute(above[cut:], axis, steps[-1])]
    ppermute x4 -> x5, waiting for transfers between devices: 0.01 us -> 5.08 us  [ring4(): above = lax.ppermute(block, axis, steps[-1])]
    ppermute x4 -> x5, starting transfers between devices: 6.36 us -> 10.4 us  [ring4(): above = lax.ppermute(block, axis, steps[-1])]
    ppermute x4 -> x5, starting transfers between devices: 1.52 us -> 5.38 us  [ring4(): far_top = lax.ppermute(below[:cut], axis, steps[1])]
    ppermute x4 -> x5, starting transfers between devices: 10.3 us -> 12.6 us  [ring4(): far_bottom = lax.ppermute(above[cut:], axis, steps[-1])]
  transfers between devices with their start and end apart: 20 -> 24, of which waited for: 7 -> 10; matrix products, arithmetic and copies ran while one was open for 16% -> 17% of each run, Pallas kernels for 0% -> 0%
where the time goes in v4:
time: 288 us; the launch traced here: 287 us
  waiting for transfers between devices  104 us (36%)
  starting transfers between devices  40.9 us (14%)
  local copies, waits for them, and re-layouts  37.4 us (13%)
  blocking collectives  24.9 us (9%)
  between operations  24.2 us (8%)
  Pallas kernels  23 us (8%)
  matrix products  20.1 us (7%)
  other arithmetic  12.7 us (4%)
    ppermute x5, waiting for transfers between devices, ring4(): below = lax.ppermute(block, axis, steps[1])  54.2 us
    ppermute x5, waiting for transfers between devices, ring4(): far_top = lax.ppermute(below[:cut], axis, steps[1])  33.1 us
    all_to_all x1, blocking collectives, shards(): pieces = lax.all_to_all(pieces, ('shard', 'example'), 0, 0, tiled=True)  24.9 us
    pallas_call x1, Pallas kernels, score_call(): pl.pallas_call(score_kernel, grid=(NSEQ,), in_specs=[pl.BlockSpec(memory_...  23 us
    unnamed x35, local copies, waits for them, and re-layouts  14 us
    ppermute x5, starting transfers between devices, ring4(): far_bottom = lax.ppermute(above[cut:], axis, steps[-1])  12.6 us
    dot_general x2, matrix products, shards(): jnp.dot(b, basis_out, preferred_element_type=F32).astype(BF16)  11.1 us
    ppermute x5, waiting for transfers between devices, ring4(): far_bottom = lax.ppermute(above[cut:], axis, steps[-1])  10.7 us
  transfers between devices with their start and end apart: 24, of which 10 were waited for; matrix products, arithmetic and copies ran while one was open for 17% of the time, Pallas kernels for 0%

profile of v4, /device:TPU:1, one launch (start us, length us, event | category | flops | bytes accessed | tf_op | source)
XLA Modules:
  0.0 287.0 jit_solution(7695332153464381987)
XLA Ops:
  6.5 2.5 collective-permute-start
  9.0 1.9 reduce_sum.27
  14.4 1.3 select_convert_fusion.1
  15.7 1.7 pad_maximum_fusion.2
  18.2 1.2 pad_maximum_fusion
  19.4 2.2 collective-permute-start.1
  21.6 1.4 collective-permute-start.2
  22.9 1.8 constant_dynamic-update-slice_fusion.5
  24.7 1.8 constant_dynamic-update-slice_fusion.4
  26.5 14.5 %collective-permute-done.1 = bf16[64,6912]{1,0:T(8,128)(2,1)S(1)} collective-permute-done((bf16[64,6912]{1,0:T(8,128)(2,1)S(1)}, bf16[64,6912]{1,0:T(8,128)(2,1)S(1)}, u32[]{:S(2)}, u32[]{:S(2)}) %collective-permute-start.1) | collective-permute-done | bytes 884768 | tf_op jit(solution)/shard_map/ppermute | solution.py:29
  41.6 2.4 collective-permute-start.4
  44.0 1.0 constant_dynamic-update-slice_fusion.3
  45.0 0.9 constant_dynamic-update-slice_fusion.2
  45.9 5.9 %collective-permute-done.3 = bf16[32,6912]{1,0:T(8,128)(2,1)S(1)} collective-permute-done((bf16[32,6912]{1,0:T(8,128)(2,1)S(1)}, bf16[32,6912]{1,0:T(8,128)(2,1)S(1)}, u32[]{:S(2)}, u32[]{:S(2)}) %collective-permute-start.3) | collective-permute-done | bytes 442400 | tf_op jit(solution)/shard_map/ppermute | solution.py:31
  53.5 3.2 %collective-permute-start.5 = (bf16[256,6912]{1,0:T(8,128)(2,1)}, bf16[256,6912]{1,0:T(8,128)(2,1)}, u32[]{:S(2)}, u32[]{:S(2)}) collective-permute-start(bf16[256,6912]{1,0:T(8,128)(2,1)} %constant_dynamic-update-slice_fusion), channel_id=1, source_target_pairs={{0,1},{1,0},{2,3},{3,2},{4,5},{5,4},{6,7},{7,6},{8,9},{9,8},{10,11... | collective-permute-start | bytes 10616840 | tf_op jit(solution)/shard_map/ppermute | solution.py:163
  57.3 2.5 convolution_convert_fusion.2
  59.8 4.9 %convolution_convert_fusion.1 = bf16[256,432]{0,1:T(8,128)(2,1)} fusion(bf16[256,6912]{1,0:T(8,128)(2,1)} %constant_dynamic-update-slice_fusion, bf16[6912,432]{0,1:T(8,128)(2,1)S(1)} %copy-done.9), kind=kOutput, calls=%fused_computation.3 | convolution fusion | flops 1528934400 | bytes 9732096 | tf_op jit(solution)/shard_map/dot_general | solution.py:168
  64.7 1.1 copy.21
  65.8 6.2 %convolution_convert_fusion = bf16[256,432]{0,1:T(8,128)(2,1)} fusion(bf16[256,6912]{1,0:T(8,128)(2,1)} %collective-permute-done.5, bf16[6912,432]{0,1:T(8,128)(2,1)} %param.12), kind=kOutput, calls=%fused_computation.2 | convolution fusion | flops 1528934400 | bytes 9732096 | tf_op jit(solution)/shard_map/dot_general | solution.py:168
  72.0 1.8 copy.22
  73.7 1.9 fusion.6.own_0
  75.6 3.3 %collective-permute-start.6 = (bf16[576,512]{1,0:T(8,128)(2,1)}, bf16[576,512]{1,0:T(8,128)(2,1)}, u32[]{:S(2)}, u32[]{:S(2)}) collective-permute-start(bf16[576,512]{1,0:T(8,128)(2,1)} %fusion.6.own_0), channel_id=1, source_target_pairs={{0,64},{16,80},{32,96},{48,112},{64,128},{80,144},{96,160},{112,17... | collective-permute-start | bytes 1769480 | tf_op jit(solution)/shard_map/ppermute | solution.py:29
  78.9 2.3 collective-permute-start.7
  81.2 1.3 collective-permute-start.8
  82.4 1.4 collective-permute-start.9
  83.9 2.2 convolution_convert_fusion.3
  86.2 34.3 %collective-permute-done.6 = bf16[576,512]{1,0:T(8,128)(2,1)} collective-permute-done((bf16[576,512]{1,0:T(8,128)(2,1)}, bf16[576,512]{1,0:T(8,128)(2,1)}, u32[]{:S(2)}, u32[]{:S(2)}) %collective-permute-start.6) | collective-permute-done | bytes 589856 | tf_op jit(solution)/shard_map/ppermute | solution.py:29
  120.5 1.2 slice.70
  121.7 5.1 %collective-permute-done.7 = bf16[576,512]{1,0:T(8,128)(2,1)} collective-permute-done((bf16[576,512]{1,0:T(8,128)(2,1)}, bf16[576,512]{1,0:T(8,128)(2,1)}, u32[]{:S(2)}, u32[]{:S(2)}) %collective-permute-start.7) | collective-permute-done | bytes 589856 | tf_op jit(solution)/shard_map/ppermute | solution.py:30
  126.7 1.3 slice.71
  129.3 1.2 slice.72
  131.2 1.2 slice.73
  133.1 5.3 %slice.74 = bf16[16,32,5120]{2,1,0:T(8,128)(2,1)} slice(bf16[16,32,5248]{2,1,0:T(8,128)(2,1)} %bitcast.48), slice={[0:16], [0:32], [0:5120]} | slice | bytes 10485760 | tf_op jit(solution)/shard_map/slice | solution.py:183
  138.4 1.6 convert_reduce_fusion
  143.5 4.4 %fusion.1 = bf16[320,512]{1,0:T(8,128)(2,1)S(1)} fusion(bf16[512,5120]{1,0:T(8,128)(2,1)} %bitcast.50, bf16[5120,320]{0,1:T(8,128)(2,1)S(1)} %copy-done, pred[512]{0:T(512)(128)(4,1)S(1)} %iota_compare_fusion.4), kind=kOutput, calls=%fused_computation.4 | convolution fusion | flops 1678049280 | bytes 8847872 | tf_op jit(solution)/shard_map/dot_general | solution.py:183
  147.9 1.4 select_convert_fusion
  149.3 0.9 pad_maximum_fusion.1
  150.2 1.1 constant_dynamic-update-slice_fusion.7
  151.3 1.1 constant_dynamic-update-slice_fusion.6.near_0
  152.5 2.7 collective-permute-start.13
  155.2 1.0 slice.80
  156.2 3.4 %collective-permute-start.16 = (bf16[288,512]{1,0:T(8,128)(2,1)S(1)}, bf16[288,512]{1,0:T(8,128)(2,1)S(1)}, u32[]{:S(2)}, u32[]{:S(2)}) collective-permute-start(bf16[288,512]{1,0:T(8,128)(2,1)S(1)} %slice.80), channel_id=1, source_target_pairs={{0,64},{16,80},{32,96},{48,112},{64,128},{80,144},{96,160},{112,17... | collective-permute-start | bytes 884744 | tf_op jit(solution)/shard_map/ppermute | solution.py:31
  159.5 1.0 slice.81
  160.5 7.6 %collective-permute-start.17 = (bf16[288,512]{1,0:T(8,128)(2,1)S(1)}, bf16[288,512]{1,0:T(8,128)(2,1)S(1)}, u32[]{:S(2)}, u32[]{:S(2)}) collective-permute-start(bf16[288,512]{1,0:T(8,128)(2,1)S(1)} %slice.81), channel_id=1, source_target_pairs={{0,192},{16,208},{32,224},{48,240},{64,0},{80,16},{96,32},{112,48}... | collective-permute-start | bytes 884744 | tf_op jit(solution)/shard_map/ppermute | solution.py:32
  168.1 18.1 %collective-permute-done.16 = bf16[288,512]{1,0:T(8,128)(2,1)S(1)} collective-permute-done((bf16[288,512]{1,0:T(8,128)(2,1)S(1)}, bf16[288,512]{1,0:T(8,128)(2,1)S(1)}, u32[]{:S(2)}, u32[]{:S(2)}) %collective-permute-start.16) | collective-permute-done | bytes 294944 | tf_op jit(solution)/shard_map/ppermute | solution.py:31
  186.4 2.7 collective-permute-start.19
  189.0 1.0 slice.76
  190.1 0.9 slice.78
  191.1 0.9 slice.79
  192.0 2.7 collective-permute-start.15
  194.6 1.7 slice.77
  196.3 5.4 %collective-permute-done.18.last_1 = bf16[576,512]{1,0:T(8,128)(2,1)S(1)} collective-permute-done((bf16[576,512]{1,0:T(8,128)(2,1)S(1)}, bf16[576,512]{1,0:T(8,128)(2,1)S(1)}, u32[]{:S(2)}, u32[]{:S(2)}) %collective-permute-start.18) | collective-permute-done | bytes 589856 | tf_op jit(solution)/shard_map/ppermute | solution.py:29
  202.5 0.8 copy-done.1
  203.3 1.5 collective-permute-start.20
  205.6 0.8 copy-done.3
  206.4 1.7 collective-permute-done.10.own_top
  209.1 10.7 %collective-permute-done.11.own_bottom = bf16[288,512]{1,0:T(8,128)(2,1)} collective-permute-done((bf16[288,512]{1,0:T(8,128)(2,1)}, bf16[288,512]{1,0:T(8,128)(2,1)}, u32[]{:S(2)}, u32[]{:S(2)}) %collective-permute-start.11) | collective-permute-done | bytes 294944 | tf_op jit(solution)/shard_map/ppermute | solution.py:32
  219.8 7.4 %collective-permute-done.20.last_top = bf16[288,512]{1,0:T(8,128)(2,1)} collective-permute-done((bf16[288,512]{1,0:T(8,128)(2,1)}, bf16[288,512]{1,0:T(8,128)(2,1)}, u32[]{:S(2)}, u32[]{:S(2)}) %collective-permute-start.20) | collective-permute-done | bytes 294944 | tf_op jit(solution)/shard_map/ppermute | solution.py:31
  227.2 1.1 copy-done.2
  228.2 1.1 copy-done.4
  229.3 1.1 copy-done.6
  230.4 1.0 copy-done.8
  231.3 23.0 %shard_map.82 = f32[32,128]{1,0:T(8,128)S(1)} custom-call(s32[16]{0:T(128)S(1)} %stack.67.place, s32[16]{0:T(128)S(1)} %fusion.7.slot, bf16[16,320,640]{2,1,0:T(8,128)(2,1)} %bitcast.57, bf16[16,320,640]{2,1,0:T(8,128)(2,1)} %bitcast.58, bf16[576,512]{1,0:T(8,128)(2,1)} %fusion.6.own_0, bf16[576,512]{1,0:T(8,128)(2,1)} %collective-permute-done.8.own_1, ...), custom_call_target="tpu_custom_call" | custom-call | flops 10000000000 | bytes 16000000 | tf_op jit(solution)/shard_map/pallas_call | solution.py:113
  254.5 24.9 %all_to_all.9 = f32[256,1,2]{2,1,0:T(1,128)S(1)} all-to-all(f32[256,1,2]{2,1,0:T(1,128)S(1)} %bitcast.55), channel_id=1, replica_groups=mesh['shard'=16,'example'=16] {'shard','example'}, dimensions={0} | all-to-all | bytes 4096 | tf_op jit(solution)/shard_map/all_to_all | solution.py:196
  (69 shorter events, 6.8 us)
Async XLA Ops:
  6.5 77.3 %copy-start = (bf16[5120,320]{0,1:T(8,128)(2,1)S(1)}, bf16[5120,320]{0,1:T(8,128)(2,1)}, u32[]{:S(2)}) copy-start(bf16[5120,320]{0,1:T(8,128)(2,1)} %param.11) | copy-start | bytes 9830404
  6.5 126.5 %all-gather.5.cloned.1.call-start = ((), (), s32[]{:S(2)}) async-start(), calls=%async_computation.1 | async-start | bytes 5709824 | tf_op jit(solution)/shard_map/all_gather | solution.py:157
  6.5 11.6 %collective-permute-start = (bf16[32,6912]{1,0:T(8,128)(2,1)}, bf16[32,6912]{1,0:T(8,128)(2,1)}, u32[]{:S(2)}, u32[]{:S(2)}) collective-permute-start(bf16[32,6912]{1,0:T(8,128)(2,1)} %bitcast.51), channel_id=1, source_target_pairs={{0,8},{1,9},{2,10},{3,11},{4,12},{5,13},{6,14},{7,15},{8,0},{9,1},... | collective-permute-start | bytes 1327112 | tf_op jit(solution)/shard_map/ppermute | solution.py:161
  17.4 209.7 %all-gather.7.cloned.1.call-start = ((), (), s32[]{:S(2)}) async-start(), calls=%async_computation.2 | async-start | bytes 6963200 | tf_op jit(solution)/shard_map/all_gather | solution.py:192
  19.4 21.7 %collective-permute-start.1 = (bf16[64,6912]{1,0:T(8,128)(2,1)S(1)}, bf16[64,6912]{1,0:T(8,128)(2,1)S(1)}, u32[]{:S(2)}, u32[]{:S(2)}) collective-permute-start(bf16[64,6912]{1,0:T(8,128)(2,1)S(1)} %pad_maximum_fusion), channel_id=1, source_target_pairs={{0,2},{1,3},{2,4},{3,5},{4,6},{5,7},{6,0},{7,1},{8,10},{9,11},{10,... | collective-permute-start | bytes 2654216 | tf_op jit(solution)/shard_map/ppermute | solution.py:29
  21.6 20.0 %collective-permute-start.2 = (bf16[64,6912]{1,0:T(8,128)(2,1)S(1)}, bf16[64,6912]{1,0:T(8,128)(2,1)S(1)}, u32[]{:S(2)}, u32[]{:S(2)}) collective-permute-start(bf16[64,6912]{1,0:T(8,128)(2,1)S(1)} %pad_maximum_fusion), channel_id=1, source_target_pairs={{0,6},{1,7},{2,0},{3,1},{4,2},{5,3},{6,4},{7,5},{8,14},{9,15},{10,... | collective-permute-start | bytes 2654216 | tf_op jit(solution)/shard_map/ppermute | solution.py:30
  26.5 30.7 %copy-start.9 = (bf16[6912,432]{0,1:T(8,128)(2,1)S(1)}, bf16[6912,432]{0,1:T(8,128)(2,1)}, u32[]{:S(2)}) copy-start(bf16[6912,432]{0,1:T(8,128)(2,1)} %param.12) | copy-start | bytes 17915908
  26.5 30.8 %copy-start.10 = (bf16[2,32,6912]{2,1,0:T(8,128)(2,1)S(1)}, bf16[2,32,6912]{2,1,0:T(8,128)(2,1)}, u32[]{:S(2)}) copy-start(bf16[2,32,6912]{2,1,0:T(8,128)(2,1)} %param.15) | copy-start | bytes 2654212
  41.1 10.7 %collective-permute-start.3 = (bf16[32,6912]{1,0:T(8,128)(2,1)S(1)}, bf16[32,6912]{1,0:T(8,128)(2,1)S(1)}, u32[]{:S(2)}, u32[]{:S(2)}) collective-permute-start(bf16[32,6912]{1,0:T(8,128)(2,1)S(1)} %slice.68), channel_id=1, source_target_pairs={{0,2},{1,3},{2,4},{3,5},{4,6},{5,7},{6,0},{7,1},{8,10},{9,11},{10,... | collective-permute-start | bytes 1327112 | tf_op jit(solution)/shard_map/ppermute | solution.py:31
  41.6 11.0 %collective-permute-start.4 = (bf16[32,6912]{1,0:T(8,128)(2,1)S(1)}, bf16[32,6912]{1,0:T(8,128)(2,1)S(1)}, u32[]{:S(2)}, u32[]{:S(2)}) collective-permute-start(bf16[32,6912]{1,0:T(8,128)(2,1)S(1)} %slice.69), channel_id=1, source_target_pairs={{0,6},{1,7},{2,0},{3,1},{4,2},{5,3},{6,4},{7,5},{8,14},{9,15},{10,... | collective-permute-start | bytes 1327112 | tf_op jit(solution)/shard_map/ppermute | solution.py:32
  53.5 12.3 %collective-permute-start.5 = (bf16[256,6912]{1,0:T(8,128)(2,1)}, bf16[256,6912]{1,0:T(8,128)(2,1)}, u32[]{:S(2)}, u32[]{:S(2)}) collective-permute-start(bf16[256,6912]{1,0:T(8,128)(2,1)} %constant_dynamic-update-slice_fusion), channel_id=1, source_target_pairs={{0,1},{1,0},{2,3},{3,2},{4,5},{5,4},{6,7},{7,6},{8,9},{9,8},{10,11... | collective-permute-start | bytes 10616840 | tf_op jit(solution)/shard_map/ppermute | solution.py:163
  75.6 44.8 %collective-permute-start.6 = (bf16[576,512]{1,0:T(8,128)(2,1)}, bf16[576,512]{1,0:T(8,128)(2,1)}, u32[]{:S(2)}, u32[]{:S(2)}) collective-permute-start(bf16[576,512]{1,0:T(8,128)(2,1)} %fusion.6.own_0), channel_id=1, source_target_pairs={{0,64},{16,80},{32,96},{48,112},{64,128},{80,144},{96,160},{112,17... | collective-permute-start | bytes 1769480 | tf_op jit(solution)/shard_map/ppermute | solution.py:29
  78.9 47.8 %collective-permute-start.7 = (bf16[576,512]{1,0:T(8,128)(2,1)}, bf16[576,512]{1,0:T(8,128)(2,1)}, u32[]{:S(2)}, u32[]{:S(2)}) collective-permute-start(bf16[576,512]{1,0:T(8,128)(2,1)} %fusion.6.own_0), channel_id=1, source_target_pairs={{0,192},{16,208},{32,224},{48,240},{64,0},{80,16},{96,32},{112,48}... | collective-permute-start | bytes 1769480 | tf_op jit(solution)/shard_map/ppermute | solution.py:30
  81.2 48.2 %collective-permute-start.8 = (bf16[576,512]{1,0:T(8,128)(2,1)}, bf16[576,512]{1,0:T(8,128)(2,1)}, u32[]{:S(2)}, u32[]{:S(2)}) collective-permute-start(bf16[576,512]{1,0:T(8,128)(2,1)} %fusion.6.own_0), channel_id=1, source_target_pairs={{0,16},{16,32},{32,48},{48,0},{64,80},{80,96},{96,112},{112,64},{1... | collective-permute-start | bytes 1769480 | tf_op jit(solution)/shard_map/ppermute | solution.py:29
  82.4 48.8 %collective-permute-start.9 = (bf16[576,512]{1,0:T(8,128)(2,1)}, bf16[576,512]{1,0:T(8,128)(2,1)}, u32[]{:S(2)}, u32[]{:S(2)}) collective-permute-start(bf16[576,512]{1,0:T(8,128)(2,1)} %fusion.6.own_0), channel_id=1, source_target_pairs={{0,48},{16,0},{32,16},{48,32},{64,112},{80,64},{96,80},{112,96},{1... | collective-permute-start | bytes 1769480 | tf_op jit(solution)/shard_map/ppermute | solution.py:30
  152.4 56.4 %copy-start.13 = (bf16[1152,512]{1,0:T(8,128)(2,1)}, bf16[1152,512]{1,0:T(8,128)(2,1)S(1)}, u32[]{:S(2)}) copy-start(bf16[1152,512]{1,0:T(8,128)(2,1)S(1)} %constant_dynamic-update-slice_fusion.6.near_0) | copy-start | bytes 3538948
  152.4 37.7 %collective-permute-start.12 = (bf16[1152,512]{1,0:T(8,128)(2,1)S(1)}, bf16[1152,512]{1,0:T(8,128)(2,1)S(1)}, u32[]{:S(2)}, u32[]{:S(2)}) collective-permute-start(bf16[1152,512]{1,0:T(8,128)(2,1)S(1)} %constant_dynamic-update-slice_fusion.6.near_0), channel_id=1, source_target_pairs={{0,16},{16,32},{32,48},{48,0},{64,80},{80,96},{96,112},{112,64},{1... | collective-permute-start | bytes 3538952 | tf_op jit(solution)/shard_map/ppermute | solution.py:29
  152.5 38.6 %collective-permute-start.13 = (bf16[1152,512]{1,0:T(8,128)(2,1)S(1)}, bf16[1152,512]{1,0:T(8,128)(2,1)S(1)}, u32[]{:S(2)}, u32[]{:S(2)}) collective-permute-start(bf16[1152,512]{1,0:T(8,128)(2,1)S(1)} %constant_dynamic-update-slice_fusion.6.near_0), channel_id=1, source_target_pairs={{0,48},{16,0},{32,16},{48,32},{64,112},{80,64},{96,80},{112,96},{1... | collective-permute-start | bytes 3538952 | tf_op jit(solution)/shard_map/ppermute | solution.py:30
  156.2 30.0 %collective-permute-start.16 = (bf16[288,512]{1,0:T(8,128)(2,1)S(1)}, bf16[288,512]{1,0:T(8,128)(2,1)S(1)}, u32[]{:S(2)}, u32[]{:S(2)}) collective-permute-start(bf16[288,512]{1,0:T(8,128)(2,1)S(1)} %slice.80), channel_id=1, source_target_pairs={{0,64},{16,80},{32,96},{48,112},{64,128},{80,144},{96,160},{112,17... | collective-permute-start | bytes 884744 | tf_op jit(solution)/shard_map/ppermute | solution.py:31
  160.5 25.7 %collective-permute-start.17 = (bf16[288,512]{1,0:T(8,128)(2,1)S(1)}, bf16[288,512]{1,0:T(8,128)(2,1)S(1)}, u32[]{:S(2)}, u32[]{:S(2)}) collective-permute-start(bf16[288,512]{1,0:T(8,128)(2,1)S(1)} %slice.81), channel_id=1, source_target_pairs={{0,192},{16,208},{32,224},{48,240},{64,0},{80,16},{96,32},{112,48}... | collective-permute-start | bytes 884744 | tf_op jit(solution)/shard_map/ppermute | solution.py:32
  186.3 19.3 %copy-start.5 = (bf16[576,512]{1,0:T(8,128)(2,1)}, bf16[576,512]{1,0:T(8,128)(2,1)S(1)}, u32[]{:S(2)}) copy-start(bf16[576,512]{1,0:T(8,128)(2,1)S(1)} %constant_dynamic-update-slice_fusion.8.last_0) | copy-start | bytes 1769476
  186.3 15.5 %collective-permute-start.18 = (bf16[576,512]{1,0:T(8,128)(2,1)S(1)}, bf16[576,512]{1,0:T(8,128)(2,1)S(1)}, u32[]{:S(2)}, u32[]{:S(2)}) collective-permute-start(bf16[576,512]{1,0:T(8,128)(2,1)S(1)} %constant_dynamic-update-slice_fusion.8.last_0), channel_id=1, source_target_pairs={{0,16},{16,32},{32,48},{48,0},{64,80},{80,96},{96,112},{112,64},{1... | collective-permute-start | bytes 1769480 | tf_op jit(solution)/shard_map/ppermute | solution.py:29
  186.4 17.0 %collective-permute-start.19 = (bf16[576,512]{1,0:T(8,128)(2,1)S(1)}, bf16[576,512]{1,0:T(8,128)(2,1)S(1)}, u32[]{:S(2)}, u32[]{:S(2)}) collective-permute-start(bf16[576,512]{1,0:T(8,128)(2,1)S(1)} %constant_dynamic-update-slice_fusion.8.last_0), channel_id=1, source_target_pairs={{0,48},{16,0},{32,16},{48,32},{64,112},{80,64},{96,80},{112,96},{1... | collective-permute-start | bytes 1769480 | tf_op jit(solution)/shard_map/ppermute | solution.py:30
  190.0 18.0 %collective-permute-start.10 = (bf16[288,512]{1,0:T(8,128)(2,1)S(1)}, bf16[288,512]{1,0:T(8,128)(2,1)S(1)}, u32[]{:S(2)}, u32[]{:S(2)}) collective-permute-start(bf16[288,512]{1,0:T(8,128)(2,1)S(1)} %slice.76), channel_id=1, source_target_pairs={{0,16},{16,32},{32,48},{48,0},{64,80},{80,96},{96,112},{112,64},{1... | collective-permute-start | bytes 884744 | tf_op jit(solution)/shard_map/ppermute | solution.py:31
  190.1 17.9 %copy-start.11 = (bf16[1152,512]{1,0:T(8,128)(2,1)}, bf16[1152,512]{1,0:T(8,128)(2,1)S(1)}, u32[]{:S(2)}) copy-start(bf16[1152,512]{1,0:T(8,128)(2,1)S(1)} %collective-permute-done.12.near_1) | copy-start | bytes 3538948
  191.1 36.1 %collective-permute-start.14 = (bf16[576,512]{1,0:T(8,128)(2,1)}, bf16[576,512]{1,0:T(8,128)(2,1)}, u32[]{:S(2)}, u32[]{:S(2)}) collective-permute-start(bf16[576,512]{1,0:T(8,128)(2,1)} %slice.78), channel_id=1, source_target_pairs={{0,16},{16,32},{32,48},{48,0},{64,80},{80,96},{96,112},{112,64},{1... | collective-permute-start | bytes 1769480 | tf_op jit(solution)/shard_map/ppermute | solution.py:31
  191.1 17.7 %copy-start.12 = (bf16[1152,512]{1,0:T(8,128)(2,1)}, bf16[1152,512]{1,0:T(8,128)(2,1)S(1)}, u32[]{:S(2)}) copy-start(bf16[1152,512]{1,0:T(8,128)(2,1)S(1)} %collective-permute-done.13.near_2) | copy-start | bytes 3538948
  192.0 35.1 %collective-permute-start.15 = (bf16[576,512]{1,0:T(8,128)(2,1)}, bf16[576,512]{1,0:T(8,128)(2,1)}, u32[]{:S(2)}, u32[]{:S(2)}) collective-permute-start(bf16[576,512]{1,0:T(8,128)(2,1)} %slice.79), channel_id=1, source_target_pairs={{0,48},{16,0},{32,16},{48,32},{64,112},{80,64},{96,80},{112,96},{1... | collective-permute-start | bytes 1769480 | tf_op jit(solution)/shard_map/ppermute | solution.py:32
  201.7 18.0 %collective-permute-start.11 = (bf16[288,512]{1,0:T(8,128)(2,1)}, bf16[288,512]{1,0:T(8,128)(2,1)}, u32[]{:S(2)}, u32[]{:S(2)}) collective-permute-start(bf16[288,512]{1,0:T(8,128)(2,1)} %slice.77), channel_id=1, source_target_pairs={{0,48},{16,0},{32,16},{48,32},{64,112},{80,64},{96,80},{112,96},{1... | collective-permute-start | bytes 884744 | tf_op jit(solution)/shard_map/ppermute | solution.py:32
  202.5 0.8 copy-start.1
  203.3 23.8 %collective-permute-start.20 = (bf16[288,512]{1,0:T(8,128)(2,1)}, bf16[288,512]{1,0:T(8,128)(2,1)}, u32[]{:S(2)}, u32[]{:S(2)}) collective-permute-start(bf16[288,512]{1,0:T(8,128)(2,1)} %slice.82), channel_id=1, source_target_pairs={{0,16},{16,32},{32,48},{48,0},{64,80},{80,96},{96,112},{112,64},{1... | collective-permute-start | bytes 884744 | tf_op jit(solution)/shard_map/ppermute | solution.py:31
  205.6 0.8 copy-start.3
  208.1 0.7 copy-start.7
  208.8 18.3 %collective-permute-start.21 = (bf16[288,512]{1,0:T(8,128)(2,1)}, bf16[288,512]{1,0:T(8,128)(2,1)}, u32[]{:S(2)}, u32[]{:S(2)}) collective-permute-start(bf16[288,512]{1,0:T(8,128)(2,1)} %slice.83), channel_id=1, source_target_pairs={{0,48},{16,0},{32,16},{48,32},{64,112},{80,64},{96,80},{112,96},{1... | collective-permute-start | bytes 884744 | tf_op jit(solution)/shard_map/ppermute | solution.py:32
  227.2 1.1 copy-start.2
  228.2 1.1 copy-start.4
  229.3 1.1 copy-start.6
  230.4 1.0 copy-start.8
Sparse Core Ops, SparseCore 0:
  17.6 109.7 all-gather.4
  150.3 63.9 all-gather.6

commit v5 on v4

--- a/solution.py
+++ b/solution.py
@@ -89,8 +89,10 @@
 
     first = pl.multiple_of(slot[n] * 32, 32)
     for k, (ref, row) in enumerate(blocks):
-        start = pl.multiple_of(place[k] * 32, 32)
-        grads[pl.ds(start, 32), :] = ref[pl.ds(row + first, 32), :]
+        start = pl.multiple_of(place[k] * 16, 16)
+        rows = ref[pl.ds(row + first, 32), :]
+        grads[pl.ds(start, 16), :] = rows[:16]
+        grads[256 + 16 * k : 256 + 16 * k + 16, :] = rows[16:]
     pair = jnp.dot(ein[0], grads[...], preferred_element_type=F32)[:, :dj]
     scaled = (pair * inverse[...]).astype(BF16)
     width = scaled.shape[1]
@@ -155,8 +157,12 @@
     row_major = Layout(major_to_minor=(0, 1))
 
     rows_all = lax.all_gather(
-        jnp.concatenate([train_in[0], corner(jnp.sum(eigvals), (32, 128))], 1), "shard", axis=0
-    )
+        jnp.concatenate([train_in[0, :16], corner(jnp.sum(eigvals), (16, 128))], 1),
+        "shard",
+        axis=0,
+    )
+    rows_ring = jnp.concatenate(ring4(train_in[0, 16:], "shard", SHARD_Z, 8), 0)
+    rows_ring = jnp.concatenate(ring4(rows_ring, "shard", SHARD_Y, 32), 0)
 
     block = jnp.concatenate([train_grad[0], lax.ppermute(train_grad[0], "example", EXAMPLE_Z)], 0)
     block = jnp.concatenate(ring4(block, "example", EXAMPLE_X, 32), 0)
@@ -179,16 +185,25 @@
         + ring4(last, "shard", SHARD_Y, 288)
     )
 
-    flag = jnp.isnan(sum(b[0, 0] for b in z_blocks[1:3] + blocks[1:3]))
-    own_in = jnp.dot(rows_all[:, :, :D].reshape(SEQLEN, D), basis_in, preferred_element_type=F32)
-    token = jnp.arange(SEQLEN, dtype=jnp.int32)[:, None]
-    live = jnp.where(flag, 0, seq_lens[0])
-    own_in = jnp.where(token < live, own_in, 0.0).astype(BF16)
+    own_in = jnp.concatenate(
+        [
+            jnp.dot(rows, basis_in, preferred_element_type=F32)
+            for rows in (rows_all[:, :, :D].reshape(256, D), rows_ring)
+        ],
+        0,
+    )
+    half = jnp.arange(16, dtype=jnp.int32)
+    token = jnp.concatenate(
+        [(half[:, None] * 32 + half).reshape(256), (place[:, None] * 32 + 16 + half).reshape(256)]
+    )
+    own_in = jnp.where(token[:, None] < seq_lens[0], own_in, 0.0).astype(BF16)
     query_left = jnp.dot(
         query_in.reshape(64, D), basis_in, preferred_element_type=F32
     ).astype(BF16)
     eig_shard = corner(jnp.sum(rows_all[:, :, D:].astype(F32)), (di, 64))
     ein = jnp.concatenate([own_in.T, query_left.T, eig_shard], 1)
+    flag = jnp.isnan(sum(b[0, 0] for b in z_blocks[1:3] + blocks[1:3]))
+    ein = jnp.where(flag, jnp.zeros_like(ein), ein)
     ein = lax.all_gather(ein, "example", axis=0)
 
     partial = score_call(place, slot, ein, blocks, eigvals)[:, :NSEQ]

time: 288 us -> 284 us (0.986)
  waiting for transfers between devices: 104 us -> 78.5 us
  starting transfers between devices: 40.9 us -> 57.4 us
  local copies, waits for them, and re-layouts: 37.4 us -> 41.1 us
    ppermute x5 -> x7, waiting for transfers between devices: 54.2 us -> 34.4 us  [ring4(): below = lax.ppermute(block, axis, steps[1])]
    ppermute x1, starting transfers between devices: 3.18 us -> 13.7 us  [shards(): other = lax.ppermute(block, 'example', EXAMPLE_CORE)]
    unnamed x35 -> x78, local copies, waits for them, and re-layouts: 14 us -> 21.4 us
    ppermute x5 -> x7, starting transfers between devices: 10.4 us -> 16 us  [ring4(): above = lax.ppermute(block, axis, steps[-1])]
    ppermute x5 -> x7, starting transfers between devices: 5.38 us -> 10.4 us  [ring4(): far_top = lax.ppermute(below[:cut], axis, steps[1])]
    ppermute x5 -> x7, waiting for transfers between devices: 5.08 us -> 0.27 us  [ring4(): above = lax.ppermute(block, axis, steps[-1])]
    ppermute x5 -> x7, starting transfers between devices: 12.6 us -> 7.89 us  [ring4(): far_bottom = lax.ppermute(above[cut:], axis, steps[-1])]
    dot_general x1, matrix products: 2.48 us -> 5.52 us  [shards(): jnp.dot(query_out.reshape(64, H), basis_out, preferred_element_type=F32)]
  transfers between devices with their start and end apart: 24 -> 32, of which waited for: 10 -> 12; matrix products, arithmetic and copies ran while one was open for 17% -> 19% of each run, Pallas kernels for 0% -> 0%
where the time goes in v5:
time: 284 us; the launch traced here: 283 us
  waiting for transfers between devices  78.5 us (28%)
  starting transfers between devices  57.4 us (20%)
  local copies, waits for them, and re-layouts  41.1 us (14%)
  between operations  24.3 us (9%)
  blocking collectives  23.9 us (8%)
  Pallas kernels  22.5 us (8%)
  matrix products  22.4 us (8%)
  other arithmetic  12.7 us (4%)
    ppermute x7, waiting for transfers between devices, ring4(): below = lax.ppermute(block, axis, steps[1])  34.4 us
    ppermute x7, waiting for transfers between devices, ring4(): far_top = lax.ppermute(below[:cut], axis, steps[1])  31.2 us
    all_to_all x1, blocking collectives, shards(): pieces = lax.all_to_all(pieces, ('shard', 'example'), 0, 0, tiled=True)  23.9 us
    pallas_call x1, Pallas kernels, score_call(): pl.pallas_call(score_kernel, grid=(NSEQ,), in_specs=[pl.BlockSpec(memory_...  22.5 us
    unnamed x78, local copies, waits for them, and re-layouts  21.4 us
    ppermute x7, starting transfers between devices, ring4(): above = lax.ppermute(block, axis, steps[-1])  16 us
    ppermute x1, starting transfers between devices, shards(): other = lax.ppermute(block, 'example', EXAMPLE_CORE)  13.7 us
    ppermute x7, waiting for transfers between devices, ring4(): far_bottom = lax.ppermute(above[cut:], axis, steps[-1])  12.5 us
  transfers between devices with their start and end apart: 32, of which 12 were waited for; matrix products, arithmetic and copies ran while one was open for 19% of the time, Pallas kernels for 0%

profile of v5, /device:TPU:1, one launch (start us, length us, event | category | flops | bytes accessed | tf_op | source)
XLA Modules:
  0.0 282.9 jit_solution(3530134341898652354)
XLA Ops:
  6.5 1.8 slice_bitcast_fusion
  8.4 3.8 %collective-permute-start.10 = (bf16[16,5120]{1,0:T(8,128)(2,1)}, bf16[16,5120]{1,0:T(8,128)(2,1)}, u32[]{:S(2)}, u32[]{:S(2)}) collective-permute-start(bf16[16,5120]{1,0:T(8,128)(2,1)} %get-tuple-element.7), channel_id=1, source_target_pairs={{0,64},{16,80},{32,96},{48,112},{64,128},{80,144},{96,160},{112,17... | collective-permute-start | bytes 491528 | tf_op jit(solution)/shard_map/ppermute | solution.py:29
  12.2 3.0 %collective-permute-start.11 = (bf16[16,5120]{1,0:T(8,128)(2,1)}, bf16[16,5120]{1,0:T(8,128)(2,1)}, u32[]{:S(2)}, u32[]{:S(2)}) collective-permute-start(bf16[16,5120]{1,0:T(8,128)(2,1)} %get-tuple-element.7), channel_id=1, source_target_pairs={{0,192},{16,208},{32,224},{48,240},{64,0},{80,16},{96,32},{112,48}... | collective-permute-start | bytes 491528 | tf_op jit(solution)/shard_map/ppermute | solution.py:30
  15.2 1.9 reduce_sum.27
  20.8 1.3 select_convert_fusion.1
  23.7 1.7 constant_dynamic-update-slice_fusion.10
  25.3 1.8 constant_dynamic-update-slice_fusion.5
  28.3 5.5 %convolution_convert_fusion.3 = bf16[64,432]{1,0:T(8,128)(2,1)} fusion(bf16[64,6912]{1,0:T(8,128)(2,1)} %bitcast.69, bf16[6912,432]{0,1:T(8,128)(2,1)} %param.12), kind=kOutput, calls=%fused_computation.7 | convolution fusion | flops 382233600 | bytes 6912000 | tf_op jit(solution)/shard_map/dot_general | solution.py:170
  33.8 1.6 fusion.3
  36.9 1.2 collective-permute-start.12
  39.0 2.4 collective-permute-start.13
  41.4 0.9 constant_dynamic-update-slice_fusion.9
  42.4 0.9 constant_dynamic-update-slice_fusion.8
  43.3 1.9 collective-permute-done.12
  45.2 1.1 pad_maximum_fusion
  46.3 2.5 collective-permute-start.1
  49.3 2.0 collective-permute-start.14
  51.4 0.9 collective-permute-start.15
  52.3 1.8 constant_dynamic-update-slice_fusion.4
  54.1 9.5 %collective-permute-done.14 = bf16[64,5120]{1,0:T(8,128)(2,1)S(1)} collective-permute-done((bf16[64,5120]{1,0:T(8,128)(2,1)S(1)}, bf16[64,5120]{1,0:T(8,128)(2,1)S(1)}, u32[]{:S(2)}, u32[]{:S(2)}) %collective-permute-start.14) | collective-permute-done | bytes 655392 | tf_op jit(solution)/shard_map/ppermute | solution.py:29
  63.6 2.3 collective-permute-start.16
  66.5 3.4 %collective-permute-start.3 = (bf16[32,6912]{1,0:T(8,128)(2,1)S(1)}, bf16[32,6912]{1,0:T(8,128)(2,1)S(1)}, u32[]{:S(2)}, u32[]{:S(2)}) collective-permute-start(bf16[32,6912]{1,0:T(8,128)(2,1)S(1)} %slice.92), channel_id=1, source_target_pairs={{0,2},{1,3},{2,4},{3,5},{4,6},{5,7},{6,0},{7,1},{8,10},{9,11},{10,... | collective-permute-start | bytes 1327112 | tf_op jit(solution)/shard_map/ppermute | solution.py:31
  70.3 1.0 constant_dynamic-update-slice_fusion.3
  71.3 1.0 constant_dynamic-update-slice_fusion.2
  72.3 3.1 %collective-permute-done.3 = bf16[32,6912]{1,0:T(8,128)(2,1)S(1)} collective-permute-done((bf16[32,6912]{1,0:T(8,128)(2,1)S(1)}, bf16[32,6912]{1,0:T(8,128)(2,1)S(1)}, u32[]{:S(2)}, u32[]{:S(2)}) %collective-permute-start.3) | collective-permute-done | bytes 442400 | tf_op jit(solution)/shard_map/ppermute | solution.py:31
  76.2 1.6 collective-permute-done.4
  78.6 13.7 %collective-permute-start.5 = (bf16[256,6912]{1,0:T(8,128)(2,1)}, bf16[256,6912]{1,0:T(8,128)(2,1)}, u32[]{:S(2)}, u32[]{:S(2)}) collective-permute-start(bf16[256,6912]{1,0:T(8,128)(2,1)} %constant_dynamic-update-slice_fusion), channel_id=1, source_target_pairs={{0,1},{1,0},{2,3},{3,2},{4,5},{5,4},{6,7},{7,6},{8,9},{9,8},{10,11... | collective-permute-start | bytes 10616840 | tf_op jit(solution)/shard_map/ppermute | solution.py:169
  92.4 1.8 fusion.15
  94.2 4.4 %convolution_convert_fusion.1 = bf16[256,432]{0,1:T(8,128)(2,1)} fusion(bf16[256,6912]{1,0:T(8,128)(2,1)} %constant_dynamic-update-slice_fusion, bf16[6912,432]{0,1:T(8,128)(2,1)S(1)} %bitcast.63), kind=kOutput, calls=%fused_computation.1 | convolution fusion | flops 1528934400 | bytes 9732096 | tf_op jit(solution)/shard_map/dot_general | solution.py:174
  98.6 1.1 copy.21
  99.7 3.5 %slice.98 = bf16[16,16,5120]{2,1,0:T(8,128)(2,1)} slice(bf16[16,16,5248]{2,1,0:T(8,128)(2,1)} %bitcast.64), slice={[0:16], [0:16], [0:5120]} | slice | bytes 5242880 | tf_op jit(solution)/shard_map/slice | solution.py:191
  103.3 1.5 convert_reduce_fusion
  108.3 2.7 fusion.8
  110.9 6.2 %convolution_convert_fusion = bf16[256,432]{0,1:T(8,128)(2,1)} fusion(bf16[256,6912]{1,0:T(8,128)(2,1)} %collective-permute-done.5, bf16[6912,432]{0,1:T(8,128)(2,1)} %param.12), kind=kOutput, calls=%fused_computation | convolution fusion | flops 1528934400 | bytes 9732096 | tf_op jit(solution)/shard_map/dot_general | solution.py:174
  117.1 1.8 copy.22
  118.9 1.1 fusion.6.own_0
  120.1 3.6 %collective-permute-start.7 = (bf16[576,512]{1,0:T(8,128)(2,1)S(1)}, bf16[576,512]{1,0:T(8,128)(2,1)S(1)}, u32[]{:S(2)}, u32[]{:S(2)}) collective-permute-start(bf16[576,512]{1,0:T(8,128)(2,1)S(1)} %fusion.6.own_0), channel_id=1, source_target_pairs={{0,192},{16,208},{32,224},{48,240},{64,0},{80,16},{96,32},{112,48}... | collective-permute-start | bytes 1769480 | tf_op jit(solution)/shard_map/ppermute | solution.py:30
  123.7 2.7 collective-permute-start.9
  126.4 2.8 %fusion.14 = bf16[256,320]{0,1:T(8,128)(2,1)S(1)} fusion(bf16[256,5120]{1,0:T(8,128)(2,1)} %bitcast.66, bf16[5120,320]{0,1:T(8,128)(2,1)S(1)} %copy-done), kind=kOutput, calls=%fused_computation.81 | convolution fusion | flops 838860800 | bytes 6062080 | tf_op jit(solution)/shard_map/dot_general | solution.py:190
  129.3 16.8 %collective-permute-done.6 = bf16[576,512]{1,0:T(8,128)(2,1)S(1)} collective-permute-done((bf16[576,512]{1,0:T(8,128)(2,1)S(1)}, bf16[576,512]{1,0:T(8,128)(2,1)S(1)}, u32[]{:S(2)}, u32[]{:S(2)}) %collective-permute-start.6) | collective-permute-done | bytes 589856 | tf_op jit(solution)/shard_map/ppermute | solution.py:29
  152.5 1.2 constant_dynamic-update-slice_fusion.21
  153.7 1.1 constant_dynamic-update-slice_fusion.20.near_0
  154.9 2.7 collective-permute-start.21
  157.5 1.0 slice.108
  158.5 1.9 collective-permute-start.24
  160.5 2.0 collective-permute-start.25
  162.5 17.1 %collective-permute-done.24 = bf16[288,512]{1,0:T(8,128)(2,1)S(1)} collective-permute-done((bf16[288,512]{1,0:T(8,128)(2,1)S(1)}, bf16[288,512]{1,0:T(8,128)(2,1)S(1)}, u32[]{:S(2)}, u32[]{:S(2)}) %collective-permute-start.24) | collective-permute-done | bytes 294944 | tf_op jit(solution)/shard_map/ppermute | solution.py:31
  179.8 2.7 collective-permute-start.27
  184.1 0.9 slice.107
  185.0 2.7 collective-permute-start.23
  188.4 7.5 %collective-permute-done.26.last_1 = bf16[576,512]{1,0:T(8,128)(2,1)S(1)} collective-permute-done((bf16[576,512]{1,0:T(8,128)(2,1)S(1)}, bf16[576,512]{1,0:T(8,128)(2,1)S(1)}, u32[]{:S(2)}, u32[]{:S(2)}) %collective-permute-start.26) | collective-permute-done | bytes 589856 | tf_op jit(solution)/shard_map/ppermute | solution.py:29
  197.5 1.5 collective-permute-start.28
  200.5 1.7 collective-permute-done.18.own_top
  203.0 10.9 %collective-permute-done.19.own_bottom = bf16[288,512]{1,0:T(8,128)(2,1)} collective-permute-done((bf16[288,512]{1,0:T(8,128)(2,1)}, bf16[288,512]{1,0:T(8,128)(2,1)}, u32[]{:S(2)}, u32[]{:S(2)}) %collective-permute-start.19) | collective-permute-done | bytes 294944 | tf_op jit(solution)/shard_map/ppermute | solution.py:32
  213.9 7.4 %collective-permute-done.28.last_top = bf16[288,512]{1,0:T(8,128)(2,1)} collective-permute-done((bf16[288,512]{1,0:T(8,128)(2,1)}, bf16[288,512]{1,0:T(8,128)(2,1)}, u32[]{:S(2)}, u32[]{:S(2)}) %collective-permute-start.28) | collective-permute-done | bytes 294944 | tf_op jit(solution)/shard_map/ppermute | solution.py:31
  221.3 1.1 copy-done.2
  222.4 1.1 copy-done.5
  223.5 1.1 copy-done.8
  224.5 1.1 copy-done.10
  225.6 1.1 copy-done.12
  226.7 1.1 copy-done.14
  227.7 1.0 copy-done.16
  228.7 22.5 %shard_map.82 = f32[32,128]{1,0:T(8,128)S(1)} custom-call(s32[16]{0:T(128)S(1)} %stack.67.place, s32[16]{0:T(128)S(1)} %fusion.9.slot, bf16[16,320,640]{2,1,0:T(8,128)(2,1)} %all-gather.4.cloned.1.call-done.ein.ql, bf16[16,320,640]{2,1,0:T(8,128)(2,1)} %all-gather.4.cloned.1.call-done.ein.ql, bf16[576,512]{1,0:T(8,128)(2,1)S(1)} %copy-done.2, ...), custom_call_target="tpu_custom_call" | custom-call | flops 10000000000 | bytes 16000000 | tf_op jit(solution)/shard_map/pallas_call | solution.py:115
  251.4 23.9 %all_to_all.9 = f32[256,1,2]{2,1,0:T(1,128)S(1)} all-to-all(f32[256,1,2]{2,1,0:T(1,128)S(1)} %bitcast.70), channel_id=1, replica_groups=mesh['shard'=16,'example'=16] {'shard','example'}, dimensions={0} | all-to-all | bytes 4096 | tf_op jit(solution)/shard_map/all_to_all | solution.py:211
  (143 shorter events, 18.9 us)
Async XLA Ops:
  6.5 27.2 %copy-start = (bf16[5120,320]{0,1:T(8,128)(2,1)S(1)}, bf16[5120,320]{0,1:T(8,128)(2,1)}, u32[]{:S(2)}) copy-start(bf16[5120,320]{0,1:T(8,128)(2,1)} %param.11) | copy-start | bytes 9830404
  6.5 93.2 %all-gather.6.cloned.1.call-start = ((), (), s32[]{:S(2)}) async-start(), calls=%async_computation.2 | async-start | bytes 2854912 | tf_op jit(solution)/shard_map/all_gather | solution.py:159
  8.4 27.7 %collective-permute-start.10 = (bf16[16,5120]{1,0:T(8,128)(2,1)}, bf16[16,5120]{1,0:T(8,128)(2,1)}, u32[]{:S(2)}, u32[]{:S(2)}) collective-permute-start(bf16[16,5120]{1,0:T(8,128)(2,1)} %get-tuple-element.7), channel_id=1, source_target_pairs={{0,64},{16,80},{32,96},{48,112},{64,128},{80,144},{96,160},{112,17... | collective-permute-start | bytes 491528 | tf_op jit(solution)/shard_map/ppermute | solution.py:29
  12.2 25.9 %collective-permute-start.11 = (bf16[16,5120]{1,0:T(8,128)(2,1)}, bf16[16,5120]{1,0:T(8,128)(2,1)}, u32[]{:S(2)}, u32[]{:S(2)}) collective-permute-start(bf16[16,5120]{1,0:T(8,128)(2,1)} %get-tuple-element.7), channel_id=1, source_target_pairs={{0,192},{16,208},{32,224},{48,240},{64,0},{80,16},{96,32},{112,48}... | collective-permute-start | bytes 491528 | tf_op jit(solution)/shard_map/ppermute | solution.py:30
  22.8 198.5 %all-gather.4.cloned.1.call-start = ((), (), s32[]{:S(2)}) async-start(), calls=%async_computation.1 | async-start | bytes 6963200 | tf_op jit(solution)/shard_map/all_gather | solution.py:207
  22.9 22.3 %collective-permute-start = (bf16[32,6912]{1,0:T(8,128)(2,1)}, bf16[32,6912]{1,0:T(8,128)(2,1)}, u32[]{:S(2)}, u32[]{:S(2)}) collective-permute-start(bf16[32,6912]{1,0:T(8,128)(2,1)} %bitcast.67), channel_id=1, source_target_pairs={{0,8},{1,9},{2,10},{3,11},{4,12},{5,13},{6,14},{7,15},{8,0},{9,1},... | collective-permute-start | bytes 1327112 | tf_op jit(solution)/shard_map/ppermute | solution.py:167
  28.2 5.5 %copy-start.29 = (bf16[2,32,5120]{2,1,0:T(8,128)(2,1)S(1)}, bf16[2,32,5120]{2,1,0:T(8,128)(2,1)}, u32[]{:S(2)}) copy-start(bf16[2,32,5120]{2,1,0:T(8,128)(2,1)} %param.14) | copy-start | bytes 1966084
  33.8 7.6 %copy-start.27 = (bf16[64,5120]{1,0:T(8,128)(2,1)S(1)}, bf16[64,5120]{1,0:T(8,128)(2,1)}, u32[]{:S(2)}) copy-start(bf16[64,5120]{1,0:T(8,128)(2,1)} %get-tuple-element.5) | copy-start | bytes 1966084
  33.8 7.6 %copy-start.28 = (bf16[256,5120]{1,0:T(8,128)(2,1)S(1)}, bf16[256,5120]{1,0:T(8,128)(2,1)}, u32[]{:S(2)}) copy-start(bf16[256,5120]{1,0:T(8,128)(2,1)} %get-tuple-element.6) | copy-start | bytes 7864324
  33.8 11.4 %copy-start.17 = (bf16[1,32,6912]{2,1,0:T(8,128)(2,1)S(1)}, bf16[1,32,6912]{2,1,0:T(8,128)(2,1)}, u32[]{:S(2)}) copy-start(bf16[1,32,6912]{2,1,0:T(8,128)(2,1)} %param.9) | copy-start | bytes 1327108
  36.9 8.2 %collective-permute-start.12 = (bf16[8,5120]{1,0:T(8,128)(2,1)S(1)}, bf16[8,5120]{1,0:T(8,128)(2,1)S(1)}, u32[]{:S(2)}, u32[]{:S(2)}) collective-permute-start(bf16[8,5120]{1,0:T(8,128)(2,1)S(1)} %slice.99), channel_id=1, source_target_pairs={{0,64},{16,80},{32,96},{48,112},{64,128},{80,144},{96,160},{112,17... | collective-permute-start | bytes 245768 | tf_op jit(solution)/shard_map/ppermute | solution.py:31
  39.0 10.3 %collective-permute-start.13 = (bf16[8,5120]{1,0:T(8,128)(2,1)S(1)}, bf16[8,5120]{1,0:T(8,128)(2,1)S(1)}, u32[]{:S(2)}, u32[]{:S(2)}) collective-permute-start(bf16[8,5120]{1,0:T(8,128)(2,1)S(1)} %slice.100), channel_id=1, source_target_pairs={{0,192},{16,208},{32,224},{48,240},{64,0},{80,16},{96,32},{112,48}... | collective-permute-start | bytes 245768 | tf_op jit(solution)/shard_map/ppermute | solution.py:32
  46.3 20.2 %collective-permute-start.1 = (bf16[64,6912]{1,0:T(8,128)(2,1)S(1)}, bf16[64,6912]{1,0:T(8,128)(2,1)S(1)}, u32[]{:S(2)}, u32[]{:S(2)}) collective-permute-start(bf16[64,6912]{1,0:T(8,128)(2,1)S(1)} %pad_maximum_fusion), channel_id=1, source_target_pairs={{0,2},{1,3},{2,4},{3,5},{4,6},{5,7},{6,0},{7,1},{8,10},{9,11},{10,... | collective-permute-start | bytes 2654216 | tf_op jit(solution)/shard_map/ppermute | solution.py:29
  48.8 21.2 %collective-permute-start.2 = (bf16[64,6912]{1,0:T(8,128)(2,1)S(1)}, bf16[64,6912]{1,0:T(8,128)(2,1)S(1)}, u32[]{:S(2)}, u32[]{:S(2)}) collective-permute-start(bf16[64,6912]{1,0:T(8,128)(2,1)S(1)} %pad_maximum_fusion), channel_id=1, source_target_pairs={{0,6},{1,7},{2,0},{3,1},{4,2},{5,3},{6,4},{7,5},{8,14},{9,15},{10,... | collective-permute-start | bytes 2654216 | tf_op jit(solution)/shard_map/ppermute | solution.py:30
  49.3 14.3 %collective-permute-start.14 = (bf16[64,5120]{1,0:T(8,128)(2,1)S(1)}, bf16[64,5120]{1,0:T(8,128)(2,1)S(1)}, u32[]{:S(2)}, u32[]{:S(2)}) collective-permute-start(bf16[64,5120]{1,0:T(8,128)(2,1)S(1)} %get-tuple-element.13), channel_id=1, source_target_pairs={{0,16},{16,32},{32,48},{48,0},{64,80},{80,96},{96,112},{112,64},{1... | collective-permute-start | bytes 1966088 | tf_op jit(solution)/shard_map/ppermute | solution.py:29
  51.4 14.6 %collective-permute-start.15 = (bf16[64,5120]{1,0:T(8,128)(2,1)S(1)}, bf16[64,5120]{1,0:T(8,128)(2,1)S(1)}, u32[]{:S(2)}, u32[]{:S(2)}) collective-permute-start(bf16[64,5120]{1,0:T(8,128)(2,1)S(1)} %get-tuple-element.13), channel_id=1, source_target_pairs={{0,48},{16,0},{32,16},{48,32},{64,112},{80,64},{96,80},{112,96},{1... | collective-permute-start | bytes 1966088 | tf_op jit(solution)/shard_map/ppermute | solution.py:30
  63.6 28.7 %collective-permute-start.16 = (bf16[32,5120]{1,0:T(8,128)(2,1)S(1)}, bf16[32,5120]{1,0:T(8,128)(2,1)S(1)}, u32[]{:S(2)}, u32[]{:S(2)}) collective-permute-start(bf16[32,5120]{1,0:T(8,128)(2,1)S(1)} %slice.101), channel_id=1, source_target_pairs={{0,16},{16,32},{32,48},{48,0},{64,80},{80,96},{96,112},{112,64},{1... | collective-permute-start | bytes 983048 | tf_op jit(solution)/shard_map/ppermute | solution.py:31
  66.0 26.4 %collective-permute-start.17 = (bf16[32,5120]{1,0:T(8,128)(2,1)S(1)}, bf16[32,5120]{1,0:T(8,128)(2,1)S(1)}, u32[]{:S(2)}, u32[]{:S(2)}) collective-permute-start(bf16[32,5120]{1,0:T(8,128)(2,1)S(1)} %slice.102), channel_id=1, source_target_pairs={{0,48},{16,0},{32,16},{48,32},{64,112},{80,64},{96,80},{112,96},{1... | collective-permute-start | bytes 983048 | tf_op jit(solution)/shard_map/ppermute | solution.py:32
  66.5 8.8 %collective-permute-start.3 = (bf16[32,6912]{1,0:T(8,128)(2,1)S(1)}, bf16[32,6912]{1,0:T(8,128)(2,1)S(1)}, u32[]{:S(2)}, u32[]{:S(2)}) collective-permute-start(bf16[32,6912]{1,0:T(8,128)(2,1)S(1)} %slice.92), channel_id=1, source_target_pairs={{0,2},{1,3},{2,4},{3,5},{4,6},{5,7},{6,0},{7,1},{8,10},{9,11},{10,... | collective-permute-start | bytes 1327112 | tf_op jit(solution)/shard_map/ppermute | solution.py:31
  70.0 7.8 %collective-permute-start.4 = (bf16[32,6912]{1,0:T(8,128)(2,1)S(1)}, bf16[32,6912]{1,0:T(8,128)(2,1)S(1)}, u32[]{:S(2)}, u32[]{:S(2)}) collective-permute-start(bf16[32,6912]{1,0:T(8,128)(2,1)S(1)} %slice.93), channel_id=1, source_target_pairs={{0,6},{1,7},{2,0},{3,1},{4,2},{5,3},{6,4},{7,5},{8,14},{9,15},{10,... | collective-permute-start | bytes 1327112 | tf_op jit(solution)/shard_map/ppermute | solution.py:32
  70.2 24.0 %slice-start = ((s8[5971968]{0:T(1024)(128)(4,1)}), s8[4194304]{0:T(1024)(128)(4,1)S(1)}, s32[]{:S(2)}) async-start(s8[5971968]{0:T(1024)(128)(4,1)} %bitcast.62), calls=%async_computation.3 | async-start | bytes 8388608
  78.6 32.4 %collective-permute-start.5 = (bf16[256,6912]{1,0:T(8,128)(2,1)}, bf16[256,6912]{1,0:T(8,128)(2,1)}, u32[]{:S(2)}, u32[]{:S(2)}) collective-permute-start(bf16[256,6912]{1,0:T(8,128)(2,1)} %constant_dynamic-update-slice_fusion), channel_id=1, source_target_pairs={{0,1},{1,0},{2,3},{3,2},{4,5},{5,4},{6,7},{7,6},{8,9},{9,8},{10,11... | collective-permute-start | bytes 10616840 | tf_op jit(solution)/shard_map/ppermute | solution.py:169
  92.3 1.9 slice-start.1
  120.0 9.2 %copy-start.1 = (bf16[576,512]{1,0:T(8,128)(2,1)}, bf16[576,512]{1,0:T(8,128)(2,1)S(1)}, u32[]{:S(2)}) copy-start(bf16[576,512]{1,0:T(8,128)(2,1)S(1)} %fusion.6.own_0) | copy-start | bytes 1769476
  120.0 26.1 %collective-permute-start.6 = (bf16[576,512]{1,0:T(8,128)(2,1)S(1)}, bf16[576,512]{1,0:T(8,128)(2,1)S(1)}, u32[]{:S(2)}, u32[]{:S(2)}) collective-permute-start(bf16[576,512]{1,0:T(8,128)(2,1)S(1)} %fusion.6.own_0), channel_id=1, source_target_pairs={{0,64},{16,80},{32,96},{48,112},{64,128},{80,144},{96,160},{112,17... | collective-permute-start | bytes 1769480 | tf_op jit(solution)/shard_map/ppermute | solution.py:29
  120.1 26.8 %collective-permute-start.7 = (bf16[576,512]{1,0:T(8,128)(2,1)S(1)}, bf16[576,512]{1,0:T(8,128)(2,1)S(1)}, u32[]{:S(2)}, u32[]{:S(2)}) collective-permute-start(bf16[576,512]{1,0:T(8,128)(2,1)S(1)} %fusion.6.own_0), channel_id=1, source_target_pairs={{0,192},{16,208},{32,224},{48,240},{64,0},{80,16},{96,32},{112,48}... | collective-permute-start | bytes 1769480 | tf_op jit(solution)/shard_map/ppermute | solution.py:30
  123.7 25.1 %collective-permute-start.8 = (bf16[576,512]{1,0:T(8,128)(2,1)S(1)}, bf16[576,512]{1,0:T(8,128)(2,1)S(1)}, u32[]{:S(2)}, u32[]{:S(2)}) collective-permute-start(bf16[576,512]{1,0:T(8,128)(2,1)S(1)} %fusion.6.own_0), channel_id=1, source_target_pairs={{0,16},{16,32},{32,48},{48,0},{64,80},{80,96},{96,112},{112,64},{1... | collective-permute-start | bytes 1769480 | tf_op jit(solution)/shard_map/ppermute | solution.py:29
  123.7 26.3 %collective-permute-start.9 = (bf16[576,512]{1,0:T(8,128)(2,1)S(1)}, bf16[576,512]{1,0:T(8,128)(2,1)S(1)}, u32[]{:S(2)}, u32[]{:S(2)}) collective-permute-start(bf16[576,512]{1,0:T(8,128)(2,1)S(1)} %fusion.6.own_0), channel_id=1, source_target_pairs={{0,48},{16,0},{32,16},{48,32},{64,112},{80,64},{96,80},{112,96},{1... | collective-permute-start | bytes 1769480 | tf_op jit(solution)/shard_map/ppermute | solution.py:30
  126.4 2.9 %copy-start.25 = (bf16[256,320]{0,1:T(8,128)(2,1)S(1)}, bf16[256,320]{0,1:T(8,128)(2,1)}, u32[]{:S(2)}) copy-start(bf16[256,320]{0,1:T(8,128)(2,1)} %fusion.15) | copy-start | bytes 491524
  126.4 25.2 %copy-start.21 = (bf16[1,320,64]{2,1,0:T(8,128)(2,1)S(1)}, bf16[1,320,64]{2,1,0:T(8,128)(2,1)}, u32[]{:S(2)}) copy-start(bf16[1,320,64]{2,1,0:T(8,128)(2,1)} %fusion.8) | copy-start | bytes 122884
  126.4 25.2 %copy-start.26 = (bf16[1,320,64]{2,1,0:T(8,128)(2,1)S(1)}, bf16[1,320,64]{2,1,0:T(8,128)(2,1)}, u32[]{:S(2)}) copy-start(bf16[1,320,64]{2,1,0:T(8,128)(2,1)} %fusion.3) | copy-start | bytes 122884
  146.1 5.4 %copy-start.20 = (bf16[576,512]{1,0:T(8,128)(2,1)}, bf16[576,512]{1,0:T(8,128)(2,1)S(1)}, u32[]{:S(2)}) copy-start(bf16[576,512]{1,0:T(8,128)(2,1)S(1)} %collective-permute-done.6) | copy-start | bytes 1769476
  146.9 4.6 %copy-start.18 = (bf16[576,512]{1,0:T(8,128)(2,1)}, bf16[576,512]{1,0:T(8,128)(2,1)S(1)}, u32[]{:S(2)}) copy-start(bf16[576,512]{1,0:T(8,128)(2,1)S(1)} %collective-permute-done.7) | copy-start | bytes 1769476
  148.8 1.2 copy-start.3
  150.0 0.8 copy-start.6
  152.4 8.0 %copy-start.19 = (bf16[576,512]{1,0:T(8,128)(2,1)S(1)}, bf16[576,512]{1,0:T(8,128)(2,1)}, u32[]{:S(2)}) copy-start(bf16[576,512]{1,0:T(8,128)(2,1)} %copy-done.18) | copy-start | bytes 1769476
  152.5 30.0 %copy-start.4 = (bf16[576,512]{1,0:T(8,128)(2,1)S(1)}, bf16[576,512]{1,0:T(8,128)(2,1)}, u32[]{:S(2)}) copy-start(bf16[576,512]{1,0:T(8,128)(2,1)} %copy-done.3) | copy-start | bytes 1769476
  154.8 30.2 %copy-start.24 = (bf16[1152,512]{1,0:T(8,128)(2,1)}, bf16[1152,512]{1,0:T(8,128)(2,1)S(1)}, u32[]{:S(2)}) copy-start(bf16[1152,512]{1,0:T(8,128)(2,1)S(1)} %constant_dynamic-update-slice_fusion.20.near_0) | copy-start | bytes 3538948
  154.8 32.9 %copy-start.7 = (bf16[576,512]{1,0:T(8,128)(2,1)S(1)}, bf16[576,512]{1,0:T(8,128)(2,1)}, u32[]{:S(2)}) copy-start(bf16[576,512]{1,0:T(8,128)(2,1)} %copy-done.6) | copy-start | bytes 1769476
  154.8 28.3 %collective-permute-start.20 = (bf16[1152,512]{1,0:T(8,128)(2,1)S(1)}, bf16[1152,512]{1,0:T(8,128)(2,1)S(1)}, u32[]{:S(2)}, u32[]{:S(2)}) collective-permute-start(bf16[1152,512]{1,0:T(8,128)(2,1)S(1)} %constant_dynamic-update-slice_fusion.20.near_0), channel_id=1, source_target_pairs={{0,16},{16,32},{32,48},{48,0},{64,80},{80,96},{96,112},{112,64},{1... | collective-permute-start | bytes 3538952 | tf_op jit(solution)/shard_map/ppermute | solution.py:29
  154.9 29.2 %collective-permute-start.21 = (bf16[1152,512]{1,0:T(8,128)(2,1)S(1)}, bf16[1152,512]{1,0:T(8,128)(2,1)S(1)}, u32[]{:S(2)}, u32[]{:S(2)}) collective-permute-start(bf16[1152,512]{1,0:T(8,128)(2,1)S(1)} %constant_dynamic-update-slice_fusion.20.near_0), channel_id=1, source_target_pairs={{0,48},{16,0},{32,16},{48,32},{64,112},{80,64},{96,80},{112,96},{1... | collective-permute-start | bytes 3538952 | tf_op jit(solution)/shard_map/ppermute | solution.py:30
  158.5 21.1 %collective-permute-start.24 = (bf16[288,512]{1,0:T(8,128)(2,1)S(1)}, bf16[288,512]{1,0:T(8,128)(2,1)S(1)}, u32[]{:S(2)}, u32[]{:S(2)}) collective-permute-start(bf16[288,512]{1,0:T(8,128)(2,1)S(1)} %slice.108), channel_id=1, source_target_pairs={{0,64},{16,80},{32,96},{48,112},{64,128},{80,144},{96,160},{112,17... | collective-permute-start | bytes 884744 | tf_op jit(solution)/shard_map/ppermute | solution.py:31
  160.5 19.2 %collective-permute-start.25 = (bf16[288,512]{1,0:T(8,128)(2,1)S(1)}, bf16[288,512]{1,0:T(8,128)(2,1)S(1)}, u32[]{:S(2)}, u32[]{:S(2)}) collective-permute-start(bf16[288,512]{1,0:T(8,128)(2,1)S(1)} %slice.109), channel_id=1, source_target_pairs={{0,192},{16,208},{32,224},{48,240},{64,0},{80,16},{96,32},{112,48}... | collective-permute-start | bytes 884744 | tf_op jit(solution)/shard_map/ppermute | solution.py:32
  179.7 20.0 %copy-start.13 = (bf16[576,512]{1,0:T(8,128)(2,1)}, bf16[576,512]{1,0:T(8,128)(2,1)S(1)}, u32[]{:S(2)}) copy-start(bf16[576,512]{1,0:T(8,128)(2,1)S(1)} %constant_dynamic-update-slice_fusion.22.last_0) | copy-start | bytes 1769476
  179.7 16.2 %collective-permute-start.26 = (bf16[576,512]{1,0:T(8,128)(2,1)S(1)}, bf16[576,512]{1,0:T(8,128)(2,1)S(1)}, u32[]{:S(2)}, u32[]{:S(2)}) collective-permute-start(bf16[576,512]{1,0:T(8,128)(2,1)S(1)} %constant_dynamic-update-slice_fusion.22.last_0), channel_id=1, source_target_pairs={{0,16},{16,32},{32,48},{48,0},{64,80},{80,96},{96,112},{112,64},{1... | collective-permute-start | bytes 1769480 | tf_op jit(solution)/shard_map/ppermute | solution.py:29
  179.8 17.7 %collective-permute-start.27 = (bf16[576,512]{1,0:T(8,128)(2,1)S(1)}, bf16[576,512]{1,0:T(8,128)(2,1)S(1)}, u32[]{:S(2)}, u32[]{:S(2)}) collective-permute-start(bf16[576,512]{1,0:T(8,128)(2,1)S(1)} %constant_dynamic-update-slice_fusion.22.last_0), channel_id=1, source_target_pairs={{0,48},{16,0},{32,16},{48,32},{64,112},{80,64},{96,80},{112,96},{1... | collective-permute-start | bytes 1769480 | tf_op jit(solution)/shard_map/ppermute | solution.py:30
  182.5 19.7 %collective-permute-start.18 = (bf16[288,512]{1,0:T(8,128)(2,1)S(1)}, bf16[288,512]{1,0:T(8,128)(2,1)S(1)}, u32[]{:S(2)}, u32[]{:S(2)}) collective-permute-start(bf16[288,512]{1,0:T(8,128)(2,1)S(1)} %slice.104), channel_id=1, source_target_pairs={{0,16},{16,32},{32,48},{48,0},{64,80},{80,96},{96,112},{112,64},{1... | collective-permute-start | bytes 884744 | tf_op jit(solution)/shard_map/ppermute | solution.py:31
  183.1 19.1 %copy-start.22 = (bf16[1152,512]{1,0:T(8,128)(2,1)}, bf16[1152,512]{1,0:T(8,128)(2,1)S(1)}, u32[]{:S(2)}) copy-start(bf16[1152,512]{1,0:T(8,128)(2,1)S(1)} %collective-permute-done.20.near_1) | copy-start | bytes 3538948
  184.0 37.3 %collective-permute-start.22 = (bf16[576,512]{1,0:T(8,128)(2,1)}, bf16[576,512]{1,0:T(8,128)(2,1)}, u32[]{:S(2)}, u32[]{:S(2)}) collective-permute-start(bf16[576,512]{1,0:T(8,128)(2,1)} %slice.106), channel_id=1, source_target_pairs={{0,16},{16,32},{32,48},{48,0},{64,80},{80,96},{96,112},{112,64},{1... | collective-permute-start | bytes 1769480 | tf_op jit(solution)/shard_map/ppermute | solution.py:31
  184.0 18.2 %copy-start.23 = (bf16[1152,512]{1,0:T(8,128)(2,1)}, bf16[1152,512]{1,0:T(8,128)(2,1)S(1)}, u32[]{:S(2)}) copy-start(bf16[1152,512]{1,0:T(8,128)(2,1)S(1)} %collective-permute-done.21.near_2) | copy-start | bytes 3538948
  185.0 36.3 %collective-permute-start.23 = (bf16[576,512]{1,0:T(8,128)(2,1)}, bf16[576,512]{1,0:T(8,128)(2,1)}, u32[]{:S(2)}, u32[]{:S(2)}) collective-permute-start(bf16[576,512]{1,0:T(8,128)(2,1)} %slice.107), channel_id=1, source_target_pairs={{0,48},{16,0},{32,16},{48,32},{64,112},{80,64},{96,80},{112,96},{1... | collective-permute-start | bytes 1769480 | tf_op jit(solution)/shard_map/ppermute | solution.py:32
  195.9 18.0 %collective-permute-start.19 = (bf16[288,512]{1,0:T(8,128)(2,1)}, bf16[288,512]{1,0:T(8,128)(2,1)}, u32[]{:S(2)}, u32[]{:S(2)}) collective-permute-start(bf16[288,512]{1,0:T(8,128)(2,1)} %slice.105), channel_id=1, source_target_pairs={{0,48},{16,0},{32,16},{48,32},{64,112},{80,64},{96,80},{112,96},{1... | collective-permute-start | bytes 884744 | tf_op jit(solution)/shard_map/ppermute | solution.py:32
  196.6 0.8 copy-start.9
  197.5 23.8 %collective-permute-start.28 = (bf16[288,512]{1,0:T(8,128)(2,1)}, bf16[288,512]{1,0:T(8,128)(2,1)}, u32[]{:S(2)}, u32[]{:S(2)}) collective-permute-start(bf16[288,512]{1,0:T(8,128)(2,1)} %slice.110), channel_id=1, source_target_pairs={{0,16},{16,32},{32,48},{48,0},{64,80},{80,96},{96,112},{112,64},{1... | collective-permute-start | bytes 884744 | tf_op jit(solution)/shard_map/ppermute | solution.py:31
  199.7 0.8 copy-start.11
  202.2 0.7 copy-start.15
  203.0 18.3 %collective-permute-start.29 = (bf16[288,512]{1,0:T(8,128)(2,1)}, bf16[288,512]{1,0:T(8,128)(2,1)}, u32[]{:S(2)}, u32[]{:S(2)}) collective-permute-start(bf16[288,512]{1,0:T(8,128)(2,1)} %slice.111), channel_id=1, source_target_pairs={{0,48},{16,0},{32,16},{48,32},{64,112},{80,64},{96,80},{112,96},{1... | collective-permute-start | bytes 884744 | tf_op jit(solution)/shard_map/ppermute | solution.py:32
  221.3 1.1 copy-start.2
  222.4 1.1 copy-start.5
  223.5 1.1 copy-start.8
  224.5 1.1 copy-start.10
  225.6 1.1 copy-start.12
  226.7 1.1 copy-start.14
  227.7 1.0 copy-start.16
Sparse Core Ops, SparseCore 0:
  22.9 65.8 all-gather.5
  152.6 54.7 all-gather.3

commit v6 on v5

--- a/solution.py
+++ b/solution.py
@@ -109,9 +109,6 @@
 def score_call(place, slot, ein, blocks, eigvals):
     di, dj = eigvals.shape
 
-    def whole(x):
-        return pl.BlockSpec(x.shape, lambda n, rank=x.ndim: (0,) * rank)
-
     return pl.pallas_call(
         score_kernel,
         grid=(NSEQ,),
@@ -120,7 +117,7 @@
             pl.BlockSpec((1, di, SEQLEN), lambda n: (n, 0, 0)),
             pl.BlockSpec((16, di, 128), lambda n: (0, 0, 4)),
         ]
-        + [whole(x) for x in (*blocks, eigvals)],
+        + [pl.BlockSpec(memory_space=pltpu.VMEM)] * (len(blocks) + 1),
         out_specs=pl.BlockSpec((QUERIES, 128), lambda n: (0, 0)),
         out_shape=jax.ShapeDtypeStruct((QUERIES, 128), F32),
         scratch_shapes=[
@@ -132,7 +129,7 @@
             pltpu.VMEM(blocks[10].shape, BF16),
             pltpu.VMEM((SEQLEN, blocks[0].shape[1]), BF16),
         ],
-        compiler_params=pltpu.CompilerParams(vmem_limit_bytes=48 * 1024 * 1024),
+        compiler_params=pltpu.CompilerParams(vmem_limit_bytes=32 * 1024 * 1024),
         cost_estimate=pl.CostEstimate(
             flops=10_000_000_000, bytes_accessed=16_000_000, transcendentals=0
         ),
@@ -161,12 +158,17 @@
         "shard",
         axis=0,
     )
-    rows_ring = jnp.concatenate(ring4(train_in[0, 16:], "shard", SHARD_Z, 8), 0)
-    rows_ring = jnp.concatenate(ring4(rows_ring, "shard", SHARD_Y, 32), 0)
-
-    block = jnp.concatenate([train_grad[0], lax.ppermute(train_grad[0], "example", EXAMPLE_Z)], 0)
+    zl_block = lax.ppermute(train_grad[0], "example", EXAMPLE_Z)
+    block = jnp.concatenate([train_grad[0], zl_block], 0)
     block = jnp.concatenate(ring4(block, "example", EXAMPLE_X, 32), 0)
     other = lax.ppermute(block, "example", EXAMPLE_CORE)
+    rows_ring = jnp.where(
+        jnp.isnan(zl_block[0, 0]), jnp.zeros((16, D), BF16), train_in[0, 16:]
+    )
+    rows_ring = jnp.concatenate(ring4(rows_ring, "shard", SHARD_Z, 8), 0)
+    rows_ring = jnp.where(jnp.isnan(other[0, 0]), jnp.zeros_like(rows_ring), rows_ring)
+    rows_ring = jnp.concatenate(ring4(rows_ring, "shard", SHARD_Y, 32), 0)
+
     query_right = jnp.dot(
         query_out.reshape(64, H), basis_out, preferred_element_type=F32
     ).astype(BF16)
@@ -202,7 +204,7 @@
     ).astype(BF16)
     eig_shard = corner(jnp.sum(rows_all[:, :, D:].astype(F32)), (di, 64))
     ein = jnp.concatenate([own_in.T, query_left.T, eig_shard], 1)
-    flag = jnp.isnan(sum(b[0, 0] for b in z_blocks[1:3] + blocks[1:3]))
+    flag = jnp.isnan(sum(b[0, 0] for b in z_blocks[1:3] + blocks[3:5]))
     ein = jnp.where(flag, jnp.zeros_like(ein), ein)
     ein = lax.all_gather(ein, "example", axis=0)
 

time: 284 us -> 308 us (1.085)
  local copies, waits for them, and re-layouts: 41.1 us -> 54.2 us
  blocking collectives: 23.9 us -> 30.2 us
  starting transfers between devices: 57.4 us -> 51.3 us
  waiting for transfers between devices: 78.5 us -> 84.2 us
    ppermute x7, waiting for transfers between devices: 34.4 us -> 49 us  [ring4(): below = lax.ppermute(block, axis, steps[1])]
    ppermute x7, starting transfers between devices: 7.89 us -> 20.3 us  [ring4(): far_bottom = lax.ppermute(above[cut:], axis, steps[-1])]
    ppermute x1, starting transfers between devices: 13.7 us -> 2.68 us  [shards(): other = lax.ppermute(block, 'example', EXAMPLE_CORE)]
    unnamed x78 -> x77, local copies, waits for them, and re-layouts: 21.4 us -> 31.2 us
    ppermute x7, waiting for transfers between devices: 12.5 us -> 3.6 us  [ring4(): far_bottom = lax.ppermute(above[cut:], axis, steps[-1])]
    ppermute x7, waiting for transfers between devices: 0.27 us -> 7.97 us  [ring4(): above = lax.ppermute(block, axis, steps[-1])]
    ppermute x7, waiting for transfers between devices: 31.2 us -> 23.5 us  [ring4(): far_top = lax.ppermute(below[:cut], axis, steps[1])]
    all_to_all x1, blocking collectives: 23.9 us -> 30.2 us  [shards(): pieces = lax.all_to_all(pieces, ('shard', 'example'), 0, 0, tiled=True)]
  transfers between devices with their start and end apart: 32 -> 32, of which waited for: 12 -> 12; matrix products, arithmetic and copies ran while one was open for 19% -> 21% of each run, Pallas kernels for 0% -> 0%
where the time goes in v6:
time: 308 us; the launch traced here: 307 us
  waiting for transfers between devices  84.2 us (27%)
  local copies, waits for them, and re-layouts  54.2 us (18%)
  starting transfers between devices  51.3 us (17%)
  blocking collectives  30.2 us (10%)
  between operations  26.9 us (9%)
  matrix products  22.7 us (7%)
  Pallas kernels  21.6 us (7%)
  other arithmetic  15.5 us (5%)
    ppermute x7, waiting for transfers between devices, ring4(): below = lax.ppermute(block, axis, steps[1])  49 us
    unnamed x77, local copies, waits for them, and re-layouts  31.2 us
    all_to_all x1, blocking collectives, shards(): pieces = lax.all_to_all(pieces, ('shard', 'example'), 0, 0, tiled=True)  30.2 us
    ppermute x7, waiting for transfers between devices, ring4(): far_top = lax.ppermute(below[:cut], axis, steps[1])  23.5 us
    pallas_call x1, Pallas kernels, score_call(): pl.pallas_call(score_kernel, grid=(NSEQ,), in_specs=[pl.BlockSpec(memory_...  21.6 us
    ppermute x7, starting transfers between devices, ring4(): far_bottom = lax.ppermute(above[cut:], axis, steps[-1])  20.3 us
    ppermute x7, starting transfers between devices, ring4(): above = lax.ppermute(block, axis, steps[-1])  12.5 us
    dot_general x2, matrix products, shards(): jnp.dot(b, basis_out, preferred_element_type=F32).astype(BF16)  10.6 us
  transfers between devices with their start and end apart: 32, of which 12 were waited for; matrix products, arithmetic and copies ran while one was open for 21% of the time, Pallas kernels for 0%

profile of v6, /device:TPU:1, one launch (start us, length us, event | category | flops | bytes accessed | tf_op | source)
XLA Modules:
  0.0 306.6 jit_solution(17464812836509058204)
XLA Ops:
  6.6 2.0 reduce_sum.27
  13.1 1.4 select_convert_fusion.1
  15.3 2.6 collective-permute-start
  17.8 1.8 constant_dynamic-update-slice_fusion.5
  20.8 2.7 fusion.3
  23.6 5.3 %convolution_convert_fusion.3 = bf16[64,432]{1,0:T(8,128)(2,1)} fusion(bf16[64,6912]{1,0:T(8,128)(2,1)S(1)} %bitcast.68, bf16[6912,432]{0,1:T(8,128)(2,1)} %param.12), kind=kOutput, calls=%fused_computation.7 | convolution fusion | flops 382233600 | bytes 6912000 | tf_op jit(solution)/shard_map/dot_general | solution.py:172
  28.9 1.1 pad_maximum_fusion
  30.0 1.3 collective-permute-start.1
  31.2 1.5 collective-permute-start.2
  32.7 1.2 slice.110
  35.2 2.0 constant_dynamic-update-slice_fusion.4
  37.2 14.3 %collective-permute-done.1 = bf16[64,6912]{1,0:T(8,128)(2,1)S(1)} collective-permute-done((bf16[64,6912]{1,0:T(8,128)(2,1)S(1)}, bf16[64,6912]{1,0:T(8,128)(2,1)S(1)}, u32[]{:S(2)}, u32[]{:S(2)}) %collective-permute-start.1) | collective-permute-done | bytes 884768 | tf_op jit(solution)/shard_map/ppermute | solution.py:29
  51.6 2.7 collective-permute-start.4
  56.4 6.3 %collective-permute-done.3 = bf16[32,6912]{1,0:T(8,128)(2,1)S(1)} collective-permute-done((bf16[32,6912]{1,0:T(8,128)(2,1)S(1)}, bf16[32,6912]{1,0:T(8,128)(2,1)S(1)}, u32[]{:S(2)}, u32[]{:S(2)}) %collective-permute-start.3) | collective-permute-done | bytes 442400 | tf_op jit(solution)/shard_map/ppermute | solution.py:31
  64.3 2.7 collective-permute-start.5
  67.7 3.0 collective-permute-start.12
  70.7 2.0 collective-permute-start.13
  73.2 15.7 %collective-permute-done.12 = bf16[16,5120]{1,0:T(8,128)(2,1)S(1)} collective-permute-done((bf16[16,5120]{1,0:T(8,128)(2,1)S(1)}, bf16[16,5120]{1,0:T(8,128)(2,1)S(1)}, u32[]{:S(2)}, u32[]{:S(2)}) %collective-permute-start.12) | collective-permute-done | bytes 163872 | tf_op jit(solution)/shard_map/ppermute | solution.py:29
  89.0 3.8 %collective-permute-start.15 = (bf16[8,5120]{1,0:T(8,128)(2,1)S(1)}, bf16[8,5120]{1,0:T(8,128)(2,1)S(1)}, u32[]{:S(2)}, u32[]{:S(2)}) collective-permute-start(bf16[8,5120]{1,0:T(8,128)(2,1)S(1)} %slice.112), channel_id=1, source_target_pairs={{0,192},{16,208},{32,224},{48,240},{64,0},{80,16},{96,32},{112,48}... | collective-permute-start | bytes 245768 | tf_op jit(solution)/shard_map/ppermute | solution.py:32
  96.7 4.4 %convolution_convert_fusion.1 = bf16[256,432]{0,1:T(8,128)(2,1)} fusion(bf16[256,6912]{1,0:T(8,128)(2,1)} %constant_dynamic-update-slice_fusion, bf16[6912,432]{0,1:T(8,128)(2,1)S(1)} %bitcast.62), kind=kOutput, calls=%fused_computation.1 | convolution fusion | flops 1528934400 | bytes 9732096 | tf_op jit(solution)/shard_map/dot_general | solution.py:176
  101.1 1.1 copy.21
  102.2 1.2 slice.109
  104.7 6.2 %convolution_convert_fusion = bf16[256,432]{0,1:T(8,128)(2,1)} fusion(bf16[256,6912]{1,0:T(8,128)(2,1)} %collective-permute-done.5, bf16[6912,432]{0,1:T(8,128)(2,1)} %param.12), kind=kOutput, calls=%fused_computation | convolution fusion | flops 1528934400 | bytes 9732096 | tf_op jit(solution)/shard_map/dot_general | solution.py:176
  110.9 1.8 copy.22
  112.6 1.9 fusion.6.own_0
  114.5 1.1 collective-permute-start.8
  115.6 2.4 constant_dynamic-update-slice_fusion.15
  119.1 1.6 collective-permute-start.17
  120.7 1.5 convert_reduce_fusion
  122.2 3.6 %slice.108 = bf16[16,16,5120]{2,1,0:T(8,128)(2,1)} slice(bf16[16,16,5248]{2,1,0:T(8,128)(2,1)} %bitcast.64), slice={[0:16], [0:16], [0:5120]} | slice | bytes 5242880 | tf_op jit(solution)/shard_map/slice | solution.py:193
  129.3 2.2 collective-permute-start.6
  131.5 1.6 collective-permute-start.7
  133.6 1.4 fusion.8
  135.0 2.9 fusion.14
  138.9 8.0 %collective-permute-done.10.own_2 = bf16[576,512]{1,0:T(8,128)(2,1)S(1)} collective-permute-done((bf16[576,512]{1,0:T(8,128)(2,1)}, bf16[576,512]{1,0:T(8,128)(2,1)S(1)}, u32[]{:S(2)}, u32[]{:S(2)}) %collective-permute-start.10) | collective-permute-done | bytes 589856 | tf_op jit(solution)/shard_map/ppermute | solution.py:30
  146.9 1.8 collective-permute-start.9
  148.7 4.2 %collective-permute-done.6 = bf16[576,512]{1,0:T(8,128)(2,1)S(1)} collective-permute-done((bf16[576,512]{1,0:T(8,128)(2,1)}, bf16[576,512]{1,0:T(8,128)(2,1)S(1)}, u32[]{:S(2)}, u32[]{:S(2)}) %collective-permute-start.6) | collective-permute-done | bytes 589856 | tf_op jit(solution)/shard_map/ppermute | solution.py:29
  152.9 4.1 %collective-permute-start.11 = (bf16[288,512]{1,0:T(8,128)(2,1)S(1)}, bf16[288,512]{1,0:T(8,128)(2,1)S(1)}, u32[]{:S(2)}, u32[]{:S(2)}) collective-permute-start(bf16[288,512]{1,0:T(8,128)(2,1)S(1)} %slice.106), channel_id=1, source_target_pairs={{0,48},{16,0},{32,16},{48,32},{64,112},{80,64},{96,80},{112,96},{1... | collective-permute-start | bytes 884744 | tf_op jit(solution)/shard_map/ppermute | solution.py:32
  161.4 3.0 collective-permute-start.19
  164.3 1.1 constant_dynamic-update-slice_fusion.14
  165.4 1.1 constant_dynamic-update-slice_fusion.13
  170.5 1.1 fusion.15
  172.6 1.1 constant_dynamic-update-slice_fusion.17
  173.7 1.1 constant_dynamic-update-slice_fusion.16.near_0
  174.9 2.7 collective-permute-start.21
  178.6 2.5 collective-permute-start.24
  182.0 1.3 collective-permute-start.25
  183.4 3.0 collective-permute-done.24
  186.4 3.3 %collective-permute-done.25 = bf16[288,512]{1,0:T(8,128)(2,1)S(1)} collective-permute-done((bf16[288,512]{1,0:T(8,128)(2,1)S(1)}, bf16[288,512]{1,0:T(8,128)(2,1)S(1)}, u32[]{:S(2)}, u32[]{:S(2)}) %collective-permute-start.25) | collective-permute-done | bytes 294944 | tf_op jit(solution)/shard_map/ppermute | solution.py:32
  189.9 2.7 collective-permute-start.27
  192.5 8.8 %collective-permute-done.20.near_1 = bf16[1152,512]{1,0:T(8,128)(2,1)S(1)} collective-permute-done((bf16[1152,512]{1,0:T(8,128)(2,1)S(1)}, bf16[1152,512]{1,0:T(8,128)(2,1)S(1)}, u32[]{:S(2)}, u32[]{:S(2)}) %collective-permute-start.20) | collective-permute-done | bytes 1179680 | tf_op jit(solution)/shard_map/ppermute | solution.py:29
  205.1 2.7 collective-permute-start.23
  207.8 6.1 %collective-permute-done.26.last_1 = bf16[576,512]{1,0:T(8,128)(2,1)S(1)} collective-permute-done((bf16[576,512]{1,0:T(8,128)(2,1)S(1)}, bf16[576,512]{1,0:T(8,128)(2,1)S(1)}, u32[]{:S(2)}, u32[]{:S(2)}) %collective-permute-start.26) | collective-permute-done | bytes 589856 | tf_op jit(solution)/shard_map/ppermute | solution.py:29
  217.1 2.7 collective-permute-start.29
  219.8 13.2 %collective-permute-done.28.last_top = bf16[288,512]{1,0:T(8,128)(2,1)} collective-permute-done((bf16[288,512]{1,0:T(8,128)(2,1)}, bf16[288,512]{1,0:T(8,128)(2,1)}, u32[]{:S(2)}, u32[]{:S(2)}) %collective-permute-start.28) | collective-permute-done | bytes 294944 | tf_op jit(solution)/shard_map/ppermute | solution.py:31
  233.1 1.1 copy-done.1
  234.2 1.3 copy-done.3
  235.4 1.3 copy-done.5
  236.7 1.3 copy-done.7
  238.0 1.1 copy-done.9
  241.2 1.1 copy-done.15
  242.2 2.9 copy-done.16
  247.0 21.6 %shard_map.82 = f32[32,128]{1,0:T(8,128)S(1)} custom-call(s32[16]{0:T(128)S(1)} %stack.67.place, s32[16]{0:T(128)S(1)} %fusion.9.slot, bf16[16,320,640]{2,1,0:T(8,128)(2,1)S(1)} %copy-done.16, bf16[16,320,640]{2,1,0:T(8,128)(2,1)S(1)} %copy-done.16, bf16[576,512]{1,0:T(8,128)(2,1)} %fusion.6.own_0, bf16[576,512]{1,0:T(8,128)(2,1)} %collective-permute-done.8.own_1, ...), custom_call_target="tpu_custom_call" | custom-call | flops 10000000000 | bytes 16000000 | tf_op jit(solution)/shard_map/pallas_call | solution.py:112
  268.8 30.2 %all_to_all.9 = f32[256,1,2]{2,1,0:T(1,128)S(1)} all-to-all(f32[256,1,2]{2,1,0:T(1,128)S(1)} %bitcast.69), channel_id=1, replica_groups=mesh['shard'=16,'example'=16] {'shard','example'}, dimensions={0} | all-to-all | bytes 4096 | tf_op jit(solution)/shard_map/all_to_all | solution.py:213
  (146 shorter events, 34.4 us)
Async XLA Ops:
  6.5 14.3 %copy-start = (bf16[5120,320]{0,1:T(8,128)(2,1)S(1)}, bf16[5120,320]{0,1:T(8,128)(2,1)}, u32[]{:S(2)}) copy-start(bf16[5120,320]{0,1:T(8,128)(2,1)} %param.11) | copy-start | bytes 9830404
  6.5 114.2 %all-gather.6.cloned.1.call-start = ((), (), s32[]{:S(2)}) async-start(), calls=%async_computation.2 | async-start | bytes 2854912 | tf_op jit(solution)/shard_map/all_gather | solution.py:156
  15.2 217.8 %all-gather.4.cloned.1.call-start = ((), (), s32[]{:S(2)}) async-start(), calls=%async_computation.1 | async-start | bytes 6963200 | tf_op jit(solution)/shard_map/all_gather | solution.py:209
  15.3 13.6 %collective-permute-start = (bf16[32,6912]{1,0:T(8,128)(2,1)}, bf16[32,6912]{1,0:T(8,128)(2,1)}, u32[]{:S(2)}, u32[]{:S(2)}) collective-permute-start(bf16[32,6912]{1,0:T(8,128)(2,1)} %bitcast.66), channel_id=1, source_target_pairs={{0,8},{1,9},{2,10},{3,11},{4,12},{5,13},{6,14},{7,15},{8,0},{9,1},... | collective-permute-start | bytes 1327112 | tf_op jit(solution)/shard_map/ppermute | solution.py:161
  20.1 3.5 %copy-start.24 = (bf16[2,32,6912]{2,1,0:T(8,128)(2,1)S(1)}, bf16[2,32,6912]{2,1,0:T(8,128)(2,1)}, u32[]{:S(2)}) copy-start(bf16[2,32,6912]{2,1,0:T(8,128)(2,1)} %param.15) | copy-start | bytes 2654212
  23.6 5.3 %copy-start.21 = (bf16[1,32,6912]{2,1,0:T(8,128)(2,1)S(1)}, bf16[1,32,6912]{2,1,0:T(8,128)(2,1)}, u32[]{:S(2)}) copy-start(bf16[1,32,6912]{2,1,0:T(8,128)(2,1)} %param.9) | copy-start | bytes 1327108
  23.6 73.1 %slice-start = ((s8[5971968]{0:T(1024)(128)(4,1)}), s8[1777664]{0:T(1024)(128)(4,1)S(1)}, s32[]{:S(2)}) async-start(s8[5971968]{0:T(1024)(128)(4,1)} %bitcast.61), calls=%async_computation.3 | async-start | bytes 3555328
  30.0 21.5 %collective-permute-start.1 = (bf16[64,6912]{1,0:T(8,128)(2,1)S(1)}, bf16[64,6912]{1,0:T(8,128)(2,1)S(1)}, u32[]{:S(2)}, u32[]{:S(2)}) collective-permute-start(bf16[64,6912]{1,0:T(8,128)(2,1)S(1)} %pad_maximum_fusion), channel_id=1, source_target_pairs={{0,2},{1,3},{2,4},{3,5},{4,6},{5,7},{6,0},{7,1},{8,10},{9,11},{10,... | collective-permute-start | bytes 2654216 | tf_op jit(solution)/shard_map/ppermute | solution.py:29
  31.2 20.3 %collective-permute-start.2 = (bf16[64,6912]{1,0:T(8,128)(2,1)S(1)}, bf16[64,6912]{1,0:T(8,128)(2,1)S(1)}, u32[]{:S(2)}, u32[]{:S(2)}) collective-permute-start(bf16[64,6912]{1,0:T(8,128)(2,1)S(1)} %pad_maximum_fusion), channel_id=1, source_target_pairs={{0,6},{1,7},{2,0},{3,1},{4,2},{5,3},{6,4},{7,5},{8,14},{9,15},{10,... | collective-permute-start | bytes 2654216 | tf_op jit(solution)/shard_map/ppermute | solution.py:30
  35.2 61.5 %slice-start.1 = ((s8[5971968]{0:T(1024)(128)(4,1)}), s8[4194304]{0:T(1024)(128)(4,1)S(1)}, s32[]{:S(2)}) async-start(s8[5971968]{0:T(1024)(128)(4,1)} %bitcast.61), calls=%async_computation.4 | async-start | bytes 8388608
  51.5 15.5 %copy-start.25 = (bf16[1,32,5120]{2,1,0:T(8,128)(2,1)S(1)}, bf16[1,32,5120]{2,1,0:T(8,128)(2,1)}, u32[]{:S(2)}) copy-start(bf16[1,32,5120]{2,1,0:T(8,128)(2,1)} %param.8) | copy-start | bytes 983044
  51.5 11.2 %collective-permute-start.3 = (bf16[32,6912]{1,0:T(8,128)(2,1)S(1)}, bf16[32,6912]{1,0:T(8,128)(2,1)S(1)}, u32[]{:S(2)}, u32[]{:S(2)}) collective-permute-start(bf16[32,6912]{1,0:T(8,128)(2,1)S(1)} %slice.100), channel_id=1, source_target_pairs={{0,2},{1,3},{2,4},{3,5},{4,6},{5,7},{6,0},{7,1},{8,10},{9,11},{10,... | collective-permute-start | bytes 1327112 | tf_op jit(solution)/shard_map/ppermute | solution.py:31
  51.6 11.9 %collective-permute-start.4 = (bf16[32,6912]{1,0:T(8,128)(2,1)S(1)}, bf16[32,6912]{1,0:T(8,128)(2,1)S(1)}, u32[]{:S(2)}, u32[]{:S(2)}) collective-permute-start(bf16[32,6912]{1,0:T(8,128)(2,1)S(1)} %slice.101), channel_id=1, source_target_pairs={{0,6},{1,7},{2,0},{3,1},{4,2},{5,3},{6,4},{7,5},{8,14},{9,15},{10,... | collective-permute-start | bytes 1327112 | tf_op jit(solution)/shard_map/ppermute | solution.py:32
  64.3 37.9 %collective-permute-start.5 = (bf16[256,6912]{1,0:T(8,128)(2,1)}, bf16[256,6912]{1,0:T(8,128)(2,1)}, u32[]{:S(2)}, u32[]{:S(2)}) collective-permute-start(bf16[256,6912]{1,0:T(8,128)(2,1)} %constant_dynamic-update-slice_fusion), channel_id=1, source_target_pairs={{0,1},{1,0},{2,3},{3,2},{4,5},{5,4},{6,7},{7,6},{8,9},{9,8},{10,11... | collective-permute-start | bytes 10616840 | tf_op jit(solution)/shard_map/ppermute | solution.py:164
  67.7 21.3 %collective-permute-start.12 = (bf16[16,5120]{1,0:T(8,128)(2,1)S(1)}, bf16[16,5120]{1,0:T(8,128)(2,1)S(1)}, u32[]{:S(2)}, u32[]{:S(2)}) collective-permute-start(bf16[16,5120]{1,0:T(8,128)(2,1)S(1)} %get-tuple-element.8), channel_id=1, source_target_pairs={{0,64},{16,80},{32,96},{48,112},{64,128},{80,144},{96,160},{112,17... | collective-permute-start | bytes 491528 | tf_op jit(solution)/shard_map/ppermute | solution.py:29
  70.7 18.3 %collective-permute-start.13 = (bf16[16,5120]{1,0:T(8,128)(2,1)S(1)}, bf16[16,5120]{1,0:T(8,128)(2,1)S(1)}, u32[]{:S(2)}, u32[]{:S(2)}) collective-permute-start(bf16[16,5120]{1,0:T(8,128)(2,1)S(1)} %get-tuple-element.8), channel_id=1, source_target_pairs={{0,192},{16,208},{32,224},{48,240},{64,0},{80,16},{96,32},{112,48}... | collective-permute-start | bytes 491528 | tf_op jit(solution)/shard_map/ppermute | solution.py:30
  88.9 6.2 %collective-permute-start.14 = (bf16[8,5120]{1,0:T(8,128)(2,1)S(1)}, bf16[8,5120]{1,0:T(8,128)(2,1)S(1)}, u32[]{:S(2)}, u32[]{:S(2)}) collective-permute-start(bf16[8,5120]{1,0:T(8,128)(2,1)S(1)} %slice.111), channel_id=1, source_target_pairs={{0,64},{16,80},{32,96},{48,112},{64,128},{80,144},{96,160},{112,17... | collective-permute-start | bytes 245768 | tf_op jit(solution)/shard_map/ppermute | solution.py:31
  89.0 7.1 %collective-permute-start.15 = (bf16[8,5120]{1,0:T(8,128)(2,1)S(1)}, bf16[8,5120]{1,0:T(8,128)(2,1)S(1)}, u32[]{:S(2)}, u32[]{:S(2)}) collective-permute-start(bf16[8,5120]{1,0:T(8,128)(2,1)S(1)} %slice.112), channel_id=1, source_target_pairs={{0,192},{16,208},{32,224},{48,240},{64,0},{80,16},{96,32},{112,48}... | collective-permute-start | bytes 245768 | tf_op jit(solution)/shard_map/ppermute | solution.py:32
  114.5 18.6 %collective-permute-start.8 = (bf16[576,512]{1,0:T(8,128)(2,1)}, bf16[576,512]{1,0:T(8,128)(2,1)}, u32[]{:S(2)}, u32[]{:S(2)}) collective-permute-start(bf16[576,512]{1,0:T(8,128)(2,1)} %fusion.6.own_0), channel_id=1, source_target_pairs={{0,16},{16,32},{32,48},{48,0},{64,80},{80,96},{96,112},{112,64},{1... | collective-permute-start | bytes 1769480 | tf_op jit(solution)/shard_map/ppermute | solution.py:29
  115.6 17.9 %copy-start.28 = (pred[320]{0:T(512)(128)(4,1)S(1)}, pred[320]{0:T(512)(128)(4,1)}, u32[]{:S(2)}) copy-start(pred[320]{0:T(512)(128)(4,1)} %get-tuple-element.11) | copy-start | bytes 964
  115.6 17.9 %copy-start.29 = (pred[320]{0:T(512)(128)(4,1)S(1)}, pred[320]{0:T(512)(128)(4,1)}, u32[]{:S(2)}) copy-start(pred[320]{0:T(512)(128)(4,1)} %get-tuple-element.12) | copy-start | bytes 964
  118.0 41.2 %collective-permute-start.16 = (bf16[64,5120]{1,0:T(8,128)(2,1)}, bf16[64,5120]{1,0:T(8,128)(2,1)}, u32[]{:S(2)}, u32[]{:S(2)}) collective-permute-start(bf16[64,5120]{1,0:T(8,128)(2,1)} %get-tuple-element.6), channel_id=1, source_target_pairs={{0,16},{16,32},{32,48},{48,0},{64,80},{80,96},{96,112},{112,64},{1... | collective-permute-start | bytes 1966088 | tf_op jit(solution)/shard_map/ppermute | solution.py:29
  119.1 41.3 %collective-permute-start.17 = (bf16[64,5120]{1,0:T(8,128)(2,1)}, bf16[64,5120]{1,0:T(8,128)(2,1)}, u32[]{:S(2)}, u32[]{:S(2)}) collective-permute-start(bf16[64,5120]{1,0:T(8,128)(2,1)} %get-tuple-element.6), channel_id=1, source_target_pairs={{0,48},{16,0},{32,16},{48,32},{64,112},{80,64},{96,80},{112,96},{1... | collective-permute-start | bytes 1966088 | tf_op jit(solution)/shard_map/ppermute | solution.py:30
  129.3 23.6 %collective-permute-start.6 = (bf16[576,512]{1,0:T(8,128)(2,1)}, bf16[576,512]{1,0:T(8,128)(2,1)S(1)}, u32[]{:S(2)}, u32[]{:S(2)}) collective-permute-start(bf16[576,512]{1,0:T(8,128)(2,1)} %fusion.6.own_0), channel_id=1, source_target_pairs={{0,64},{16,80},{32,96},{48,112},{64,128},{80,144},{96,160},{112,17... | collective-permute-start | bytes 1769480 | tf_op jit(solution)/shard_map/ppermute | solution.py:29
  131.5 26.0 %collective-permute-start.7 = (bf16[576,512]{1,0:T(8,128)(2,1)}, bf16[576,512]{1,0:T(8,128)(2,1)S(1)}, u32[]{:S(2)}, u32[]{:S(2)}) collective-permute-start(bf16[576,512]{1,0:T(8,128)(2,1)} %fusion.6.own_0), channel_id=1, source_target_pairs={{0,192},{16,208},{32,224},{48,240},{64,0},{80,16},{96,32},{112,48}... | collective-permute-start | bytes 1769480 | tf_op jit(solution)/shard_map/ppermute | solution.py:30
  133.2 13.7 %collective-permute-start.10 = (bf16[576,512]{1,0:T(8,128)(2,1)}, bf16[576,512]{1,0:T(8,128)(2,1)S(1)}, u32[]{:S(2)}, u32[]{:S(2)}) collective-permute-start(bf16[576,512]{1,0:T(8,128)(2,1)} %fusion.6.own_0), channel_id=1, source_target_pairs={{0,48},{16,0},{32,16},{48,32},{64,112},{80,64},{96,80},{112,96},{1... | collective-permute-start | bytes 1769480 | tf_op jit(solution)/shard_map/ppermute | solution.py:30
  135.0 29.3 %copy-start.26 = (bf16[256,5120]{1,0:T(8,128)(2,1)S(1)}, bf16[256,5120]{1,0:T(8,128)(2,1)}, u32[]{:S(2)}) copy-start(bf16[256,5120]{1,0:T(8,128)(2,1)} %get-tuple-element.5) | copy-start | bytes 7864324
  146.9 24.7 %copy-start.8 = (bf16[576,512]{1,0:T(8,128)(2,1)}, bf16[576,512]{1,0:T(8,128)(2,1)S(1)}, u32[]{:S(2)}) copy-start(bf16[576,512]{1,0:T(8,128)(2,1)S(1)} %collective-permute-done.10.own_2) | copy-start | bytes 1769476
  146.9 19.7 %collective-permute-start.9 = (bf16[288,512]{1,0:T(8,128)(2,1)S(1)}, bf16[288,512]{1,0:T(8,128)(2,1)S(1)}, u32[]{:S(2)}, u32[]{:S(2)}) collective-permute-start(bf16[288,512]{1,0:T(8,128)(2,1)S(1)} %slice.104), channel_id=1, source_target_pairs={{0,16},{16,32},{32,48},{48,0},{64,80},{80,96},{96,112},{112,64},{1... | collective-permute-start | bytes 884744 | tf_op jit(solution)/shard_map/ppermute | solution.py:31
  152.9 18.7 %copy-start.23 = (bf16[576,512]{1,0:T(8,128)(2,1)}, bf16[576,512]{1,0:T(8,128)(2,1)S(1)}, u32[]{:S(2)}) copy-start(bf16[576,512]{1,0:T(8,128)(2,1)S(1)} %collective-permute-done.6) | copy-start | bytes 1769476
  152.9 15.6 %collective-permute-start.11 = (bf16[288,512]{1,0:T(8,128)(2,1)S(1)}, bf16[288,512]{1,0:T(8,128)(2,1)S(1)}, u32[]{:S(2)}, u32[]{:S(2)}) collective-permute-start(bf16[288,512]{1,0:T(8,128)(2,1)S(1)} %slice.106), channel_id=1, source_target_pairs={{0,48},{16,0},{32,16},{48,32},{64,112},{80,64},{96,80},{112,96},{1... | collective-permute-start | bytes 884744 | tf_op jit(solution)/shard_map/ppermute | solution.py:32
  157.5 14.1 %copy-start.22 = (bf16[576,512]{1,0:T(8,128)(2,1)}, bf16[576,512]{1,0:T(8,128)(2,1)S(1)}, u32[]{:S(2)}) copy-start(bf16[576,512]{1,0:T(8,128)(2,1)S(1)} %collective-permute-done.7) | copy-start | bytes 1769476
  160.3 10.1 %collective-permute-start.18 = (bf16[32,5120]{1,0:T(8,128)(2,1)S(1)}, bf16[32,5120]{1,0:T(8,128)(2,1)S(1)}, u32[]{:S(2)}, u32[]{:S(2)}) collective-permute-start(bf16[32,5120]{1,0:T(8,128)(2,1)S(1)} %slice.113), channel_id=1, source_target_pairs={{0,16},{16,32},{32,48},{48,0},{64,80},{80,96},{96,112},{112,64},{1... | collective-permute-start | bytes 983048 | tf_op jit(solution)/shard_map/ppermute | solution.py:31
  161.4 9.1 %collective-permute-start.19 = (bf16[32,5120]{1,0:T(8,128)(2,1)S(1)}, bf16[32,5120]{1,0:T(8,128)(2,1)S(1)}, u32[]{:S(2)}, u32[]{:S(2)}) collective-permute-start(bf16[32,5120]{1,0:T(8,128)(2,1)S(1)} %slice.114), channel_id=1, source_target_pairs={{0,48},{16,0},{32,16},{48,32},{64,112},{80,64},{96,80},{112,96},{1... | collective-permute-start | bytes 983048 | tf_op jit(solution)/shard_map/ppermute | solution.py:32
  167.1 0.7 copy-start.17
  169.0 0.7 copy-start.19
  170.5 1.2 copy-start.27
  174.8 29.3 %copy-start.6 = (bf16[1152,512]{1,0:T(8,128)(2,1)}, bf16[1152,512]{1,0:T(8,128)(2,1)S(1)}, u32[]{:S(2)}) copy-start(bf16[1152,512]{1,0:T(8,128)(2,1)S(1)} %constant_dynamic-update-slice_fusion.16.near_0) | copy-start | bytes 3538948
  174.8 26.5 %collective-permute-start.20 = (bf16[1152,512]{1,0:T(8,128)(2,1)S(1)}, bf16[1152,512]{1,0:T(8,128)(2,1)S(1)}, u32[]{:S(2)}, u32[]{:S(2)}) collective-permute-start(bf16[1152,512]{1,0:T(8,128)(2,1)S(1)} %constant_dynamic-update-slice_fusion.16.near_0), channel_id=1, source_target_pairs={{0,16},{16,32},{32,48},{48,0},{64,80},{80,96},{96,112},{112,64},{1... | collective-permute-start | bytes 3538952 | tf_op jit(solution)/shard_map/ppermute | solution.py:29
  174.9 28.3 %collective-permute-start.21 = (bf16[1152,512]{1,0:T(8,128)(2,1)S(1)}, bf16[1152,512]{1,0:T(8,128)(2,1)S(1)}, u32[]{:S(2)}, u32[]{:S(2)}) collective-permute-start(bf16[1152,512]{1,0:T(8,128)(2,1)S(1)} %constant_dynamic-update-slice_fusion.16.near_0), channel_id=1, source_target_pairs={{0,48},{16,0},{32,16},{48,32},{64,112},{80,64},{96,80},{112,96},{1... | collective-permute-start | bytes 3538952 | tf_op jit(solution)/shard_map/ppermute | solution.py:30
  178.6 7.8 %collective-permute-start.24 = (bf16[288,512]{1,0:T(8,128)(2,1)S(1)}, bf16[288,512]{1,0:T(8,128)(2,1)S(1)}, u32[]{:S(2)}, u32[]{:S(2)}) collective-permute-start(bf16[288,512]{1,0:T(8,128)(2,1)S(1)} %slice.118), channel_id=1, source_target_pairs={{0,64},{16,80},{32,96},{48,112},{64,128},{80,144},{96,160},{112,17... | collective-permute-start | bytes 884744 | tf_op jit(solution)/shard_map/ppermute | solution.py:31
  182.0 7.7 %collective-permute-start.25 = (bf16[288,512]{1,0:T(8,128)(2,1)S(1)}, bf16[288,512]{1,0:T(8,128)(2,1)S(1)}, u32[]{:S(2)}, u32[]{:S(2)}) collective-permute-start(bf16[288,512]{1,0:T(8,128)(2,1)S(1)} %slice.119), channel_id=1, source_target_pairs={{0,192},{16,208},{32,224},{48,240},{64,0},{80,16},{96,32},{112,48}... | collective-permute-start | bytes 884744 | tf_op jit(solution)/shard_map/ppermute | solution.py:32
  189.8 26.5 %copy-start.14 = (bf16[576,512]{1,0:T(8,128)(2,1)}, bf16[576,512]{1,0:T(8,128)(2,1)S(1)}, u32[]{:S(2)}) copy-start(bf16[576,512]{1,0:T(8,128)(2,1)S(1)} %constant_dynamic-update-slice_fusion.18.last_0) | copy-start | bytes 1769476
  189.8 24.2 %collective-permute-start.26 = (bf16[576,512]{1,0:T(8,128)(2,1)S(1)}, bf16[576,512]{1,0:T(8,128)(2,1)S(1)}, u32[]{:S(2)}, u32[]{:S(2)}) collective-permute-start(bf16[576,512]{1,0:T(8,128)(2,1)S(1)} %constant_dynamic-update-slice_fusion.18.last_0), channel_id=1, source_target_pairs={{0,16},{16,32},{32,48},{48,0},{64,80},{80,96},{96,112},{112,64},{1... | collective-permute-start | bytes 1769480 | tf_op jit(solution)/shard_map/ppermute | solution.py:29
  189.9 25.7 %collective-permute-start.27 = (bf16[576,512]{1,0:T(8,128)(2,1)S(1)}, bf16[576,512]{1,0:T(8,128)(2,1)S(1)}, u32[]{:S(2)}, u32[]{:S(2)}) collective-permute-start(bf16[576,512]{1,0:T(8,128)(2,1)S(1)} %constant_dynamic-update-slice_fusion.18.last_0), channel_id=1, source_target_pairs={{0,48},{16,0},{32,16},{48,32},{64,112},{80,64},{96,80},{112,96},{1... | collective-permute-start | bytes 1769480 | tf_op jit(solution)/shard_map/ppermute | solution.py:30
  202.2 1.0 copy-start.2
  203.2 29.8 %collective-permute-start.22 = (bf16[576,512]{1,0:T(8,128)(2,1)}, bf16[576,512]{1,0:T(8,128)(2,1)}, u32[]{:S(2)}, u32[]{:S(2)}) collective-permute-start(bf16[576,512]{1,0:T(8,128)(2,1)} %slice.116), channel_id=1, source_target_pairs={{0,16},{16,32},{32,48},{48,0},{64,80},{80,96},{96,112},{112,64},{1... | collective-permute-start | bytes 1769480 | tf_op jit(solution)/shard_map/ppermute | solution.py:31
  204.1 1.0 copy-start.4
  205.1 27.9 %collective-permute-start.23 = (bf16[576,512]{1,0:T(8,128)(2,1)}, bf16[576,512]{1,0:T(8,128)(2,1)}, u32[]{:S(2)}, u32[]{:S(2)}) collective-permute-start(bf16[576,512]{1,0:T(8,128)(2,1)} %slice.117), channel_id=1, source_target_pairs={{0,48},{16,0},{32,16},{48,32},{64,112},{80,64},{96,80},{112,96},{1... | collective-permute-start | bytes 1769480 | tf_op jit(solution)/shard_map/ppermute | solution.py:32
  214.7 0.8 copy-start.10
  215.5 17.5 %collective-permute-start.28 = (bf16[288,512]{1,0:T(8,128)(2,1)}, bf16[288,512]{1,0:T(8,128)(2,1)}, u32[]{:S(2)}, u32[]{:S(2)}) collective-permute-start(bf16[288,512]{1,0:T(8,128)(2,1)} %slice.120), channel_id=1, source_target_pairs={{0,16},{16,32},{32,48},{48,0},{64,80},{80,96},{96,112},{112,64},{1... | collective-permute-start | bytes 884744 | tf_op jit(solution)/shard_map/ppermute | solution.py:31
  216.3 0.8 copy-start.12
  217.1 15.9 %collective-permute-start.29 = (bf16[288,512]{1,0:T(8,128)(2,1)}, bf16[288,512]{1,0:T(8,128)(2,1)}, u32[]{:S(2)}, u32[]{:S(2)}) collective-permute-start(bf16[288,512]{1,0:T(8,128)(2,1)} %slice.121), channel_id=1, source_target_pairs={{0,48},{16,0},{32,16},{48,32},{64,112},{80,64},{96,80},{112,96},{1... | collective-permute-start | bytes 884744 | tf_op jit(solution)/shard_map/ppermute | solution.py:32
  233.1 1.1 copy-start.1
  234.2 1.3 copy-start.3
  235.4 1.3 copy-start.5
  236.7 1.3 copy-start.7
  238.0 1.1 copy-start.9
  239.0 1.1 copy-start.11
  240.1 1.1 copy-start.13
  241.2 1.1 copy-start.15
  242.2 2.9 copy-start.16
  245.1 1.0 copy-start.18
  246.1 1.0 copy-start.20
Sparse Core Ops, SparseCore 0:
  15.3 74.6 all-gather.5
  172.7 58.7 all-gather.3

commit v7 on v5

--- a/solution.py
+++ b/solution.py
@@ -25,12 +25,25 @@
 AWAY = (0, -1, 1, 2)
 
 
+def after(block, *others):
+    flag = jnp.isnan(sum(other[0, 0] for other in others))
+    return jnp.where(flag, jnp.zeros_like(block), block)
+
+
+def hop(block, axis, steps):
+    return lax.ppermute(block, axis, steps[1]), lax.ppermute(block, axis, steps[-1])
+
+
+def relay(near, axis, steps, cut, first=()):
+    top, bottom = near[0][:cut], near[1][cut:]
+    if first:
+        top, bottom = after(top, *first), after(bottom, *first)
+    return lax.ppermute(top, axis, steps[1]), lax.ppermute(bottom, axis, steps[-1])
+
+
 def ring4(block, axis, steps, cut):
-    below = lax.ppermute(block, axis, steps[1])
-    above = lax.ppermute(block, axis, steps[-1])
-    far_top = lax.ppermute(below[:cut], axis, steps[1])
-    far_bottom = lax.ppermute(above[cut:], axis, steps[-1])
-    return [block, below, above, far_top, far_bottom]
+    near = hop(block, axis, steps)
+    return [block, *near, *relay(near, axis, steps, cut)]
 
 
 def three_terms(value):
@@ -67,7 +80,7 @@
         (own_3, near_3, last_3),
     ):
         blocks += [(own, 0), (near, 0), (near, size), (last, 0)]
-    after = NSEQ * 32
+    gradient_rows = NSEQ * 32
 
     @pl.when(n == 0)
     def _():
@@ -80,7 +93,7 @@
             far[top.shape[0] :, :] = bottom[...]
         for k, (ref, row) in enumerate(blocks):
             start = pl.multiple_of(place[k] * 64, 64)
-            right[pl.ds(start, 64), :] = ref[row + after : row + after + 64, :dj]
+            right[pl.ds(start, 64), :] = ref[row + gradient_rows : row + size, :dj]
         total = jnp.sum(ql[:, :, 64:].astype(F32))
         inverse[...] = 1.0 / (eig[...] + (0.1 / (D * H)) * total)
         for e in range(NSEQ):
@@ -110,7 +123,9 @@
     di, dj = eigvals.shape
 
     def whole(x):
-        return pl.BlockSpec(x.shape, lambda n, rank=x.ndim: (0,) * rank)
+        return pl.BlockSpec(
+            x.shape, lambda n, rank=x.ndim: (0,) * rank, pipeline_mode=pl.Buffered(1)
+        )
 
     return pl.pallas_call(
         score_kernel,
@@ -132,7 +147,7 @@
             pltpu.VMEM(blocks[10].shape, BF16),
             pltpu.VMEM((SEQLEN, blocks[0].shape[1]), BF16),
         ],
-        compiler_params=pltpu.CompilerParams(vmem_limit_bytes=48 * 1024 * 1024),
+        compiler_params=pltpu.CompilerParams(vmem_limit_bytes=28 * 1024 * 1024),
         cost_estimate=pl.CostEstimate(
             flops=10_000_000_000, bytes_accessed=16_000_000, transcendentals=0
         ),
@@ -161,11 +176,15 @@
         "shard",
         axis=0,
     )
-    rows_ring = jnp.concatenate(ring4(train_in[0, 16:], "shard", SHARD_Z, 8), 0)
-    rows_ring = jnp.concatenate(ring4(rows_ring, "shard", SHARD_Y, 32), 0)
-
     block = jnp.concatenate([train_grad[0], lax.ppermute(train_grad[0], "example", EXAMPLE_Z)], 0)
-    block = jnp.concatenate(ring4(block, "example", EXAMPLE_X, 32), 0)
+    rows_own = train_in[0, 16:]
+    rows_near = hop(rows_own, "shard", SHARD_Z)
+    near = hop(block, "example", EXAMPLE_X)
+    rows_far = relay(rows_near, "shard", SHARD_Z, 8, near)
+    far = relay(near, "example", EXAMPLE_X, 32, rows_near)
+    block = jnp.concatenate([block, *near, after(far[0], *rows_far), far[1]], 0)
+    rows_z = jnp.concatenate([rows_own, *rows_near, *rows_far], 0)
+    rows_y = hop(rows_z, "shard", SHARD_Y)
     other = lax.ppermute(block, "example", EXAMPLE_CORE)
     query_right = jnp.dot(
         query_out.reshape(64, H), basis_out, preferred_element_type=F32
@@ -174,7 +193,10 @@
         jnp.dot(b, basis_out, preferred_element_type=F32).astype(BF16)
         for b in (block, other)
     ]
-    part_out = jnp.concatenate(part_out + [query_right], 0)
+    rows_ring = jnp.concatenate(
+        [rows_z, *rows_y, *relay(rows_y, "shard", SHARD_Y, 32, part_out[1:])], 0
+    )
+    part_out = jnp.concatenate(part_out + [after(query_right, *rows_y)], 0)
     part_out = with_layout_constraint(jnp.pad(part_out, ((0, 0), (0, 512 - dj))), row_major)
     z_blocks = ring4(part_out, "shard", SHARD_Z, 288)
     near = jnp.concatenate(z_blocks[1:3], 0)
@@ -202,8 +224,7 @@
     ).astype(BF16)
     eig_shard = corner(jnp.sum(rows_all[:, :, D:].astype(F32)), (di, 64))
     ein = jnp.concatenate([own_in.T, query_left.T, eig_shard], 1)
-    flag = jnp.isnan(sum(b[0, 0] for b in z_blocks[1:3] + blocks[1:3]))
-    ein = jnp.where(flag, jnp.zeros_like(ein), ein)
+    ein = after(ein, *z_blocks[1:3], *blocks[3:5])
     ein = lax.all_gather(ein, "example", axis=0)
 
     partial = score_call(place, slot, ein, blocks, eigvals)[:, :NSEQ]

time: 284 us -> 315 us (1.11)
  local copies, waits for them, and re-layouts: 41.1 us -> 63.3 us
  starting transfers between devices: 57.4 us -> 44.7 us
  waiting for transfers between devices: 78.5 us -> 85.2 us
  between operations: 24.3 us -> 30.9 us
  matrix products: 22.4 us -> 25.8 us
  other arithmetic: 12.7 us -> 16.1 us
    unnamed x78 -> x73, local copies, waits for them, and re-layouts: 21.4 us -> 39.3 us
    ppermute x1, starting transfers between devices: 13.7 us -> 2.2 us  [shards(): other = lax.ppermute(block, 'example', EXAMPLE_CORE)]
    ppermute x28, waiting for transfers between devices: 78.4 us -> 84.8 us  [the longest x7 41.6 us: relay(): lax.ppermute(top, axis, steps[1])]
    slice x18 -> x21, local copies, waits for them, and re-layouts: 9.16 us -> 13.8 us  [the longest x13 9.59 us: after(): flag = jnp.isnan(sum((other[0, 0] for other in others)))]
    select_n x1 -> x7, other arithmetic: 0.87 us -> 4.75 us  [after(): return jnp.where(flag, jnp.zeros_like(block), block)]
  transfers between devices with their start and end apart: 32 -> 32, of which waited for: 12 -> 10; matrix products, arithmetic and copies ran while one was open for 19% -> 23% of each run, Pallas kernels for 0% -> 0%
where the time goes in v7:
time: 315 us; the launch traced here: 313 us
  waiting for transfers between devices  85.2 us (27%)
  local copies, waits for them, and re-layouts  63.3 us (20%)
  starting transfers between devices  44.7 us (14%)
  between operations  30.9 us (10%)
  matrix products  25.8 us (8%)
  blocking collectives  25.8 us (8%)
  Pallas kernels  21.3 us (7%)
  other arithmetic  16.1 us (5%)
    ppermute x7, waiting for transfers between devices, relay(): lax.ppermute(top, axis, steps[1])  41.6 us
    unnamed x73, local copies, waits for them, and re-layouts  39.3 us
    ppermute x7, waiting for transfers between devices, hop(): lax.ppermute(block, axis, steps[1])  31.4 us
    all_to_all x1, blocking collectives, shards(): pieces = lax.all_to_all(pieces, ('shard', 'example'), 0, 0, tiled=True)  25.8 us
    pallas_call x1, Pallas kernels, score_call(): pl.pallas_call(score_kernel, grid=(NSEQ,), in_specs=[pl.BlockSpec(memory_...  21.3 us
    ppermute x7, starting transfers between devices, hop(): lax.ppermute(block, axis, steps[-1])  14.5 us
    ppermute x7, starting transfers between devices, relay(): lax.ppermute(bottom, axis, steps[-1])  14 us
    dot_general x2, matrix products, shards(): jnp.dot(b, basis_out, preferred_element_type=F32).astype(BF16)  12 us
  transfers between devices with their start and end apart: 32, of which 10 were waited for; matrix products, arithmetic and copies ran while one was open for 23% of the time, Pallas kernels for 0%

profile of v7, /device:TPU:1, one launch (start us, length us, event | category | flops | bytes accessed | tf_op | source)
XLA Modules:
  0.0 312.9 jit_solution(3671326280219907489)
XLA Ops:
  6.5 1.8 slice_bitcast_fusion.1
  8.4 3.8 %collective-permute-start.3 = (bf16[16,5120]{1,0:T(8,128)(2,1)}, bf16[16,5120]{1,0:T(8,128)(2,1)}, u32[]{:S(2)}, u32[]{:S(2)}) collective-permute-start(bf16[16,5120]{1,0:T(8,128)(2,1)} %get-tuple-element.7), channel_id=1, source_target_pairs={{0,64},{16,80},{32,96},{48,112},{64,128},{80,144},{96,160},{112,17... | collective-permute-start | bytes 491528 | tf_op jit(solution)/shard_map/ppermute | solution.py:34
  12.2 3.0 collective-permute-start.5
  16.0 1.9 reduce_sum.27
  21.5 1.4 select_convert_fusion.1
  23.6 1.7 constant_dynamic-update-slice_fusion.9
  25.3 1.8 constant_dynamic-update-slice_fusion.4
  27.4 2.7 fusion.3
  31.5 1.7 constant_dynamic-update-slice_fusion.8
  33.4 1.2 pad_maximum_fusion
  34.6 1.3 collective-permute-start.1
  35.9 1.5 collective-permute-start.2
  37.4 1.7 constant_dynamic-update-slice_fusion.7
  39.1 1.2 slice.139
  40.2 1.2 slice.140
  42.8 1.8 constant_dynamic-update-slice_fusion.3
  44.6 11.5 %collective-permute-done.1 = bf16[64,6912]{1,0:T(8,128)(2,1)S(1)} collective-permute-done((bf16[64,6912]{1,0:T(8,128)(2,1)S(1)}, bf16[64,6912]{1,0:T(8,128)(2,1)S(1)}, u32[]{:S(2)}, u32[]{:S(2)}) %collective-permute-start.1) | collective-permute-done | bytes 884768 | tf_op jit(solution)/shard_map/ppermute | solution.py:34
  60.9 3.1 collective-permute-start.6
  64.5 2.3 collective-permute-start.8
  69.4 5.4 %collective-permute-done.6 = bf16[8,5120]{1,0:T(8,128)(2,1)S(1)} collective-permute-done((bf16[8,5120]{1,0:T(8,128)(2,1)S(1)}, bf16[8,5120]{1,0:T(8,128)(2,1)S(1)}, u32[]{:S(2)}, u32[]{:S(2)}) %collective-permute-start.6) | collective-permute-done | bytes 81952 | tf_op jit(solution)/shard_map/ppermute | solution.py:41
  79.0 2.2 collective-permute-start.9
  82.9 1.7 collective-permute-start.11
  84.6 6.2 %convolution_convert_fusion.1 = bf16[256,432]{0,1:T(8,128)(2,1)} fusion(bf16[256,6912]{1,0:T(8,128)(2,1)} %constant_dynamic-update-slice_fusion, bf16[6912,432]{0,1:T(8,128)(2,1)} %param.12), kind=kOutput, calls=%fused_computation.1 | convolution fusion | flops 1528934400 | bytes 9732096 | tf_op jit(solution)/shard_map/dot_general | solution.py:193
  90.8 1.1 copy.22
  91.9 11.1 %collective-permute-done.10 = bf16[64,5120]{1,0:T(8,128)(2,1)} collective-permute-done((bf16[64,5120]{1,0:T(8,128)(2,1)}, bf16[64,5120]{1,0:T(8,128)(2,1)}, u32[]{:S(2)}, u32[]{:S(2)}) %collective-permute-start.10) | collective-permute-done | bytes 655392 | tf_op jit(solution)/shard_map/ppermute | solution.py:34
  103.0 1.2 slice.143
  104.2 1.2 slice.144
  106.6 5.5 %broadcast_select_fusion = bf16[64,432]{1,0:T(8,128)(2,1)} fusion(pred[]{:T(512)} %bitcast.21, bf16[64,6912]{1,0:T(8,128)(2,1)} %bitcast.72, bf16[6912,432]{0,1:T(8,128)(2,1)} %param.12), kind=kOutput, calls=%fused_computation.29 | convolution fusion | flops 382261248 | bytes 6912001 | tf_op jit(solution)/shard_map/dot_general | solution.py:189
  112.1 1.9 constant_dynamic-update-slice_fusion.13
  114.0 2.0 constant_dynamic-update-slice_fusion.12
  116.0 3.4 %slice.151 = bf16[16,16,5120]{2,1,0:T(8,128)(2,1)} slice(bf16[16,16,5248]{2,1,0:T(8,128)(2,1)} %bitcast.67), slice={[0:16], [0:16], [0:5120]} | slice | bytes 5242880 | tf_op jit(solution)/shard_map/slice | solution.py:213
  119.4 1.5 convert_reduce_fusion
  124.6 2.2 fusion.8
  126.8 2.8 fusion.14
  129.6 5.8 %convolution_convert_fusion = bf16[256,432]{1,0:T(8,128)(2,1)S(1)} fusion(bf16[256,6912]{1,0:T(8,128)(2,1)} %collective-permute-done.9, bf16[6912,432]{0,1:T(8,128)(2,1)} %param.12), kind=kOutput, calls=%fused_computation | convolution fusion | flops 1528934400 | bytes 9732096 | tf_op jit(solution)/shard_map/dot_general | solution.py:193
  135.5 3.3 %collective-permute-start.12 = (bf16[576,512]{1,0:T(8,128)(2,1)S(1)}, bf16[576,512]{1,0:T(8,128)(2,1)S(1)}, u32[]{:S(2)}, u32[]{:S(2)}) collective-permute-start(bf16[576,512]{1,0:T(8,128)(2,1)S(1)} %fusion.6.own_0), channel_id=1, source_target_pairs={{0,64},{16,80},{32,96},{48,112},{64,128},{80,144},{96,160},{112,17... | collective-permute-start | bytes 1769480 | tf_op jit(solution)/shard_map/ppermute | solution.py:34
  139.2 2.7 collective-permute-start.16
  145.8 15.3 %collective-permute-done.18 = bf16[32,5120]{1,0:T(8,128)(2,1)S(1)} collective-permute-done((bf16[32,5120]{1,0:T(8,128)(2,1)S(1)}, bf16[32,5120]{1,0:T(8,128)(2,1)S(1)}, u32[]{:S(2)}, u32[]{:S(2)}) %collective-permute-start.18) | collective-permute-done | bytes 327712 | tf_op jit(solution)/shard_map/ppermute | solution.py:41
  161.9 6.4 %collective-permute-done.19 = bf16[32,5120]{1,0:T(8,128)(2,1)S(1)} collective-permute-done((bf16[32,5120]{1,0:T(8,128)(2,1)S(1)}, bf16[32,5120]{1,0:T(8,128)(2,1)S(1)}, u32[]{:S(2)}, u32[]{:S(2)}) %collective-permute-start.19) | collective-permute-done | bytes 327712 | tf_op jit(solution)/shard_map/ppermute | solution.py:41
  170.7 2.0 collective-permute-start.17
  172.7 2.8 fusion.15
  182.7 1.2 constant_dynamic-update-slice_fusion.20
  183.9 1.1 constant_dynamic-update-slice_fusion.19.near_0
  185.1 2.7 collective-permute-start.21
  188.7 2.3 collective-permute-start.24
  191.1 1.4 collective-permute-start.25
  192.5 12.2 %collective-permute-done.24 = bf16[288,512]{1,0:T(8,128)(2,1)S(1)} collective-permute-done((bf16[288,512]{1,0:T(8,128)(2,1)S(1)}, bf16[288,512]{1,0:T(8,128)(2,1)S(1)}, u32[]{:S(2)}, u32[]{:S(2)}) %collective-permute-start.24) | collective-permute-done | bytes 294944 | tf_op jit(solution)/shard_map/ppermute | solution.py:41
  204.8 2.7 collective-permute-start.27
  207.5 2.7 collective-permute-done.20.near_1
  211.1 1.1 copy-done.4
  214.1 2.7 collective-permute-start.23
  216.8 6.1 %collective-permute-done.26.last_1 = bf16[576,512]{1,0:T(8,128)(2,1)S(1)} collective-permute-done((bf16[576,512]{1,0:T(8,128)(2,1)S(1)}, bf16[576,512]{1,0:T(8,128)(2,1)S(1)}, u32[]{:S(2)}, u32[]{:S(2)}) %collective-permute-start.26) | collective-permute-done | bytes 589856 | tf_op jit(solution)/shard_map/ppermute | solution.py:34
  225.4 2.5 collective-permute-start.29
  227.9 14.0 %collective-permute-done.28.last_top = bf16[288,512]{1,0:T(8,128)(2,1)} collective-permute-done((bf16[288,512]{1,0:T(8,128)(2,1)}, bf16[288,512]{1,0:T(8,128)(2,1)}, u32[]{:S(2)}, u32[]{:S(2)}) %collective-permute-start.28) | collective-permute-done | bytes 294944 | tf_op jit(solution)/shard_map/ppermute | solution.py:41
  242.0 1.1 copy-done.1
  243.1 1.1 copy-done.3
  244.1 1.3 copy-done.5
  245.4 1.3 copy-done.7
  246.7 1.3 copy-done.9
  247.9 1.1 copy-done.11
  252.2 1.1 copy-done.19
  253.3 2.9 copy-done.20
  258.1 21.3 %shard_map.82 = f32[32,128]{1,0:T(8,128)S(1)} custom-call(s32[16]{0:T(128)S(1)} %stack.67.place, s32[16]{0:T(128)S(1)} %fusion.9.slot, bf16[16,320,640]{2,1,0:T(8,128)(2,1)S(1)} %copy-done.20, bf16[16,320,640]{2,1,0:T(8,128)(2,1)S(1)} %copy-done.20, bf16[576,512]{1,0:T(8,128)(2,1)S(1)} %copy-done.3, bf16[576,512]{1,0:T(8,128)(2,1)S(1)} %copy-done.11, ...), custom_call_target="tpu_custom_call" | custom-call | flops 10000000000 | bytes 16000000 | tf_op jit(solution)/shard_map/pallas_call | solution.py:130
  279.5 25.8 %all_to_all.9 = f32[256,1,2]{2,1,0:T(1,128)S(1)} all-to-all(f32[256,1,2]{2,1,0:T(1,128)S(1)} %bitcast.73), channel_id=1, replica_groups=mesh['shard'=16,'example'=16] {'shard','example'}, dimensions={0} | all-to-all | bytes 4096 | tf_op jit(solution)/shard_map/all_to_all | solution.py:232
  (146 shorter events, 37.2 us)
Async XLA Ops:
  6.5 20.8 %copy-start = (bf16[5120,320]{0,1:T(8,128)(2,1)S(1)}, bf16[5120,320]{0,1:T(8,128)(2,1)}, u32[]{:S(2)}) copy-start(bf16[5120,320]{0,1:T(8,128)(2,1)} %param.11) | copy-start | bytes 9830404
  6.5 109.4 %all-gather.6.cloned.1.call-start = ((), (), s32[]{:S(2)}) async-start(), calls=%async_computation.2 | async-start | bytes 2854912 | tf_op jit(solution)/shard_map/all_gather | solution.py:174
  8.4 23.1 %collective-permute-start.3 = (bf16[16,5120]{1,0:T(8,128)(2,1)}, bf16[16,5120]{1,0:T(8,128)(2,1)}, u32[]{:S(2)}, u32[]{:S(2)}) collective-permute-start(bf16[16,5120]{1,0:T(8,128)(2,1)} %get-tuple-element.7), channel_id=1, source_target_pairs={{0,64},{16,80},{32,96},{48,112},{64,128},{80,144},{96,160},{112,17... | collective-permute-start | bytes 491528 | tf_op jit(solution)/shard_map/ppermute | solution.py:34
  12.2 25.2 %collective-permute-start.5 = (bf16[16,5120]{1,0:T(8,128)(2,1)}, bf16[16,5120]{1,0:T(8,128)(2,1)}, u32[]{:S(2)}, u32[]{:S(2)}) collective-permute-start(bf16[16,5120]{1,0:T(8,128)(2,1)} %get-tuple-element.7), channel_id=1, source_target_pairs={{0,192},{16,208},{32,224},{48,240},{64,0},{80,16},{96,32},{112,48}... | collective-permute-start | bytes 491528 | tf_op jit(solution)/shard_map/ppermute | solution.py:34
  15.2 18.2 %collective-permute-start = (bf16[32,6912]{1,0:T(8,128)(2,1)}, bf16[32,6912]{1,0:T(8,128)(2,1)}, u32[]{:S(2)}, u32[]{:S(2)}) collective-permute-start(bf16[32,6912]{1,0:T(8,128)(2,1)} %bitcast.70), channel_id=1, source_target_pairs={{0,8},{1,9},{2,10},{3,11},{4,12},{5,13},{6,14},{7,15},{8,0},{9,1},... | collective-permute-start | bytes 1327112 | tf_op jit(solution)/shard_map/ppermute | solution.py:179
  23.5 218.4 %all-gather.4.cloned.1.call-start = ((), (), s32[]{:S(2)}) async-start(), calls=%async_computation.1 | async-start | bytes 6963200 | tf_op jit(solution)/shard_map/all_gather | solution.py:228
  34.6 21.4 %collective-permute-start.1 = (bf16[64,6912]{1,0:T(8,128)(2,1)S(1)}, bf16[64,6912]{1,0:T(8,128)(2,1)S(1)}, u32[]{:S(2)}, u32[]{:S(2)}) collective-permute-start(bf16[64,6912]{1,0:T(8,128)(2,1)S(1)} %pad_maximum_fusion), channel_id=1, source_target_pairs={{0,2},{1,3},{2,4},{3,5},{4,6},{5,7},{6,0},{7,1},{8,10},{9,11},{10,... | collective-permute-start | bytes 2654216 | tf_op jit(solution)/shard_map/ppermute | solution.py:34
  35.9 20.7 %collective-permute-start.2 = (bf16[64,6912]{1,0:T(8,128)(2,1)S(1)}, bf16[64,6912]{1,0:T(8,128)(2,1)S(1)}, u32[]{:S(2)}, u32[]{:S(2)}) collective-permute-start(bf16[64,6912]{1,0:T(8,128)(2,1)S(1)} %pad_maximum_fusion), channel_id=1, source_target_pairs={{0,6},{1,7},{2,0},{3,1},{4,2},{5,3},{6,4},{7,5},{8,14},{9,15},{10,... | collective-permute-start | bytes 2654216 | tf_op jit(solution)/shard_map/ppermute | solution.py:34
  59.4 9.5 %collective-permute-start.4 = (bf16[8,5120]{1,0:T(8,128)(2,1)S(1)}, bf16[8,5120]{1,0:T(8,128)(2,1)S(1)}, u32[]{:S(2)}, u32[]{:S(2)}) collective-permute-start(bf16[8,5120]{1,0:T(8,128)(2,1)S(1)} %slice_select_fusion.5), channel_id=1, source_target_pairs={{0,64},{16,80},{32,96},{48,112},{64,128},{80,144},{96,160},{112,17... | collective-permute-start | bytes 245768 | tf_op jit(solution)/shard_map/ppermute | solution.py:41
  60.9 13.9 %collective-permute-start.6 = (bf16[8,5120]{1,0:T(8,128)(2,1)S(1)}, bf16[8,5120]{1,0:T(8,128)(2,1)S(1)}, u32[]{:S(2)}, u32[]{:S(2)}) collective-permute-start(bf16[8,5120]{1,0:T(8,128)(2,1)S(1)} %slice_select_fusion.4), channel_id=1, source_target_pairs={{0,192},{16,208},{32,224},{48,240},{64,0},{80,16},{96,32},{112,48}... | collective-permute-start | bytes 245768 | tf_op jit(solution)/shard_map/ppermute | solution.py:41
  64.0 13.3 %collective-permute-start.7 = (bf16[32,6912]{1,0:T(8,128)(2,1)S(1)}, bf16[32,6912]{1,0:T(8,128)(2,1)S(1)}, u32[]{:S(2)}, u32[]{:S(2)}) collective-permute-start(bf16[32,6912]{1,0:T(8,128)(2,1)S(1)} %slice_select_fusion.1), channel_id=1, source_target_pairs={{0,2},{1,3},{2,4},{3,5},{4,6},{5,7},{6,0},{7,1},{8,10},{9,11},{10,... | collective-permute-start | bytes 1327112 | tf_op jit(solution)/shard_map/ppermute | solution.py:41
  64.5 13.7 %collective-permute-start.8 = (bf16[32,6912]{1,0:T(8,128)(2,1)S(1)}, bf16[32,6912]{1,0:T(8,128)(2,1)S(1)}, u32[]{:S(2)}, u32[]{:S(2)}) collective-permute-start(bf16[32,6912]{1,0:T(8,128)(2,1)S(1)} %slice_select_fusion), channel_id=1, source_target_pairs={{0,6},{1,7},{2,0},{3,1},{4,2},{5,3},{6,4},{7,5},{8,14},{9,15},{10,... | collective-permute-start | bytes 1327112 | tf_op jit(solution)/shard_map/ppermute | solution.py:41
  79.0 50.6 %collective-permute-start.9 = (bf16[256,6912]{1,0:T(8,128)(2,1)}, bf16[256,6912]{1,0:T(8,128)(2,1)}, u32[]{:S(2)}, u32[]{:S(2)}) collective-permute-start(bf16[256,6912]{1,0:T(8,128)(2,1)} %constant_dynamic-update-slice_fusion), channel_id=1, source_target_pairs={{0,1},{1,0},{2,3},{3,2},{4,5},{5,4},{6,7},{7,6},{8,9},{9,8},{10,11... | collective-permute-start | bytes 10616840 | tf_op jit(solution)/shard_map/ppermute | solution.py:188
  81.9 21.1 %collective-permute-start.10 = (bf16[64,5120]{1,0:T(8,128)(2,1)}, bf16[64,5120]{1,0:T(8,128)(2,1)}, u32[]{:S(2)}, u32[]{:S(2)}) collective-permute-start(bf16[64,5120]{1,0:T(8,128)(2,1)} %get-tuple-element.13), channel_id=1, source_target_pairs={{0,16},{16,32},{32,48},{48,0},{64,80},{80,96},{96,112},{112,64},{1... | collective-permute-start | bytes 1966088 | tf_op jit(solution)/shard_map/ppermute | solution.py:34
  82.9 21.3 %collective-permute-start.11 = (bf16[64,5120]{1,0:T(8,128)(2,1)}, bf16[64,5120]{1,0:T(8,128)(2,1)}, u32[]{:S(2)}, u32[]{:S(2)}) collective-permute-start(bf16[64,5120]{1,0:T(8,128)(2,1)} %get-tuple-element.13), channel_id=1, source_target_pairs={{0,48},{16,0},{32,16},{48,32},{64,112},{80,64},{96,80},{112,96},{1... | collective-permute-start | bytes 1966088 | tf_op jit(solution)/shard_map/ppermute | solution.py:34
  129.6 5.8 %copy-start.28 = (bf16[64,432]{1,0:T(8,128)(2,1)S(1)}, bf16[64,432]{1,0:T(8,128)(2,1)}, u32[]{:S(2)}) copy-start(bf16[64,432]{1,0:T(8,128)(2,1)} %broadcast_select_fusion) | copy-start | bytes 165892
  135.5 40.0 %copy-start.2 = (bf16[576,512]{1,0:T(8,128)(2,1)}, bf16[576,512]{1,0:T(8,128)(2,1)S(1)}, u32[]{:S(2)}) copy-start(bf16[576,512]{1,0:T(8,128)(2,1)S(1)} %fusion.6.own_0) | copy-start | bytes 1769476
  135.5 40.0 %collective-permute-start.12 = (bf16[576,512]{1,0:T(8,128)(2,1)S(1)}, bf16[576,512]{1,0:T(8,128)(2,1)S(1)}, u32[]{:S(2)}, u32[]{:S(2)}) collective-permute-start(bf16[576,512]{1,0:T(8,128)(2,1)S(1)} %fusion.6.own_0), channel_id=1, source_target_pairs={{0,64},{16,80},{32,96},{48,112},{64,128},{80,144},{96,160},{112,17... | collective-permute-start | bytes 1769480 | tf_op jit(solution)/shard_map/ppermute | solution.py:34
  138.9 37.3 %collective-permute-start.13 = (bf16[576,512]{1,0:T(8,128)(2,1)S(1)}, bf16[576,512]{1,0:T(8,128)(2,1)S(1)}, u32[]{:S(2)}, u32[]{:S(2)}) collective-permute-start(bf16[576,512]{1,0:T(8,128)(2,1)S(1)} %fusion.6.own_0), channel_id=1, source_target_pairs={{0,192},{16,208},{32,224},{48,240},{64,0},{80,16},{96,32},{112,48}... | collective-permute-start | bytes 1769480 | tf_op jit(solution)/shard_map/ppermute | solution.py:34
  139.2 29.9 %collective-permute-start.14 = (bf16[576,512]{1,0:T(8,128)(2,1)S(1)}, bf16[576,512]{1,0:T(8,128)(2,1)S(1)}, u32[]{:S(2)}, u32[]{:S(2)}) collective-permute-start(bf16[576,512]{1,0:T(8,128)(2,1)S(1)} %fusion.6.own_0), channel_id=1, source_target_pairs={{0,16},{16,32},{32,48},{48,0},{64,80},{80,96},{96,112},{112,64},{1... | collective-permute-start | bytes 1769480 | tf_op jit(solution)/shard_map/ppermute | solution.py:34
  139.2 30.0 %collective-permute-start.16 = (bf16[576,512]{1,0:T(8,128)(2,1)S(1)}, bf16[576,512]{1,0:T(8,128)(2,1)S(1)}, u32[]{:S(2)}, u32[]{:S(2)}) collective-permute-start(bf16[576,512]{1,0:T(8,128)(2,1)S(1)} %fusion.6.own_0), channel_id=1, source_target_pairs={{0,48},{16,0},{32,16},{48,32},{64,112},{80,64},{96,80},{112,96},{1... | collective-permute-start | bytes 1769480 | tf_op jit(solution)/shard_map/ppermute | solution.py:34
  144.7 16.4 %collective-permute-start.18 = (bf16[32,5120]{1,0:T(8,128)(2,1)S(1)}, bf16[32,5120]{1,0:T(8,128)(2,1)S(1)}, u32[]{:S(2)}, u32[]{:S(2)}) collective-permute-start(bf16[32,5120]{1,0:T(8,128)(2,1)S(1)} %slice_select_fusion.3), channel_id=1, source_target_pairs={{0,16},{16,32},{32,48},{48,0},{64,80},{80,96},{96,112},{112,64},{1... | collective-permute-start | bytes 983048 | tf_op jit(solution)/shard_map/ppermute | solution.py:41
  161.1 7.2 %collective-permute-start.19 = (bf16[32,5120]{1,0:T(8,128)(2,1)S(1)}, bf16[32,5120]{1,0:T(8,128)(2,1)S(1)}, u32[]{:S(2)}, u32[]{:S(2)}) collective-permute-start(bf16[32,5120]{1,0:T(8,128)(2,1)S(1)} %slice_select_fusion.2), channel_id=1, source_target_pairs={{0,48},{16,0},{32,16},{48,32},{64,112},{80,64},{96,80},{112,96},{1... | collective-permute-start | bytes 983048 | tf_op jit(solution)/shard_map/ppermute | solution.py:41
  169.1 0.8 copy-start.10
  169.1 8.9 %collective-permute-start.15 = (bf16[288,512]{1,0:T(8,128)(2,1)S(1)}, bf16[288,512]{1,0:T(8,128)(2,1)S(1)}, u32[]{:S(2)}, u32[]{:S(2)}) collective-permute-start(bf16[288,512]{1,0:T(8,128)(2,1)S(1)} %slice.147), channel_id=1, source_target_pairs={{0,16},{16,32},{32,48},{48,0},{64,80},{80,96},{96,112},{112,64},{1... | collective-permute-start | bytes 884744 | tf_op jit(solution)/shard_map/ppermute | solution.py:41
  169.9 0.8 copy-start.12
  170.7 11.1 %copy-start.29 = (bf16[1,320,64]{2,1,0:T(8,128)(2,1)S(1)}, bf16[1,320,64]{2,1,0:T(8,128)(2,1)}, u32[]{:S(2)}) copy-start(bf16[1,320,64]{2,1,0:T(8,128)(2,1)} %fusion.3) | copy-start | bytes 122884
  170.7 9.2 %collective-permute-start.17 = (bf16[288,512]{1,0:T(8,128)(2,1)S(1)}, bf16[288,512]{1,0:T(8,128)(2,1)S(1)}, u32[]{:S(2)}, u32[]{:S(2)}) collective-permute-start(bf16[288,512]{1,0:T(8,128)(2,1)S(1)} %slice.149), channel_id=1, source_target_pairs={{0,48},{16,0},{32,16},{48,32},{64,112},{80,64},{96,80},{112,96},{1... | collective-permute-start | bytes 884744 | tf_op jit(solution)/shard_map/ppermute | solution.py:41
  175.6 6.2 %copy-start.27 = (bf16[576,512]{1,0:T(8,128)(2,1)}, bf16[576,512]{1,0:T(8,128)(2,1)S(1)}, u32[]{:S(2)}) copy-start(bf16[576,512]{1,0:T(8,128)(2,1)S(1)} %collective-permute-done.12) | copy-start | bytes 1769476
  176.1 4.3 %copy-start.25 = (bf16[576,512]{1,0:T(8,128)(2,1)}, bf16[576,512]{1,0:T(8,128)(2,1)S(1)}, u32[]{:S(2)}) copy-start(bf16[576,512]{1,0:T(8,128)(2,1)S(1)} %collective-permute-done.13) | copy-start | bytes 1769476
  178.5 0.7 copy-start.21
  180.4 0.7 copy-start.23
  182.7 8.4 %copy-start.26 = (bf16[576,512]{1,0:T(8,128)(2,1)S(1)}, bf16[576,512]{1,0:T(8,128)(2,1)}, u32[]{:S(2)}) copy-start(bf16[576,512]{1,0:T(8,128)(2,1)} %copy-done.25) | copy-start | bytes 1769476
  185.0 38.6 %copy-start.8 = (bf16[1152,512]{1,0:T(8,128)(2,1)}, bf16[1152,512]{1,0:T(8,128)(2,1)S(1)}, u32[]{:S(2)}) copy-start(bf16[1152,512]{1,0:T(8,128)(2,1)S(1)} %constant_dynamic-update-slice_fusion.19.near_0) | copy-start | bytes 3538948
  185.0 25.2 %collective-permute-start.20 = (bf16[1152,512]{1,0:T(8,128)(2,1)S(1)}, bf16[1152,512]{1,0:T(8,128)(2,1)S(1)}, u32[]{:S(2)}, u32[]{:S(2)}) collective-permute-start(bf16[1152,512]{1,0:T(8,128)(2,1)S(1)} %constant_dynamic-update-slice_fusion.19.near_0), channel_id=1, source_target_pairs={{0,16},{16,32},{32,48},{48,0},{64,80},{80,96},{96,112},{112,64},{1... | collective-permute-start | bytes 3538952 | tf_op jit(solution)/shard_map/ppermute | solution.py:34
  185.1 27.1 %collective-permute-start.21 = (bf16[1152,512]{1,0:T(8,128)(2,1)S(1)}, bf16[1152,512]{1,0:T(8,128)(2,1)S(1)}, u32[]{:S(2)}, u32[]{:S(2)}) collective-permute-start(bf16[1152,512]{1,0:T(8,128)(2,1)S(1)} %constant_dynamic-update-slice_fusion.19.near_0), channel_id=1, source_target_pairs={{0,48},{16,0},{32,16},{48,32},{64,112},{80,64},{96,80},{112,96},{1... | collective-permute-start | bytes 3538952 | tf_op jit(solution)/shard_map/ppermute | solution.py:34
  188.7 15.9 %collective-permute-start.24 = (bf16[288,512]{1,0:T(8,128)(2,1)S(1)}, bf16[288,512]{1,0:T(8,128)(2,1)S(1)}, u32[]{:S(2)}, u32[]{:S(2)}) collective-permute-start(bf16[288,512]{1,0:T(8,128)(2,1)S(1)} %slice.158), channel_id=1, source_target_pairs={{0,64},{16,80},{32,96},{48,112},{64,128},{80,144},{96,160},{112,17... | collective-permute-start | bytes 884744 | tf_op jit(solution)/shard_map/ppermute | solution.py:41
  191.1 13.6 %collective-permute-start.25 = (bf16[288,512]{1,0:T(8,128)(2,1)S(1)}, bf16[288,512]{1,0:T(8,128)(2,1)S(1)}, u32[]{:S(2)}, u32[]{:S(2)}) collective-permute-start(bf16[288,512]{1,0:T(8,128)(2,1)S(1)} %slice.159), channel_id=1, source_target_pairs={{0,192},{16,208},{32,224},{48,240},{64,0},{80,16},{96,32},{112,48}... | collective-permute-start | bytes 884744 | tf_op jit(solution)/shard_map/ppermute | solution.py:41
  204.7 19.8 %copy-start.18 = (bf16[576,512]{1,0:T(8,128)(2,1)}, bf16[576,512]{1,0:T(8,128)(2,1)S(1)}, u32[]{:S(2)}) copy-start(bf16[576,512]{1,0:T(8,128)(2,1)S(1)} %constant_dynamic-update-slice_fusion.21.last_0) | copy-start | bytes 1769476
  204.7 18.1 %collective-permute-start.26 = (bf16[576,512]{1,0:T(8,128)(2,1)S(1)}, bf16[576,512]{1,0:T(8,128)(2,1)S(1)}, u32[]{:S(2)}, u32[]{:S(2)}) collective-permute-start(bf16[576,512]{1,0:T(8,128)(2,1)S(1)} %constant_dynamic-update-slice_fusion.21.last_0), channel_id=1, source_target_pairs={{0,16},{16,32},{32,48},{48,0},{64,80},{80,96},{96,112},{112,64},{1... | collective-permute-start | bytes 1769480 | tf_op jit(solution)/shard_map/ppermute | solution.py:34
  204.8 19.0 %collective-permute-start.27 = (bf16[576,512]{1,0:T(8,128)(2,1)S(1)}, bf16[576,512]{1,0:T(8,128)(2,1)S(1)}, u32[]{:S(2)}, u32[]{:S(2)}) collective-permute-start(bf16[576,512]{1,0:T(8,128)(2,1)S(1)} %constant_dynamic-update-slice_fusion.21.last_0), channel_id=1, source_target_pairs={{0,48},{16,0},{32,16},{48,32},{64,112},{80,64},{96,80},{112,96},{1... | collective-permute-start | bytes 1769480 | tf_op jit(solution)/shard_map/ppermute | solution.py:34
  211.1 1.1 copy-start.4
  212.2 29.8 %collective-permute-start.22 = (bf16[576,512]{1,0:T(8,128)(2,1)}, bf16[576,512]{1,0:T(8,128)(2,1)}, u32[]{:S(2)}, u32[]{:S(2)}) collective-permute-start(bf16[576,512]{1,0:T(8,128)(2,1)} %slice.156), channel_id=1, source_target_pairs={{0,16},{16,32},{32,48},{48,0},{64,80},{80,96},{96,112},{112,64},{1... | collective-permute-start | bytes 1769480 | tf_op jit(solution)/shard_map/ppermute | solution.py:41
  213.1 1.0 copy-start.6
  214.1 27.9 %collective-permute-start.23 = (bf16[576,512]{1,0:T(8,128)(2,1)}, bf16[576,512]{1,0:T(8,128)(2,1)}, u32[]{:S(2)}, u32[]{:S(2)}) collective-permute-start(bf16[576,512]{1,0:T(8,128)(2,1)} %slice.157), channel_id=1, source_target_pairs={{0,48},{16,0},{32,16},{48,32},{64,112},{80,64},{96,80},{112,96},{1... | collective-permute-start | bytes 1769480 | tf_op jit(solution)/shard_map/ppermute | solution.py:41
  222.9 0.9 copy-start.14
  223.6 18.3 %collective-permute-start.28 = (bf16[288,512]{1,0:T(8,128)(2,1)}, bf16[288,512]{1,0:T(8,128)(2,1)}, u32[]{:S(2)}, u32[]{:S(2)}) collective-permute-start(bf16[288,512]{1,0:T(8,128)(2,1)} %slice.160), channel_id=1, source_target_pairs={{0,16},{16,32},{32,48},{48,0},{64,80},{80,96},{96,112},{112,64},{1... | collective-permute-start | bytes 884744 | tf_op jit(solution)/shard_map/ppermute | solution.py:41
  224.5 0.8 copy-start.16
  225.4 16.6 %collective-permute-start.29 = (bf16[288,512]{1,0:T(8,128)(2,1)}, bf16[288,512]{1,0:T(8,128)(2,1)}, u32[]{:S(2)}, u32[]{:S(2)}) collective-permute-start(bf16[288,512]{1,0:T(8,128)(2,1)} %slice.161), channel_id=1, source_target_pairs={{0,48},{16,0},{32,16},{48,32},{64,112},{80,64},{96,80},{112,96},{1... | collective-permute-start | bytes 884744 | tf_op jit(solution)/shard_map/ppermute | solution.py:41
  242.0 1.1 copy-start.1
  243.1 1.1 copy-start.3
  244.1 1.3 copy-start.5
  245.4 1.3 copy-start.7
  246.7 1.3 copy-start.9
  247.9 1.1 copy-start.11
  249.0 1.1 copy-start.13
  250.1 1.1 copy-start.15
  251.1 1.1 copy-start.17
  252.2 1.1 copy-start.19
  253.3 2.9 copy-start.20
  256.1 1.0 copy-start.22
  257.1 1.0 copy-start.24
Sparse Core Ops, SparseCore 0:
  23.7 69.1 all-gather.5
  182.8 53.8 all-gather.3

commit v8 on v5

--- a/solution.py
+++ b/solution.py
@@ -162,13 +162,16 @@
         axis=0,
     )
     rows_ring = jnp.concatenate(ring4(train_in[0, 16:], "shard", SHARD_Z, 8), 0)
-    rows_ring = jnp.concatenate(ring4(rows_ring, "shard", SHARD_Y, 32), 0)
+    rows_y = ring4(rows_ring, "shard", SHARD_Y, 32)
+    rows_ring = jnp.concatenate(rows_y, 0)
 
     block = jnp.concatenate([train_grad[0], lax.ppermute(train_grad[0], "example", EXAMPLE_Z)], 0)
     block = jnp.concatenate(ring4(block, "example", EXAMPLE_X, 32), 0)
     other = lax.ppermute(block, "example", EXAMPLE_CORE)
     query_right = jnp.dot(
-        query_out.reshape(64, H), basis_out, preferred_element_type=F32
+        jnp.where(jnp.isnan(rows_y[1][0, 0]), jnp.zeros((64, H), BF16), query_out.reshape(64, H)),
+        basis_out,
+        preferred_element_type=F32,
     ).astype(BF16)
     part_out = [
         jnp.dot(b, basis_out, preferred_element_type=F32).astype(BF16)

time: 284 us -> 279 us (0.982)
  starting transfers between devices: 57.4 us -> 52.3 us
    ppermute x1, starting transfers between devices: 13.7 us -> 6.38 us  [shards(): other = lax.ppermute(block, 'example', EXAMPLE_CORE)]
    ppermute x7, starting transfers between devices: 10.4 us -> 3.97 us  [ring4(): far_top = lax.ppermute(below[:cut], axis, steps[1])]
    ppermute x7, starting transfers between devices: 7.89 us -> 14 us  [ring4(): far_bottom = lax.ppermute(above[cut:], axis, steps[-1])]
    ppermute x7, waiting for transfers between devices: 34.4 us -> 38.2 us  [ring4(): below = lax.ppermute(block, axis, steps[1])]
    ppermute x7, waiting for transfers between devices: 31.2 us -> 27.6 us  [ring4(): far_top = lax.ppermute(below[:cut], axis, steps[1])]
    dot_general x1, matrix products: 5.52 us -> 2.49 us  [shards(): jnp.dot(jnp.where(jnp.isnan(rows_y[1][0, 0]), jnp.zeros((64, H), BF16), q...]
where the time goes in v8:
time: 279 us; the launch traced here: 277 us
  waiting for transfers between devices  79.4 us (28%)
  starting transfers between devices  52.3 us (19%)
  local copies, waits for them, and re-layouts  41.7 us (15%)
  between operations  25.6 us (9%)
  Pallas kernels  22.5 us (8%)
  blocking collectives  22.5 us (8%)
  matrix products  20.6 us (7%)
  other arithmetic  12.8 us (5%)
    ppermute x7, waiting for transfers between devices, ring4(): below = lax.ppermute(block, axis, steps[1])  38.2 us
    ppermute x7, waiting for transfers between devices, ring4(): far_top = lax.ppermute(below[:cut], axis, steps[1])  27.6 us
    pallas_call x1, Pallas kernels, score_call(): pl.pallas_call(score_kernel, grid=(NSEQ,), in_specs=[pl.BlockSpec(memory_...  22.5 us
    all_to_all x1, blocking collectives, shards(): pieces = lax.all_to_all(pieces, ('shard', 'example'), 0, 0, tiled=True)  22.5 us
    unnamed x78, local copies, waits for them, and re-layouts  21.5 us
    ppermute x7, starting transfers between devices, ring4(): above = lax.ppermute(block, axis, steps[-1])  16.5 us
    ppermute x7, starting transfers between devices, ring4(): far_bottom = lax.ppermute(above[cut:], axis, steps[-1])  14 us
    ppermute x7, waiting for transfers between devices, ring4(): far_bottom = lax.ppermute(above[cut:], axis, steps[-1])  12.4 us
  transfers between devices with their start and end apart: 32, of which 12 were waited for; matrix products, arithmetic and copies ran while one was open for 19% of the time, Pallas kernels for 0%

profile of v8, /device:TPU:1, one launch (start us, length us, event | category | flops | bytes accessed | tf_op | source)
XLA Modules:
  0.0 277.4 jit_solution(9811568128562967973)
XLA Ops:
  6.5 1.8 slice_bitcast_fusion.1
  8.4 3.8 %collective-permute-start.6 = (bf16[16,5120]{1,0:T(8,128)(2,1)}, bf16[16,5120]{1,0:T(8,128)(2,1)}, u32[]{:S(2)}, u32[]{:S(2)}) collective-permute-start(bf16[16,5120]{1,0:T(8,128)(2,1)} %get-tuple-element.7), channel_id=1, source_target_pairs={{0,64},{16,80},{32,96},{48,112},{64,128},{80,144},{96,160},{112,17... | collective-permute-start | bytes 491528 | tf_op jit(solution)/shard_map/ppermute | solution.py:29
  12.2 3.0 %collective-permute-start.7 = (bf16[16,5120]{1,0:T(8,128)(2,1)}, bf16[16,5120]{1,0:T(8,128)(2,1)}, u32[]{:S(2)}, u32[]{:S(2)}) collective-permute-start(bf16[16,5120]{1,0:T(8,128)(2,1)} %get-tuple-element.7), channel_id=1, source_target_pairs={{0,192},{16,208},{32,224},{48,240},{64,0},{80,16},{96,32},{112,48}... | collective-permute-start | bytes 491528 | tf_op jit(solution)/shard_map/ppermute | solution.py:30
  16.0 1.9 reduce_sum.27
  21.5 1.3 select_convert_fusion.1
  23.6 1.7 constant_dynamic-update-slice_fusion.10
  25.3 1.8 constant_dynamic-update-slice_fusion.5
  28.3 2.9 %fusion.3 = bf16[1,320,64]{2,1,0:T(8,128)(2,1)} fusion(bf16[5120,320]{0,1:T(8,128)(2,1)S(1)} %copy-done, bf16[64,5120]{1,0:T(8,128)(2,1)} %bitcast.72), kind=kOutput, calls=%fused_computation.8 | convolution fusion | flops 209735680 | bytes 3973120 | tf_op jit(solution)/shard_map/dot_general | solution.py:203
  32.6 1.2 collective-permute-start.8
  34.6 2.4 collective-permute-start.9
  37.0 1.0 constant_dynamic-update-slice_fusion.9
  39.1 2.0 collective-permute-done.9
  41.0 1.4 collective-permute-start.10
  42.4 1.5 collective-permute-start.15
  43.9 1.2 pad_maximum_fusion
  45.2 1.3 collective-permute-start.1
  46.5 1.5 collective-permute-start.2
  47.9 1.8 constant_dynamic-update-slice_fusion.4
  49.7 7.0 %collective-permute-done.10 = bf16[64,5120]{1,0:T(8,128)(2,1)S(1)} collective-permute-done((bf16[64,5120]{1,0:T(8,128)(2,1)S(1)}, bf16[64,5120]{1,0:T(8,128)(2,1)S(1)}, u32[]{:S(2)}, u32[]{:S(2)}) %collective-permute-start.10) | collective-permute-done | bytes 655392 | tf_op jit(solution)/shard_map/ppermute | solution.py:29
  58.9 2.6 collective-permute-start.17
  61.6 1.2 collective-permute-done.1
  63.0 2.7 collective-permute-start.4
  65.7 1.0 constant_dynamic-update-slice_fusion.3
  66.7 1.0 constant_dynamic-update-slice_fusion.2
  67.7 5.3 %collective-permute-done.3 = bf16[32,6912]{1,0:T(8,128)(2,1)S(1)} collective-permute-done((bf16[32,6912]{1,0:T(8,128)(2,1)S(1)}, bf16[32,6912]{1,0:T(8,128)(2,1)S(1)}, u32[]{:S(2)}, u32[]{:S(2)}) %collective-permute-start.3) | collective-permute-done | bytes 442400 | tf_op jit(solution)/shard_map/ppermute | solution.py:31
  74.6 6.4 %collective-permute-start.5 = (bf16[256,6912]{1,0:T(8,128)(2,1)}, bf16[256,6912]{1,0:T(8,128)(2,1)}, u32[]{:S(2)}, u32[]{:S(2)}) collective-permute-start(bf16[256,6912]{1,0:T(8,128)(2,1)} %constant_dynamic-update-slice_fusion), channel_id=1, source_target_pairs={{0,1},{1,0},{2,3},{3,2},{4,5},{5,4},{6,7},{7,6},{8,9},{9,8},{10,11... | collective-permute-start | bytes 10616840 | tf_op jit(solution)/shard_map/ppermute | solution.py:170
  81.0 2.5 convolution_convert_fusion.3
  83.6 1.8 fusion.15
  85.4 4.4 %convolution_convert_fusion.1 = bf16[256,432]{0,1:T(8,128)(2,1)} fusion(bf16[256,6912]{1,0:T(8,128)(2,1)} %constant_dynamic-update-slice_fusion, bf16[6912,432]{0,1:T(8,128)(2,1)S(1)} %bitcast.64), kind=kOutput, calls=%fused_computation.1 | convolution fusion | flops 1528934400 | bytes 9732096 | tf_op jit(solution)/shard_map/dot_general | solution.py:177
  89.8 1.1 copy.21
  90.9 3.5 %slice.105 = bf16[16,16,5120]{2,1,0:T(8,128)(2,1)} slice(bf16[16,16,5248]{2,1,0:T(8,128)(2,1)} %bitcast.66), slice={[0:16], [0:16], [0:5120]} | slice | bytes 5242880 | tf_op jit(solution)/shard_map/slice | solution.py:194
  94.4 1.5 convert_reduce_fusion
  99.4 2.6 fusion.8
  102.1 6.2 %convolution_convert_fusion = bf16[256,432]{0,1:T(8,128)(2,1)} fusion(bf16[256,6912]{1,0:T(8,128)(2,1)} %collective-permute-done.5, bf16[6912,432]{0,1:T(8,128)(2,1)} %param.12), kind=kOutput, calls=%fused_computation | convolution fusion | flops 1528934400 | bytes 9732096 | tf_op jit(solution)/shard_map/dot_general | solution.py:177
  108.3 1.8 copy.22
  110.0 1.1 fusion.6.own_0
  111.1 3.9 %collective-permute-start.11 = (bf16[576,512]{1,0:T(8,128)(2,1)S(1)}, bf16[576,512]{1,0:T(8,128)(2,1)S(1)}, u32[]{:S(2)}, u32[]{:S(2)}) collective-permute-start(bf16[576,512]{1,0:T(8,128)(2,1)S(1)} %fusion.6.own_0), channel_id=1, source_target_pairs={{0,64},{16,80},{32,96},{48,112},{64,128},{80,144},{96,160},{112,17... | collective-permute-start | bytes 1769480 | tf_op jit(solution)/shard_map/ppermute | solution.py:29
  115.0 2.6 collective-permute-start.12
  117.6 2.7 collective-permute-start.14
  120.3 2.8 %fusion.14 = bf16[256,320]{0,1:T(8,128)(2,1)S(1)} fusion(bf16[256,5120]{1,0:T(8,128)(2,1)} %bitcast.68, bf16[5120,320]{0,1:T(8,128)(2,1)S(1)} %copy-done), kind=kOutput, calls=%fused_computation.82 | convolution fusion | flops 838860800 | bytes 6062080 | tf_op jit(solution)/shard_map/dot_general | solution.py:193
  123.2 18.1 %collective-permute-done.11 = bf16[576,512]{1,0:T(8,128)(2,1)S(1)} collective-permute-done((bf16[576,512]{1,0:T(8,128)(2,1)S(1)}, bf16[576,512]{1,0:T(8,128)(2,1)S(1)}, u32[]{:S(2)}, u32[]{:S(2)}) %collective-permute-start.11) | collective-permute-done | bytes 589856 | tf_op jit(solution)/shard_map/ppermute | solution.py:29
  141.9 1.1 collective-permute-done.12
  148.5 1.2 constant_dynamic-update-slice_fusion.21
  149.7 1.1 constant_dynamic-update-slice_fusion.20.near_0
  151.0 2.6 collective-permute-start.21
  153.6 1.0 slice.113
  154.6 1.4 collective-permute-start.24
  156.0 2.5 collective-permute-start.25
  158.6 13.2 %collective-permute-done.24 = bf16[288,512]{1,0:T(8,128)(2,1)S(1)} collective-permute-done((bf16[288,512]{1,0:T(8,128)(2,1)S(1)}, bf16[288,512]{1,0:T(8,128)(2,1)S(1)}, u32[]{:S(2)}, u32[]{:S(2)}) %collective-permute-start.24) | collective-permute-done | bytes 294944 | tf_op jit(solution)/shard_map/ppermute | solution.py:31
  172.0 2.7 collective-permute-start.27
  174.7 4.5 %collective-permute-done.20.near_1 = bf16[1152,512]{1,0:T(8,128)(2,1)S(1)} collective-permute-done((bf16[1152,512]{1,0:T(8,128)(2,1)S(1)}, bf16[1152,512]{1,0:T(8,128)(2,1)S(1)}, u32[]{:S(2)}, u32[]{:S(2)}) %collective-permute-start.20) | collective-permute-done | bytes 1179680 | tf_op jit(solution)/shard_map/ppermute | solution.py:29
  181.1 2.7 collective-permute-start.23
  184.5 7.4 %collective-permute-done.26.last_1 = bf16[576,512]{1,0:T(8,128)(2,1)S(1)} collective-permute-done((bf16[576,512]{1,0:T(8,128)(2,1)S(1)}, bf16[576,512]{1,0:T(8,128)(2,1)S(1)}, u32[]{:S(2)}, u32[]{:S(2)}) %collective-permute-start.26) | collective-permute-done | bytes 589856 | tf_op jit(solution)/shard_map/ppermute | solution.py:29
  196.5 1.7 collective-permute-done.18.own_top
  199.5 10.4 %collective-permute-done.19.own_bottom = bf16[288,512]{1,0:T(8,128)(2,1)} collective-permute-done((bf16[288,512]{1,0:T(8,128)(2,1)}, bf16[288,512]{1,0:T(8,128)(2,1)}, u32[]{:S(2)}, u32[]{:S(2)}) %collective-permute-start.19) | collective-permute-done | bytes 294944 | tf_op jit(solution)/shard_map/ppermute | solution.py:32
  209.9 7.4 %collective-permute-done.28.last_top = bf16[288,512]{1,0:T(8,128)(2,1)} collective-permute-done((bf16[288,512]{1,0:T(8,128)(2,1)}, bf16[288,512]{1,0:T(8,128)(2,1)}, u32[]{:S(2)}, u32[]{:S(2)}) %collective-permute-start.28) | collective-permute-done | bytes 294944 | tf_op jit(solution)/shard_map/ppermute | solution.py:31
  217.3 1.1 copy-done.2
  218.4 1.1 copy-done.5
  219.4 1.1 copy-done.8
  220.5 1.1 copy-done.10
  221.6 1.1 copy-done.12
  222.6 1.1 copy-done.14
  224.6 22.5 %shard_map.82 = f32[32,128]{1,0:T(8,128)S(1)} custom-call(s32[16]{0:T(128)S(1)} %stack.67.place, s32[16]{0:T(128)S(1)} %fusion.9.slot, bf16[16,320,640]{2,1,0:T(8,128)(2,1)} %all-gather.4.cloned.1.call-done.ein.ql, bf16[16,320,640]{2,1,0:T(8,128)(2,1)} %all-gather.4.cloned.1.call-done.ein.ql, bf16[576,512]{1,0:T(8,128)(2,1)S(1)} %copy-done.2, ...), custom_call_target="tpu_custom_call" | custom-call | flops 10000000000 | bytes 16000000 | tf_op jit(solution)/shard_map/pallas_call | solution.py:115
  247.3 22.5 %all_to_all.9 = f32[256,1,2]{2,1,0:T(1,128)S(1)} all-to-all(f32[256,1,2]{2,1,0:T(1,128)S(1)} %bitcast.71), channel_id=1, replica_groups=mesh['shard'=16,'example'=16] {'shard','example'}, dimensions={0} | all-to-all | bytes 4096 | tf_op jit(solution)/shard_map/all_to_all | solution.py:214
  (145 shorter events, 22.4 us)
Async XLA Ops:
  6.5 21.7 %copy-start = (bf16[5120,320]{0,1:T(8,128)(2,1)S(1)}, bf16[5120,320]{0,1:T(8,128)(2,1)}, u32[]{:S(2)}) copy-start(bf16[5120,320]{0,1:T(8,128)(2,1)} %param.11) | copy-start | bytes 9830404
  6.5 84.3 %all-gather.6.cloned.1.call-start = ((), (), s32[]{:S(2)}) async-start(), calls=%async_computation.2 | async-start | bytes 2854912 | tf_op jit(solution)/shard_map/all_gather | solution.py:159
  8.4 23.3 %collective-permute-start.6 = (bf16[16,5120]{1,0:T(8,128)(2,1)}, bf16[16,5120]{1,0:T(8,128)(2,1)}, u32[]{:S(2)}, u32[]{:S(2)}) collective-permute-start(bf16[16,5120]{1,0:T(8,128)(2,1)} %get-tuple-element.7), channel_id=1, source_target_pairs={{0,64},{16,80},{32,96},{48,112},{64,128},{80,144},{96,160},{112,17... | collective-permute-start | bytes 491528 | tf_op jit(solution)/shard_map/ppermute | solution.py:29
  12.2 21.5 %collective-permute-start.7 = (bf16[16,5120]{1,0:T(8,128)(2,1)}, bf16[16,5120]{1,0:T(8,128)(2,1)}, u32[]{:S(2)}, u32[]{:S(2)}) collective-permute-start(bf16[16,5120]{1,0:T(8,128)(2,1)} %get-tuple-element.7), channel_id=1, source_target_pairs={{0,192},{16,208},{32,224},{48,240},{64,0},{80,16},{96,32},{112,48}... | collective-permute-start | bytes 491528 | tf_op jit(solution)/shard_map/ppermute | solution.py:30
  15.2 28.7 %collective-permute-start = (bf16[32,6912]{1,0:T(8,128)(2,1)}, bf16[32,6912]{1,0:T(8,128)(2,1)}, u32[]{:S(2)}, u32[]{:S(2)}) collective-permute-start(bf16[32,6912]{1,0:T(8,128)(2,1)} %bitcast.69), channel_id=1, source_target_pairs={{0,8},{1,9},{2,10},{3,11},{4,12},{5,13},{6,14},{7,15},{8,0},{9,1},... | collective-permute-start | bytes 1327112 | tf_op jit(solution)/shard_map/ppermute | solution.py:168
  23.6 193.7 %all-gather.4.cloned.1.call-start = ((), (), s32[]{:S(2)}) async-start(), calls=%async_computation.1 | async-start | bytes 6963200 | tf_op jit(solution)/shard_map/all_gather | solution.py:210
  28.2 8.8 %copy-start.28 = (bf16[64,5120]{1,0:T(8,128)(2,1)S(1)}, bf16[64,5120]{1,0:T(8,128)(2,1)}, u32[]{:S(2)}) copy-start(bf16[64,5120]{1,0:T(8,128)(2,1)} %get-tuple-element.5) | copy-start | bytes 1966084
  28.2 8.8 %copy-start.29 = (bf16[256,5120]{1,0:T(8,128)(2,1)S(1)}, bf16[256,5120]{1,0:T(8,128)(2,1)}, u32[]{:S(2)}) copy-start(bf16[256,5120]{1,0:T(8,128)(2,1)} %get-tuple-element.6) | copy-start | bytes 7864324
  28.3 15.7 %copy-start.17 = (bf16[1,32,6912]{2,1,0:T(8,128)(2,1)S(1)}, bf16[1,32,6912]{2,1,0:T(8,128)(2,1)}, u32[]{:S(2)}) copy-start(bf16[1,32,6912]{2,1,0:T(8,128)(2,1)} %param.9) | copy-start | bytes 1327108
  32.6 6.5 %collective-permute-start.8 = (bf16[8,5120]{1,0:T(8,128)(2,1)S(1)}, bf16[8,5120]{1,0:T(8,128)(2,1)S(1)}, u32[]{:S(2)}, u32[]{:S(2)}) collective-permute-start(bf16[8,5120]{1,0:T(8,128)(2,1)S(1)} %slice.98), channel_id=1, source_target_pairs={{0,64},{16,80},{32,96},{48,112},{64,128},{80,144},{96,160},{112,17... | collective-permute-start | bytes 245768 | tf_op jit(solution)/shard_map/ppermute | solution.py:31
  34.6 6.4 %collective-permute-start.9 = (bf16[8,5120]{1,0:T(8,128)(2,1)S(1)}, bf16[8,5120]{1,0:T(8,128)(2,1)S(1)}, u32[]{:S(2)}, u32[]{:S(2)}) collective-permute-start(bf16[8,5120]{1,0:T(8,128)(2,1)S(1)} %slice.99), channel_id=1, source_target_pairs={{0,192},{16,208},{32,224},{48,240},{64,0},{80,16},{96,32},{112,48}... | collective-permute-start | bytes 245768 | tf_op jit(solution)/shard_map/ppermute | solution.py:32
  37.0 24.4 %copy-start.21 = (bf16[2,32,6912]{2,1,0:T(8,128)(2,1)S(1)}, bf16[2,32,6912]{2,1,0:T(8,128)(2,1)}, u32[]{:S(2)}) copy-start(bf16[2,32,6912]{2,1,0:T(8,128)(2,1)} %param.15) | copy-start | bytes 2654212
  41.0 15.7 %collective-permute-start.10 = (bf16[64,5120]{1,0:T(8,128)(2,1)S(1)}, bf16[64,5120]{1,0:T(8,128)(2,1)S(1)}, u32[]{:S(2)}, u32[]{:S(2)}) collective-permute-start(bf16[64,5120]{1,0:T(8,128)(2,1)S(1)} %get-tuple-element.13), channel_id=1, source_target_pairs={{0,16},{16,32},{32,48},{48,0},{64,80},{80,96},{96,112},{112,64},{1... | collective-permute-start | bytes 1966088 | tf_op jit(solution)/shard_map/ppermute | solution.py:29
  42.4 16.5 %collective-permute-start.15 = (bf16[64,5120]{1,0:T(8,128)(2,1)S(1)}, bf16[64,5120]{1,0:T(8,128)(2,1)S(1)}, u32[]{:S(2)}, u32[]{:S(2)}) collective-permute-start(bf16[64,5120]{1,0:T(8,128)(2,1)S(1)} %get-tuple-element.13), channel_id=1, source_target_pairs={{0,48},{16,0},{32,16},{48,32},{64,112},{80,64},{96,80},{112,96},{1... | collective-permute-start | bytes 1966088 | tf_op jit(solution)/shard_map/ppermute | solution.py:30
  43.9 37.0 %slice-start = ((s8[5971968]{0:T(1024)(128)(4,1)}), s8[4194304]{0:T(1024)(128)(4,1)S(1)}, s32[]{:S(2)}) async-start(s8[5971968]{0:T(1024)(128)(4,1)} %bitcast.63), calls=%async_computation.3 | async-start | bytes 8388608
  45.2 17.7 %collective-permute-start.1 = (bf16[64,6912]{1,0:T(8,128)(2,1)S(1)}, bf16[64,6912]{1,0:T(8,128)(2,1)S(1)}, u32[]{:S(2)}, u32[]{:S(2)}) collective-permute-start(bf16[64,6912]{1,0:T(8,128)(2,1)S(1)} %pad_maximum_fusion), channel_id=1, source_target_pairs={{0,2},{1,3},{2,4},{3,5},{4,6},{5,7},{6,0},{7,1},{8,10},{9,11},{10,... | collective-permute-start | bytes 2654216 | tf_op jit(solution)/shard_map/ppermute | solution.py:29
  46.5 16.5 %collective-permute-start.2 = (bf16[64,6912]{1,0:T(8,128)(2,1)S(1)}, bf16[64,6912]{1,0:T(8,128)(2,1)S(1)}, u32[]{:S(2)}, u32[]{:S(2)}) collective-permute-start(bf16[64,6912]{1,0:T(8,128)(2,1)S(1)} %pad_maximum_fusion), channel_id=1, source_target_pairs={{0,6},{1,7},{2,0},{3,1},{4,2},{5,3},{6,4},{7,5},{8,14},{9,15},{10,... | collective-permute-start | bytes 2654216 | tf_op jit(solution)/shard_map/ppermute | solution.py:30
  58.6 24.9 %collective-permute-start.16 = (bf16[32,5120]{1,0:T(8,128)(2,1)S(1)}, bf16[32,5120]{1,0:T(8,128)(2,1)S(1)}, u32[]{:S(2)}, u32[]{:S(2)}) collective-permute-start(bf16[32,5120]{1,0:T(8,128)(2,1)S(1)} %slice.106), channel_id=1, source_target_pairs={{0,16},{16,32},{32,48},{48,0},{64,80},{80,96},{96,112},{112,64},{1... | collective-permute-start | bytes 983048 | tf_op jit(solution)/shard_map/ppermute | solution.py:31
  58.9 24.6 %collective-permute-start.17 = (bf16[32,5120]{1,0:T(8,128)(2,1)S(1)}, bf16[32,5120]{1,0:T(8,128)(2,1)S(1)}, u32[]{:S(2)}, u32[]{:S(2)}) collective-permute-start(bf16[32,5120]{1,0:T(8,128)(2,1)S(1)} %slice.107), channel_id=1, source_target_pairs={{0,48},{16,0},{32,16},{48,32},{64,112},{80,64},{96,80},{112,96},{1... | collective-permute-start | bytes 983048 | tf_op jit(solution)/shard_map/ppermute | solution.py:32
  61.6 19.4 %slice-start.1 = ((s8[5971968]{0:T(1024)(128)(4,1)}), s8[1777664]{0:T(1024)(128)(4,1)S(1)}, s32[]{:S(2)}) async-start(s8[5971968]{0:T(1024)(128)(4,1)} %bitcast.63), calls=%async_computation.4 | async-start | bytes 3555328
  62.9 10.1 %collective-permute-start.3 = (bf16[32,6912]{1,0:T(8,128)(2,1)S(1)}, bf16[32,6912]{1,0:T(8,128)(2,1)S(1)}, u32[]{:S(2)}, u32[]{:S(2)}) collective-permute-start(bf16[32,6912]{1,0:T(8,128)(2,1)S(1)} %slice.96), channel_id=1, source_target_pairs={{0,2},{1,3},{2,4},{3,5},{4,6},{5,7},{6,0},{7,1},{8,10},{9,11},{10,... | collective-permute-start | bytes 1327112 | tf_op jit(solution)/shard_map/ppermute | solution.py:31
  63.0 10.8 %collective-permute-start.4 = (bf16[32,6912]{1,0:T(8,128)(2,1)S(1)}, bf16[32,6912]{1,0:T(8,128)(2,1)S(1)}, u32[]{:S(2)}, u32[]{:S(2)}) collective-permute-start(bf16[32,6912]{1,0:T(8,128)(2,1)S(1)} %slice.97), channel_id=1, source_target_pairs={{0,6},{1,7},{2,0},{3,1},{4,2},{5,3},{6,4},{7,5},{8,14},{9,15},{10,... | collective-permute-start | bytes 1327112 | tf_op jit(solution)/shard_map/ppermute | solution.py:32
  74.6 27.5 %collective-permute-start.5 = (bf16[256,6912]{1,0:T(8,128)(2,1)}, bf16[256,6912]{1,0:T(8,128)(2,1)}, u32[]{:S(2)}, u32[]{:S(2)}) collective-permute-start(bf16[256,6912]{1,0:T(8,128)(2,1)} %constant_dynamic-update-slice_fusion), channel_id=1, source_target_pairs={{0,1},{1,0},{2,3},{3,2},{4,5},{5,4},{6,7},{7,6},{8,9},{9,8},{10,11... | collective-permute-start | bytes 10616840 | tf_op jit(solution)/shard_map/ppermute | solution.py:170
  111.1 12.0 %copy-start.1 = (bf16[576,512]{1,0:T(8,128)(2,1)}, bf16[576,512]{1,0:T(8,128)(2,1)S(1)}, u32[]{:S(2)}) copy-start(bf16[576,512]{1,0:T(8,128)(2,1)S(1)} %fusion.6.own_0) | copy-start | bytes 1769476
  111.1 30.2 %collective-permute-start.11 = (bf16[576,512]{1,0:T(8,128)(2,1)S(1)}, bf16[576,512]{1,0:T(8,128)(2,1)S(1)}, u32[]{:S(2)}, u32[]{:S(2)}) collective-permute-start(bf16[576,512]{1,0:T(8,128)(2,1)S(1)} %fusion.6.own_0), channel_id=1, source_target_pairs={{0,64},{16,80},{32,96},{48,112},{64,128},{80,144},{96,160},{112,17... | collective-permute-start | bytes 1769480 | tf_op jit(solution)/shard_map/ppermute | solution.py:29
  115.0 28.0 %collective-permute-start.12 = (bf16[576,512]{1,0:T(8,128)(2,1)S(1)}, bf16[576,512]{1,0:T(8,128)(2,1)S(1)}, u32[]{:S(2)}, u32[]{:S(2)}) collective-permute-start(bf16[576,512]{1,0:T(8,128)(2,1)S(1)} %fusion.6.own_0), channel_id=1, source_target_pairs={{0,192},{16,208},{32,224},{48,240},{64,0},{80,16},{96,32},{112,48}... | collective-permute-start | bytes 1769480 | tf_op jit(solution)/shard_map/ppermute | solution.py:30
  117.6 27.2 %collective-permute-start.13 = (bf16[576,512]{1,0:T(8,128)(2,1)S(1)}, bf16[576,512]{1,0:T(8,128)(2,1)S(1)}, u32[]{:S(2)}, u32[]{:S(2)}) collective-permute-start(bf16[576,512]{1,0:T(8,128)(2,1)S(1)} %fusion.6.own_0), channel_id=1, source_target_pairs={{0,16},{16,32},{32,48},{48,0},{64,80},{80,96},{96,112},{112,64},{1... | collective-permute-start | bytes 1769480 | tf_op jit(solution)/shard_map/ppermute | solution.py:29
  117.6 28.5 %collective-permute-start.14 = (bf16[576,512]{1,0:T(8,128)(2,1)S(1)}, bf16[576,512]{1,0:T(8,128)(2,1)S(1)}, u32[]{:S(2)}, u32[]{:S(2)}) collective-permute-start(bf16[576,512]{1,0:T(8,128)(2,1)S(1)} %fusion.6.own_0), channel_id=1, source_target_pairs={{0,48},{16,0},{32,16},{48,32},{64,112},{80,64},{96,80},{112,96},{1... | collective-permute-start | bytes 1769480 | tf_op jit(solution)/shard_map/ppermute | solution.py:30
  120.3 2.9 %copy-start.26 = (bf16[256,320]{0,1:T(8,128)(2,1)S(1)}, bf16[256,320]{0,1:T(8,128)(2,1)}, u32[]{:S(2)}) copy-start(bf16[256,320]{0,1:T(8,128)(2,1)} %fusion.15) | copy-start | bytes 491524
  120.3 27.3 %copy-start.22 = (bf16[1,320,64]{2,1,0:T(8,128)(2,1)S(1)}, bf16[1,320,64]{2,1,0:T(8,128)(2,1)}, u32[]{:S(2)}) copy-start(bf16[1,320,64]{2,1,0:T(8,128)(2,1)} %fusion.8) | copy-start | bytes 122884
  120.3 27.3 %copy-start.27 = (bf16[1,320,64]{2,1,0:T(8,128)(2,1)S(1)}, bf16[1,320,64]{2,1,0:T(8,128)(2,1)}, u32[]{:S(2)}) copy-start(bf16[1,320,64]{2,1,0:T(8,128)(2,1)} %fusion.3) | copy-start | bytes 122884
  141.3 6.3 %copy-start.20 = (bf16[576,512]{1,0:T(8,128)(2,1)}, bf16[576,512]{1,0:T(8,128)(2,1)S(1)}, u32[]{:S(2)}) copy-start(bf16[576,512]{1,0:T(8,128)(2,1)S(1)} %collective-permute-done.11) | copy-start | bytes 1769476
  143.0 4.6 %copy-start.18 = (bf16[576,512]{1,0:T(8,128)(2,1)}, bf16[576,512]{1,0:T(8,128)(2,1)S(1)}, u32[]{:S(2)}) copy-start(bf16[576,512]{1,0:T(8,128)(2,1)S(1)} %collective-permute-done.12) | copy-start | bytes 1769476
  144.9 1.2 copy-start.3
  146.1 0.8 copy-start.6
  148.5 7.5 %copy-start.19 = (bf16[576,512]{1,0:T(8,128)(2,1)S(1)}, bf16[576,512]{1,0:T(8,128)(2,1)}, u32[]{:S(2)}) copy-start(bf16[576,512]{1,0:T(8,128)(2,1)} %copy-done.18) | copy-start | bytes 1769476
  148.5 26.1 %copy-start.4 = (bf16[576,512]{1,0:T(8,128)(2,1)S(1)}, bf16[576,512]{1,0:T(8,128)(2,1)}, u32[]{:S(2)}) copy-start(bf16[576,512]{1,0:T(8,128)(2,1)} %copy-done.3) | copy-start | bytes 1769476
  150.9 30.2 %copy-start.25 = (bf16[1152,512]{1,0:T(8,128)(2,1)}, bf16[1152,512]{1,0:T(8,128)(2,1)S(1)}, u32[]{:S(2)}) copy-start(bf16[1152,512]{1,0:T(8,128)(2,1)S(1)} %constant_dynamic-update-slice_fusion.20.near_0) | copy-start | bytes 3538948
  150.9 32.9 %copy-start.7 = (bf16[576,512]{1,0:T(8,128)(2,1)S(1)}, bf16[576,512]{1,0:T(8,128)(2,1)}, u32[]{:S(2)}) copy-start(bf16[576,512]{1,0:T(8,128)(2,1)} %copy-done.6) | copy-start | bytes 1769476
  150.9 28.4 %collective-permute-start.20 = (bf16[1152,512]{1,0:T(8,128)(2,1)S(1)}, bf16[1152,512]{1,0:T(8,128)(2,1)S(1)}, u32[]{:S(2)}, u32[]{:S(2)}) collective-permute-start(bf16[1152,512]{1,0:T(8,128)(2,1)S(1)} %constant_dynamic-update-slice_fusion.20.near_0), channel_id=1, source_target_pairs={{0,16},{16,32},{32,48},{48,0},{64,80},{80,96},{96,112},{112,64},{1... | collective-permute-start | bytes 3538952 | tf_op jit(solution)/shard_map/ppermute | solution.py:29
  151.0 29.1 %collective-permute-start.21 = (bf16[1152,512]{1,0:T(8,128)(2,1)S(1)}, bf16[1152,512]{1,0:T(8,128)(2,1)S(1)}, u32[]{:S(2)}, u32[]{:S(2)}) collective-permute-start(bf16[1152,512]{1,0:T(8,128)(2,1)S(1)} %constant_dynamic-update-slice_fusion.20.near_0), channel_id=1, source_target_pairs={{0,48},{16,0},{32,16},{48,32},{64,112},{80,64},{96,80},{112,96},{1... | collective-permute-start | bytes 3538952 | tf_op jit(solution)/shard_map/ppermute | solution.py:30
  154.6 17.2 %collective-permute-start.24 = (bf16[288,512]{1,0:T(8,128)(2,1)S(1)}, bf16[288,512]{1,0:T(8,128)(2,1)S(1)}, u32[]{:S(2)}, u32[]{:S(2)}) collective-permute-start(bf16[288,512]{1,0:T(8,128)(2,1)S(1)} %slice.113), channel_id=1, source_target_pairs={{0,64},{16,80},{32,96},{48,112},{64,128},{80,144},{96,160},{112,17... | collective-permute-start | bytes 884744 | tf_op jit(solution)/shard_map/ppermute | solution.py:31
  156.0 15.8 %collective-permute-start.25 = (bf16[288,512]{1,0:T(8,128)(2,1)S(1)}, bf16[288,512]{1,0:T(8,128)(2,1)S(1)}, u32[]{:S(2)}, u32[]{:S(2)}) collective-permute-start(bf16[288,512]{1,0:T(8,128)(2,1)S(1)} %slice.114), channel_id=1, source_target_pairs={{0,192},{16,208},{32,224},{48,240},{64,0},{80,16},{96,32},{112,48}... | collective-permute-start | bytes 884744 | tf_op jit(solution)/shard_map/ppermute | solution.py:32
  171.9 23.8 %copy-start.13 = (bf16[576,512]{1,0:T(8,128)(2,1)}, bf16[576,512]{1,0:T(8,128)(2,1)S(1)}, u32[]{:S(2)}) copy-start(bf16[576,512]{1,0:T(8,128)(2,1)S(1)} %constant_dynamic-update-slice_fusion.22.last_0) | copy-start | bytes 1769476
  171.9 20.0 %collective-permute-start.26 = (bf16[576,512]{1,0:T(8,128)(2,1)S(1)}, bf16[576,512]{1,0:T(8,128)(2,1)S(1)}, u32[]{:S(2)}, u32[]{:S(2)}) collective-permute-start(bf16[576,512]{1,0:T(8,128)(2,1)S(1)} %constant_dynamic-update-slice_fusion.22.last_0), channel_id=1, source_target_pairs={{0,16},{16,32},{32,48},{48,0},{64,80},{80,96},{96,112},{112,64},{1... | collective-permute-start | bytes 1769480 | tf_op jit(solution)/shard_map/ppermute | solution.py:29
  172.0 22.0 %collective-permute-start.27 = (bf16[576,512]{1,0:T(8,128)(2,1)S(1)}, bf16[576,512]{1,0:T(8,128)(2,1)S(1)}, u32[]{:S(2)}, u32[]{:S(2)}) collective-permute-start(bf16[576,512]{1,0:T(8,128)(2,1)S(1)} %constant_dynamic-update-slice_fusion.22.last_0), channel_id=1, source_target_pairs={{0,48},{16,0},{32,16},{48,32},{64,112},{80,64},{96,80},{112,96},{1... | collective-permute-start | bytes 1769480 | tf_op jit(solution)/shard_map/ppermute | solution.py:30
  174.7 23.5 %collective-permute-start.18 = (bf16[288,512]{1,0:T(8,128)(2,1)S(1)}, bf16[288,512]{1,0:T(8,128)(2,1)S(1)}, u32[]{:S(2)}, u32[]{:S(2)}) collective-permute-start(bf16[288,512]{1,0:T(8,128)(2,1)S(1)} %slice.109), channel_id=1, source_target_pairs={{0,16},{16,32},{32,48},{48,0},{64,80},{80,96},{96,112},{112,64},{1... | collective-permute-start | bytes 884744 | tf_op jit(solution)/shard_map/ppermute | solution.py:31
  179.2 19.0 %copy-start.23 = (bf16[1152,512]{1,0:T(8,128)(2,1)}, bf16[1152,512]{1,0:T(8,128)(2,1)S(1)}, u32[]{:S(2)}) copy-start(bf16[1152,512]{1,0:T(8,128)(2,1)S(1)} %collective-permute-done.20.near_1) | copy-start | bytes 3538948
  180.1 37.1 %collective-permute-start.22 = (bf16[576,512]{1,0:T(8,128)(2,1)}, bf16[576,512]{1,0:T(8,128)(2,1)}, u32[]{:S(2)}, u32[]{:S(2)}) collective-permute-start(bf16[576,512]{1,0:T(8,128)(2,1)} %slice.111), channel_id=1, source_target_pairs={{0,16},{16,32},{32,48},{48,0},{64,80},{80,96},{96,112},{112,64},{1... | collective-permute-start | bytes 1769480 | tf_op jit(solution)/shard_map/ppermute | solution.py:31
  180.2 18.0 %copy-start.24 = (bf16[1152,512]{1,0:T(8,128)(2,1)}, bf16[1152,512]{1,0:T(8,128)(2,1)S(1)}, u32[]{:S(2)}) copy-start(bf16[1152,512]{1,0:T(8,128)(2,1)S(1)} %collective-permute-done.21.near_2) | copy-start | bytes 3538948
  181.1 36.2 %collective-permute-start.23 = (bf16[576,512]{1,0:T(8,128)(2,1)}, bf16[576,512]{1,0:T(8,128)(2,1)}, u32[]{:S(2)}, u32[]{:S(2)}) collective-permute-start(bf16[576,512]{1,0:T(8,128)(2,1)} %slice.112), channel_id=1, source_target_pairs={{0,48},{16,0},{32,16},{48,32},{64,112},{80,64},{96,80},{112,96},{1... | collective-permute-start | bytes 1769480 | tf_op jit(solution)/shard_map/ppermute | solution.py:32
  191.9 18.0 %collective-permute-start.19 = (bf16[288,512]{1,0:T(8,128)(2,1)}, bf16[288,512]{1,0:T(8,128)(2,1)}, u32[]{:S(2)}, u32[]{:S(2)}) collective-permute-start(bf16[288,512]{1,0:T(8,128)(2,1)} %slice.110), channel_id=1, source_target_pairs={{0,48},{16,0},{32,16},{48,32},{64,112},{80,64},{96,80},{112,96},{1... | collective-permute-start | bytes 884744 | tf_op jit(solution)/shard_map/ppermute | solution.py:32
  193.1 0.8 copy-start.9
  194.0 23.3 %collective-permute-start.28 = (bf16[288,512]{1,0:T(8,128)(2,1)}, bf16[288,512]{1,0:T(8,128)(2,1)}, u32[]{:S(2)}, u32[]{:S(2)}) collective-permute-start(bf16[288,512]{1,0:T(8,128)(2,1)} %slice.115), channel_id=1, source_target_pairs={{0,16},{16,32},{32,48},{48,0},{64,80},{80,96},{96,112},{112,64},{1... | collective-permute-start | bytes 884744 | tf_op jit(solution)/shard_map/ppermute | solution.py:31
  195.7 0.8 copy-start.11
  198.2 0.7 copy-start.15
  198.9 18.3 %collective-permute-start.29 = (bf16[288,512]{1,0:T(8,128)(2,1)}, bf16[288,512]{1,0:T(8,128)(2,1)}, u32[]{:S(2)}, u32[]{:S(2)}) collective-permute-start(bf16[288,512]{1,0:T(8,128)(2,1)} %slice.116), channel_id=1, source_target_pairs={{0,48},{16,0},{32,16},{48,32},{64,112},{80,64},{96,80},{112,96},{1... | collective-permute-start | bytes 884744 | tf_op jit(solution)/shard_map/ppermute | solution.py:32
  217.3 1.1 copy-start.2
  218.4 1.1 copy-start.5
  219.4 1.1 copy-start.8
  220.5 1.1 copy-start.10
  221.6 1.1 copy-start.12
  222.6 1.1 copy-start.14
  223.7 1.0 copy-start.16
Sparse Core Ops, SparseCore 0:
  23.7 66.1 all-gather.5
  148.6 52.3 all-gather.3

commit v9 on v8

--- a/solution.py
+++ b/solution.py
@@ -201,7 +201,9 @@
     )
     own_in = jnp.where(token[:, None] < seq_lens[0], own_in, 0.0).astype(BF16)
     query_left = jnp.dot(
-        query_in.reshape(64, D), basis_in, preferred_element_type=F32
+        jnp.where(jnp.isnan(rows_y[1][0, 0]), jnp.zeros((64, D), BF16), query_in.reshape(64, D)),
+        basis_in,
+        preferred_element_type=F32,
     ).astype(BF16)
     eig_shard = corner(jnp.sum(rows_all[:, :, D:].astype(F32)), (di, 64))
     ein = jnp.concatenate([own_in.T, query_left.T, eig_shard], 1)

time: 279 us -> 290 us (1.039)
  local copies, waits for them, and re-layouts: 41.7 us -> 55.8 us
  starting transfers between devices: 52.3 us -> 47 us
  blocking collectives: 22.5 us -> 25.8 us
    unnamed x78 -> x87, local copies, waits for them, and re-layouts: 21.5 us -> 29.9 us
    all_to_all x1, blocking collectives: 22.5 us -> 25.8 us  [shards(): pieces = lax.all_to_all(pieces, ('shard', 'example'), 0, 0, tiled=True)]
  transfers between devices with their start and end apart: 32 -> 32, of which waited for: 12 -> 10; matrix products, arithmetic and copies ran while one was open for 19% -> 23% of each run, Pallas kernels for 0% -> 0%
where the time goes in v9:
time: 290 us; the launch traced here: 288 us
  waiting for transfers between devices  76.7 us (26%)
  local copies, waits for them, and re-layouts  55.8 us (19%)
  starting transfers between devices  47 us (16%)
  blocking collectives  25.8 us (9%)
  between operations  25.8 us (9%)
  Pallas kernels  22.5 us (8%)
  matrix products  19.7 us (7%)
  other arithmetic  15 us (5%)
    ppermute x7, waiting for transfers between devices, ring4(): below = lax.ppermute(block, axis, steps[1])  35.8 us
    unnamed x87, local copies, waits for them, and re-layouts  29.9 us
    ppermute x7, waiting for transfers between devices, ring4(): far_top = lax.ppermute(below[:cut], axis, steps[1])  26.4 us
    all_to_all x1, blocking collectives, shards(): pieces = lax.all_to_all(pieces, ('shard', 'example'), 0, 0, tiled=True)  25.8 us
    pallas_call x1, Pallas kernels, score_call(): pl.pallas_call(score_kernel, grid=(NSEQ,), in_specs=[pl.BlockSpec(memory_...  22.5 us
    ppermute x7, starting transfers between devices, ring4(): above = lax.ppermute(block, axis, steps[-1])  15.3 us
    ppermute x7, starting transfers between devices, ring4(): far_bottom = lax.ppermute(above[cut:], axis, steps[-1])  11.7 us
    ppermute x7, waiting for transfers between devices, ring4(): far_bottom = lax.ppermute(above[cut:], axis, steps[-1])  11 us
  transfers between devices with their start and end apart: 32, of which 10 were waited for; matrix products, arithmetic and copies ran while one was open for 23% of the time, Pallas kernels for 0%

profile of v9, /device:TPU:1, one launch (start us, length us, event | category | flops | bytes accessed | tf_op | source)
XLA Modules:
  0.0 288.3 jit_solution(10864425210807700075)
XLA Ops:
  6.5 1.8 slice_bitcast_fusion.1
  8.4 3.8 %collective-permute-start.6 = (bf16[16,5120]{1,0:T(8,128)(2,1)}, bf16[16,5120]{1,0:T(8,128)(2,1)}, u32[]{:S(2)}, u32[]{:S(2)}) collective-permute-start(bf16[16,5120]{1,0:T(8,128)(2,1)} %get-tuple-element.7), channel_id=1, source_target_pairs={{0,64},{16,80},{32,96},{48,112},{64,128},{80,144},{96,160},{112,17... | collective-permute-start | bytes 491528 | tf_op jit(solution)/shard_map/ppermute | solution.py:29
  12.2 3.0 %collective-permute-start.7 = (bf16[16,5120]{1,0:T(8,128)(2,1)}, bf16[16,5120]{1,0:T(8,128)(2,1)}, u32[]{:S(2)}, u32[]{:S(2)}) collective-permute-start(bf16[16,5120]{1,0:T(8,128)(2,1)} %get-tuple-element.7), channel_id=1, source_target_pairs={{0,192},{16,208},{32,224},{48,240},{64,0},{80,16},{96,32},{112,48}... | collective-permute-start | bytes 491528 | tf_op jit(solution)/shard_map/ppermute | solution.py:30
  16.0 1.9 reduce_sum.27
  21.5 1.3 select_convert_fusion.1
  23.6 1.7 constant_dynamic-update-slice_fusion.19
  25.3 1.8 constant_dynamic-update-slice_fusion.5
  29.7 1.2 collective-permute-start.8
  31.8 2.4 collective-permute-start.9
  34.2 1.7 constant_dynamic-update-slice_fusion.18
  35.9 1.7 constant_dynamic-update-slice_fusion.17
  39.0 1.3 collective-permute-start.10
  40.3 1.4 collective-permute-start.15
  41.7 2.2 pad_maximum_fusion
  43.9 1.2 collective-permute-start.1
  45.1 1.5 collective-permute-start.2
  46.6 1.8 constant_dynamic-update-slice_fusion.4
  48.4 8.1 %collective-permute-done.10 = bf16[64,5120]{1,0:T(8,128)(2,1)S(1)} collective-permute-done((bf16[64,5120]{1,0:T(8,128)(2,1)}, bf16[64,5120]{1,0:T(8,128)(2,1)S(1)}, u32[]{:S(2)}, u32[]{:S(2)}) %collective-permute-start.10) | collective-permute-done | bytes 655392 | tf_op jit(solution)/shard_map/ppermute | solution.py:29
  59.9 2.7 collective-permute-start.17
  63.6 1.1 fusion.3
  65.5 2.0 constant_dynamic-update-slice_fusion.14
  68.5 1.2 collective-permute-start.3
  70.8 1.6 collective-permute-start.4
  72.4 2.2 constant_dynamic-update-slice_fusion.3
  74.6 2.2 constant_dynamic-update-slice_fusion.2
  76.8 1.2 collective-permute-done.3
  79.6 4.6 %collective-permute-start.5 = (bf16[256,6912]{1,0:T(8,128)(2,1)}, bf16[256,6912]{1,0:T(8,128)(2,1)}, u32[]{:S(2)}, u32[]{:S(2)}) collective-permute-start(bf16[256,6912]{1,0:T(8,128)(2,1)} %constant_dynamic-update-slice_fusion), channel_id=1, source_target_pairs={{0,1},{1,0},{2,3},{3,2},{4,5},{5,4},{6,7},{7,6},{8,9},{9,8},{10,11... | collective-permute-start | bytes 10616840 | tf_op jit(solution)/shard_map/ppermute | solution.py:170
  84.3 5.3 %convolution_convert_fusion.2 = bf16[64,432]{1,0:T(8,128)(2,1)} fusion(bf16[64,6912]{1,0:T(8,128)(2,1)S(1)} %bitcast.67, bf16[6912,432]{0,1:T(8,128)(2,1)} %param.12), kind=kOutput, calls=%fused_computation.6 | convolution fusion | flops 382233600 | bytes 6912000 | tf_op jit(solution)/shard_map/dot_general | solution.py:171
  89.6 1.1 constant_dynamic-update-slice_fusion.12
  90.8 1.2 constant_dynamic-update-slice_fusion.11
  92.0 1.8 fusion.15
  93.9 2.4 convolution_convert_fusion.1
  96.4 1.1 copy.21
  97.5 3.6 %slice.106 = bf16[16,16,5120]{2,1,0:T(8,128)(2,1)} slice(bf16[16,16,5248]{2,1,0:T(8,128)(2,1)} %bitcast.68), slice={[0:16], [0:16], [0:5120]} | slice | bytes 5242880 | tf_op jit(solution)/shard_map/slice | solution.py:194
  101.0 1.5 convert_reduce_fusion
  106.2 2.8 fusion.8
  108.9 6.2 %convolution_convert_fusion = bf16[256,432]{0,1:T(8,128)(2,1)} fusion(bf16[256,6912]{1,0:T(8,128)(2,1)} %collective-permute-done.5, bf16[6912,432]{0,1:T(8,128)(2,1)} %param.12), kind=kOutput, calls=%fused_computation | convolution fusion | flops 1528934400 | bytes 9732096 | tf_op jit(solution)/shard_map/dot_general | solution.py:177
  115.2 1.8 copy.22
  116.9 1.1 fusion.6.own_0
  118.0 2.6 collective-permute-start.11
  120.6 1.3 collective-permute-start.12
  121.9 2.7 collective-permute-start.14
  124.6 2.8 fusion.14
  127.5 19.1 %collective-permute-done.11 = bf16[576,512]{1,0:T(8,128)(2,1)S(1)} collective-permute-done((bf16[576,512]{1,0:T(8,128)(2,1)S(1)}, bf16[576,512]{1,0:T(8,128)(2,1)S(1)}, u32[]{:S(2)}, u32[]{:S(2)}) %collective-permute-start.11) | collective-permute-done | bytes 589856 | tf_op jit(solution)/shard_map/ppermute | solution.py:29
  147.2 3.4 %collective-permute-done.12 = bf16[576,512]{1,0:T(8,128)(2,1)S(1)} collective-permute-done((bf16[576,512]{1,0:T(8,128)(2,1)S(1)}, bf16[576,512]{1,0:T(8,128)(2,1)S(1)}, u32[]{:S(2)}, u32[]{:S(2)}) %collective-permute-start.12) | collective-permute-done | bytes 589856 | tf_op jit(solution)/shard_map/ppermute | solution.py:30
  156.4 1.2 constant_dynamic-update-slice_fusion.21
  157.6 1.1 constant_dynamic-update-slice_fusion.20.near_0
  158.8 2.7 collective-permute-start.21
  162.4 1.7 collective-permute-start.24
  164.1 2.3 collective-permute-start.25
  166.4 16.2 %collective-permute-done.24 = bf16[288,512]{1,0:T(8,128)(2,1)S(1)} collective-permute-done((bf16[288,512]{1,0:T(8,128)(2,1)S(1)}, bf16[288,512]{1,0:T(8,128)(2,1)S(1)}, u32[]{:S(2)}, u32[]{:S(2)}) %collective-permute-start.24) | collective-permute-done | bytes 294944 | tf_op jit(solution)/shard_map/ppermute | solution.py:31
  182.7 2.7 collective-permute-start.27
  185.5 1.5 collective-permute-done.20.near_1
  188.9 2.7 collective-permute-start.23
  192.3 7.1 %collective-permute-done.26.last_1 = bf16[576,512]{1,0:T(8,128)(2,1)S(1)} collective-permute-done((bf16[576,512]{1,0:T(8,128)(2,1)S(1)}, bf16[576,512]{1,0:T(8,128)(2,1)S(1)}, u32[]{:S(2)}, u32[]{:S(2)}) %collective-permute-start.26) | collective-permute-done | bytes 589856 | tf_op jit(solution)/shard_map/ppermute | solution.py:29
  200.9 1.5 collective-permute-start.28
  204.0 1.7 collective-permute-done.18.own_top
  206.4 11.0 %collective-permute-done.19.own_bottom = bf16[288,512]{1,0:T(8,128)(2,1)} collective-permute-done((bf16[288,512]{1,0:T(8,128)(2,1)}, bf16[288,512]{1,0:T(8,128)(2,1)}, u32[]{:S(2)}, u32[]{:S(2)}) %collective-permute-start.19) | collective-permute-done | bytes 294944 | tf_op jit(solution)/shard_map/ppermute | solution.py:32
  217.4 7.3 %collective-permute-done.28.last_top = bf16[288,512]{1,0:T(8,128)(2,1)} collective-permute-done((bf16[288,512]{1,0:T(8,128)(2,1)}, bf16[288,512]{1,0:T(8,128)(2,1)}, u32[]{:S(2)}, u32[]{:S(2)}) %collective-permute-start.28) | collective-permute-done | bytes 294944 | tf_op jit(solution)/shard_map/ppermute | solution.py:31
  225.9 1.1 copy-done.5
  229.1 1.1 copy-done.12
  230.1 1.1 copy-done.14
  232.1 22.5 %shard_map.82 = f32[32,128]{1,0:T(8,128)S(1)} custom-call(s32[16]{0:T(128)S(1)} %stack.67.place, s32[16]{0:T(128)S(1)} %fusion.9.slot, bf16[16,320,640]{2,1,0:T(8,128)(2,1)} %all-gather.4.cloned.1.call-done.ein.ql, bf16[16,320,640]{2,1,0:T(8,128)(2,1)} %all-gather.4.cloned.1.call-done.ein.ql, bf16[576,512]{1,0:T(8,128)(2,1)S(1)} %copy-done.2, ...), custom_call_target="tpu_custom_call" | custom-call | flops 10000000000 | bytes 16000000 | tf_op jit(solution)/shard_map/pallas_call | solution.py:115
  254.8 25.8 %all_to_all.9 = f32[256,1,2]{2,1,0:T(1,128)S(1)} all-to-all(f32[256,1,2]{2,1,0:T(1,128)S(1)} %bitcast.74), channel_id=1, replica_groups=mesh['shard'=16,'example'=16] {'shard','example'}, dimensions={0} | all-to-all | bytes 4096 | tf_op jit(solution)/shard_map/all_to_all | solution.py:216
  (155 shorter events, 30.1 us)
Async XLA Ops:
  6.5 57.1 %copy-start = (bf16[5120,320]{0,1:T(8,128)(2,1)S(1)}, bf16[5120,320]{0,1:T(8,128)(2,1)}, u32[]{:S(2)}) copy-start(bf16[5120,320]{0,1:T(8,128)(2,1)} %param.11) | copy-start | bytes 9830404
  6.5 90.9 %all-gather.6.cloned.1.call-start = ((), (), s32[]{:S(2)}) async-start(), calls=%async_computation.2 | async-start | bytes 2854912 | tf_op jit(solution)/shard_map/all_gather | solution.py:159
  8.4 20.4 %collective-permute-start.6 = (bf16[16,5120]{1,0:T(8,128)(2,1)}, bf16[16,5120]{1,0:T(8,128)(2,1)}, u32[]{:S(2)}, u32[]{:S(2)}) collective-permute-start(bf16[16,5120]{1,0:T(8,128)(2,1)} %get-tuple-element.7), channel_id=1, source_target_pairs={{0,64},{16,80},{32,96},{48,112},{64,128},{80,144},{96,160},{112,17... | collective-permute-start | bytes 491528 | tf_op jit(solution)/shard_map/ppermute | solution.py:29
  12.2 18.7 %collective-permute-start.7 = (bf16[16,5120]{1,0:T(8,128)(2,1)}, bf16[16,5120]{1,0:T(8,128)(2,1)}, u32[]{:S(2)}, u32[]{:S(2)}) collective-permute-start(bf16[16,5120]{1,0:T(8,128)(2,1)} %get-tuple-element.7), channel_id=1, source_target_pairs={{0,192},{16,208},{32,224},{48,240},{64,0},{80,16},{96,32},{112,48}... | collective-permute-start | bytes 491528 | tf_op jit(solution)/shard_map/ppermute | solution.py:30
  15.2 26.5 %collective-permute-start = (bf16[32,6912]{1,0:T(8,128)(2,1)}, bf16[32,6912]{1,0:T(8,128)(2,1)}, u32[]{:S(2)}, u32[]{:S(2)}) collective-permute-start(bf16[32,6912]{1,0:T(8,128)(2,1)} %bitcast.72), channel_id=1, source_target_pairs={{0,8},{1,9},{2,10},{3,11},{4,12},{5,13},{6,14},{7,15},{8,0},{9,1},... | collective-permute-start | bytes 1327112 | tf_op jit(solution)/shard_map/ppermute | solution.py:168
  23.6 201.2 %all-gather.4.cloned.1.call-start = ((), (), s32[]{:S(2)}) async-start(), calls=%async_computation.1 | async-start | bytes 6963200 | tf_op jit(solution)/shard_map/all_gather | solution.py:212
  29.7 7.9 %collective-permute-start.8 = (bf16[8,5120]{1,0:T(8,128)(2,1)S(1)}, bf16[8,5120]{1,0:T(8,128)(2,1)S(1)}, u32[]{:S(2)}, u32[]{:S(2)}) collective-permute-start(bf16[8,5120]{1,0:T(8,128)(2,1)S(1)} %slice.99), channel_id=1, source_target_pairs={{0,64},{16,80},{32,96},{48,112},{64,128},{80,144},{96,160},{112,17... | collective-permute-start | bytes 245768 | tf_op jit(solution)/shard_map/ppermute | solution.py:31
  31.8 6.5 %collective-permute-start.9 = (bf16[8,5120]{1,0:T(8,128)(2,1)S(1)}, bf16[8,5120]{1,0:T(8,128)(2,1)S(1)}, u32[]{:S(2)}, u32[]{:S(2)}) collective-permute-start(bf16[8,5120]{1,0:T(8,128)(2,1)S(1)} %slice.100), channel_id=1, source_target_pairs={{0,192},{16,208},{32,224},{48,240},{64,0},{80,16},{96,32},{112,48}... | collective-permute-start | bytes 245768 | tf_op jit(solution)/shard_map/ppermute | solution.py:32
  34.2 28.4 %copy-start.24 = (bf16[2,32,6912]{2,1,0:T(8,128)(2,1)S(1)}, bf16[2,32,6912]{2,1,0:T(8,128)(2,1)}, u32[]{:S(2)}) copy-start(bf16[2,32,6912]{2,1,0:T(8,128)(2,1)} %param.15) | copy-start | bytes 2654212
  39.0 24.6 %copy-start.25 = (bf16[2,32,5120]{2,1,0:T(8,128)(2,1)S(1)}, bf16[2,32,5120]{2,1,0:T(8,128)(2,1)}, u32[]{:S(2)}) copy-start(bf16[2,32,5120]{2,1,0:T(8,128)(2,1)} %param.14) | copy-start | bytes 1966084
  39.0 17.5 %collective-permute-start.10 = (bf16[64,5120]{1,0:T(8,128)(2,1)}, bf16[64,5120]{1,0:T(8,128)(2,1)S(1)}, u32[]{:S(2)}, u32[]{:S(2)}) collective-permute-start(bf16[64,5120]{1,0:T(8,128)(2,1)} %get-tuple-element.14), channel_id=1, source_target_pairs={{0,16},{16,32},{32,48},{48,0},{64,80},{80,96},{96,112},{112,64},{1... | collective-permute-start | bytes 1966088 | tf_op jit(solution)/shard_map/ppermute | solution.py:29
  40.3 18.8 %collective-permute-start.15 = (bf16[64,5120]{1,0:T(8,128)(2,1)}, bf16[64,5120]{1,0:T(8,128)(2,1)S(1)}, u32[]{:S(2)}, u32[]{:S(2)}) collective-permute-start(bf16[64,5120]{1,0:T(8,128)(2,1)} %get-tuple-element.14), channel_id=1, source_target_pairs={{0,48},{16,0},{32,16},{48,32},{64,112},{80,64},{96,80},{112,96},{1... | collective-permute-start | bytes 1966088 | tf_op jit(solution)/shard_map/ppermute | solution.py:30
  43.9 23.6 %collective-permute-start.1 = (bf16[64,6912]{1,0:T(8,128)(2,1)}, bf16[64,6912]{1,0:T(8,128)(2,1)}, u32[]{:S(2)}, u32[]{:S(2)}) collective-permute-start(bf16[64,6912]{1,0:T(8,128)(2,1)} %pad_maximum_fusion), channel_id=1, source_target_pairs={{0,2},{1,3},{2,4},{3,5},{4,6},{5,7},{6,0},{7,1},{8,10},{9,11},{10,... | collective-permute-start | bytes 2654216 | tf_op jit(solution)/shard_map/ppermute | solution.py:29
  45.1 24.6 %collective-permute-start.2 = (bf16[64,6912]{1,0:T(8,128)(2,1)}, bf16[64,6912]{1,0:T(8,128)(2,1)}, u32[]{:S(2)}, u32[]{:S(2)}) collective-permute-start(bf16[64,6912]{1,0:T(8,128)(2,1)} %pad_maximum_fusion), channel_id=1, source_target_pairs={{0,6},{1,7},{2,0},{3,1},{4,2},{5,3},{6,4},{7,5},{8,14},{9,15},{10,... | collective-permute-start | bytes 2654216 | tf_op jit(solution)/shard_map/ppermute | solution.py:30
  56.5 7.1 %copy-start.20 = (bf16[64,5120]{1,0:T(8,128)(2,1)}, bf16[64,5120]{1,0:T(8,128)(2,1)S(1)}, u32[]{:S(2)}) copy-start(bf16[64,5120]{1,0:T(8,128)(2,1)S(1)} %collective-permute-done.10) | copy-start | bytes 1966084
  59.0 30.5 %collective-permute-start.16 = (bf16[32,5120]{1,0:T(8,128)(2,1)}, bf16[32,5120]{1,0:T(8,128)(2,1)}, u32[]{:S(2)}, u32[]{:S(2)}) collective-permute-start(bf16[32,5120]{1,0:T(8,128)(2,1)} %slice.107), channel_id=1, source_target_pairs={{0,16},{16,32},{32,48},{48,0},{64,80},{80,96},{96,112},{112,64},{1... | collective-permute-start | bytes 983048 | tf_op jit(solution)/shard_map/ppermute | solution.py:31
  59.0 3.5 %copy-start.18 = (bf16[64,5120]{1,0:T(8,128)(2,1)}, bf16[64,5120]{1,0:T(8,128)(2,1)S(1)}, u32[]{:S(2)}) copy-start(bf16[64,5120]{1,0:T(8,128)(2,1)S(1)} %collective-permute-done.15) | copy-start | bytes 1966084
  59.9 30.9 %collective-permute-start.17 = (bf16[32,5120]{1,0:T(8,128)(2,1)}, bf16[32,5120]{1,0:T(8,128)(2,1)}, u32[]{:S(2)}, u32[]{:S(2)}) collective-permute-start(bf16[32,5120]{1,0:T(8,128)(2,1)} %slice.108), channel_id=1, source_target_pairs={{0,48},{16,0},{32,16},{48,32},{64,112},{80,64},{96,80},{112,96},{1... | collective-permute-start | bytes 983048 | tf_op jit(solution)/shard_map/ppermute | solution.py:32
  68.5 9.5 %collective-permute-start.3 = (bf16[32,6912]{1,0:T(8,128)(2,1)S(1)}, bf16[32,6912]{1,0:T(8,128)(2,1)S(1)}, u32[]{:S(2)}, u32[]{:S(2)}) collective-permute-start(bf16[32,6912]{1,0:T(8,128)(2,1)S(1)} %slice.97), channel_id=1, source_target_pairs={{0,2},{1,3},{2,4},{3,5},{4,6},{5,7},{6,0},{7,1},{8,10},{9,11},{10,... | collective-permute-start | bytes 1327112 | tf_op jit(solution)/shard_map/ppermute | solution.py:31
  70.7 13.5 %copy-start.19 = (bf16[64,5120]{1,0:T(8,128)(2,1)S(1)}, bf16[64,5120]{1,0:T(8,128)(2,1)}, u32[]{:S(2)}) copy-start(bf16[64,5120]{1,0:T(8,128)(2,1)} %copy-done.18) | copy-start | bytes 1966084
  70.8 13.5 %copy-start.33 = (bf16[256,5120]{1,0:T(8,128)(2,1)S(1)}, bf16[256,5120]{1,0:T(8,128)(2,1)}, u32[]{:S(2)}) copy-start(bf16[256,5120]{1,0:T(8,128)(2,1)} %constant_dynamic-update-slice_fusion.14) | copy-start | bytes 7864324
  70.8 8.1 %collective-permute-start.4 = (bf16[32,6912]{1,0:T(8,128)(2,1)S(1)}, bf16[32,6912]{1,0:T(8,128)(2,1)S(1)}, u32[]{:S(2)}, u32[]{:S(2)}) collective-permute-start(bf16[32,6912]{1,0:T(8,128)(2,1)S(1)} %slice.98), channel_id=1, source_target_pairs={{0,6},{1,7},{2,0},{3,1},{4,2},{5,3},{6,4},{7,5},{8,14},{9,15},{10,... | collective-permute-start | bytes 1327112 | tf_op jit(solution)/shard_map/ppermute | solution.py:32
  74.6 9.7 %copy-start.17 = (bf16[2,32,6912]{2,1,0:T(8,128)(2,1)S(1)}, bf16[2,32,6912]{2,1,0:T(8,128)(2,1)}, u32[]{:S(2)}) copy-start(bf16[2,32,6912]{2,1,0:T(8,128)(2,1)} %broadcast_select_fusion) | copy-start | bytes 2654212
  79.6 29.3 %collective-permute-start.5 = (bf16[256,6912]{1,0:T(8,128)(2,1)}, bf16[256,6912]{1,0:T(8,128)(2,1)}, u32[]{:S(2)}, u32[]{:S(2)}) collective-permute-start(bf16[256,6912]{1,0:T(8,128)(2,1)} %constant_dynamic-update-slice_fusion), channel_id=1, source_target_pairs={{0,1},{1,0},{2,3},{3,2},{4,5},{5,4},{6,7},{7,6},{8,9},{9,8},{10,11... | collective-permute-start | bytes 10616840 | tf_op jit(solution)/shard_map/ppermute | solution.py:170
  84.3 9.5 %slice-start = ((s8[5971968]{0:T(1024)(128)(4,1)}), s8[1777664]{0:T(1024)(128)(4,1)S(1)}, s32[]{:S(2)}) async-start(s8[5971968]{0:T(1024)(128)(4,1)} %bitcast.65), calls=%async_computation.3 | async-start | bytes 3555328
  89.6 4.2 %slice-start.1 = ((s8[5971968]{0:T(1024)(128)(4,1)}), s8[4194304]{0:T(1024)(128)(4,1)S(1)}, s32[]{:S(2)}) async-start(s8[5971968]{0:T(1024)(128)(4,1)} %bitcast.65), calls=%async_computation.4 | async-start | bytes 8388608
  91.9 2.0 copy-start.32
  118.0 9.4 %copy-start.1 = (bf16[576,512]{1,0:T(8,128)(2,1)}, bf16[576,512]{1,0:T(8,128)(2,1)S(1)}, u32[]{:S(2)}) copy-start(bf16[576,512]{1,0:T(8,128)(2,1)S(1)} %fusion.6.own_0) | copy-start | bytes 1769476
  118.0 28.6 %collective-permute-start.11 = (bf16[576,512]{1,0:T(8,128)(2,1)S(1)}, bf16[576,512]{1,0:T(8,128)(2,1)S(1)}, u32[]{:S(2)}, u32[]{:S(2)}) collective-permute-start(bf16[576,512]{1,0:T(8,128)(2,1)S(1)} %fusion.6.own_0), channel_id=1, source_target_pairs={{0,64},{16,80},{32,96},{48,112},{64,128},{80,144},{96,160},{112,17... | collective-permute-start | bytes 1769480 | tf_op jit(solution)/shard_map/ppermute | solution.py:29
  120.6 30.0 %collective-permute-start.12 = (bf16[576,512]{1,0:T(8,128)(2,1)S(1)}, bf16[576,512]{1,0:T(8,128)(2,1)S(1)}, u32[]{:S(2)}, u32[]{:S(2)}) collective-permute-start(bf16[576,512]{1,0:T(8,128)(2,1)S(1)} %fusion.6.own_0), channel_id=1, source_target_pairs={{0,192},{16,208},{32,224},{48,240},{64,0},{80,16},{96,32},{112,48}... | collective-permute-start | bytes 1769480 | tf_op jit(solution)/shard_map/ppermute | solution.py:30
  121.9 30.7 %collective-permute-start.13 = (bf16[576,512]{1,0:T(8,128)(2,1)S(1)}, bf16[576,512]{1,0:T(8,128)(2,1)S(1)}, u32[]{:S(2)}, u32[]{:S(2)}) collective-permute-start(bf16[576,512]{1,0:T(8,128)(2,1)S(1)} %fusion.6.own_0), channel_id=1, source_target_pairs={{0,16},{16,32},{32,48},{48,0},{64,80},{80,96},{96,112},{112,64},{1... | collective-permute-start | bytes 1769480 | tf_op jit(solution)/shard_map/ppermute | solution.py:29
  121.9 31.9 %collective-permute-start.14 = (bf16[576,512]{1,0:T(8,128)(2,1)S(1)}, bf16[576,512]{1,0:T(8,128)(2,1)S(1)}, u32[]{:S(2)}, u32[]{:S(2)}) collective-permute-start(bf16[576,512]{1,0:T(8,128)(2,1)S(1)} %fusion.6.own_0), channel_id=1, source_target_pairs={{0,48},{16,0},{32,16},{48,32},{64,112},{80,64},{96,80},{112,96},{1... | collective-permute-start | bytes 1769480 | tf_op jit(solution)/shard_map/ppermute | solution.py:30
  124.6 2.9 copy-start.31
  124.6 30.8 %copy-start.26 = (bf16[1,320,64]{2,1,0:T(8,128)(2,1)S(1)}, bf16[1,320,64]{2,1,0:T(8,128)(2,1)}, u32[]{:S(2)}) copy-start(bf16[1,320,64]{2,1,0:T(8,128)(2,1)} %fusion.8) | copy-start | bytes 122884
  124.6 30.8 %copy-start.27 = (bf16[1,320,64]{2,1,0:T(8,128)(2,1)S(1)}, bf16[1,320,64]{2,1,0:T(8,128)(2,1)}, u32[]{:S(2)}) copy-start(bf16[1,320,64]{2,1,0:T(8,128)(2,1)} %copy.23) | copy-start | bytes 122884
  146.6 8.7 %copy-start.23 = (bf16[576,512]{1,0:T(8,128)(2,1)}, bf16[576,512]{1,0:T(8,128)(2,1)S(1)}, u32[]{:S(2)}) copy-start(bf16[576,512]{1,0:T(8,128)(2,1)S(1)} %collective-permute-done.11) | copy-start | bytes 1769476
  150.6 4.7 %copy-start.21 = (bf16[576,512]{1,0:T(8,128)(2,1)}, bf16[576,512]{1,0:T(8,128)(2,1)S(1)}, u32[]{:S(2)}) copy-start(bf16[576,512]{1,0:T(8,128)(2,1)S(1)} %collective-permute-done.12) | copy-start | bytes 1769476
  152.6 1.2 copy-start.3
  156.3 7.8 %copy-start.22 = (bf16[576,512]{1,0:T(8,128)(2,1)S(1)}, bf16[576,512]{1,0:T(8,128)(2,1)}, u32[]{:S(2)}) copy-start(bf16[576,512]{1,0:T(8,128)(2,1)} %copy-done.21) | copy-start | bytes 1769476
  156.3 29.0 %copy-start.4 = (bf16[576,512]{1,0:T(8,128)(2,1)S(1)}, bf16[576,512]{1,0:T(8,128)(2,1)}, u32[]{:S(2)}) copy-start(bf16[576,512]{1,0:T(8,128)(2,1)} %copy-done.3) | copy-start | bytes 1769476
  158.7 30.2 %copy-start.30 = (bf16[1152,512]{1,0:T(8,128)(2,1)}, bf16[1152,512]{1,0:T(8,128)(2,1)S(1)}, u32[]{:S(2)}) copy-start(bf16[1152,512]{1,0:T(8,128)(2,1)S(1)} %constant_dynamic-update-slice_fusion.20.near_0) | copy-start | bytes 3538948
  158.7 32.9 %copy-start.7 = (bf16[576,512]{1,0:T(8,128)(2,1)S(1)}, bf16[576,512]{1,0:T(8,128)(2,1)}, u32[]{:S(2)}) copy-start(bf16[576,512]{1,0:T(8,128)(2,1)} %copy-done.6) | copy-start | bytes 1769476
  158.7 28.3 %collective-permute-start.20 = (bf16[1152,512]{1,0:T(8,128)(2,1)S(1)}, bf16[1152,512]{1,0:T(8,128)(2,1)S(1)}, u32[]{:S(2)}, u32[]{:S(2)}) collective-permute-start(bf16[1152,512]{1,0:T(8,128)(2,1)S(1)} %constant_dynamic-update-slice_fusion.20.near_0), channel_id=1, source_target_pairs={{0,16},{16,32},{32,48},{48,0},{64,80},{80,96},{96,112},{112,64},{1... | collective-permute-start | bytes 3538952 | tf_op jit(solution)/shard_map/ppermute | solution.py:29
  158.8 29.1 %collective-permute-start.21 = (bf16[1152,512]{1,0:T(8,128)(2,1)S(1)}, bf16[1152,512]{1,0:T(8,128)(2,1)S(1)}, u32[]{:S(2)}, u32[]{:S(2)}) collective-permute-start(bf16[1152,512]{1,0:T(8,128)(2,1)S(1)} %constant_dynamic-update-slice_fusion.20.near_0), channel_id=1, source_target_pairs={{0,48},{16,0},{32,16},{48,32},{64,112},{80,64},{96,80},{112,96},{1... | collective-permute-start | bytes 3538952 | tf_op jit(solution)/shard_map/ppermute | solution.py:30
  162.4 20.1 %collective-permute-start.24 = (bf16[288,512]{1,0:T(8,128)(2,1)S(1)}, bf16[288,512]{1,0:T(8,128)(2,1)S(1)}, u32[]{:S(2)}, u32[]{:S(2)}) collective-permute-start(bf16[288,512]{1,0:T(8,128)(2,1)S(1)} %slice.114), channel_id=1, source_target_pairs={{0,64},{16,80},{32,96},{48,112},{64,128},{80,144},{96,160},{112,17... | collective-permute-start | bytes 884744 | tf_op jit(solution)/shard_map/ppermute | solution.py:31
  164.1 18.5 %collective-permute-start.25 = (bf16[288,512]{1,0:T(8,128)(2,1)S(1)}, bf16[288,512]{1,0:T(8,128)(2,1)S(1)}, u32[]{:S(2)}, u32[]{:S(2)}) collective-permute-start(bf16[288,512]{1,0:T(8,128)(2,1)S(1)} %slice.115), channel_id=1, source_target_pairs={{0,192},{16,208},{32,224},{48,240},{64,0},{80,16},{96,32},{112,48}... | collective-permute-start | bytes 884744 | tf_op jit(solution)/shard_map/ppermute | solution.py:32
  182.6 20.5 %copy-start.13 = (bf16[576,512]{1,0:T(8,128)(2,1)}, bf16[576,512]{1,0:T(8,128)(2,1)S(1)}, u32[]{:S(2)}) copy-start(bf16[576,512]{1,0:T(8,128)(2,1)S(1)} %constant_dynamic-update-slice_fusion.22.last_0) | copy-start | bytes 1769476
  182.6 16.7 %collective-permute-start.26 = (bf16[576,512]{1,0:T(8,128)(2,1)S(1)}, bf16[576,512]{1,0:T(8,128)(2,1)S(1)}, u32[]{:S(2)}, u32[]{:S(2)}) collective-permute-start(bf16[576,512]{1,0:T(8,128)(2,1)S(1)} %constant_dynamic-update-slice_fusion.22.last_0), channel_id=1, source_target_pairs={{0,16},{16,32},{32,48},{48,0},{64,80},{80,96},{96,112},{112,64},{1... | collective-permute-start | bytes 1769480 | tf_op jit(solution)/shard_map/ppermute | solution.py:29
  182.7 18.2 %collective-permute-start.27 = (bf16[576,512]{1,0:T(8,128)(2,1)S(1)}, bf16[576,512]{1,0:T(8,128)(2,1)S(1)}, u32[]{:S(2)}, u32[]{:S(2)}) collective-permute-start(bf16[576,512]{1,0:T(8,128)(2,1)S(1)} %constant_dynamic-update-slice_fusion.22.last_0), channel_id=1, source_target_pairs={{0,48},{16,0},{32,16},{48,32},{64,112},{80,64},{96,80},{112,96},{1... | collective-permute-start | bytes 1769480 | tf_op jit(solution)/shard_map/ppermute | solution.py:30
  185.4 20.3 %collective-permute-start.18 = (bf16[288,512]{1,0:T(8,128)(2,1)S(1)}, bf16[288,512]{1,0:T(8,128)(2,1)S(1)}, u32[]{:S(2)}, u32[]{:S(2)}) collective-permute-start(bf16[288,512]{1,0:T(8,128)(2,1)S(1)} %slice.110), channel_id=1, source_target_pairs={{0,16},{16,32},{32,48},{48,0},{64,80},{80,96},{96,112},{112,64},{1... | collective-permute-start | bytes 884744 | tf_op jit(solution)/shard_map/ppermute | solution.py:31
  187.0 18.7 %copy-start.28 = (bf16[1152,512]{1,0:T(8,128)(2,1)}, bf16[1152,512]{1,0:T(8,128)(2,1)S(1)}, u32[]{:S(2)}) copy-start(bf16[1152,512]{1,0:T(8,128)(2,1)S(1)} %collective-permute-done.20.near_1) | copy-start | bytes 3538948
  187.9 36.8 %collective-permute-start.22 = (bf16[576,512]{1,0:T(8,128)(2,1)}, bf16[576,512]{1,0:T(8,128)(2,1)}, u32[]{:S(2)}, u32[]{:S(2)}) collective-permute-start(bf16[576,512]{1,0:T(8,128)(2,1)} %slice.112), channel_id=1, source_target_pairs={{0,16},{16,32},{32,48},{48,0},{64,80},{80,96},{96,112},{112,64},{1... | collective-permute-start | bytes 1769480 | tf_op jit(solution)/shard_map/ppermute | solution.py:31
  187.9 17.8 %copy-start.29 = (bf16[1152,512]{1,0:T(8,128)(2,1)}, bf16[1152,512]{1,0:T(8,128)(2,1)S(1)}, u32[]{:S(2)}) copy-start(bf16[1152,512]{1,0:T(8,128)(2,1)S(1)} %collective-permute-done.21.near_2) | copy-start | bytes 3538948
  188.9 35.9 %collective-permute-start.23 = (bf16[576,512]{1,0:T(8,128)(2,1)}, bf16[576,512]{1,0:T(8,128)(2,1)}, u32[]{:S(2)}, u32[]{:S(2)}) collective-permute-start(bf16[576,512]{1,0:T(8,128)(2,1)} %slice.113), channel_id=1, source_target_pairs={{0,48},{16,0},{32,16},{48,32},{64,112},{80,64},{96,80},{112,96},{1... | collective-permute-start | bytes 1769480 | tf_op jit(solution)/shard_map/ppermute | solution.py:32
  199.4 18.1 %collective-permute-start.19 = (bf16[288,512]{1,0:T(8,128)(2,1)}, bf16[288,512]{1,0:T(8,128)(2,1)}, u32[]{:S(2)}, u32[]{:S(2)}) collective-permute-start(bf16[288,512]{1,0:T(8,128)(2,1)} %slice.111), channel_id=1, source_target_pairs={{0,48},{16,0},{32,16},{48,32},{64,112},{80,64},{96,80},{112,96},{1... | collective-permute-start | bytes 884744 | tf_op jit(solution)/shard_map/ppermute | solution.py:32
  200.9 23.8 %collective-permute-start.28 = (bf16[288,512]{1,0:T(8,128)(2,1)}, bf16[288,512]{1,0:T(8,128)(2,1)}, u32[]{:S(2)}, u32[]{:S(2)}) collective-permute-start(bf16[288,512]{1,0:T(8,128)(2,1)} %slice.116), channel_id=1, source_target_pairs={{0,16},{16,32},{32,48},{48,0},{64,80},{80,96},{96,112},{112,64},{1... | collective-permute-start | bytes 884744 | tf_op jit(solution)/shard_map/ppermute | solution.py:31
  206.4 18.3 %collective-permute-start.29 = (bf16[288,512]{1,0:T(8,128)(2,1)}, bf16[288,512]{1,0:T(8,128)(2,1)}, u32[]{:S(2)}, u32[]{:S(2)}) collective-permute-start(bf16[288,512]{1,0:T(8,128)(2,1)} %slice.117), channel_id=1, source_target_pairs={{0,48},{16,0},{32,16},{48,32},{64,112},{80,64},{96,80},{112,96},{1... | collective-permute-start | bytes 884744 | tf_op jit(solution)/shard_map/ppermute | solution.py:32
  224.8 1.1 copy-start.2
  225.9 1.1 copy-start.5
  226.9 1.1 copy-start.8
  228.0 1.1 copy-start.10
  229.1 1.1 copy-start.12
  230.1 1.1 copy-start.14
  231.2 1.0 copy-start.16
  (4 other events, 3.2 us)
Sparse Core Ops, SparseCore 0:
  23.7 65.4 all-gather.5
  156.5 56.1 all-gather.3
